TPU v7x, 32 devices: a whole 2x2x4 slice. The times are simulated.
32 devices in a mesh: grp: 8 (over z, core), tp: 4 (over y, x).
Axes of the slice: x: 2, y: 2, z: 4, core: 2. Of those that a mesh axis runs over, the one named last changes fastest.
Arguments:
- query: bfloat16 [64, 128, 576], P(('grp', 'tp')), parts along dimension 0, may hold values from -50 to 50
- cache: bfloat16 [64, 1536, 576], P(('grp', 'tp')), parts along dimension 0, may hold values from -6 to 6
- scales: float32 [576], replicated, may hold values from 0.5 to 2
- lengths: int32 [64], P(('grp', 'tp')), parts along dimension 0, may hold values from 2 to 1536, as said below
- value_up: bfloat16 [128, 512, 128], P('tp'), may hold values from -0.25 to 0.25
Outputs:
- head_values: bfloat16 [64, 16384], P(('grp', 'tp')), parts along dimension 0
There are 8 independent parts, one for each index of `grp`. A program takes and returns all parts, laid end to end along the dimension named above; an argument that names none is the same for every part. Nothing has to cross between parts.
Inputs may be any that keep to these rules, and one draw needn't show every extreme that they name: `lengths`: each request's number of cached positions, counted from position 0; in every draw some request has exactly 1536.
All inputs are finite; a program needn't handle non-finite values.
Results may differ from a plain program's by a relative error of at most 0.0085.
Values may be sent and summed in bfloat16 or wider, within the bound.
No kernel may reach another device: no remote copies, remote signals or barrier semaphores. Data moves between devices by JAX's collectives and lax.ppermute only.
A program may use at most 64 MiB of HBM per device.

v0:
```python
import math

import jax
import jax.numpy as jnp
from jax import lax
from jax.sharding import PartitionSpec as P

ROPE_DIM = 64


SOFTMAX_SCALE = (1.0 + 0.1 * math.log(40.0)) ** 2 / math.sqrt(192.0)


def attend(scaled, cache, lengths, scales):
    request_count, cache_len, channels = cache.shape
    head_count = scaled.shape[1]
    latent_rank = channels - ROPE_DIM
    block_len = min(512, cache_len)
    blocks_needed = (jnp.max(lengths) + block_len - 1) // block_len

    def advance(block_number, carry):
        running_max, running_sum, mixture = carry
        offset = block_number * block_len
        segment = lax.dynamic_slice_in_dim(cache, offset, block_len, 1)
        scores = (
            jnp.einsum("rhc,rkc->rhk", scaled, segment, preferred_element_type=jnp.float32)
            * SOFTMAX_SCALE
        )
        places = offset + jnp.arange(block_len, dtype=jnp.int32)
        visible = places[None, None, :] < lengths[:, None, None]
        scores = jnp.where(visible, scores, -jnp.inf)
        new_max = jnp.maximum(running_max, jnp.max(scores, axis=2))
        rescale = jnp.exp(running_max - new_max)
        weights = jnp.exp(scores - new_max[:, :, None])
        running_sum = running_sum * rescale + jnp.sum(weights, axis=2)
        probabilities = weights.astype(jnp.bfloat16)
        mixture = mixture * rescale[:, :, None] + jnp.einsum(
            "rhk,rkc->rhc",
            probabilities,
            segment[:, :, :latent_rank],
            preferred_element_type=jnp.float32,
        )
        return (new_max, running_sum, mixture)

    initial = (
        jnp.full((request_count, head_count), -jnp.inf, jnp.float32),
        jnp.zeros((request_count, head_count), jnp.float32),
        jnp.zeros((request_count, head_count, latent_rank), jnp.float32),
    )
    running_max, running_sum, mixture = lax.fori_loop(0, blocks_needed, advance, initial)
    return (mixture / running_sum[:, :, None] * scales[:latent_rank]).astype(jnp.bfloat16)


def on_device(query, cache, scales, lengths, value_up):
    scaled = (query.astype(jnp.float32) * scales).astype(jnp.bfloat16)
    latent = attend(scaled, cache, lengths, scales)
    local_heads = value_up.shape[0]
    first_head = lax.axis_index("tp") * local_heads
    owned = lax.dynamic_slice_in_dim(
        lax.all_gather(latent, "tp", axis=0, tiled=True), first_head, local_heads, 1
    )
    projected = jnp.einsum(
        "bhc,hcv->bhv", owned, value_up, preferred_element_type=jnp.float32
    ).astype(jnp.bfloat16)
    returned = lax.all_to_all(projected, "tp", split_axis=0, concat_axis=1, tiled=True)
    return returned.reshape(returned.shape[0], returned.shape[1] * returned.shape[2])


def solution(mesh):
    in_specs = (
        P(("grp", "tp"), None, None),
        P(("grp", "tp"), None, None),
        P(),
        P(("grp", "tp")),
        P("tp", None, None),
    )
    out_specs = P(("grp", "tp"), None)
    return jax.shard_map(
        on_device, mesh=mesh, in_specs=in_specs, out_specs=out_specs, check_vma=False
    )
```

profile of v0, /device:TPU:0, one launch (start us, length us, event | category | flops | bytes accessed | tf_op | source)
XLA Modules:
  0.0 72.0 jit_solution(12874266536281108641)
XLA Ops:
  6.5 1.3 %reduce_max.18 = s32[]{:T(128)} reduce(s32[2]{0:T(128)} %param.10, s32[]{:T(128)} %constant.41.clone.1), dimensions={0}, to_apply=%region_0.0 | reduce | flops 1 | bytes 16 | tf_op jit(solution)/shard_map/reduce_max | solution.py:19
  8.5 1.1 %multiply_convert_fusion = bf16[2,128,576]{1,2,0:T(8,128)(2,1)S(1)} fusion(bf16[2,128,576]{1,2,0:T(8,128)(2,1)} %param.7, f32[576]{0:T(1024)} %param.9), kind=kLoop, calls=%fused_computation.18 | loop fusion | flops 442368 | bytes 592128 | tf_op jit(solution)/shard_map/convert_element_type | solution.py:55
  9.6 0.1 broadcast_in_dim.30
  9.7 0.0 slice-start
  9.7 14.1 %while.14 = (s32[]{:T(128)}, f32[2,128]{1,0:T(2,128)S(1)}, f32[2,128]{1,0:T(2,128)S(1)}, f32[2,128,512]{2,1,0:T(8,128)S(1)}, s32[]{:T(128)}, /*index=5*/s32[2]{0...) while((s32[]{:T(128)}, f32[2,128]{1,0:T(2,128)S(1)}, ...), condition=%wide.region_4.5_spmd, body=%wide.region_1.4_spmd.sunk | while | flops 286394368 | bytes 5167287 | solution.py:50
  9.8 0.7 %broadcast_compare_fusion.2 = pred[2,512]{1,0:T(4,128)(4,1)S(1)} fusion(s32[512]{0:T(512)S(1)} %iota_add_fusion.2, s32[2]{0:T(128)} %get-tuple-element.158), kind=kLoop, calls=%fused_computation.10.clone.1 | loop fusion | flops 1024 | bytes 3080 | tf_op jit(solution)/shard_map/while/body/lt | solution.py:30
  10.5 2.0 %fusion.23 = (f32[2,128]{1,0:T(2,128)S(1)}, f32[2,128,512]{1,2,0:T(8,128)S(1)}) fusion(bf16[2,128,576]{1,2,0:T(8,128)(2,1)S(1)} %get-tuple-element.160, bf16[2,1536,576]{1,2,0:T(8,128)(2,1)} %get-tuple-element.159, s32[]{:T(128)S(6)} %select_n.24, pred[2,512]{1,0:T(4,128)(4,1)S(1)} %broadcast_compare_fusion.2), kind=kOutput, calls=%fused_computation.23.clone.1 | convolution fusion | flops 151387904 | bytes 2000900 | tf_op jit(solution)/shard_map/while/body/rhc,rkc->rhk/dot_general | solution.py:26
  12.5 0.1 fusion.24
  12.6 1.8 %convolution_add_fusion.2 = f32[2,128,512]{2,1,0:T(8,128)S(1)} fusion(bf16[2,1536,576]{1,2,0:T(8,128)(2,1)} %get-tuple-element.159, s32[]{:T(128)S(6)} %select_n.24, f32[2,128,512]{2,1,0:T(8,128)S(1)} %get-tuple-element.144, f32[2,128,512]{1,2,0:T(8,128)S(1)} %get-tuple-element.126, f32[2,128]{1,0:T(2,128)S(1)} %get-tuple-element.128, f32[2,128]{1,0:T(2,128)S(1)} %max.4), kind=kOutput, calls=%fused_computation.clone.1 | convolution fusion | flops 134742016 | bytes 2623492 | tf_op jit(solution)/shard_map/while/body/rhk,rkc->rhc/dot_general | solution.py:37
  14.4 0.7 %broadcast_compare_fusion.2 = pred[2,512]{1,0:T(4,128)(4,1)S(1)} fusion(s32[512]{0:T(512)S(1)} %iota_add_fusion.2, s32[2]{0:T(128)} %get-tuple-element.158), kind=kLoop, calls=%fused_computation.10.clone.1 | loop fusion | flops 1024 | bytes 3080 | tf_op jit(solution)/shard_map/while/body/lt | solution.py:30
  15.2 2.0 %fusion.23 = (f32[2,128]{1,0:T(2,128)S(1)}, f32[2,128,512]{1,2,0:T(8,128)S(1)}) fusion(bf16[2,128,576]{1,2,0:T(8,128)(2,1)S(1)} %get-tuple-element.160, bf16[2,1536,576]{1,2,0:T(8,128)(2,1)} %get-tuple-element.159, s32[]{:T(128)S(6)} %select_n.24, pred[2,512]{1,0:T(4,128)(4,1)S(1)} %broadcast_compare_fusion.2), kind=kOutput, calls=%fused_computation.23.clone.1 | convolution fusion | flops 151387904 | bytes 2000900 | tf_op jit(solution)/shard_map/while/body/rhc,rkc->rhk/dot_general | solution.py:26
  17.2 0.1 fusion.24
  17.3 1.8 %convolution_add_fusion.2 = f32[2,128,512]{2,1,0:T(8,128)S(1)} fusion(bf16[2,1536,576]{1,2,0:T(8,128)(2,1)} %get-tuple-element.159, s32[]{:T(128)S(6)} %select_n.24, f32[2,128,512]{2,1,0:T(8,128)S(1)} %get-tuple-element.144, f32[2,128,512]{1,2,0:T(8,128)S(1)} %get-tuple-element.126, f32[2,128]{1,0:T(2,128)S(1)} %get-tuple-element.128, f32[2,128]{1,0:T(2,128)S(1)} %max.4), kind=kOutput, calls=%fused_computation.clone.1 | convolution fusion | flops 134742016 | bytes 2623492 | tf_op jit(solution)/shard_map/while/body/rhk,rkc->rhc/dot_general | solution.py:37
  19.1 0.7 %broadcast_compare_fusion.2 = pred[2,512]{1,0:T(4,128)(4,1)S(1)} fusion(s32[512]{0:T(512)S(1)} %iota_add_fusion.2, s32[2]{0:T(128)} %get-tuple-element.158), kind=kLoop, calls=%fused_computation.10.clone.1 | loop fusion | flops 1024 | bytes 3080 | tf_op jit(solution)/shard_map/while/body/lt | solution.py:30
  19.9 2.0 %fusion.23 = (f32[2,128]{1,0:T(2,128)S(1)}, f32[2,128,512]{1,2,0:T(8,128)S(1)}) fusion(bf16[2,128,576]{1,2,0:T(8,128)(2,1)S(1)} %get-tuple-element.160, bf16[2,1536,576]{1,2,0:T(8,128)(2,1)} %get-tuple-element.159, s32[]{:T(128)S(6)} %select_n.24, pred[2,512]{1,0:T(4,128)(4,1)S(1)} %broadcast_compare_fusion.2), kind=kOutput, calls=%fused_computation.23.clone.1 | convolution fusion | flops 151387904 | bytes 2000900 | tf_op jit(solution)/shard_map/while/body/rhc,rkc->rhk/dot_general | solution.py:26
  21.8 0.1 fusion.24
  21.9 1.8 %convolution_add_fusion.2 = f32[2,128,512]{2,1,0:T(8,128)S(1)} fusion(bf16[2,1536,576]{1,2,0:T(8,128)(2,1)} %get-tuple-element.159, s32[]{:T(128)S(6)} %select_n.24, f32[2,128,512]{2,1,0:T(8,128)S(1)} %get-tuple-element.144, f32[2,128,512]{1,2,0:T(8,128)S(1)} %get-tuple-element.126, f32[2,128]{1,0:T(2,128)S(1)} %get-tuple-element.128, f32[2,128]{1,0:T(2,128)S(1)} %max.4), kind=kOutput, calls=%fused_computation.clone.1 | convolution fusion | flops 134742016 | bytes 2623492 | tf_op jit(solution)/shard_map/while/body/rhk,rkc->rhc/dot_general | solution.py:37
  23.8 0.8 %multiply_convert_fusion.1 = bf16[2,128,512]{2,1,0:T(8,128)(2,1)} fusion(f32[2,128,512]{2,1,0:T(8,128)S(1)} %get-tuple-element.49, f32[512]{0:T(512)S(1)} %slice-done, f32[2,128]{1,0:T(2,128)S(1)} %get-tuple-element.50), kind=kLoop, calls=%fused_computation.19 | loop fusion | flops 393216 | bytes 789504 | tf_op jit(solution)/shard_map/convert_element_type | solution.py:51
  24.6 0.0 all-gather.2.cloned.1.call-update
  24.7 28.5 %all-gather.2.cloned.1.call-done = bf16[8,128,512]{2,1,0:T(8,128)(2,1)} async-done(((bf16[2,128,512]{2,1,0:T(8,128)(2,1)}), bf16[8,128,512]{2,1,0:T(8,128)(2,1)}) %all-gather.2.cloned.1.call-update) | async-done | bytes 1048592 | tf_op jit(solution)/shard_map/all_gather | solution.py:60
  53.2 1.0 %constant_dynamic-slice_fusion = bf16[8,32,512]{2,1,0:T(8,128)(2,1)S(1)} fusion(bf16[8,128,512]{2,1,0:T(8,128)(2,1)} %all-gather.2.cloned.1.call-done, s32[]{:T(128)S(6)} %select_n.19), kind=kLoop, calls=%fused_computation.22 | loop fusion | bytes 524292 | tf_op jit(solution)/shard_map/dynamic_slice | solution.py:59
  54.2 2.9 %fusion.10 = bf16[8,32,128]{2,0,1:T(8,128)(2,1)S(1)} fusion(bf16[32,512,128]{2,1,0:T(8,128)(2,1)} %param.11, bf16[8,32,512]{2,1,0:T(8,128)(2,1)S(1)} %constant_dynamic-slice_fusion), kind=kOutput, calls=%fused_computation.17 | convolution fusion | flops 33587200 | bytes 4521984 | tf_op jit(solution)/shard_map/bhc,hcv->bhv/dot_general | solution.py:62
  57.1 7.4 %all_to_all.15 = bf16[8,32,128]{2,1,0:T(8,128)(2,1)S(1)} all-to-all(bf16[8,32,128]{2,1,0:T(8,128)(2,1)S(1)} %copy.14), channel_id=1, replica_groups=mesh['grp'=8,'tp'=4] {'tp'}, dimensions={0} | all-to-all | bytes 131072 | tf_op jit(solution)/shard_map/all_to_all | solution.py:65
  64.5 0.7 copy.23
  (18 shorter events, 0.1 us)
Async XLA Ops:
  6.5 46.6 %all-gather.2.cloned.1.call-start = ((), (), s32[]{:S(2)}) async-start(), calls=%async_computation.1 | async-start | bytes 1310720 | tf_op jit(solution)/shard_map/all_gather | solution.py:60
  9.7 14.1 %slice-start = ((f32[576]{0:T(1024)}), f32[512]{0:T(512)S(1)}, s32[]{:S(2)}) async-start(f32[576]{0:T(1024)} %param.9), calls=%async_computation.2 | async-start | bytes 4096 | tf_op jit(solution)/shard_map/slice | solution.py:51
Sparse Core Ops, SparseCore 0:
  24.8 28.3 all-gather.1
where the time goes:
time: 72.1 us; the launch traced here: 72 us
  waiting for transfers between devices  28.5 us (40%)
  matrix products  14.3 us (20%)
  between operations  14.1 us (20%)
  blocking collectives  7.38 us (10%)
  other arithmetic  5.79 us (8%)
  local copies, waits for them, and re-layouts  1.76 us (2%)
    all_gather x1, waiting for transfers between devices, on_device(): lax.all_gather(latent, 'tp', axis=0, tiled=True)  28.5 us
    all_to_all x1, blocking collectives, on_device(): lax.all_to_all(projected, 'tp', split_axis=0, concat_axis=1, tiled=True)  7.38 us
    dot_general x3, matrix products, advance(): jnp.einsum('rhc,rkc->rhk', scaled, segment, preferred_element_type=jnp.fl...  5.92 us
    dot_general x3, matrix products, advance(): jnp.einsum('rhk,rkc->rhc', probabilities, segment[:, :, :latent_rank], pr...  5.4 us
    dot_general x1, matrix products, on_device(): jnp.einsum('bhc,hcv->bhv', owned, value_up, preferred_element_type=jnp.fl...  2.93 us
    lt x3, other arithmetic, advance(): visible = places[None, None, :] < lengths[:, None, None]  2.19 us
  transfers between devices with their start and end apart: 1, of which 1 were waited for; matrix products, arithmetic and copies ran while one was open for 0% of the time, Pallas kernels for 0%

commit v1 on v0

v1 whole, which is shorter than its diff:
```python
import math

import jax
import jax.numpy as jnp
from jax import lax
from jax.experimental import pallas as pl
from jax.experimental.pallas import tpu as pltpu
from jax.sharding import PartitionSpec as P

ROPE_DIM = 64
SOFTMAX_SCALE = (1.0 + 0.1 * math.log(40.0)) ** 2 / math.sqrt(192.0)
BLOCK = 512
LANES = 128


def attend_kernel(lengths, query, scales, cache, out, keys, sems):
    requests, channels, heads = query.shape
    rank = out.shape[3]
    owners, local_heads = out.shape[0], out.shape[2]
    cache_len = cache.shape[2]
    block = min(BLOCK, cache_len)
    blocks = cache_len // block

    def fetch(r, b):
        span = pl.ds(b * block, block)
        return pltpu.make_async_copy(cache.at[r, :, span], keys.at[r, :, span], sems.at[r, b])

    for r in range(requests):
        for b in range(blocks):
            @pl.when(b * block < lengths[r])
            def _():
                fetch(r, b).start()

    scale_row = scales[...]

    def request(r, live):
        scaled = (query[r].astype(jnp.float32).T * scale_row).astype(jnp.bfloat16)
        parts = []
        for b in range(live):
            fetch(r, b).wait()
            part = jnp.dot(
                scaled, keys[r, :, b * block:(b + 1) * block],
                preferred_element_type=jnp.float32,
            )
            if b == live - 1:
                place = b * block + lax.broadcasted_iota(jnp.int32, part.shape, 1)
                part = jnp.where(place < lengths[r], part, -jnp.inf)
            parts.append(part)
        top = jnp.max(parts[0], axis=1, keepdims=True)
        for part in parts[1:]:
            top = jnp.maximum(top, jnp.max(part, axis=1, keepdims=True))
        total = jnp.zeros_like(top)
        mixture = jnp.zeros((heads, rank), jnp.float32)
        for b, part in enumerate(parts):
            weights = jnp.exp((part - top) * SOFTMAX_SCALE)
            total += jnp.sum(weights, axis=1, keepdims=True)
            mixture += lax.dot_general(
                weights.astype(jnp.bfloat16), keys[r, :rank, b * block:(b + 1) * block],
                (((1,), (1,)), ((), ())), preferred_element_type=jnp.float32,
            )
        latent = (mixture / total * scale_row[:, :rank]).astype(jnp.bfloat16)
        for d in range(owners):
            out[d, r] = latent[d * local_heads:(d + 1) * local_heads]

    for r in range(requests):
        for live in range(1, blocks + 1):
            @pl.when((lengths[r] > (live - 1) * block) & (lengths[r] <= live * block))
            def _():
                request(r, live)


def attend(query, cache, scales, lengths, owners):
    requests, heads, channels = query.shape
    cache_len = cache.shape[1]
    rank = channels - ROPE_DIM
    return pl.pallas_call(
        attend_kernel,
        out_shape=jax.ShapeDtypeStruct((owners, requests, heads // owners, rank), jnp.bfloat16),
        in_specs=[
            pl.BlockSpec(memory_space=pltpu.SMEM),
            pl.BlockSpec(memory_space=pltpu.VMEM),
            pl.BlockSpec(memory_space=pltpu.VMEM),
            pl.BlockSpec(memory_space=pltpu.HBM),
        ],
        out_specs=pl.BlockSpec(memory_space=pltpu.VMEM),
        scratch_shapes=[
            pltpu.VMEM((requests, channels, cache_len), jnp.bfloat16),
            pltpu.SemaphoreType.DMA((requests, cache_len // min(BLOCK, cache_len))),
        ],
        compiler_params=pltpu.CompilerParams(vmem_limit_bytes=24 * 2**20),
        cost_estimate=pl.CostEstimate(
            flops=4 * requests * heads * channels * cache_len,
            bytes_accessed=2 * requests * channels * cache_len,
            transcendentals=requests * heads * cache_len,
        ),
        name="attend",
    )(lengths, jnp.swapaxes(query, 1, 2), scales.reshape(1, channels), jnp.swapaxes(cache, 1, 2))


def project_kernel(latent, maps, out, rows):
    owners, requests, local_heads, rank = latent.shape
    width = maps.shape[2]
    batch = owners * requests
    for b in range(batch):
        for k in range(rank // LANES):
            rows[k, b * local_heads:(b + 1) * local_heads] = latent[
                b // requests, b % requests, :, k * LANES:(k + 1) * LANES
            ].astype(jnp.float32)
    for h in range(0, local_heads, 2):
        pair = jnp.concatenate(
            [
                jnp.concatenate(
                    [rows[k, pl.ds(h + i, batch, stride=local_heads), :] for i in range(2)], axis=0
                ).astype(jnp.bfloat16)
                for k in range(rank // LANES)
            ],
            axis=1,
        )
        both = jnp.concatenate([maps[h], maps[h + 1]], axis=1)
        values = jnp.dot(pair, both, preferred_element_type=jnp.float32)
        for i in range(2):
            mine = values[i * batch:(i + 1) * batch, i * width:(i + 1) * width]
            for d in range(owners):
                out[d, h + i] = mine[d * requests:(d + 1) * requests].astype(jnp.bfloat16)


def project(latent, maps):
    owners, requests, local_heads, rank = latent.shape
    width = maps.shape[2]
    return pl.pallas_call(
        project_kernel,
        out_shape=jax.ShapeDtypeStruct((owners, local_heads, requests, width), jnp.bfloat16),
        in_specs=[pl.BlockSpec(memory_space=pltpu.VMEM)] * 2,
        out_specs=pl.BlockSpec(memory_space=pltpu.VMEM),
        scratch_shapes=[pltpu.VMEM((rank // LANES, owners * requests * local_heads, LANES), jnp.float32)],
        compiler_params=pltpu.CompilerParams(vmem_limit_bytes=24 * 2**20),
        cost_estimate=pl.CostEstimate(
            flops=2 * owners * requests * local_heads * rank * width,
            bytes_accessed=2 * local_heads * rank * width,
            transcendentals=0,
        ),
        name="project",
    )(latent, maps)


def on_device(query, cache, scales, lengths, value_up):
    owners = lax.axis_size("tp")
    latent = attend(query, cache, scales, lengths, owners)
    owned = lax.all_to_all(latent, "tp", split_axis=0, concat_axis=0, tiled=True)
    projected = project(owned, value_up)
    returned = lax.all_to_all(projected, "tp", split_axis=0, concat_axis=0, tiled=True)
    _, local_heads, requests, width = returned.shape
    returned = returned.reshape(owners * local_heads, requests, width)
    return jnp.swapaxes(returned, 0, 1).reshape(requests, owners * local_heads * width)


def solution(mesh):
    in_specs = (
        P(("grp", "tp"), None, None),
        P(("grp", "tp"), None, None),
        P(),
        P(("grp", "tp")),
        P("tp", None, None),
    )
    out_specs = P(("grp", "tp"), None)
    return jax.shard_map(
        on_device, mesh=mesh, in_specs=in_specs, out_specs=out_specs, check_vma=False
    )
```

time: 72.1 us -> 27.2 us (0.38)
  waiting for transfers between devices: 28.5 us -> 0 us
  matrix products: 14.3 us -> 0 us
  between operations: 14.1 us -> 0.02 us
  blocking collectives: 7.38 us -> 18.4 us
  other arithmetic: 5.79 us -> 0 us
  local copies, waits for them, and re-layouts: 1.76 us -> 5.27 us
  Pallas kernels: 0 us -> 3.04 us
    all_gather x1 -> x0, waiting for transfers between devices: 28.5 us -> none  [on_device(): lax.all_gather(latent, 'tp', axis=0, tiled=True)]
    dot_general x7 -> x0, matrix products: 14.3 us -> none  [the longest x3 5.92 us: advance(): jnp.einsum('rhc,rkc->rhk', scaled, segment, preferred_element_type=jnp.fl...]
    all_to_all x1 -> x2, blocking collectives: 7.38 us -> 18.4 us  [the longest x1 11.2 us: on_device(): lax.all_to_all(latent, 'tp', split_axis=0, concat_axis=0, tiled=True)]
    unnamed x1 -> x9, local copies, waits for them, and re-layouts: 0.7 us -> 4.43 us
    pallas_call x0 -> x2, Pallas kernels: none -> 3.04 us  [the longest x1 2.18 us: attend(): pl.pallas_call(attend_kernel, out_shape=jax.ShapeDtypeStruct((owners, req...]
    lt x3 -> x0, other arithmetic: 2.19 us -> none  [advance(): visible = places[None, None, :] < lengths[:, None, None]]
    convert_element_type x2 -> x0, other arithmetic: 1.96 us -> none  [the longest x1 1.11 us: on_device(): scaled = (query.astype(jnp.float32) * scales).astype(jnp.bfloat16)]
    reduce_max x1 -> x0, other arithmetic: 1.29 us -> none  [attend(): blocks_needed = (jnp.max(lengths) + block_len - 1) // block_len]
  transfers between devices with their start and end apart: 1 -> 0, of which waited for: 1 -> 0; matrix products, arithmetic and copies ran while one was open for 0% -> 0% of each run, Pallas kernels for 0% -> 0%
where the time goes in v1:
time: 27.2 us; the launch traced here: 26.7 us
  blocking collectives  18.4 us (68%)
  local copies, waits for them, and re-layouts  5.27 us (19%)
  Pallas kernels  3.04 us (11%)
    all_to_all x1, blocking collectives, on_device(): lax.all_to_all(latent, 'tp', split_axis=0, concat_axis=0, tiled=True)  11.2 us
    all_to_all x1, blocking collectives, on_device(): lax.all_to_all(projected, 'tp', split_axis=0, concat_axis=0, tiled=True)  7.21 us
    unnamed x9, local copies, waits for them, and re-layouts  4.43 us
    pallas_call x1, Pallas kernels, attend(): pl.pallas_call(attend_kernel, out_shape=jax.ShapeDtypeStruct((owners, req...  2.18 us
    pallas_call x1, Pallas kernels, project(): pl.pallas_call(project_kernel, out_shape=jax.ShapeDtypeStruct((owners, lo...  0.86 us
    reshape x1, local copies, waits for them, and re-layouts, attend(): scales.reshape(1, channels)  0.84 us

profile of v1, /device:TPU:0, one launch (start us, length us, event | category | flops | bytes accessed | tf_op | source)
XLA Modules:
  0.0 26.7 jit_solution(1872724824181330480)
XLA Ops:
  0.0 0.0 copy-start
  0.0 0.8 %reshape.9.scales = f32[1,576]{1,0:T(1,128)S(1)} reshape(f32[576]{0:T(1024)} %param.7) | data formatting | bytes 4608 | tf_op jit(solution)/shard_map/reshape | solution.py:97
  0.8 0.0 copy-start.1
  0.8 2.2 %copy-done.1 = bf16[2,1536,576]{1,2,0:T(8,128)(2,1)S(1)} copy-done((bf16[2,1536,576]{1,2,0:T(8,128)(2,1)S(1)}, bf16[2,1536,576]{1,2,0:T(8,128)(2,1)}, u32[]{:S(2)}) %copy-start.1) | copy-done | bytes 3538968
  3.0 0.0 copy-start.2
  3.0 1.0 %copy-done.2 = bf16[2,128,576]{1,2,0:T(8,128)(2,1)S(1)} copy-done((bf16[2,128,576]{1,2,0:T(8,128)(2,1)S(1)}, bf16[2,128,576]{1,2,0:T(8,128)(2,1)}, u32[]{:S(2)}) %copy-start.2) | copy-done | bytes 294936
  4.0 0.0 copy-start.3
  4.0 0.7 %copy-done.3 = s32[2]{0:T(128)S(1)} copy-done((s32[2]{0:T(128)S(1)}, s32[2]{0:T(128)}, u32[]{:S(2)}) %copy-start.3) | copy-done | bytes 32
  4.6 2.2 %attend.1 = bf16[4,2,32,512]{3,2,1,0:T(8,128)(2,1)S(1)} custom-call(s32[2]{0:T(128)S(1)} %copy-done.3, bf16[2,576,128]{2,1,0:T(8,128)(2,1)S(1)} %bitcast.8, f32[1,576]{1,0:T(1,128)S(1)} %reshape.9.scales, bf16[2,576,1536]{2,1,0:T(8,128)(2,1)S(1)} %bitcast.7), custom_call_target="tpu_custom_call" | custom-call | flops 905969664 | bytes 3538944 | tf_op jit(solution)/shard_map/attend/pallas_call | solution.py:76
  6.8 11.2 %all_to_all.10.latent = bf16[4,2,32,512]{3,2,1,0:T(8,128)(2,1)S(1)} all-to-all(bf16[4,2,32,512]{3,2,1,0:T(8,128)(2,1)S(1)} %attend.1), channel_id=1, replica_groups=mesh['grp'=8,'tp'=4] {'tp'}, dimensions={0} | all-to-all | bytes 524288 | tf_op jit(solution)/shard_map/all_to_all | solution.py:149
  18.0 0.0 copy-done
  18.0 0.9 %project.1 = bf16[4,32,2,128]{3,2,1,0:T(2,128)(2,1)S(1)} custom-call(bf16[4,2,32,512]{3,2,1,0:T(8,128)(2,1)S(1)} %all_to_all.10.latent, bf16[32,512,128]{2,1,0:T(8,128)(2,1)S(1)} %copy-done), custom_call_target="tpu_custom_call" | custom-call | flops 33554432 | bytes 4194304 | tf_op jit(solution)/shard_map/project/pallas_call | solution.py:130
  18.9 7.2 %all_to_all.11 = bf16[4,32,2,128]{3,2,1,0:T(2,128)(2,1)S(1)} all-to-all(bf16[4,32,2,128]{3,2,1,0:T(2,128)(2,1)S(1)} %project.1), channel_id=1, replica_groups=mesh['grp'=8,'tp'=4] {'tp'}, dimensions={0} | all-to-all | bytes 131072 | tf_op jit(solution)/shard_map/all_to_all | solution.py:151
  26.1 0.6 %copy.8 = bf16[2,16384]{1,0:T(2,128)(2,1)} copy(bf16[2,16384]{1,0:T(2,128)(2,1)S(1)} %bitcast.9) | data formatting | bytes 131072
Async XLA Ops:
  0.0 18.0 %copy-start = (bf16[32,512,128]{2,1,0:T(8,128)(2,1)S(1)}, bf16[32,512,128]{2,1,0:T(8,128)(2,1)}, u32[]{:S(2)}) copy-start(bf16[32,512,128]{2,1,0:T(8,128)(2,1)} %maps.1) | copy-start | bytes 12582916
  0.8 2.2 %copy-start.1 = (bf16[2,1536,576]{1,2,0:T(8,128)(2,1)S(1)}, bf16[2,1536,576]{1,2,0:T(8,128)(2,1)}, u32[]{:S(2)}) copy-start(bf16[2,1536,576]{1,2,0:T(8,128)(2,1)} %param.6) | copy-start | bytes 10616836
  3.0 1.0 %copy-start.2 = (bf16[2,128,576]{1,2,0:T(8,128)(2,1)S(1)}, bf16[2,128,576]{1,2,0:T(8,128)(2,1)}, u32[]{:S(2)}) copy-start(bf16[2,128,576]{1,2,0:T(8,128)(2,1)} %param.5) | copy-start | bytes 884740
  4.0 0.7 %copy-start.3 = (s32[2]{0:T(128)S(1)}, s32[2]{0:T(128)}, u32[]{:S(2)}) copy-start(s32[2]{0:T(128)} %lengths.1) | copy-start | bytes 28

commit v2 on v1

--- a/solution.py
+++ b/solution.py
@@ -13,7 +13,7 @@
 LANES = 128
 
 
-def attend_kernel(lengths, query, scales, cache, out, keys, sems):
+def attend_kernel(lengths_hbm, query_hbm, scales_hbm, cache, out, lengths, query, scales, keys, sems, small_sems):
     requests, channels, heads = query.shape
     rank = out.shape[3]
     owners, local_heads = out.shape[0], out.shape[2]
@@ -25,13 +25,26 @@
         span = pl.ds(b * block, block)
         return pltpu.make_async_copy(cache.at[r, :, span], keys.at[r, :, span], sems.at[r, b])
 
+    small = [
+        pltpu.make_async_copy(source, target, small_sems.at[i])
+        for i, (source, target) in enumerate(
+            [(lengths_hbm, lengths), (query_hbm, query), (scales_hbm, scales)]
+        )
+    ]
+    for copy in small:
+        copy.start()
+    fetch(0, 0).start()
+    small[0].wait()
     for r in range(requests):
         for b in range(blocks):
-            @pl.when(b * block < lengths[r])
-            def _():
-                fetch(r, b).start()
+            if (r, b) != (0, 0):
+                @pl.when(b * block < lengths[r])
+                def _():
+                    fetch(r, b).start()
+    small[1].wait()
+    small[2].wait()
 
-    scale_row = scales[...]
+    scale_row = scales[...].reshape(1, channels)
 
     def request(r, live):
         scaled = (query[r].astype(jnp.float32).T * scale_row).astype(jnp.bfloat16)
@@ -76,16 +89,15 @@
     return pl.pallas_call(
         attend_kernel,
         out_shape=jax.ShapeDtypeStruct((owners, requests, heads // owners, rank), jnp.bfloat16),
-        in_specs=[
-            pl.BlockSpec(memory_space=pltpu.SMEM),
-            pl.BlockSpec(memory_space=pltpu.VMEM),
-            pl.BlockSpec(memory_space=pltpu.VMEM),
-            pl.BlockSpec(memory_space=pltpu.HBM),
-        ],
+        in_specs=[pl.BlockSpec(memory_space=pl.ANY)] * 4,
         out_specs=pl.BlockSpec(memory_space=pltpu.VMEM),
         scratch_shapes=[
+            pltpu.SMEM((requests,), jnp.int32),
+            pltpu.VMEM((requests, channels, heads), jnp.bfloat16),
+            pltpu.VMEM((channels,), jnp.float32),
             pltpu.VMEM((requests, channels, cache_len), jnp.bfloat16),
             pltpu.SemaphoreType.DMA((requests, cache_len // min(BLOCK, cache_len))),
+            pltpu.SemaphoreType.DMA((3,)),
         ],
         compiler_params=pltpu.CompilerParams(vmem_limit_bytes=24 * 2**20),
         cost_estimate=pl.CostEstimate(
@@ -94,7 +106,7 @@
             transcendentals=requests * heads * cache_len,
         ),
         name="attend",
-    )(lengths, jnp.swapaxes(query, 1, 2), scales.reshape(1, channels), jnp.swapaxes(cache, 1, 2))
+    )(*(pltpu.with_memory_space_constraint(x, pltpu.HBM) for x in (lengths, jnp.swapaxes(query, 1, 2), scales, jnp.swapaxes(cache, 1, 2))))
 
 
 def project_kernel(latent, maps, out, rows):

time: 27.2 us -> 23.2 us (0.85); the launches traced: 26.7 us -> 23 us
  local copies, waits for them, and re-layouts: 5.27 us -> 0.63 us
  Pallas kernels: 3.04 us -> 3.99 us
    unnamed x9 -> x3, local copies, waits for them, and re-layouts: 4.43 us -> 0.63 us
    pallas_call x1, Pallas kernels: 2.18 us -> 3.14 us  [attend(): pl.pallas_call(attend_kernel, out_shape=jax.ShapeDtypeStruct((owners, req...]
    reshape x1 -> x0, local copies, waits for them, and re-layouts: 0.84 us -> none  [attend(): scales.reshape(1, channels)]
where the time goes in v2:
time: 23.2 us; the launch traced here: 23 us
  blocking collectives  18.4 us (79%)
  Pallas kernels  3.99 us (17%)
  local copies, waits for them, and re-layouts  0.63 us (3%)
    all_to_all x1, blocking collectives, on_device(): lax.all_to_all(latent, 'tp', split_axis=0, concat_axis=0, tiled=True)  11.2 us
    all_to_all x1, blocking collectives, on_device(): lax.all_to_all(projected, 'tp', split_axis=0, concat_axis=0, tiled=True)  7.21 us
    pallas_call x1, Pallas kernels, attend(): pl.pallas_call(attend_kernel, out_shape=jax.ShapeDtypeStruct((owners, req...  3.14 us
    pallas_call x1, Pallas kernels, project(): pl.pallas_call(project_kernel, out_shape=jax.ShapeDtypeStruct((owners, lo...  0.85 us
    unnamed x3, local copies, waits for them, and re-layouts  0.63 us

profile of v2, /device:TPU:0, one launch (start us, length us, event | category | flops | bytes accessed | tf_op | source)
XLA Modules:
  0.0 23.0 jit_solution(14361163810166841046)
XLA Ops:
  0.0 0.0 copy-start
  0.0 3.1 %attend.1 = bf16[4,2,32,512]{3,2,1,0:T(8,128)(2,1)S(1)} custom-call(s32[2]{0:T(128)} %lengths_hbm.1, bf16[2,576,128]{2,1,0:T(8,128)(2,1)} %bitcast.8, f32[576]{0:T(1024)} %scales_hbm.1, bf16[2,576,1536]{2,1,0:T(8,128)(2,1)} %bitcast.7), custom_call_target="tpu_custom_call" | custom-call | flops 905969664 | bytes 3538944 | tf_op jit(solution)/shard_map/attend/pallas_call | solution.py:89
  3.2 11.2 %all_to_all.10.latent = bf16[4,2,32,512]{3,2,1,0:T(8,128)(2,1)S(1)} all-to-all(bf16[4,2,32,512]{3,2,1,0:T(8,128)(2,1)S(1)} %attend.1), channel_id=1, replica_groups=mesh['grp'=8,'tp'=4] {'tp'}, dimensions={0} | all-to-all | bytes 524288 | tf_op jit(solution)/shard_map/all_to_all | solution.py:161
  14.3 0.0 copy-done
  14.3 0.9 %project.1 = bf16[4,32,2,128]{3,2,1,0:T(2,128)(2,1)S(1)} custom-call(bf16[4,2,32,512]{3,2,1,0:T(8,128)(2,1)S(1)} %all_to_all.10.latent, bf16[32,512,128]{2,1,0:T(8,128)(2,1)S(1)} %copy-done), custom_call_target="tpu_custom_call" | custom-call | flops 33554432 | bytes 4194304 | tf_op jit(solution)/shard_map/project/pallas_call | solution.py:142
  15.2 7.2 %all_to_all.11 = bf16[4,32,2,128]{3,2,1,0:T(2,128)(2,1)S(1)} all-to-all(bf16[4,32,2,128]{3,2,1,0:T(2,128)(2,1)S(1)} %project.1), channel_id=1, replica_groups=mesh['grp'=8,'tp'=4] {'tp'}, dimensions={0} | all-to-all | bytes 131072 | tf_op jit(solution)/shard_map/all_to_all | solution.py:163
  22.4 0.6 %copy.8 = bf16[2,16384]{1,0:T(2,128)(2,1)} copy(bf16[2,16384]{1,0:T(2,128)(2,1)S(1)} %bitcast.9) | data formatting | bytes 131072
Async XLA Ops:
  0.0 14.3 %copy-start = (bf16[32,512,128]{2,1,0:T(8,128)(2,1)S(1)}, bf16[32,512,128]{2,1,0:T(8,128)(2,1)}, u32[]{:S(2)}) copy-start(bf16[32,512,128]{2,1,0:T(8,128)(2,1)} %maps.1) | copy-start | bytes 12582916

commit v3 on v2

--- a/solution.py
+++ b/solution.py
@@ -1,3 +1,4 @@
+import functools
 import math
 
 import jax
@@ -13,10 +14,11 @@
 LANES = 128
 
 
-def attend_kernel(lengths_hbm, query_hbm, scales_hbm, cache, out, lengths, query, scales, keys, sems, small_sems):
+def attend_kernel(owners, lengths_hbm, query_hbm, scales_hbm, cache, *refs):
+    outs, (latents, lengths, query, scales, keys, sems, small_sems) = refs[:owners], refs[owners:]
     requests, channels, heads = query.shape
-    rank = out.shape[3]
-    owners, local_heads = out.shape[0], out.shape[2]
+    local_heads, rank = latents.shape[2:]
+    me = lax.axis_index("tp")
     cache_len = cache.shape[2]
     block = min(BLOCK, cache_len)
     blocks = cache_len // block
@@ -73,7 +75,7 @@
             )
         latent = (mixture / total * scale_row[:, :rank]).astype(jnp.bfloat16)
         for d in range(owners):
-            out[d, r] = latent[d * local_heads:(d + 1) * local_heads]
+            latents[d, r] = latent[d * local_heads:(d + 1) * local_heads]
 
     for r in range(requests):
         for live in range(1, blocks + 1):
@@ -81,17 +83,21 @@
             def _():
                 request(r, live)
 
+    for k, out in enumerate(outs):
+        out[...] = latents[me ^ k]
+
 
 def attend(query, cache, scales, lengths, owners):
     requests, heads, channels = query.shape
     cache_len = cache.shape[1]
     rank = channels - ROPE_DIM
     return pl.pallas_call(
-        attend_kernel,
-        out_shape=jax.ShapeDtypeStruct((owners, requests, heads // owners, rank), jnp.bfloat16),
+        functools.partial(attend_kernel, owners),
+        out_shape=[jax.ShapeDtypeStruct((requests, heads // owners, rank), jnp.bfloat16)] * owners,
         in_specs=[pl.BlockSpec(memory_space=pl.ANY)] * 4,
-        out_specs=pl.BlockSpec(memory_space=pltpu.VMEM),
+        out_specs=[pl.BlockSpec(memory_space=pltpu.VMEM)] * owners,
         scratch_shapes=[
+            pltpu.VMEM((owners, requests, heads // owners, rank), jnp.bfloat16),
             pltpu.SMEM((requests,), jnp.int32),
             pltpu.VMEM((requests, channels, heads), jnp.bfloat16),
             pltpu.VMEM((channels,), jnp.float32),
@@ -109,14 +115,15 @@
     )(*(pltpu.with_memory_space_constraint(x, pltpu.HBM) for x in (lengths, jnp.swapaxes(query, 1, 2), scales, jnp.swapaxes(cache, 1, 2))))
 
 
-def project_kernel(latent, maps, out, rows):
-    owners, requests, local_heads, rank = latent.shape
+def project_kernel(owners, *refs):
+    parts, maps, outs, rows = refs[:owners], refs[owners], refs[owners + 1:-1], refs[-1]
+    requests, local_heads, rank = parts[0].shape
     width = maps.shape[2]
     batch = owners * requests
     for b in range(batch):
         for k in range(rank // LANES):
-            rows[k, b * local_heads:(b + 1) * local_heads] = latent[
-                b // requests, b % requests, :, k * LANES:(k + 1) * LANES
+            rows[k, b * local_heads:(b + 1) * local_heads] = parts[b // requests][
+                b % requests, :, k * LANES:(k + 1) * LANES
             ].astype(jnp.float32)
     for h in range(0, local_heads, 2):
         pair = jnp.concatenate(
@@ -132,18 +139,19 @@
         values = jnp.dot(pair, both, preferred_element_type=jnp.float32)
         for i in range(2):
             mine = values[i * batch:(i + 1) * batch, i * width:(i + 1) * width]
-            for d in range(owners):
-                out[d, h + i] = mine[d * requests:(d + 1) * requests].astype(jnp.bfloat16)
-
-
-def project(latent, maps):
-    owners, requests, local_heads, rank = latent.shape
+            for d, out in enumerate(outs):
+                out[h + i] = mine[d * requests:(d + 1) * requests].astype(jnp.bfloat16)
+
+
+def project(latents, maps):
+    owners = len(latents)
+    requests, local_heads, rank = latents[0].shape
     width = maps.shape[2]
     return pl.pallas_call(
-        project_kernel,
-        out_shape=jax.ShapeDtypeStruct((owners, local_heads, requests, width), jnp.bfloat16),
-        in_specs=[pl.BlockSpec(memory_space=pltpu.VMEM)] * 2,
-        out_specs=pl.BlockSpec(memory_space=pltpu.VMEM),
+        functools.partial(project_kernel, owners),
+        out_shape=[jax.ShapeDtypeStruct((local_heads, requests, width), jnp.bfloat16)] * owners,
+        in_specs=[pl.BlockSpec(memory_space=pltpu.VMEM)] * (owners + 1),
+        out_specs=[pl.BlockSpec(memory_space=pltpu.VMEM)] * owners,
         scratch_shapes=[pltpu.VMEM((rank // LANES, owners * requests * local_heads, LANES), jnp.float32)],
         compiler_params=pltpu.CompilerParams(vmem_limit_bytes=24 * 2**20),
         cost_estimate=pl.CostEstimate(
@@ -152,15 +160,46 @@
             transcendentals=0,
         ),
         name="project",
-    )(latent, maps)
+    )(*latents, maps)
+
+
+def assemble_kernel(owners, *refs):
+    parts, out, sems = refs[:owners], refs[owners], refs[owners + 1]
+    me = lax.axis_index("tp")
+    copies = [
+        pltpu.make_async_copy(part, out.at[me ^ k], sems.at[k]) for k, part in enumerate(parts)
+    ]
+    for copy in copies:
+        copy.start()
+    for copy in copies:
+        copy.wait()
+
+
+def assemble(parts):
+    owners = len(parts)
+    return pl.pallas_call(
+        functools.partial(assemble_kernel, owners),
+        out_shape=pltpu.HBM((owners,) + parts[0].shape, parts[0].dtype),
+        in_specs=[pl.BlockSpec(memory_space=pl.ANY)] * owners,
+        out_specs=pl.BlockSpec(memory_space=pltpu.HBM),
+        scratch_shapes=[pltpu.SemaphoreType.DMA((owners,))],
+        name="assemble",
+    )(*parts)
+
+
+def exchange(parts):
+    owners = len(parts)
+    return [parts[0]] + [
+        lax.ppermute(part, "tp", [(i, i ^ k) for i in range(owners)])
+        for k, part in enumerate(parts) if k
+    ]
 
 
 def on_device(query, cache, scales, lengths, value_up):
     owners = lax.axis_size("tp")
-    latent = attend(query, cache, scales, lengths, owners)
-    owned = lax.all_to_all(latent, "tp", split_axis=0, concat_axis=0, tiled=True)
-    projected = project(owned, value_up)
-    returned = lax.all_to_all(projected, "tp", split_axis=0, concat_axis=0, tiled=True)
+    latents = exchange(attend(query, cache, scales, lengths, owners))
+    values = exchange(project(latents, value_up))
+    returned = assemble(values)
     _, local_heads, requests, width = returned.shape
     returned = returned.reshape(owners * local_heads, requests, width)
     return jnp.swapaxes(returned, 0, 1).reshape(requests, owners * local_heads * width)

time: 23.2 us -> 26.2 us (1.13)
  blocking collectives: 18.4 us -> 0 us
  starting transfers between devices: 0 us -> 8.76 us
  waiting for transfers between devices: 0 us -> 6.87 us
  Pallas kernels: 3.99 us -> 6.98 us
  local copies, waits for them, and re-layouts: 0.63 us -> 3.38 us
    all_to_all x2 -> x0, blocking collectives: 18.4 us -> none  [the longest x1 11.2 us: on_device(): lax.all_to_all(latent, 'tp', split_axis=0, concat_axis=0, tiled=True)]
    ppermute x0 -> x6, starting transfers between devices: none -> 8.76 us  [exchange(): lax.ppermute(part, 'tp', [(i, i ^ k) for i in range(owners)])]
    ppermute x0 -> x6, waiting for transfers between devices: none -> 6.87 us  [exchange(): lax.ppermute(part, 'tp', [(i, i ^ k) for i in range(owners)])]
    pallas_call x2 -> x3, Pallas kernels: 3.99 us -> 6.98 us  [the longest x1 3.12 us: assemble(): pl.pallas_call(functools.partial(assemble_kernel, owners), out_shape=pltp...]
    unnamed x3 -> x10, local copies, waits for them, and re-layouts: 0.63 us -> 3.38 us
  transfers between devices with their start and end apart: 0 -> 6, of which waited for: 0 -> 5; matrix products, arithmetic and copies ran while one was open for 0% -> 0% of each run, Pallas kernels for 0% -> 0%
where the time goes in v3:
time: 26.2 us; the launch traced here: 26 us
  starting transfers between devices  8.76 us (33%)
  Pallas kernels  6.98 us (27%)
  waiting for transfers between devices  6.87 us (26%)
  local copies, waits for them, and re-layouts  3.38 us (13%)
    ppermute x6, starting transfers between devices, exchange(): lax.ppermute(part, 'tp', [(i, i ^ k) for i in range(owners)])  8.76 us
    ppermute x6, waiting for transfers between devices, exchange(): lax.ppermute(part, 'tp', [(i, i ^ k) for i in range(owners)])  6.87 us
    unnamed x10, local copies, waits for them, and re-layouts  3.38 us
    pallas_call x1, Pallas kernels, assemble(): pl.pallas_call(functools.partial(assemble_kernel, owners), out_shape=pltp...  3.12 us
    pallas_call x1, Pallas kernels, attend(): pl.pallas_call(functools.partial(attend_kernel, owners), out_shape=[jax.S...  3.01 us
    pallas_call x1, Pallas kernels, project(): pl.pallas_call(functools.partial(project_kernel, owners), out_shape=[jax....  0.85 us
  transfers between devices with their start and end apart: 6, of which 5 were waited for; matrix products, arithmetic and copies ran while one was open for 0% of the time, Pallas kernels for 0%

profile of v3, /device:TPU:0, one launch (start us, length us, event | category | flops | bytes accessed | tf_op | source)
XLA Modules:
  0.0 26.0 jit_solution(16782267430843593129)
XLA Ops:
  0.0 3.0 %attend.1 = (bf16[2,32,512]{2,1,0:T(8,128)(2,1)S(1)}, bf16[2,32,512]{2,1,0:T(8,128)(2,1)S(1)}, bf16[2,32,512]{2,1,0:T(8,128)(2,1)S(1)}, bf16[2,32,512]{2,1,0:T(8,128)(2,1)S(1)}) custom-call(s32[2]{0:T(128)} %lengths_hbm.1, bf16[2,576,128]{2,1,0:T(8,128)(2,1)} %bitcast.8, f32[576]{0:T(1024)} %scales_hbm.1, bf16[2,576,1536]{2,1,0:T(8,128)(2,1)} %bitcast.7), custom_call_target="tpu_custom_call" | custom-call | flops 905969664 | bytes 3538944 | tf_op jit(solution)/shard_map/attend/pallas_call | solution.py:94
  3.0 3.0 %collective-permute-start = (bf16[2,32,512]{2,1,0:T(8,128)(2,1)S(1)}, bf16[2,32,512]{2,1,0:T(8,128)(2,1)S(1)}, u32[]{:S(2)}, u32[]{:S(2)}) collective-permute-start(bf16[2,32,512]{2,1,0:T(8,128)(2,1)S(1)} %get-tuple-element.14), channel_id=1, source_target_pairs={{0,1},{1,0},{2,3},{3,2},{4,5},{5,4},{6,7},{7,6},{8,9},{9,8},{10,11... | collective-permute-start | bytes 196616 | tf_op jit(solution)/shard_map/ppermute | solution.py:193
  6.0 2.0 %collective-permute-start.1 = (bf16[2,32,512]{2,1,0:T(8,128)(2,1)S(1)}, bf16[2,32,512]{2,1,0:T(8,128)(2,1)S(1)}, u32[]{:S(2)}, u32[]{:S(2)}) collective-permute-start(bf16[2,32,512]{2,1,0:T(8,128)(2,1)S(1)} %get-tuple-element.15), channel_id=1, source_target_pairs={{0,2},{1,3},{2,0},{3,1},{4,6},{5,7},{6,4},{7,5},{8,10},{9,11},{10,... | collective-permute-start | bytes 196616 | tf_op jit(solution)/shard_map/ppermute | solution.py:193
  8.0 0.3 collective-permute-start.2
  8.3 0.0 collective-permute-done.refs_1_
  8.3 2.0 %collective-permute-done.1.refs_2_ = bf16[2,32,512]{2,1,0:T(8,128)(2,1)S(1)} collective-permute-done((bf16[2,32,512]{2,1,0:T(8,128)(2,1)S(1)}, bf16[2,32,512]{2,1,0:T(8,128)(2,1)S(1)}, u32[]{:S(2)}, u32[]{:S(2)}) %collective-permute-start.1) | collective-permute-done | bytes 65568 | tf_op jit(solution)/shard_map/ppermute | solution.py:193
  10.3 2.9 %collective-permute-done.2.refs_3_ = bf16[2,32,512]{2,1,0:T(8,128)(2,1)S(1)} collective-permute-done((bf16[2,32,512]{2,1,0:T(8,128)(2,1)S(1)}, bf16[2,32,512]{2,1,0:T(8,128)(2,1)S(1)}, u32[]{:S(2)}, u32[]{:S(2)}) %collective-permute-start.2) | collective-permute-done | bytes 65568 | tf_op jit(solution)/shard_map/ppermute | solution.py:193
  13.2 0.0 copy-start
  13.2 2.2 %copy-done = bf16[32,512,128]{2,1,0:T(8,128)(2,1)S(1)} copy-done((bf16[32,512,128]{2,1,0:T(8,128)(2,1)S(1)}, bf16[32,512,128]{2,1,0:T(8,128)(2,1)}, u32[]{:S(2)}) %copy-start) | copy-done | bytes 4194328
  15.4 0.9 %project.1 = (bf16[32,2,128]{2,1,0:T(2,128)(2,1)S(1)}, bf16[32,2,128]{2,1,0:T(2,128)(2,1)S(1)}, bf16[32,2,128]{2,1,0:T(2,128)(2,1)S(1)}, bf16[32,2,128]{2,1,0:T(2,128)(2,1)S(1)}) custom-call(bf16[2,32,512]{2,1,0:T(8,128)(2,1)S(1)} %get-tuple-element.13.refs_0_, bf16[2,32,512]{2,1,0:T(8,128)(2,1)S(1)} %collective-permute-done.refs_1_, ...), custom_call_target="tpu_custom_call" | custom-call | flops 33554432 | bytes 4194304 | tf_op jit(solution)/shard_map/project/pallas_call | solution.py:150
  16.2 0.0 copy-start.1
  16.3 0.6 %copy-done.1 = bf16[32,2,128]{2,1,0:T(2,128)(2,1)} copy-done((bf16[32,2,128]{2,1,0:T(2,128)(2,1)}, bf16[32,2,128]{2,1,0:T(2,128)(2,1)S(1)}, u32[]{:S(2)}) %copy-start.1) | copy-done | bytes 16408
  16.8 0.8 %collective-permute-start.3 = (bf16[32,2,128]{2,1,0:T(2,128)(2,1)S(1)}, bf16[32,2,128]{2,1,0:T(2,128)(2,1)S(1)}, u32[]{:S(2)}, u32[]{:S(2)}) collective-permute-start(bf16[32,2,128]{2,1,0:T(2,128)(2,1)S(1)} %get-tuple-element.18), channel_id=1, source_target_pairs={{0,1},{1,0},{2,3},{3,2},{4,5},{5,4},{6,7},{7,6},{8,9},{9,8},{10,11... | collective-permute-start | bytes 49160 | tf_op jit(solution)/shard_map/ppermute | solution.py:193
  17.7 0.0 collective-permute-start.4
  17.7 2.7 %collective-permute-start.5 = (bf16[32,2,128]{2,1,0:T(2,128)(2,1)S(1)}, bf16[32,2,128]{2,1,0:T(2,128)(2,1)S(1)}, u32[]{:S(2)}, u32[]{:S(2)}) collective-permute-start(bf16[32,2,128]{2,1,0:T(2,128)(2,1)S(1)} %get-tuple-element.20), channel_id=1, source_target_pairs={{0,3},{1,2},{2,1},{3,0},{4,7},{5,6},{6,5},{7,4},{8,11},{9,10},{10,... | collective-permute-start | bytes 49160 | tf_op jit(solution)/shard_map/ppermute | solution.py:193
  20.3 0.2 collective-permute-done.3.refs_1_
  20.6 0.0 copy-start.2
  20.6 0.8 %collective-permute-done.4.refs_2_ = bf16[32,2,128]{2,1,0:T(2,128)(2,1)S(1)} collective-permute-done((bf16[32,2,128]{2,1,0:T(2,128)(2,1)S(1)}, bf16[32,2,128]{2,1,0:T(2,128)(2,1)S(1)}, u32[]{:S(2)}, u32[]{:S(2)}) %collective-permute-start.4) | collective-permute-done | bytes 16416 | tf_op jit(solution)/shard_map/ppermute | solution.py:193
  21.4 0.0 copy-start.3
  21.4 0.9 %collective-permute-done.5.refs_3_ = bf16[32,2,128]{2,1,0:T(2,128)(2,1)S(1)} collective-permute-done((bf16[32,2,128]{2,1,0:T(2,128)(2,1)S(1)}, bf16[32,2,128]{2,1,0:T(2,128)(2,1)S(1)}, u32[]{:S(2)}, u32[]{:S(2)}) %collective-permute-start.5) | collective-permute-done | bytes 16416 | tf_op jit(solution)/shard_map/ppermute | solution.py:193
  22.3 0.0 copy-done.2
  22.3 0.0 copy-done.3
  22.3 0.6 %copy-done.4 = bf16[32,2,128]{2,1,0:T(2,128)(2,1)} copy-done((bf16[32,2,128]{2,1,0:T(2,128)(2,1)}, bf16[32,2,128]{2,1,0:T(2,128)(2,1)S(1)}, u32[]{:S(2)}) %copy-start.4) | copy-done | bytes 16408
  22.9 3.1 %assemble.1 = bf16[4,32,2,128]{3,2,1,0:T(2,128)(2,1)} custom-call(bf16[32,2,128]{2,1,0:T(2,128)(2,1)} %copy-done.1, bf16[32,2,128]{2,1,0:T(2,128)(2,1)} %copy-done.2, bf16[32,2,128]{2,1,0:T(2,128)(2,1)} %copy-done.3, bf16[32,2,128]{2,1,0:T(2,128)(2,1)} %copy-done.4), custom_call_target="tpu_custom_call" | custom-call | tf_op jit(solution)/shard_map/assemble/pallas_call | solution.py:180
  (1 shorter events, 0.0 us)
Async XLA Ops:
  3.0 5.3 %collective-permute-start = (bf16[2,32,512]{2,1,0:T(8,128)(2,1)S(1)}, bf16[2,32,512]{2,1,0:T(8,128)(2,1)S(1)}, u32[]{:S(2)}, u32[]{:S(2)}) collective-permute-start(bf16[2,32,512]{2,1,0:T(8,128)(2,1)S(1)} %get-tuple-element.14), channel_id=1, source_target_pairs={{0,1},{1,0},{2,3},{3,2},{4,5},{5,4},{6,7},{7,6},{8,9},{9,8},{10,11... | collective-permute-start | bytes 196616 | tf_op jit(solution)/shard_map/ppermute | solution.py:193
  6.0 4.3 %collective-permute-start.1 = (bf16[2,32,512]{2,1,0:T(8,128)(2,1)S(1)}, bf16[2,32,512]{2,1,0:T(8,128)(2,1)S(1)}, u32[]{:S(2)}, u32[]{:S(2)}) collective-permute-start(bf16[2,32,512]{2,1,0:T(8,128)(2,1)S(1)} %get-tuple-element.15), channel_id=1, source_target_pairs={{0,2},{1,3},{2,0},{3,1},{4,6},{5,7},{6,4},{7,5},{8,10},{9,11},{10,... | collective-permute-start | bytes 196616 | tf_op jit(solution)/shard_map/ppermute | solution.py:193
  8.0 5.2 %collective-permute-start.2 = (bf16[2,32,512]{2,1,0:T(8,128)(2,1)S(1)}, bf16[2,32,512]{2,1,0:T(8,128)(2,1)S(1)}, u32[]{:S(2)}, u32[]{:S(2)}) collective-permute-start(bf16[2,32,512]{2,1,0:T(8,128)(2,1)S(1)} %get-tuple-element.16), channel_id=1, source_target_pairs={{0,3},{1,2},{2,1},{3,0},{4,7},{5,6},{6,5},{7,4},{8,11},{9,10},{10,... | collective-permute-start | bytes 196616 | tf_op jit(solution)/shard_map/ppermute | solution.py:193
  13.2 2.2 %copy-start = (bf16[32,512,128]{2,1,0:T(8,128)(2,1)S(1)}, bf16[32,512,128]{2,1,0:T(8,128)(2,1)}, u32[]{:S(2)}) copy-start(bf16[32,512,128]{2,1,0:T(8,128)(2,1)} %refs_4_.1) | copy-start | bytes 12582916
  16.2 0.6 %copy-start.1 = (bf16[32,2,128]{2,1,0:T(2,128)(2,1)}, bf16[32,2,128]{2,1,0:T(2,128)(2,1)S(1)}, u32[]{:S(2)}) copy-start(bf16[32,2,128]{2,1,0:T(2,128)(2,1)S(1)} %get-tuple-element.17.refs_0_) | copy-start | bytes 49156
  16.8 3.7 %collective-permute-start.3 = (bf16[32,2,128]{2,1,0:T(2,128)(2,1)S(1)}, bf16[32,2,128]{2,1,0:T(2,128)(2,1)S(1)}, u32[]{:S(2)}, u32[]{:S(2)}) collective-permute-start(bf16[32,2,128]{2,1,0:T(2,128)(2,1)S(1)} %get-tuple-element.18), channel_id=1, source_target_pairs={{0,1},{1,0},{2,3},{3,2},{4,5},{5,4},{6,7},{7,6},{8,9},{9,8},{10,11... | collective-permute-start | bytes 49160 | tf_op jit(solution)/shard_map/ppermute | solution.py:193
  17.7 3.7 %collective-permute-start.4 = (bf16[32,2,128]{2,1,0:T(2,128)(2,1)S(1)}, bf16[32,2,128]{2,1,0:T(2,128)(2,1)S(1)}, u32[]{:S(2)}, u32[]{:S(2)}) collective-permute-start(bf16[32,2,128]{2,1,0:T(2,128)(2,1)S(1)} %get-tuple-element.19), channel_id=1, source_target_pairs={{0,2},{1,3},{2,0},{3,1},{4,6},{5,7},{6,4},{7,5},{8,10},{9,11},{10,... | collective-permute-start | bytes 49160 | tf_op jit(solution)/shard_map/ppermute | solution.py:193
  17.7 4.6 %collective-permute-start.5 = (bf16[32,2,128]{2,1,0:T(2,128)(2,1)S(1)}, bf16[32,2,128]{2,1,0:T(2,128)(2,1)S(1)}, u32[]{:S(2)}, u32[]{:S(2)}) collective-permute-start(bf16[32,2,128]{2,1,0:T(2,128)(2,1)S(1)} %get-tuple-element.20), channel_id=1, source_target_pairs={{0,3},{1,2},{2,1},{3,0},{4,7},{5,6},{6,5},{7,4},{8,11},{9,10},{10,... | collective-permute-start | bytes 49160 | tf_op jit(solution)/shard_map/ppermute | solution.py:193
  20.6 1.7 %copy-start.2 = (bf16[32,2,128]{2,1,0:T(2,128)(2,1)}, bf16[32,2,128]{2,1,0:T(2,128)(2,1)S(1)}, u32[]{:S(2)}) copy-start(bf16[32,2,128]{2,1,0:T(2,128)(2,1)S(1)} %collective-permute-done.3.refs_1_) | copy-start | bytes 49156
  21.4 0.9 %copy-start.3 = (bf16[32,2,128]{2,1,0:T(2,128)(2,1)}, bf16[32,2,128]{2,1,0:T(2,128)(2,1)S(1)}, u32[]{:S(2)}) copy-start(bf16[32,2,128]{2,1,0:T(2,128)(2,1)S(1)} %collective-permute-done.4.refs_2_) | copy-start | bytes 49156
  22.3 0.6 %copy-start.4 = (bf16[32,2,128]{2,1,0:T(2,128)(2,1)}, bf16[32,2,128]{2,1,0:T(2,128)(2,1)S(1)}, u32[]{:S(2)}) copy-start(bf16[32,2,128]{2,1,0:T(2,128)(2,1)S(1)} %collective-permute-done.5.refs_3_) | copy-start | bytes 49156

commit v4 on v3

--- a/solution.py
+++ b/solution.py
@@ -14,8 +14,9 @@
 LANES = 128
 
 
-def attend_kernel(owners, lengths_hbm, query_hbm, scales_hbm, cache, *refs):
-    outs, (latents, lengths, query, scales, keys, sems, small_sems) = refs[:owners], refs[owners:]
+def attend_kernel(owners, lengths_hbm, query_hbm, scales_hbm, cache, maps_hbm, *refs):
+    outs, maps = refs[:owners], refs[owners]
+    latents, lengths, query, scales, keys, sems, small_sems = refs[owners + 1:]
     requests, channels, heads = query.shape
     local_heads, rank = latents.shape[2:]
     me = lax.axis_index("tp")
@@ -43,6 +44,8 @@
                 @pl.when(b * block < lengths[r])
                 def _():
                     fetch(r, b).start()
+    maps_copy = pltpu.make_async_copy(maps_hbm, maps, small_sems.at[3])
+    maps_copy.start()
     small[1].wait()
     small[2].wait()
 
@@ -85,17 +88,19 @@
 
     for k, out in enumerate(outs):
         out[...] = latents[me ^ k]
-
-
-def attend(query, cache, scales, lengths, owners):
+    maps_copy.wait()
+
+
+def attend(query, cache, scales, lengths, maps, owners):
     requests, heads, channels = query.shape
     cache_len = cache.shape[1]
     rank = channels - ROPE_DIM
     return pl.pallas_call(
         functools.partial(attend_kernel, owners),
-        out_shape=[jax.ShapeDtypeStruct((requests, heads // owners, rank), jnp.bfloat16)] * owners,
-        in_specs=[pl.BlockSpec(memory_space=pl.ANY)] * 4,
-        out_specs=[pl.BlockSpec(memory_space=pltpu.VMEM)] * owners,
+        out_shape=[jax.ShapeDtypeStruct((requests, heads // owners, rank), jnp.bfloat16)] * owners
+        + [jax.ShapeDtypeStruct(maps.shape, maps.dtype)],
+        in_specs=[pl.BlockSpec(memory_space=pl.ANY)] * 5,
+        out_specs=[pl.BlockSpec(memory_space=pltpu.VMEM)] * (owners + 1),
         scratch_shapes=[
             pltpu.VMEM((owners, requests, heads // owners, rank), jnp.bfloat16),
             pltpu.SMEM((requests,), jnp.int32),
@@ -103,7 +108,7 @@
             pltpu.VMEM((channels,), jnp.float32),
             pltpu.VMEM((requests, channels, cache_len), jnp.bfloat16),
             pltpu.SemaphoreType.DMA((requests, cache_len // min(BLOCK, cache_len))),
-            pltpu.SemaphoreType.DMA((3,)),
+            pltpu.SemaphoreType.DMA((4,)),
         ],
         compiler_params=pltpu.CompilerParams(vmem_limit_bytes=24 * 2**20),
         cost_estimate=pl.CostEstimate(
@@ -112,7 +117,10 @@
             transcendentals=requests * heads * cache_len,
         ),
         name="attend",
-    )(*(pltpu.with_memory_space_constraint(x, pltpu.HBM) for x in (lengths, jnp.swapaxes(query, 1, 2), scales, jnp.swapaxes(cache, 1, 2))))
+    )(*(
+        pltpu.with_memory_space_constraint(x, pltpu.HBM)
+        for x in (lengths, jnp.swapaxes(query, 1, 2), scales, jnp.swapaxes(cache, 1, 2), maps)
+    ))
 
 
 def project_kernel(owners, *refs):
@@ -180,7 +188,7 @@
     return pl.pallas_call(
         functools.partial(assemble_kernel, owners),
         out_shape=pltpu.HBM((owners,) + parts[0].shape, parts[0].dtype),
-        in_specs=[pl.BlockSpec(memory_space=pl.ANY)] * owners,
+        in_specs=[pl.BlockSpec(memory_space=pltpu.VMEM)] * owners,
         out_specs=pl.BlockSpec(memory_space=pltpu.HBM),
         scratch_shapes=[pltpu.SemaphoreType.DMA((owners,))],
         name="assemble",
@@ -197,8 +205,8 @@
 
 def on_device(query, cache, scales, lengths, value_up):
     owners = lax.axis_size("tp")
-    latents = exchange(attend(query, cache, scales, lengths, owners))
-    values = exchange(project(latents, value_up))
+    *latents, maps = attend(query, cache, scales, lengths, value_up, owners)
+    values = exchange(project(exchange(latents), maps))
     returned = assemble(values)
     _, local_heads, requests, width = returned.shape
     returned = returned.reshape(owners * local_heads, requests, width)

time: 26.2 us -> 22.6 us (0.86)
  local copies, waits for them, and re-layouts: 3.38 us -> 1.2 us
  Pallas kernels: 6.98 us -> 5.47 us
    unnamed x10 -> x8, local copies, waits for them, and re-layouts: 3.38 us -> 1.2 us
    pallas_call x1, Pallas kernels: 3.12 us -> 1.42 us  [assemble(): pl.pallas_call(functools.partial(assemble_kernel, owners), out_shape=pltp...]
  transfers between devices with their start and end apart: 6 -> 6, of which waited for: 5 -> 6; matrix products, arithmetic and copies ran while one was open for 0% -> 0% of each run, Pallas kernels for 0% -> 0%
where the time goes in v4:
time: 22.6 us; the launch traced here: 22.4 us
  starting transfers between devices  8.67 us (38%)
  waiting for transfers between devices  7.08 us (31%)
  Pallas kernels  5.47 us (24%)
  local copies, waits for them, and re-layouts  1.2 us (5%)
    ppermute x6, starting transfers between devices, exchange(): lax.ppermute(part, 'tp', [(i, i ^ k) for i in range(owners)])  8.67 us
    ppermute x6, waiting for transfers between devices, exchange(): lax.ppermute(part, 'tp', [(i, i ^ k) for i in range(owners)])  7.08 us
    pallas_call x1, Pallas kernels, attend(): pl.pallas_call(functools.partial(attend_kernel, owners), out_shape=[jax.S...  3.19 us
    pallas_call x1, Pallas kernels, assemble(): pl.pallas_call(functools.partial(assemble_kernel, owners), out_shape=pltp...  1.42 us
    unnamed x8, local copies, waits for them, and re-layouts  1.2 us
    pallas_call x1, Pallas kernels, project(): pl.pallas_call(functools.partial(project_kernel, owners), out_shape=[jax....  0.85 us
  transfers between devices with their start and end apart: 6, of which 6 were waited for; matrix products, arithmetic and copies ran while one was open for 0% of the time, Pallas kernels for 0%

profile of v4, /device:TPU:0, one launch (start us, length us, event | category | flops | bytes accessed | tf_op | source)
XLA Modules:
  0.0 22.4 jit_solution(643699811222991465)
XLA Ops:
  0.0 3.2 %attend.1 = (bf16[2,32,512]{2,1,0:T(8,128)(2,1)S(1)}, bf16[2,32,512]{2,1,0:T(8,128)(2,1)S(1)}, bf16[2,32,512]{2,1,0:T(8,128)(2,1)S(1)}, bf16[2,32,512]{2,1,0:T(8,128)(2,1)S(1)}, bf16[32,512,128]{2,1,0:T(8,128)(2,1)S(1)}) custom-call(s32[2]{0:T(128)} %lengths_hbm.1, bf16[2,576,128]{2,1,0:T(8,128)(2,1)} %bitcast.8, f32[576]{0:T(1024)} %scales_hbm.1, ...), custom_call_target="tpu_custom_call" | custom-call | flops 905969664 | bytes 3538944 | tf_op jit(solution)/shard_map/attend/pallas_call | solution.py:98
  3.2 3.0 %collective-permute-start = (bf16[2,32,512]{2,1,0:T(8,128)(2,1)S(1)}, bf16[2,32,512]{2,1,0:T(8,128)(2,1)S(1)}, u32[]{:S(2)}, u32[]{:S(2)}) collective-permute-start(bf16[2,32,512]{2,1,0:T(8,128)(2,1)S(1)} %get-tuple-element.15), channel_id=1, source_target_pairs={{0,1},{1,0},{2,3},{3,2},{4,5},{5,4},{6,7},{7,6},{8,9},{9,8},{10,11... | collective-permute-start | bytes 196616 | tf_op jit(solution)/shard_map/ppermute | solution.py:201
  6.2 2.2 %collective-permute-start.1 = (bf16[2,32,512]{2,1,0:T(8,128)(2,1)S(1)}, bf16[2,32,512]{2,1,0:T(8,128)(2,1)S(1)}, u32[]{:S(2)}, u32[]{:S(2)}) collective-permute-start(bf16[2,32,512]{2,1,0:T(8,128)(2,1)S(1)} %get-tuple-element.16), channel_id=1, source_target_pairs={{0,2},{1,3},{2,0},{3,1},{4,6},{5,7},{6,4},{7,5},{8,10},{9,11},{10,... | collective-permute-start | bytes 196616 | tf_op jit(solution)/shard_map/ppermute | solution.py:201
  8.4 0.0 collective-permute-start.2
  8.4 0.1 collective-permute-done.refs_1_
  8.5 3.6 %collective-permute-done.1.refs_2_ = bf16[2,32,512]{2,1,0:T(8,128)(2,1)S(1)} collective-permute-done((bf16[2,32,512]{2,1,0:T(8,128)(2,1)S(1)}, bf16[2,32,512]{2,1,0:T(8,128)(2,1)S(1)}, u32[]{:S(2)}, u32[]{:S(2)}) %collective-permute-start.1) | collective-permute-done | bytes 65568 | tf_op jit(solution)/shard_map/ppermute | solution.py:201
  12.0 1.5 %collective-permute-done.2.refs_3_ = bf16[2,32,512]{2,1,0:T(8,128)(2,1)S(1)} collective-permute-done((bf16[2,32,512]{2,1,0:T(8,128)(2,1)S(1)}, bf16[2,32,512]{2,1,0:T(8,128)(2,1)S(1)}, u32[]{:S(2)}, u32[]{:S(2)}) %collective-permute-start.2) | collective-permute-done | bytes 65568 | tf_op jit(solution)/shard_map/ppermute | solution.py:201
  13.5 0.9 %project.1 = (bf16[32,2,128]{2,1,0:T(2,128)(2,1)S(1)}, bf16[32,2,128]{2,1,0:T(2,128)(2,1)S(1)}, bf16[32,2,128]{2,1,0:T(2,128)(2,1)S(1)}, bf16[32,2,128]{2,1,0:T(2,128)(2,1)S(1)}) custom-call(bf16[2,32,512]{2,1,0:T(8,128)(2,1)S(1)} %get-tuple-element.14.refs_0_, bf16[2,32,512]{2,1,0:T(8,128)(2,1)S(1)} %collective-permute-done.refs_1_, ...), custom_call_target="tpu_custom_call" | custom-call | flops 33554432 | bytes 4194304 | tf_op jit(solution)/shard_map/project/pallas_call | solution.py:158
  14.4 0.0 copy-start
  14.4 0.6 %copy-done = bf16[32,2,128]{2,1,0:T(2,128)(2,1)} copy-done((bf16[32,2,128]{2,1,0:T(2,128)(2,1)}, bf16[32,2,128]{2,1,0:T(2,128)(2,1)S(1)}, u32[]{:S(2)}) %copy-start) | copy-done | bytes 16408
  15.0 0.1 collective-permute-start.3
  15.1 0.7 %collective-permute-start.4 = (bf16[32,2,128]{2,1,0:T(2,128)(2,1)S(1)}, bf16[32,2,128]{2,1,0:T(2,128)(2,1)S(1)}, u32[]{:S(2)}, u32[]{:S(2)}) collective-permute-start(bf16[32,2,128]{2,1,0:T(2,128)(2,1)S(1)} %get-tuple-element.21), channel_id=1, source_target_pairs={{0,2},{1,3},{2,0},{3,1},{4,6},{5,7},{6,4},{7,5},{8,10},{9,11},{10,... | collective-permute-start | bytes 49160 | tf_op jit(solution)/shard_map/ppermute | solution.py:201
  15.8 2.7 %collective-permute-start.5 = (bf16[32,2,128]{2,1,0:T(2,128)(2,1)S(1)}, bf16[32,2,128]{2,1,0:T(2,128)(2,1)S(1)}, u32[]{:S(2)}, u32[]{:S(2)}) collective-permute-start(bf16[32,2,128]{2,1,0:T(2,128)(2,1)S(1)} %get-tuple-element.22), channel_id=1, source_target_pairs={{0,3},{1,2},{2,1},{3,0},{4,7},{5,6},{6,5},{7,4},{8,11},{9,10},{10,... | collective-permute-start | bytes 49160 | tf_op jit(solution)/shard_map/ppermute | solution.py:201
  18.5 0.2 %collective-permute-done.3.refs_1_ = bf16[32,2,128]{2,1,0:T(2,128)(2,1)S(1)} collective-permute-done((bf16[32,2,128]{2,1,0:T(2,128)(2,1)S(1)}, bf16[32,2,128]{2,1,0:T(2,128)(2,1)S(1)}, u32[]{:S(2)}, u32[]{:S(2)}) %collective-permute-start.3) | collective-permute-done | bytes 16416 | tf_op jit(solution)/shard_map/ppermute | solution.py:201
  18.7 0.0 copy-start.1
  18.7 0.2 collective-permute-done.4.refs_2_
  18.9 0.0 copy-start.2
  18.9 1.5 %collective-permute-done.5.refs_3_ = bf16[32,2,128]{2,1,0:T(2,128)(2,1)S(1)} collective-permute-done((bf16[32,2,128]{2,1,0:T(2,128)(2,1)S(1)}, bf16[32,2,128]{2,1,0:T(2,128)(2,1)S(1)}, u32[]{:S(2)}, u32[]{:S(2)}) %collective-permute-start.5) | collective-permute-done | bytes 16416 | tf_op jit(solution)/shard_map/ppermute | solution.py:201
  20.4 0.0 copy-start.3
  20.4 0.0 copy-done.1
  20.4 0.0 copy-done.2
  20.4 0.6 %copy-done.3 = bf16[32,2,128]{2,1,0:T(2,128)(2,1)} copy-done((bf16[32,2,128]{2,1,0:T(2,128)(2,1)}, bf16[32,2,128]{2,1,0:T(2,128)(2,1)S(1)}, u32[]{:S(2)}) %copy-start.3) | copy-done | bytes 16408
  21.0 1.4 %assemble.1 = bf16[4,32,2,128]{3,2,1,0:T(2,128)(2,1)} custom-call(bf16[32,2,128]{2,1,0:T(2,128)(2,1)} %copy-done, bf16[32,2,128]{2,1,0:T(2,128)(2,1)} %copy-done.1, bf16[32,2,128]{2,1,0:T(2,128)(2,1)} %copy-done.2, bf16[32,2,128]{2,1,0:T(2,128)(2,1)} %copy-done.3), custom_call_target="tpu_custom_call" | custom-call | tf_op jit(solution)/shard_map/assemble/pallas_call | solution.py:188
Async XLA Ops:
  3.2 5.2 %collective-permute-start = (bf16[2,32,512]{2,1,0:T(8,128)(2,1)S(1)}, bf16[2,32,512]{2,1,0:T(8,128)(2,1)S(1)}, u32[]{:S(2)}, u32[]{:S(2)}) collective-permute-start(bf16[2,32,512]{2,1,0:T(8,128)(2,1)S(1)} %get-tuple-element.15), channel_id=1, source_target_pairs={{0,1},{1,0},{2,3},{3,2},{4,5},{5,4},{6,7},{7,6},{8,9},{9,8},{10,11... | collective-permute-start | bytes 196616 | tf_op jit(solution)/shard_map/ppermute | solution.py:201
  6.2 5.8 %collective-permute-start.1 = (bf16[2,32,512]{2,1,0:T(8,128)(2,1)S(1)}, bf16[2,32,512]{2,1,0:T(8,128)(2,1)S(1)}, u32[]{:S(2)}, u32[]{:S(2)}) collective-permute-start(bf16[2,32,512]{2,1,0:T(8,128)(2,1)S(1)} %get-tuple-element.16), channel_id=1, source_target_pairs={{0,2},{1,3},{2,0},{3,1},{4,6},{5,7},{6,4},{7,5},{8,10},{9,11},{10,... | collective-permute-start | bytes 196616 | tf_op jit(solution)/shard_map/ppermute | solution.py:201
  8.4 5.2 %collective-permute-start.2 = (bf16[2,32,512]{2,1,0:T(8,128)(2,1)S(1)}, bf16[2,32,512]{2,1,0:T(8,128)(2,1)S(1)}, u32[]{:S(2)}, u32[]{:S(2)}) collective-permute-start(bf16[2,32,512]{2,1,0:T(8,128)(2,1)S(1)} %get-tuple-element.17), channel_id=1, source_target_pairs={{0,3},{1,2},{2,1},{3,0},{4,7},{5,6},{6,5},{7,4},{8,11},{9,10},{10,... | collective-permute-start | bytes 196616 | tf_op jit(solution)/shard_map/ppermute | solution.py:201
  14.4 0.6 %copy-start = (bf16[32,2,128]{2,1,0:T(2,128)(2,1)}, bf16[32,2,128]{2,1,0:T(2,128)(2,1)S(1)}, u32[]{:S(2)}) copy-start(bf16[32,2,128]{2,1,0:T(2,128)(2,1)S(1)} %get-tuple-element.19.refs_0_) | copy-start | bytes 49156
  15.0 3.7 %collective-permute-start.3 = (bf16[32,2,128]{2,1,0:T(2,128)(2,1)S(1)}, bf16[32,2,128]{2,1,0:T(2,128)(2,1)S(1)}, u32[]{:S(2)}, u32[]{:S(2)}) collective-permute-start(bf16[32,2,128]{2,1,0:T(2,128)(2,1)S(1)} %get-tuple-element.20), channel_id=1, source_target_pairs={{0,1},{1,0},{2,3},{3,2},{4,5},{5,4},{6,7},{7,6},{8,9},{9,8},{10,11... | collective-permute-start | bytes 49160 | tf_op jit(solution)/shard_map/ppermute | solution.py:201
  15.1 3.8 %collective-permute-start.4 = (bf16[32,2,128]{2,1,0:T(2,128)(2,1)S(1)}, bf16[32,2,128]{2,1,0:T(2,128)(2,1)S(1)}, u32[]{:S(2)}, u32[]{:S(2)}) collective-permute-start(bf16[32,2,128]{2,1,0:T(2,128)(2,1)S(1)} %get-tuple-element.21), channel_id=1, source_target_pairs={{0,2},{1,3},{2,0},{3,1},{4,6},{5,7},{6,4},{7,5},{8,10},{9,11},{10,... | collective-permute-start | bytes 49160 | tf_op jit(solution)/shard_map/ppermute | solution.py:201
  15.8 4.6 %collective-permute-start.5 = (bf16[32,2,128]{2,1,0:T(2,128)(2,1)S(1)}, bf16[32,2,128]{2,1,0:T(2,128)(2,1)S(1)}, u32[]{:S(2)}, u32[]{:S(2)}) collective-permute-start(bf16[32,2,128]{2,1,0:T(2,128)(2,1)S(1)} %get-tuple-element.22), channel_id=1, source_target_pairs={{0,3},{1,2},{2,1},{3,0},{4,7},{5,6},{6,5},{7,4},{8,11},{9,10},{10,... | collective-permute-start | bytes 49160 | tf_op jit(solution)/shard_map/ppermute | solution.py:201
  18.7 1.7 %copy-start.1 = (bf16[32,2,128]{2,1,0:T(2,128)(2,1)}, bf16[32,2,128]{2,1,0:T(2,128)(2,1)S(1)}, u32[]{:S(2)}) copy-start(bf16[32,2,128]{2,1,0:T(2,128)(2,1)S(1)} %collective-permute-done.3.refs_1_) | copy-start | bytes 49156
  18.9 1.5 %copy-start.2 = (bf16[32,2,128]{2,1,0:T(2,128)(2,1)}, bf16[32,2,128]{2,1,0:T(2,128)(2,1)S(1)}, u32[]{:S(2)}) copy-start(bf16[32,2,128]{2,1,0:T(2,128)(2,1)S(1)} %collective-permute-done.4.refs_2_) | copy-start | bytes 49156
  20.4 0.6 %copy-start.3 = (bf16[32,2,128]{2,1,0:T(2,128)(2,1)}, bf16[32,2,128]{2,1,0:T(2,128)(2,1)S(1)}, u32[]{:S(2)}) copy-start(bf16[32,2,128]{2,1,0:T(2,128)(2,1)S(1)} %collective-permute-done.5.refs_3_) | copy-start | bytes 49156

commit v5 on v4

--- a/solution.py
+++ b/solution.py
@@ -191,16 +191,18 @@
         in_specs=[pl.BlockSpec(memory_space=pltpu.VMEM)] * owners,
         out_specs=pl.BlockSpec(memory_space=pltpu.HBM),
         scratch_shapes=[pltpu.SemaphoreType.DMA((owners,))],
+        compiler_params=pltpu.CompilerParams(vmem_limit_bytes=2 * 2**20),
         name="assemble",
     )(*parts)
 
 
 def exchange(parts):
     owners = len(parts)
-    return [parts[0]] + [
-        lax.ppermute(part, "tp", [(i, i ^ k) for i in range(owners)])
-        for k, part in enumerate(parts) if k
-    ]
+    moved = {
+        k: lax.ppermute(parts[k], "tp", [(i, i ^ k) for i in range(owners)])
+        for k in range(owners - 1, 0, -1)
+    }
+    return [parts[0]] + [moved[k] for k in range(1, owners)]
 
 
 def on_device(query, cache, scales, lengths, value_up):

time: 22.6 us -> 20.7 us (0.916)
  local copies, waits for them, and re-layouts: 1.2 us -> 0 us
  Pallas kernels: 5.47 us -> 4.89 us
  waiting for transfers between devices: 7.08 us -> 7.33 us
    unnamed x8 -> x0, local copies, waits for them, and re-layouts: 1.2 us -> none
    pallas_call x1, Pallas kernels: 1.42 us -> 0.66 us  [assemble(): pl.pallas_call(functools.partial(assemble_kernel, owners), out_shape=pltp...]
    ppermute x6, waiting for transfers between devices: 7.08 us -> 7.33 us  [exchange(): lax.ppermute(parts[k], 'tp', [(i, i ^ k) for i in range(owners)])]
where the time goes in v5:
time: 20.7 us; the launch traced here: 20.8 us
  starting transfers between devices  8.52 us (41%)
  waiting for transfers between devices  7.33 us (35%)
  Pallas kernels  4.89 us (24%)
    ppermute x6, starting transfers between devices, exchange(): lax.ppermute(parts[k], 'tp', [(i, i ^ k) for i in range(owners)])  8.52 us
    ppermute x6, waiting for transfers between devices, exchange(): lax.ppermute(parts[k], 'tp', [(i, i ^ k) for i in range(owners)])  7.33 us
    pallas_call x1, Pallas kernels, attend(): pl.pallas_call(functools.partial(attend_kernel, owners), out_shape=[jax.S...  3.38 us
    pallas_call x1, Pallas kernels, project(): pl.pallas_call(functools.partial(project_kernel, owners), out_shape=[jax....  0.85 us
    pallas_call x1, Pallas kernels, assemble(): pl.pallas_call(functools.partial(assemble_kernel, owners), out_shape=pltp...  0.66 us
  transfers between devices with their start and end apart: 6, of which 6 were waited for; matrix products, arithmetic and copies ran while one was open for 0% of the time, Pallas kernels for 0%

profile of v5, /device:TPU:0, one launch (start us, length us, event | category | flops | bytes accessed | tf_op | source)
XLA Modules:
  0.0 20.8 jit_solution(13383923816269810216)
XLA Ops:
  0.0 3.4 %attend.1 = (bf16[2,32,512]{2,1,0:T(8,128)(2,1)S(1)}, bf16[2,32,512]{2,1,0:T(8,128)(2,1)S(1)}, bf16[2,32,512]{2,1,0:T(8,128)(2,1)S(1)}, bf16[2,32,512]{2,1,0:T(8,128)(2,1)S(1)}, bf16[32,512,128]{2,1,0:T(8,128)(2,1)S(1)}) custom-call(s32[2]{0:T(128)} %lengths_hbm.1, bf16[2,576,128]{2,1,0:T(8,128)(2,1)} %bitcast.8, f32[576]{0:T(1024)} %scales_hbm.1, ...), custom_call_target="tpu_custom_call" | custom-call | flops 905969664 | bytes 3538944 | tf_op jit(solution)/shard_map/attend/pallas_call | solution.py:98
  3.4 3.4 %collective-permute-start = (bf16[2,32,512]{2,1,0:T(8,128)(2,1)S(1)}, bf16[2,32,512]{2,1,0:T(8,128)(2,1)S(1)}, u32[]{:S(2)}, u32[]{:S(2)}) collective-permute-start(bf16[2,32,512]{2,1,0:T(8,128)(2,1)S(1)} %get-tuple-element.15), channel_id=1, source_target_pairs={{0,1},{1,0},{2,3},{3,2},{4,5},{5,4},{6,7},{7,6},{8,9},{9,8},{10,11... | collective-permute-start | bytes 196616 | tf_op jit(solution)/shard_map/ppermute | solution.py:202
  6.8 0.9 %collective-permute-start.1 = (bf16[2,32,512]{2,1,0:T(8,128)(2,1)S(1)}, bf16[2,32,512]{2,1,0:T(8,128)(2,1)S(1)}, u32[]{:S(2)}, u32[]{:S(2)}) collective-permute-start(bf16[2,32,512]{2,1,0:T(8,128)(2,1)S(1)} %get-tuple-element.16), channel_id=1, source_target_pairs={{0,2},{1,3},{2,0},{3,1},{4,6},{5,7},{6,4},{7,5},{8,10},{9,11},{10,... | collective-permute-start | bytes 196616 | tf_op jit(solution)/shard_map/ppermute | solution.py:202
  7.7 0.6 %collective-permute-start.2 = (bf16[2,32,512]{2,1,0:T(8,128)(2,1)S(1)}, bf16[2,32,512]{2,1,0:T(8,128)(2,1)S(1)}, u32[]{:S(2)}, u32[]{:S(2)}) collective-permute-start(bf16[2,32,512]{2,1,0:T(8,128)(2,1)S(1)} %get-tuple-element.17), channel_id=1, source_target_pairs={{0,3},{1,2},{2,1},{3,0},{4,7},{5,6},{6,5},{7,4},{8,11},{9,10},{10,... | collective-permute-start | bytes 196616 | tf_op jit(solution)/shard_map/ppermute | solution.py:202
  8.4 0.7 %collective-permute-done.refs_1_ = bf16[2,32,512]{2,1,0:T(8,128)(2,1)S(1)} collective-permute-done((bf16[2,32,512]{2,1,0:T(8,128)(2,1)S(1)}, bf16[2,32,512]{2,1,0:T(8,128)(2,1)S(1)}, u32[]{:S(2)}, u32[]{:S(2)}) %collective-permute-start) | collective-permute-done | bytes 65568 | tf_op jit(solution)/shard_map/ppermute | solution.py:202
  9.1 2.0 %collective-permute-done.1.refs_2_ = bf16[2,32,512]{2,1,0:T(8,128)(2,1)S(1)} collective-permute-done((bf16[2,32,512]{2,1,0:T(8,128)(2,1)S(1)}, bf16[2,32,512]{2,1,0:T(8,128)(2,1)S(1)}, u32[]{:S(2)}, u32[]{:S(2)}) %collective-permute-start.1) | collective-permute-done | bytes 65568 | tf_op jit(solution)/shard_map/ppermute | solution.py:202
  11.1 1.9 %collective-permute-done.2.refs_3_ = bf16[2,32,512]{2,1,0:T(8,128)(2,1)S(1)} collective-permute-done((bf16[2,32,512]{2,1,0:T(8,128)(2,1)S(1)}, bf16[2,32,512]{2,1,0:T(8,128)(2,1)S(1)}, u32[]{:S(2)}, u32[]{:S(2)}) %collective-permute-start.2) | collective-permute-done | bytes 65568 | tf_op jit(solution)/shard_map/ppermute | solution.py:202
  13.0 0.9 %project.1 = (bf16[32,2,128]{2,1,0:T(2,128)(2,1)S(1)}, bf16[32,2,128]{2,1,0:T(2,128)(2,1)S(1)}, bf16[32,2,128]{2,1,0:T(2,128)(2,1)S(1)}, bf16[32,2,128]{2,1,0:T(2,128)(2,1)S(1)}) custom-call(bf16[2,32,512]{2,1,0:T(8,128)(2,1)S(1)} %get-tuple-element.14.refs_0_, bf16[2,32,512]{2,1,0:T(8,128)(2,1)S(1)} %collective-permute-done.refs_1_, ...), custom_call_target="tpu_custom_call" | custom-call | flops 33554432 | bytes 4194304 | tf_op jit(solution)/shard_map/project/pallas_call | solution.py:158
  13.8 1.2 %collective-permute-start.3 = (bf16[32,2,128]{2,1,0:T(2,128)(2,1)S(1)}, bf16[32,2,128]{2,1,0:T(2,128)(2,1)S(1)}, u32[]{:S(2)}, u32[]{:S(2)}) collective-permute-start(bf16[32,2,128]{2,1,0:T(2,128)(2,1)S(1)} %get-tuple-element.20), channel_id=1, source_target_pairs={{0,1},{1,0},{2,3},{3,2},{4,5},{5,4},{6,7},{7,6},{8,9},{9,8},{10,11... | collective-permute-start | bytes 49160 | tf_op jit(solution)/shard_map/ppermute | solution.py:202
  15.0 0.5 %collective-permute-start.4 = (bf16[32,2,128]{2,1,0:T(2,128)(2,1)S(1)}, bf16[32,2,128]{2,1,0:T(2,128)(2,1)S(1)}, u32[]{:S(2)}, u32[]{:S(2)}) collective-permute-start(bf16[32,2,128]{2,1,0:T(2,128)(2,1)S(1)} %get-tuple-element.21), channel_id=1, source_target_pairs={{0,2},{1,3},{2,0},{3,1},{4,6},{5,7},{6,4},{7,5},{8,10},{9,11},{10,... | collective-permute-start | bytes 49160 | tf_op jit(solution)/shard_map/ppermute | solution.py:202
  15.5 1.9 %collective-permute-start.5 = (bf16[32,2,128]{2,1,0:T(2,128)(2,1)S(1)}, bf16[32,2,128]{2,1,0:T(2,128)(2,1)S(1)}, u32[]{:S(2)}, u32[]{:S(2)}) collective-permute-start(bf16[32,2,128]{2,1,0:T(2,128)(2,1)S(1)} %get-tuple-element.22), channel_id=1, source_target_pairs={{0,3},{1,2},{2,1},{3,0},{4,7},{5,6},{6,5},{7,4},{8,11},{9,10},{10,... | collective-permute-start | bytes 49160 | tf_op jit(solution)/shard_map/ppermute | solution.py:202
  17.4 0.3 %collective-permute-done.3.refs_1_ = bf16[32,2,128]{2,1,0:T(2,128)(2,1)S(1)} collective-permute-done((bf16[32,2,128]{2,1,0:T(2,128)(2,1)S(1)}, bf16[32,2,128]{2,1,0:T(2,128)(2,1)S(1)}, u32[]{:S(2)}, u32[]{:S(2)}) %collective-permute-start.3) | collective-permute-done | bytes 16416 | tf_op jit(solution)/shard_map/ppermute | solution.py:202
  17.6 1.1 %collective-permute-done.4.refs_2_ = bf16[32,2,128]{2,1,0:T(2,128)(2,1)S(1)} collective-permute-done((bf16[32,2,128]{2,1,0:T(2,128)(2,1)S(1)}, bf16[32,2,128]{2,1,0:T(2,128)(2,1)S(1)}, u32[]{:S(2)}, u32[]{:S(2)}) %collective-permute-start.4) | collective-permute-done | bytes 16416 | tf_op jit(solution)/shard_map/ppermute | solution.py:202
  18.7 1.4 %collective-permute-done.5.refs_3_ = bf16[32,2,128]{2,1,0:T(2,128)(2,1)S(1)} collective-permute-done((bf16[32,2,128]{2,1,0:T(2,128)(2,1)S(1)}, bf16[32,2,128]{2,1,0:T(2,128)(2,1)S(1)}, u32[]{:S(2)}, u32[]{:S(2)}) %collective-permute-start.5) | collective-permute-done | bytes 16416 | tf_op jit(solution)/shard_map/ppermute | solution.py:202
  20.1 0.7 %assemble.1 = bf16[4,32,2,128]{3,2,1,0:T(2,128)(2,1)} custom-call(bf16[32,2,128]{2,1,0:T(2,128)(2,1)S(1)} %get-tuple-element.19.refs_0_, bf16[32,2,128]{2,1,0:T(2,128)(2,1)S(1)} %collective-permute-done.3.refs_1_, bf16[32,2,128]{2,1,0:T(2,128)(2,1)S(1)} %collective-permute-done.4.refs_2_, bf16[32,2,128]{2,1,0:T(2,128)(2,1)S(1)} %collective-permute-done.5.refs_3_), custom_call_target="tpu_custom_call" | custom-call | tf_op jit(solution)/shard_map/assemble/pallas_call | solution.py:188
Async XLA Ops:
  3.4 5.7 %collective-permute-start = (bf16[2,32,512]{2,1,0:T(8,128)(2,1)S(1)}, bf16[2,32,512]{2,1,0:T(8,128)(2,1)S(1)}, u32[]{:S(2)}, u32[]{:S(2)}) collective-permute-start(bf16[2,32,512]{2,1,0:T(8,128)(2,1)S(1)} %get-tuple-element.15), channel_id=1, source_target_pairs={{0,1},{1,0},{2,3},{3,2},{4,5},{5,4},{6,7},{7,6},{8,9},{9,8},{10,11... | collective-permute-start | bytes 196616 | tf_op jit(solution)/shard_map/ppermute | solution.py:202
  6.8 4.3 %collective-permute-start.1 = (bf16[2,32,512]{2,1,0:T(8,128)(2,1)S(1)}, bf16[2,32,512]{2,1,0:T(8,128)(2,1)S(1)}, u32[]{:S(2)}, u32[]{:S(2)}) collective-permute-start(bf16[2,32,512]{2,1,0:T(8,128)(2,1)S(1)} %get-tuple-element.16), channel_id=1, source_target_pairs={{0,2},{1,3},{2,0},{3,1},{4,6},{5,7},{6,4},{7,5},{8,10},{9,11},{10,... | collective-permute-start | bytes 196616 | tf_op jit(solution)/shard_map/ppermute | solution.py:202
  7.7 5.3 %collective-permute-start.2 = (bf16[2,32,512]{2,1,0:T(8,128)(2,1)S(1)}, bf16[2,32,512]{2,1,0:T(8,128)(2,1)S(1)}, u32[]{:S(2)}, u32[]{:S(2)}) collective-permute-start(bf16[2,32,512]{2,1,0:T(8,128)(2,1)S(1)} %get-tuple-element.17), channel_id=1, source_target_pairs={{0,3},{1,2},{2,1},{3,0},{4,7},{5,6},{6,5},{7,4},{8,11},{9,10},{10,... | collective-permute-start | bytes 196616 | tf_op jit(solution)/shard_map/ppermute | solution.py:202
  13.8 3.8 %collective-permute-start.3 = (bf16[32,2,128]{2,1,0:T(2,128)(2,1)S(1)}, bf16[32,2,128]{2,1,0:T(2,128)(2,1)S(1)}, u32[]{:S(2)}, u32[]{:S(2)}) collective-permute-start(bf16[32,2,128]{2,1,0:T(2,128)(2,1)S(1)} %get-tuple-element.20), channel_id=1, source_target_pairs={{0,1},{1,0},{2,3},{3,2},{4,5},{5,4},{6,7},{7,6},{8,9},{9,8},{10,11... | collective-permute-start | bytes 49160 | tf_op jit(solution)/shard_map/ppermute | solution.py:202
  15.0 3.7 %collective-permute-start.4 = (bf16[32,2,128]{2,1,0:T(2,128)(2,1)S(1)}, bf16[32,2,128]{2,1,0:T(2,128)(2,1)S(1)}, u32[]{:S(2)}, u32[]{:S(2)}) collective-permute-start(bf16[32,2,128]{2,1,0:T(2,128)(2,1)S(1)} %get-tuple-element.21), channel_id=1, source_target_pairs={{0,2},{1,3},{2,0},{3,1},{4,6},{5,7},{6,4},{7,5},{8,10},{9,11},{10,... | collective-permute-start | bytes 49160 | tf_op jit(solution)/shard_map/ppermute | solution.py:202
  15.5 4.6 %collective-permute-start.5 = (bf16[32,2,128]{2,1,0:T(2,128)(2,1)S(1)}, bf16[32,2,128]{2,1,0:T(2,128)(2,1)S(1)}, u32[]{:S(2)}, u32[]{:S(2)}) collective-permute-start(bf16[32,2,128]{2,1,0:T(2,128)(2,1)S(1)} %get-tuple-element.22), channel_id=1, source_target_pairs={{0,3},{1,2},{2,1},{3,0},{4,7},{5,6},{6,5},{7,4},{8,11},{9,10},{10,... | collective-permute-start | bytes 49160 | tf_op jit(solution)/shard_map/ppermute | solution.py:202

commit v6 on v4

--- a/solution.py
+++ b/solution.py
@@ -14,9 +14,26 @@
 LANES = 128
 
 
+def plan(owners):
+    if owners != 4:
+        return [(k, [(i, i ^ k) for i in range(owners)]) for k in range(1, owners)]
+    return [
+        (3, [(0, 3), (3, 0)]),
+        (1, [(0, 1), (3, 2)]),
+        (2, [(0, 2), (3, 1)]),
+        (3, [(1, 2), (2, 1)]),
+        (1, [(1, 0), (2, 3)]),
+        (2, [(1, 3), (2, 0)]),
+    ]
+
+
+def partners(owners):
+    return [0] + [k for k, _ in plan(owners)]
+
+
 def attend_kernel(owners, lengths_hbm, query_hbm, scales_hbm, cache, maps_hbm, *refs):
-    outs, maps = refs[:owners], refs[owners]
-    latents, lengths, query, scales, keys, sems, small_sems = refs[owners + 1:]
+    *outs, maps = refs[:-7]
+    latents, lengths, query, scales, keys, sems, small_sems = refs[-7:]
     requests, channels, heads = query.shape
     local_heads, rank = latents.shape[2:]
     me = lax.axis_index("tp")
@@ -86,7 +103,7 @@
             def _():
                 request(r, live)
 
-    for k, out in enumerate(outs):
+    for out, k in zip(outs, partners(owners)):
         out[...] = latents[me ^ k]
     maps_copy.wait()
 
@@ -97,10 +114,11 @@
     rank = channels - ROPE_DIM
     return pl.pallas_call(
         functools.partial(attend_kernel, owners),
-        out_shape=[jax.ShapeDtypeStruct((requests, heads // owners, rank), jnp.bfloat16)] * owners
+        out_shape=[jax.ShapeDtypeStruct((requests, heads // owners, rank), jnp.bfloat16)]
+        * len(partners(owners))
         + [jax.ShapeDtypeStruct(maps.shape, maps.dtype)],
         in_specs=[pl.BlockSpec(memory_space=pl.ANY)] * 5,
-        out_specs=[pl.BlockSpec(memory_space=pltpu.VMEM)] * (owners + 1),
+        out_specs=[pl.BlockSpec(memory_space=pltpu.VMEM)] * (len(partners(owners)) + 1),
         scratch_shapes=[
             pltpu.VMEM((owners, requests, heads // owners, rank), jnp.bfloat16),
             pltpu.SMEM((requests,), jnp.int32),
@@ -123,16 +141,20 @@
     ))
 
 
-def project_kernel(owners, *refs):
-    parts, maps, outs, rows = refs[:owners], refs[owners], refs[owners + 1:-1], refs[-1]
+def project_kernel(owners, count, *refs):
+    parts, maps, outs, rows = refs[:count], refs[count], refs[count + 1:-1], refs[-1]
     requests, local_heads, rank = parts[0].shape
     width = maps.shape[2]
     batch = owners * requests
-    for b in range(batch):
-        for k in range(rank // LANES):
-            rows[k, b * local_heads:(b + 1) * local_heads] = parts[b // requests][
-                b % requests, :, k * LANES:(k + 1) * LANES
-            ].astype(jnp.float32)
+
+    def lay(received):
+        for b in range(batch):
+            for k in range(rank // LANES):
+                rows[k, b * local_heads:(b + 1) * local_heads] = received[b // requests][
+                    b % requests, :, k * LANES:(k + 1) * LANES
+                ].astype(jnp.float32)
+
+    by_role(owners, parts, lay)
     for h in range(0, local_heads, 2):
         pair = jnp.concatenate(
             [
@@ -147,19 +169,19 @@
         values = jnp.dot(pair, both, preferred_element_type=jnp.float32)
         for i in range(2):
             mine = values[i * batch:(i + 1) * batch, i * width:(i + 1) * width]
-            for d, out in enumerate(outs):
-                out[h + i] = mine[d * requests:(d + 1) * requests].astype(jnp.bfloat16)
-
-
-def project(latents, maps):
-    owners = len(latents)
-    requests, local_heads, rank = latents[0].shape
+            for out, k in zip(outs, partners(owners)):
+                out[h + i] = mine[k * requests:(k + 1) * requests].astype(jnp.bfloat16)
+
+
+def project(parts, maps, owners):
+    requests, local_heads, rank = parts[0].shape
     width = maps.shape[2]
     return pl.pallas_call(
-        functools.partial(project_kernel, owners),
-        out_shape=[jax.ShapeDtypeStruct((local_heads, requests, width), jnp.bfloat16)] * owners,
-        in_specs=[pl.BlockSpec(memory_space=pltpu.VMEM)] * (owners + 1),
-        out_specs=[pl.BlockSpec(memory_space=pltpu.VMEM)] * owners,
+        functools.partial(project_kernel, owners, len(parts)),
+        out_shape=[jax.ShapeDtypeStruct((local_heads, requests, width), jnp.bfloat16)]
+        * len(partners(owners)),
+        in_specs=[pl.BlockSpec(memory_space=pltpu.VMEM)] * (len(parts) + 1),
+        out_specs=[pl.BlockSpec(memory_space=pltpu.VMEM)] * len(partners(owners)),
         scratch_shapes=[pltpu.VMEM((rank // LANES, owners * requests * local_heads, LANES), jnp.float32)],
         compiler_params=pltpu.CompilerParams(vmem_limit_bytes=24 * 2**20),
         cost_estimate=pl.CostEstimate(
@@ -168,46 +190,67 @@
             transcendentals=0,
         ),
         name="project",
-    )(*latents, maps)
-
-
-def assemble_kernel(owners, *refs):
-    parts, out, sems = refs[:owners], refs[owners], refs[owners + 1]
+    )(*parts, maps)
+
+
+def assemble_kernel(owners, count, *refs):
+    parts, out, sems = refs[:count], refs[count], refs[count + 1]
     me = lax.axis_index("tp")
-    copies = [
-        pltpu.make_async_copy(part, out.at[me ^ k], sems.at[k]) for k, part in enumerate(parts)
-    ]
-    for copy in copies:
-        copy.start()
-    for copy in copies:
-        copy.wait()
-
-
-def assemble(parts):
-    owners = len(parts)
+
+    def place(received):
+        copies = [
+            pltpu.make_async_copy(part, out.at[me ^ k], sems.at[k])
+            for k, part in enumerate(received)
+        ]
+        for copy in copies:
+            copy.start()
+        for copy in copies:
+            copy.wait()
+
+    by_role(owners, parts, place)
+
+
+def assemble(parts, owners):
     return pl.pallas_call(
-        functools.partial(assemble_kernel, owners),
+        functools.partial(assemble_kernel, owners, len(parts)),
         out_shape=pltpu.HBM((owners,) + parts[0].shape, parts[0].dtype),
-        in_specs=[pl.BlockSpec(memory_space=pltpu.VMEM)] * owners,
+        in_specs=[pl.BlockSpec(memory_space=pltpu.VMEM)] * len(parts),
         out_specs=pl.BlockSpec(memory_space=pltpu.HBM),
         scratch_shapes=[pltpu.SemaphoreType.DMA((owners,))],
+        compiler_params=pltpu.CompilerParams(vmem_limit_bytes=2 * 2**20),
         name="assemble",
     )(*parts)
 
 
-def exchange(parts):
-    owners = len(parts)
-    return [parts[0]] + [
-        lax.ppermute(part, "tp", [(i, i ^ k) for i in range(owners)])
-        for k, part in enumerate(parts) if k
+def exchange(parts, owners):
+    mine, *sent = parts
+    return [mine] + [
+        lax.ppermute(part, "tp", pairs) for part, (_, pairs) in zip(sent, plan(owners))
     ]
+
+
+def by_role(owners, parts, act):
+    if len(parts) == owners:
+        act(parts)
+        return
+    mine, opposite, one, two, across, back_one, back_two = parts
+    me = lax.axis_index("tp")
+    outer = (me == 0) | (me == owners - 1)
+
+    @pl.when(outer)
+    def _():
+        act([mine, back_one, back_two, opposite])
+
+    @pl.when(jnp.logical_not(outer))
+    def _():
+        act([mine, one, two, across])
 
 
 def on_device(query, cache, scales, lengths, value_up):
     owners = lax.axis_size("tp")
     *latents, maps = attend(query, cache, scales, lengths, value_up, owners)
-    values = exchange(project(exchange(latents), maps))
-    returned = assemble(values)
+    values = project(exchange(latents, owners), maps, owners)
+    returned = assemble(exchange(values, owners), owners)
     _, local_heads, requests, width = returned.shape
     returned = returned.reshape(owners * local_heads, requests, width)
     return jnp.swapaxes(returned, 0, 1).reshape(requests, owners * local_heads * width)

time: 22.6 us -> 35.5 us (1.57)
  starting transfers between devices: 8.67 us -> 20.8 us
  waiting for transfers between devices: 7.08 us -> 9.15 us
  local copies, waits for them, and re-layouts: 1.2 us -> 0 us
    ppermute x6 -> x12, starting transfers between devices: 8.67 us -> 20.8 us  [exchange(): lax.ppermute(part, 'tp', pairs)]
    ppermute x6 -> x12, waiting for transfers between devices: 7.08 us -> 9.15 us  [exchange(): lax.ppermute(part, 'tp', pairs)]
    unnamed x8 -> x0, local copies, waits for them, and re-layouts: 1.2 us -> none
    pallas_call x2, Pallas kernels: 2.28 us -> 1.5 us  [the longest x1 0.85 us: project(): pl.pallas_call(functools.partial(project_kernel, owners, len(parts)), out...]
    pallas_call x1, Pallas kernels: 3.19 us -> 3.86 us  [attend(): pl.pallas_call(functools.partial(attend_kernel, owners), out_shape=[jax.S...]
  transfers between devices with their start and end apart: 6 -> 12, of which waited for: 6 -> 4; matrix products, arithmetic and copies ran while one was open for 0% -> 0% of each run, Pallas kernels for 0% -> 0%
where the time goes in v6:
time: 35.5 us
  starting transfers between devices  20.8 us (59%)
  waiting for transfers between devices  9.15 us (26%)
  Pallas kernels  5.36 us (15%)
    ppermute x12, starting transfers between devices, exchange(): lax.ppermute(part, 'tp', pairs)  20.8 us
    ppermute x12, waiting for transfers between devices, exchange(): lax.ppermute(part, 'tp', pairs)  9.15 us
    pallas_call x1, Pallas kernels, attend(): pl.pallas_call(functools.partial(attend_kernel, owners), out_shape=[jax.S...  3.86 us
    pallas_call x1, Pallas kernels, project(): pl.pallas_call(functools.partial(project_kernel, owners, len(parts)), out...  0.85 us
  transfers between devices with their start and end apart: 12, of which 4 were waited for; matrix products, arithmetic and copies ran while one was open for 0% of the time, Pallas kernels for 0%

profile of v6, /device:TPU:0, one launch (start us, length us, event | category | flops | bytes accessed | tf_op | source)
XLA Modules:
  0.0 35.5 jit_solution(17531118200781584814)
XLA Ops:
  0.0 3.9 %attend.1 = (bf16[2,32,512]{2,1,0:T(8,128)(2,1)S(1)}, bf16[2,32,512]{2,1,0:T(8,128)(2,1)S(1)}, bf16[2,32,512]{2,1,0:T(8,128)(2,1)S(1)}, bf16[2,32,512]{2,1,0:T(8...) custom-call(s32[2]{0:T(128)} %lengths_hbm.1, ...), custom_call_target="tpu_custom_call" | custom-call | flops 905969664 | bytes 3538944 | tf_op jit(solution)/shard_map/attend/pallas_call | solution.py:115
  3.9 5.7 %collective-permute-start = (bf16[2,32,512]{2,1,0:T(8,128)(2,1)S(1)}, bf16[2,32,512]{2,1,0:T(8,128)(2,1)S(1)}, u32[]{:S(2)}, u32[]{:S(2)}) collective-permute-start(bf16[2,32,512]{2,1,0:T(8,128)(2,1)S(1)} %get-tuple-element.21), channel_id=1, source_target_pairs={{0,3},{3,0},{4,7},{7,4},{8,11},{11,8},{12,15},{15,12},{16,19},{19,... | collective-permute-start | bytes 196616 | tf_op jit(solution)/shard_map/ppermute | solution.py:228
  9.6 1.3 %collective-permute-start.1 = (bf16[2,32,512]{2,1,0:T(8,128)(2,1)S(1)}, bf16[2,32,512]{2,1,0:T(8,128)(2,1)S(1)}, u32[]{:S(2)}, u32[]{:S(2)}) collective-permute-start(bf16[2,32,512]{2,1,0:T(8,128)(2,1)S(1)} %get-tuple-element.22), channel_id=1, source_target_pairs={{0,1},{3,2},{4,5},{7,6},{8,9},{11,10},{12,13},{15,14},{16,17},{19,... | collective-permute-start | bytes 196616 | tf_op jit(solution)/shard_map/ppermute | solution.py:228
  10.9 1.3 %collective-permute-start.2 = (bf16[2,32,512]{2,1,0:T(8,128)(2,1)S(1)}, bf16[2,32,512]{2,1,0:T(8,128)(2,1)S(1)}, u32[]{:S(2)}, u32[]{:S(2)}) collective-permute-start(bf16[2,32,512]{2,1,0:T(8,128)(2,1)S(1)} %get-tuple-element.23), channel_id=1, source_target_pairs={{0,2},{3,1},{4,6},{7,5},{8,10},{11,9},{12,14},{15,13},{16,18},{19,... | collective-permute-start | bytes 196616 | tf_op jit(solution)/shard_map/ppermute | solution.py:228
  12.2 0.7 %collective-permute-start.3 = (bf16[2,32,512]{2,1,0:T(8,128)(2,1)S(1)}, bf16[2,32,512]{2,1,0:T(8,128)(2,1)S(1)}, u32[]{:S(2)}, u32[]{:S(2)}) collective-permute-start(bf16[2,32,512]{2,1,0:T(8,128)(2,1)S(1)} %get-tuple-element.24), channel_id=1, source_target_pairs={{1,2},{2,1},{5,6},{6,5},{9,10},{10,9},{13,14},{14,13},{17,18},{18,... | collective-permute-start | bytes 196616 | tf_op jit(solution)/shard_map/ppermute | solution.py:228
  12.9 1.3 %collective-permute-start.4 = (bf16[2,32,512]{2,1,0:T(8,128)(2,1)S(1)}, bf16[2,32,512]{2,1,0:T(8,128)(2,1)S(1)}, u32[]{:S(2)}, u32[]{:S(2)}) collective-permute-start(bf16[2,32,512]{2,1,0:T(8,128)(2,1)S(1)} %get-tuple-element.25), channel_id=1, source_target_pairs={{1,0},{2,3},{5,4},{6,7},{9,8},{10,11},{13,12},{14,15},{17,16},{18,... | collective-permute-start | bytes 196616 | tf_op jit(solution)/shard_map/ppermute | solution.py:228
  14.2 0.0 collective-permute-done.refs_1_
  14.2 1.3 %collective-permute-start.5 = (bf16[2,32,512]{2,1,0:T(8,128)(2,1)S(1)}, bf16[2,32,512]{2,1,0:T(8,128)(2,1)S(1)}, u32[]{:S(2)}, u32[]{:S(2)}) collective-permute-start(bf16[2,32,512]{2,1,0:T(8,128)(2,1)S(1)} %get-tuple-element.26), channel_id=1, source_target_pairs={{1,3},{2,0},{5,7},{6,4},{9,11},{10,8},{13,15},{14,12},{17,19},{18,... | collective-permute-start | bytes 196616 | tf_op jit(solution)/shard_map/ppermute | solution.py:228
  15.5 0.0 collective-permute-done.1.refs_2_
  15.5 0.0 collective-permute-done.2.refs_3_
  15.5 3.5 %collective-permute-done.4.refs_5_ = bf16[2,32,512]{2,1,0:T(8,128)(2,1)S(1)} collective-permute-done((bf16[2,32,512]{2,1,0:T(8,128)(2,1)S(1)}, bf16[2,32,512]{2,1,0:T(8,128)(2,1)S(1)}, u32[]{:S(2)}, u32[]{:S(2)}) %collective-permute-start.4) | collective-permute-done | bytes 65568 | tf_op jit(solution)/shard_map/ppermute | solution.py:228
  19.1 1.3 %collective-permute-done.5.refs_6_ = bf16[2,32,512]{2,1,0:T(8,128)(2,1)S(1)} collective-permute-done((bf16[2,32,512]{2,1,0:T(8,128)(2,1)S(1)}, bf16[2,32,512]{2,1,0:T(8,128)(2,1)S(1)}, u32[]{:S(2)}, u32[]{:S(2)}) %collective-permute-start.5) | collective-permute-done | bytes 65568 | tf_op jit(solution)/shard_map/ppermute | solution.py:228
  20.4 0.8 %project.1 = (bf16[32,2,128]{2,1,0:T(2,128)(2,1)S(1)}, bf16[32,2,128]{2,1,0:T(2,128)(2,1)S(1)}, bf16[32,2,128]{2,1,0:T(2,128)(2,1)S(1)}, bf16[32,2,128]{2,1,0:T(...) custom-call(bf16[2,32,512]{2,1,0:T(8,128)(2,1)S(1)} %get-tuple-eleme, ...), custom_call_target="tpu_custom_call" | custom-call | flops 33554432 | bytes 4194304 | tf_op jit(solution)/shard_map/project/pallas_call | solution.py:179
  21.2 3.4 %collective-permute-start.6 = (bf16[32,2,128]{2,1,0:T(2,128)(2,1)S(1)}, bf16[32,2,128]{2,1,0:T(2,128)(2,1)S(1)}, u32[]{:S(2)}, u32[]{:S(2)}) collective-permute-start(bf16[32,2,128]{2,1,0:T(2,128)(2,1)S(1)} %get-tuple-element.29), channel_id=1, source_target_pairs={{0,3},{3,0},{4,7},{7,4},{8,11},{11,8},{12,15},{15,12},{16,19},{19,... | collective-permute-start | bytes 49160 | tf_op jit(solution)/shard_map/ppermute | solution.py:228
  24.6 1.3 %collective-permute-start.7 = (bf16[32,2,128]{2,1,0:T(2,128)(2,1)S(1)}, bf16[32,2,128]{2,1,0:T(2,128)(2,1)S(1)}, u32[]{:S(2)}, u32[]{:S(2)}) collective-permute-start(bf16[32,2,128]{2,1,0:T(2,128)(2,1)S(1)} %get-tuple-element.30), channel_id=1, source_target_pairs={{0,1},{3,2},{4,5},{7,6},{8,9},{11,10},{12,13},{15,14},{16,17},{19,... | collective-permute-start | bytes 49160 | tf_op jit(solution)/shard_map/ppermute | solution.py:228
  25.9 1.3 %collective-permute-start.8 = (bf16[32,2,128]{2,1,0:T(2,128)(2,1)S(1)}, bf16[32,2,128]{2,1,0:T(2,128)(2,1)S(1)}, u32[]{:S(2)}, u32[]{:S(2)}) collective-permute-start(bf16[32,2,128]{2,1,0:T(2,128)(2,1)S(1)} %get-tuple-element.31), channel_id=1, source_target_pairs={{0,2},{3,1},{4,6},{7,5},{8,10},{11,9},{12,14},{15,13},{16,18},{19,... | collective-permute-start | bytes 49160 | tf_op jit(solution)/shard_map/ppermute | solution.py:228
  27.2 0.7 %collective-permute-start.9 = (bf16[32,2,128]{2,1,0:T(2,128)(2,1)S(1)}, bf16[32,2,128]{2,1,0:T(2,128)(2,1)S(1)}, u32[]{:S(2)}, u32[]{:S(2)}) collective-permute-start(bf16[32,2,128]{2,1,0:T(2,128)(2,1)S(1)} %get-tuple-element.32), channel_id=1, source_target_pairs={{1,2},{2,1},{5,6},{6,5},{9,10},{10,9},{13,14},{14,13},{17,18},{18,... | collective-permute-start | bytes 49160 | tf_op jit(solution)/shard_map/ppermute | solution.py:228
  27.9 1.3 %collective-permute-start.10 = (bf16[32,2,128]{2,1,0:T(2,128)(2,1)S(1)}, bf16[32,2,128]{2,1,0:T(2,128)(2,1)S(1)}, u32[]{:S(2)}, u32[]{:S(2)}) collective-permute-start(bf16[32,2,128]{2,1,0:T(2,128)(2,1)S(1)} %get-tuple-element.33), channel_id=1, source_target_pairs={{1,0},{2,3},{5,4},{6,7},{9,8},{10,11},{13,12},{14,15},{17,16},{18,... | collective-permute-start | bytes 49160 | tf_op jit(solution)/shard_map/ppermute | solution.py:228
  29.2 0.0 collective-permute-done.6.refs_1_
  29.2 1.3 %collective-permute-start.11 = (bf16[32,2,128]{2,1,0:T(2,128)(2,1)S(1)}, bf16[32,2,128]{2,1,0:T(2,128)(2,1)S(1)}, u32[]{:S(2)}, u32[]{:S(2)}) collective-permute-start(bf16[32,2,128]{2,1,0:T(2,128)(2,1)S(1)} %get-tuple-element.34), channel_id=1, source_target_pairs={{1,3},{2,0},{5,7},{6,4},{9,11},{10,8},{13,15},{14,12},{17,19},{18,... | collective-permute-start | bytes 49160 | tf_op jit(solution)/shard_map/ppermute | solution.py:228
  30.5 0.0 collective-permute-done.7.refs_2_
  30.5 3.0 %collective-permute-done.10.refs_5_ = bf16[32,2,128]{2,1,0:T(2,128)(2,1)S(1)} collective-permute-done((bf16[32,2,128]{2,1,0:T(2,128)(2,1)S(1)}, bf16[32,2,128]{2,1,0:T(2,128)(2,1)S(1)}, u32[]{:S(2)}, u32[]{:S(2)}) %collective-permute-start.10) | collective-permute-done | bytes 16416 | tf_op jit(solution)/shard_map/ppermute | solution.py:228
  33.5 1.3 %collective-permute-done.11.refs_6_ = bf16[32,2,128]{2,1,0:T(2,128)(2,1)S(1)} collective-permute-done((bf16[32,2,128]{2,1,0:T(2,128)(2,1)S(1)}, bf16[32,2,128]{2,1,0:T(2,128)(2,1)S(1)}, u32[]{:S(2)}, u32[]{:S(2)}) %collective-permute-start.11) | collective-permute-done | bytes 16416 | tf_op jit(solution)/shard_map/ppermute | solution.py:228
  34.8 0.7 %assemble.1 = bf16[4,32,2,128]{3,2,1,0:T(2,128)(2,1)} custom-call(bf16[32,2,128]{2,1,0:T(2,128)(2,1)S(1)} %get-tuple-element.28.refs_0_, bf16[32,2,128]{2,1,0:T(2,128)(2,1)S(1)} %collective-permute-done.6.refs_1_, bf16[32,2,128]{2,1,0:T(2,128)(2,1)S(1)} %collective-permute-done.7.refs_2_, bf16[32,2,128]{2,1,0:T(2,128)(2,1)S(1)} %collective-permute-done.8.refs_3_, ...), custom_call_target="tpu_custom_call" | custom-call | tf_op jit(solution)/shard_map/assemble/pallas_call | solution.py:214
  (3 shorter events, 0.0 us)
Async XLA Ops:
  3.9 10.3 %collective-permute-start = (bf16[2,32,512]{2,1,0:T(8,128)(2,1)S(1)}, bf16[2,32,512]{2,1,0:T(8,128)(2,1)S(1)}, u32[]{:S(2)}, u32[]{:S(2)}) collective-permute-start(bf16[2,32,512]{2,1,0:T(8,128)(2,1)S(1)} %get-tuple-element.21), channel_id=1, source_target_pairs={{0,3},{3,0},{4,7},{7,4},{8,11},{11,8},{12,15},{15,12},{16,19},{19,... | collective-permute-start | bytes 196616 | tf_op jit(solution)/shard_map/ppermute | solution.py:228
  9.6 5.9 %collective-permute-start.1 = (bf16[2,32,512]{2,1,0:T(8,128)(2,1)S(1)}, bf16[2,32,512]{2,1,0:T(8,128)(2,1)S(1)}, u32[]{:S(2)}, u32[]{:S(2)}) collective-permute-start(bf16[2,32,512]{2,1,0:T(8,128)(2,1)S(1)} %get-tuple-element.22), channel_id=1, source_target_pairs={{0,1},{3,2},{4,5},{7,6},{8,9},{11,10},{12,13},{15,14},{16,17},{19,... | collective-permute-start | bytes 196616 | tf_op jit(solution)/shard_map/ppermute | solution.py:228
  10.9 4.6 %collective-permute-start.2 = (bf16[2,32,512]{2,1,0:T(8,128)(2,1)S(1)}, bf16[2,32,512]{2,1,0:T(8,128)(2,1)S(1)}, u32[]{:S(2)}, u32[]{:S(2)}) collective-permute-start(bf16[2,32,512]{2,1,0:T(8,128)(2,1)S(1)} %get-tuple-element.23), channel_id=1, source_target_pairs={{0,2},{3,1},{4,6},{7,5},{8,10},{11,9},{12,14},{15,13},{16,18},{19,... | collective-permute-start | bytes 196616 | tf_op jit(solution)/shard_map/ppermute | solution.py:228
  12.2 3.3 %collective-permute-start.3 = (bf16[2,32,512]{2,1,0:T(8,128)(2,1)S(1)}, bf16[2,32,512]{2,1,0:T(8,128)(2,1)S(1)}, u32[]{:S(2)}, u32[]{:S(2)}) collective-permute-start(bf16[2,32,512]{2,1,0:T(8,128)(2,1)S(1)} %get-tuple-element.24), channel_id=1, source_target_pairs={{1,2},{2,1},{5,6},{6,5},{9,10},{10,9},{13,14},{14,13},{17,18},{18,... | collective-permute-start | bytes 196616 | tf_op jit(solution)/shard_map/ppermute | solution.py:228
  12.9 6.2 %collective-permute-start.4 = (bf16[2,32,512]{2,1,0:T(8,128)(2,1)S(1)}, bf16[2,32,512]{2,1,0:T(8,128)(2,1)S(1)}, u32[]{:S(2)}, u32[]{:S(2)}) collective-permute-start(bf16[2,32,512]{2,1,0:T(8,128)(2,1)S(1)} %get-tuple-element.25), channel_id=1, source_target_pairs={{1,0},{2,3},{5,4},{6,7},{9,8},{10,11},{13,12},{14,15},{17,16},{18,... | collective-permute-start | bytes 196616 | tf_op jit(solution)/shard_map/ppermute | solution.py:228
  14.2 6.2 %collective-permute-start.5 = (bf16[2,32,512]{2,1,0:T(8,128)(2,1)S(1)}, bf16[2,32,512]{2,1,0:T(8,128)(2,1)S(1)}, u32[]{:S(2)}, u32[]{:S(2)}) collective-permute-start(bf16[2,32,512]{2,1,0:T(8,128)(2,1)S(1)} %get-tuple-element.26), channel_id=1, source_target_pairs={{1,3},{2,0},{5,7},{6,4},{9,11},{10,8},{13,15},{14,12},{17,19},{18,... | collective-permute-start | bytes 196616 | tf_op jit(solution)/shard_map/ppermute | solution.py:228
  21.2 7.9 %collective-permute-start.6 = (bf16[32,2,128]{2,1,0:T(2,128)(2,1)S(1)}, bf16[32,2,128]{2,1,0:T(2,128)(2,1)S(1)}, u32[]{:S(2)}, u32[]{:S(2)}) collective-permute-start(bf16[32,2,128]{2,1,0:T(2,128)(2,1)S(1)} %get-tuple-element.29), channel_id=1, source_target_pairs={{0,3},{3,0},{4,7},{7,4},{8,11},{11,8},{12,15},{15,12},{16,19},{19,... | collective-permute-start | bytes 49160 | tf_op jit(solution)/shard_map/ppermute | solution.py:228
  24.6 5.9 %collective-permute-start.7 = (bf16[32,2,128]{2,1,0:T(2,128)(2,1)S(1)}, bf16[32,2,128]{2,1,0:T(2,128)(2,1)S(1)}, u32[]{:S(2)}, u32[]{:S(2)}) collective-permute-start(bf16[32,2,128]{2,1,0:T(2,128)(2,1)S(1)} %get-tuple-element.30), channel_id=1, source_target_pairs={{0,1},{3,2},{4,5},{7,6},{8,9},{11,10},{12,13},{15,14},{16,17},{19,... | collective-permute-start | bytes 49160 | tf_op jit(solution)/shard_map/ppermute | solution.py:228
  25.9 4.6 %collective-permute-start.8 = (bf16[32,2,128]{2,1,0:T(2,128)(2,1)S(1)}, bf16[32,2,128]{2,1,0:T(2,128)(2,1)S(1)}, u32[]{:S(2)}, u32[]{:S(2)}) collective-permute-start(bf16[32,2,128]{2,1,0:T(2,128)(2,1)S(1)} %get-tuple-element.31), channel_id=1, source_target_pairs={{0,2},{3,1},{4,6},{7,5},{8,10},{11,9},{12,14},{15,13},{16,18},{19,... | collective-permute-start | bytes 49160 | tf_op jit(solution)/shard_map/ppermute | solution.py:228
  27.2 3.3 %collective-permute-start.9 = (bf16[32,2,128]{2,1,0:T(2,128)(2,1)S(1)}, bf16[32,2,128]{2,1,0:T(2,128)(2,1)S(1)}, u32[]{:S(2)}, u32[]{:S(2)}) collective-permute-start(bf16[32,2,128]{2,1,0:T(2,128)(2,1)S(1)} %get-tuple-element.32), channel_id=1, source_target_pairs={{1,2},{2,1},{5,6},{6,5},{9,10},{10,9},{13,14},{14,13},{17,18},{18,... | collective-permute-start | bytes 49160 | tf_op jit(solution)/shard_map/ppermute | solution.py:228
  27.9 5.6 %collective-permute-start.10 = (bf16[32,2,128]{2,1,0:T(2,128)(2,1)S(1)}, bf16[32,2,128]{2,1,0:T(2,128)(2,1)S(1)}, u32[]{:S(2)}, u32[]{:S(2)}) collective-permute-start(bf16[32,2,128]{2,1,0:T(2,128)(2,1)S(1)} %get-tuple-element.33), channel_id=1, source_target_pairs={{1,0},{2,3},{5,4},{6,7},{9,8},{10,11},{13,12},{14,15},{17,16},{18,... | collective-permute-start | bytes 49160 | tf_op jit(solution)/shard_map/ppermute | solution.py:228
  29.2 5.6 %collective-permute-start.11 = (bf16[32,2,128]{2,1,0:T(2,128)(2,1)S(1)}, bf16[32,2,128]{2,1,0:T(2,128)(2,1)S(1)}, u32[]{:S(2)}, u32[]{:S(2)}) collective-permute-start(bf16[32,2,128]{2,1,0:T(2,128)(2,1)S(1)} %get-tuple-element.34), channel_id=1, source_target_pairs={{1,3},{2,0},{5,7},{6,4},{9,11},{10,8},{13,15},{14,12},{17,19},{18,... | collective-permute-start | bytes 49160 | tf_op jit(solution)/shard_map/ppermute | solution.py:228

commit v7 on v3

--- a/solution.py
+++ b/solution.py
@@ -10,18 +10,24 @@
 
 ROPE_DIM = 64
 SOFTMAX_SCALE = (1.0 + 0.1 * math.log(40.0)) ** 2 / math.sqrt(192.0)
+EXP2_SCALE = SOFTMAX_SCALE * math.log2(math.e)
 BLOCK = 512
 LANES = 128
 
 
+def order(owners):
+    return [0] + list(range(owners - 1, 0, -1))
+
+
 def attend_kernel(owners, lengths_hbm, query_hbm, scales_hbm, cache, *refs):
-    outs, (latents, lengths, query, scales, keys, sems, small_sems) = refs[:owners], refs[owners:]
+    outs, refs = refs[:owners], refs[owners:]
+    latents, lengths, query, scales, keys, scaled, scores, weights, sems, small_sems = refs
     requests, channels, heads = query.shape
     local_heads, rank = latents.shape[2:]
-    me = lax.axis_index("tp")
     cache_len = cache.shape[2]
     block = min(BLOCK, cache_len)
     blocks = cache_len // block
+    me = lax.axis_index("tp")
 
     def fetch(r, b):
         span = pl.ds(b * block, block)
@@ -35,73 +41,101 @@
     ]
     for copy in small:
         copy.start()
-    fetch(0, 0).start()
-    small[0].wait()
-    for r in range(requests):
-        for b in range(blocks):
-            if (r, b) != (0, 0):
-                @pl.when(b * block < lengths[r])
-                def _():
-                    fetch(r, b).start()
+    for b in range(blocks):
+        for r in range(requests):
+            fetch(r, b).start()
     small[1].wait()
     small[2].wait()
-
     scale_row = scales[...].reshape(1, channels)
-
-    def request(r, live):
-        scaled = (query[r].astype(jnp.float32).T * scale_row).astype(jnp.bfloat16)
-        parts = []
+    for r in range(requests):
+        scaled[r] = (query[r].astype(jnp.float32).T * scale_row).astype(jnp.bfloat16)
+    small[0].wait()
+
+    def score(slot, r, live):
+        top = None
         for b in range(live):
             fetch(r, b).wait()
-            part = jnp.dot(
-                scaled, keys[r, :, b * block:(b + 1) * block],
-                preferred_element_type=jnp.float32,
-            )
+            span = slice(b * block, (b + 1) * block)
+            part = jnp.dot(scaled[r], keys[r, :, span], preferred_element_type=jnp.float32)
             if b == live - 1:
                 place = b * block + lax.broadcasted_iota(jnp.int32, part.shape, 1)
                 part = jnp.where(place < lengths[r], part, -jnp.inf)
-            parts.append(part)
-        top = jnp.max(parts[0], axis=1, keepdims=True)
-        for part in parts[1:]:
-            top = jnp.maximum(top, jnp.max(part, axis=1, keepdims=True))
+            scores[slot, :, span] = part
+            high = jnp.max(part, axis=1, keepdims=True)
+            top = high if top is None else jnp.maximum(top, high)
+        return top
+
+    def weigh(slot, live, top):
         total = jnp.zeros_like(top)
-        mixture = jnp.zeros((heads, rank), jnp.float32)
-        for b, part in enumerate(parts):
-            weights = jnp.exp((part - top) * SOFTMAX_SCALE)
-            total += jnp.sum(weights, axis=1, keepdims=True)
-            mixture += lax.dot_general(
-                weights.astype(jnp.bfloat16), keys[r, :rank, b * block:(b + 1) * block],
-                (((1,), (1,)), ((), ())), preferred_element_type=jnp.float32,
-            )
-        latent = (mixture / total * scale_row[:, :rank]).astype(jnp.bfloat16)
+        for b in range(live):
+            span = slice(b * block, (b + 1) * block)
+            weight = jnp.exp2((scores[slot, :, span] - top) * EXP2_SCALE)
+            total += jnp.sum(weight, axis=1, keepdims=True)
+            weights[slot, :, span] = weight.astype(jnp.bfloat16)
+        return total
+
+    def mix(slot, r, live):
+        return lax.dot_general(
+            weights[slot, :, :live * block], keys[r, :rank, :live * block],
+            (((1,), (1,)), ((), ())), preferred_element_type=jnp.float32,
+        )
+
+    def finish(r, mixture, total):
+        latent = (mixture * (1.0 / total) * scale_row[:, :rank]).astype(jnp.bfloat16)
         for d in range(owners):
             latents[d, r] = latent[d * local_heads:(d + 1) * local_heads]
 
-    for r in range(requests):
-        for live in range(1, blocks + 1):
-            @pl.when((lengths[r] > (live - 1) * block) & (lengths[r] <= live * block))
-            def _():
-                request(r, live)
-
-    for k, out in enumerate(outs):
+    def pair(r, s, live_r, live_s):
+        top_r = score(0, r, live_r)
+        top_s = score(1, s, live_s)
+        total_r = weigh(0, live_r, top_r)
+        mixture_r = mix(0, r, live_r)
+        total_s = weigh(1, live_s, top_s)
+        finish(r, mixture_r, total_r)
+        mixture_s = mix(1, s, live_s)
+        finish(s, mixture_s, total_s)
+        for b in range(live_r, blocks):
+            fetch(r, b).wait()
+        for b in range(live_s, blocks):
+            fetch(s, b).wait()
+
+    for first in range(0, requests, 2):
+        swap = (lengths[first] < lengths[first + 1]).astype(jnp.int32)
+        longer, shorter = first + swap, first + 1 - swap
+        live = [(lengths[r] + (block - 1)) // block for r in (longer, shorter)]
+        for live_r in range(1, blocks + 1):
+            for live_s in range(1, live_r + 1):
+                @pl.when((live[0] == live_r) & (live[1] == live_s))
+                def _():
+                    pair(longer, shorter, live_r, live_s)
+
+    for out, k in zip(outs, order(owners)):
         out[...] = latents[me ^ k]
+
+
+def in_hbm(*arrays):
+    return [pltpu.with_memory_space_constraint(array, pltpu.HBM) for array in arrays]
 
 
 def attend(query, cache, scales, lengths, owners):
     requests, heads, channels = query.shape
     cache_len = cache.shape[1]
     rank = channels - ROPE_DIM
+    part = jax.ShapeDtypeStruct((requests, heads // owners, rank), jnp.bfloat16)
     return pl.pallas_call(
         functools.partial(attend_kernel, owners),
-        out_shape=[jax.ShapeDtypeStruct((requests, heads // owners, rank), jnp.bfloat16)] * owners,
+        out_shape=[part] * owners,
         in_specs=[pl.BlockSpec(memory_space=pl.ANY)] * 4,
         out_specs=[pl.BlockSpec(memory_space=pltpu.VMEM)] * owners,
         scratch_shapes=[
-            pltpu.VMEM((owners, requests, heads // owners, rank), jnp.bfloat16),
+            pltpu.VMEM((owners,) + part.shape, part.dtype),
             pltpu.SMEM((requests,), jnp.int32),
             pltpu.VMEM((requests, channels, heads), jnp.bfloat16),
             pltpu.VMEM((channels,), jnp.float32),
             pltpu.VMEM((requests, channels, cache_len), jnp.bfloat16),
+            pltpu.VMEM((requests, heads, channels), jnp.bfloat16),
+            pltpu.VMEM((2, heads, cache_len), jnp.float32),
+            pltpu.VMEM((2, heads, cache_len), jnp.bfloat16),
             pltpu.SemaphoreType.DMA((requests, cache_len // min(BLOCK, cache_len))),
             pltpu.SemaphoreType.DMA((3,)),
         ],
@@ -112,7 +146,28 @@
             transcendentals=requests * heads * cache_len,
         ),
         name="attend",
-    )(*(pltpu.with_memory_space_constraint(x, pltpu.HBM) for x in (lengths, jnp.swapaxes(query, 1, 2), scales, jnp.swapaxes(cache, 1, 2))))
+    )(*in_hbm(lengths, jnp.swapaxes(query, 1, 2), scales, jnp.swapaxes(cache, 1, 2)))
+
+
+def stage_kernel(maps_hbm, after, maps, sem):
+    copy = pltpu.make_async_copy(maps_hbm, maps, sem)
+    copy.start()
+    copy.wait()
+
+
+def stage(maps, after):
+    return pl.pallas_call(
+        stage_kernel,
+        out_shape=jax.ShapeDtypeStruct(maps.shape, maps.dtype),
+        in_specs=[pl.BlockSpec(memory_space=pl.ANY)] * 2,
+        out_specs=pl.BlockSpec(memory_space=pltpu.VMEM),
+        scratch_shapes=[pltpu.SemaphoreType.DMA(())],
+        compiler_params=pltpu.CompilerParams(vmem_limit_bytes=8 * 2**20),
+        cost_estimate=pl.CostEstimate(
+            flops=0, bytes_accessed=4 * maps.size, transcendentals=0
+        ),
+        name="stage",
+    )(*in_hbm(maps), after)
 
 
 def project_kernel(owners, *refs):
@@ -167,7 +222,8 @@
     parts, out, sems = refs[:owners], refs[owners], refs[owners + 1]
     me = lax.axis_index("tp")
     copies = [
-        pltpu.make_async_copy(part, out.at[me ^ k], sems.at[k]) for k, part in enumerate(parts)
+        pltpu.make_async_copy(part, out.at[me ^ k], sems.at[k])
+        for k, part in zip(order(owners), parts)
     ]
     for copy in copies:
         copy.start()
@@ -180,25 +236,27 @@
     return pl.pallas_call(
         functools.partial(assemble_kernel, owners),
         out_shape=pltpu.HBM((owners,) + parts[0].shape, parts[0].dtype),
-        in_specs=[pl.BlockSpec(memory_space=pl.ANY)] * owners,
+        in_specs=[pl.BlockSpec(memory_space=pltpu.VMEM)] * owners,
         out_specs=pl.BlockSpec(memory_space=pltpu.HBM),
         scratch_shapes=[pltpu.SemaphoreType.DMA((owners,))],
+        compiler_params=pltpu.CompilerParams(vmem_limit_bytes=2 * 2**20),
         name="assemble",
     )(*parts)
 
 
 def exchange(parts):
     owners = len(parts)
-    return [parts[0]] + [
-        lax.ppermute(part, "tp", [(i, i ^ k) for i in range(owners)])
-        for k, part in enumerate(parts) if k
+    return [
+        lax.ppermute(part, "tp", [(i, i ^ k) for i in range(owners)]) if k else part
+        for k, part in zip(order(owners), parts)
     ]
 
 
 def on_device(query, cache, scales, lengths, value_up):
     owners = lax.axis_size("tp")
-    latents = exchange(attend(query, cache, scales, lengths, owners))
-    values = exchange(project(latents, value_up))
+    latents = attend(query, cache, scales, lengths, owners)
+    maps = stage(value_up, latents[0])
+    values = exchange(project(exchange(latents), maps))
     returned = assemble(values)
     _, local_heads, requests, width = returned.shape
     returned = returned.reshape(owners * local_heads, requests, width)

time: 26.2 us -> 20.4 us (0.78)
  local copies, waits for them, and re-layouts: 3.38 us -> 0 us
  waiting for transfers between devices: 6.87 us -> 4.24 us
  Pallas kernels: 6.98 us -> 8.75 us
  starting transfers between devices: 8.76 us -> 7.12 us
    pallas_call x1 -> x2, Pallas kernels: 3.01 us -> 7.24 us  [the longest x1 5.05 us: attend(): pl.pallas_call(functools.partial(attend_kernel, owners), out_shape=[part]...]
    unnamed x10 -> x0, local copies, waits for them, and re-layouts: 3.38 us -> none
    ppermute x6, waiting for transfers between devices: 6.87 us -> 4.24 us  [exchange(): lax.ppermute(part, 'tp', [(i, i ^ k) for i in range(owners)])]
    pallas_call x1, Pallas kernels: 3.12 us -> 0.66 us  [assemble(): pl.pallas_call(functools.partial(assemble_kernel, owners), out_shape=pltp...]
    ppermute x6, starting transfers between devices: 8.76 us -> 7.12 us  [exchange(): lax.ppermute(part, 'tp', [(i, i ^ k) for i in range(owners)])]
  transfers between devices with their start and end apart: 6 -> 6, of which waited for: 5 -> 5; matrix products, arithmetic and copies ran while one was open for 0% -> 0% of each run, Pallas kernels for 0% -> 11%
where the time goes in v7:
time: 20.4 us; the launch traced here: 20.1 us
  Pallas kernels  8.75 us (43%)
  starting transfers between devices  7.12 us (35%)
  waiting for transfers between devices  4.24 us (21%)
    ppermute x6, starting transfers between devices, exchange(): lax.ppermute(part, 'tp', [(i, i ^ k) for i in range(owners)])  7.12 us
    pallas_call x1, Pallas kernels, attend(): pl.pallas_call(functools.partial(attend_kernel, owners), out_shape=[part]...  5.05 us
    ppermute x6, waiting for transfers between devices, exchange(): lax.ppermute(part, 'tp', [(i, i ^ k) for i in range(owners)])  4.24 us
    pallas_call x1, Pallas kernels, stage(): pl.pallas_call(stage_kernel, out_shape=jax.ShapeDtypeStruct(maps.shape, m...  2.2 us
    pallas_call x1, Pallas kernels, project(): pl.pallas_call(functools.partial(project_kernel, owners), out_shape=[jax....  0.85 us
    pallas_call x1, Pallas kernels, assemble(): pl.pallas_call(functools.partial(assemble_kernel, owners), out_shape=pltp...  0.66 us
  transfers between devices with their start and end apart: 6, of which 5 were waited for; matrix products, arithmetic and copies ran while one was open for 0% of the time, Pallas kernels for 11%

profile of v7, /device:TPU:0, one launch (start us, length us, event | category | flops | bytes accessed | tf_op | source)
XLA Modules:
  0.0 20.1 jit_solution(5640003553799468067)
XLA Ops:
  0.0 5.0 %attend.1 = (bf16[2,32,512]{2,1,0:T(8,128)(2,1)S(1)}, bf16[2,32,512]{2,1,0:T(8,128)(2,1)S(1)}, bf16[2,32,512]{2,1,0:T(8,128)(2,1)S(1)}, bf16[2,32,512]{2,1,0:T(8,128)(2,1)S(1)}) custom-call(s32[2]{0:T(128)} %lengths_hbm.1, bf16[2,576,128]{2,1,0:T(8,128)(2,1)} %bitcast.8, f32[576]{0:T(1024)} %scales_hbm.1, bf16[2,576,1536]{2,1,0:T(8,128)(2,1)} %bitcast.7), custom_call_target="tpu_custom_call" | custom-call | flops 905969664 | bytes 3538944 | tf_op jit(solution)/shard_map/attend/pallas_call | solution.py:125
  5.1 1.9 %collective-permute-start = (bf16[2,32,512]{2,1,0:T(8,128)(2,1)S(1)}, bf16[2,32,512]{2,1,0:T(8,128)(2,1)S(1)}, u32[]{:S(2)}, u32[]{:S(2)}) collective-permute-start(bf16[2,32,512]{2,1,0:T(8,128)(2,1)S(1)} %get-tuple-element.14), channel_id=1, source_target_pairs={{0,3},{1,2},{2,1},{3,0},{4,7},{5,6},{6,5},{7,4},{8,11},{9,10},{10,... | collective-permute-start | bytes 196616 | tf_op jit(solution)/shard_map/ppermute | solution.py:250
  7.0 1.0 %collective-permute-start.1 = (bf16[2,32,512]{2,1,0:T(8,128)(2,1)S(1)}, bf16[2,32,512]{2,1,0:T(8,128)(2,1)S(1)}, u32[]{:S(2)}, u32[]{:S(2)}) collective-permute-start(bf16[2,32,512]{2,1,0:T(8,128)(2,1)S(1)} %get-tuple-element.15), channel_id=1, source_target_pairs={{0,2},{1,3},{2,0},{3,1},{4,6},{5,7},{6,4},{7,5},{8,10},{9,11},{10,... | collective-permute-start | bytes 196616 | tf_op jit(solution)/shard_map/ppermute | solution.py:250
  8.0 0.7 %collective-permute-start.2 = (bf16[2,32,512]{2,1,0:T(8,128)(2,1)S(1)}, bf16[2,32,512]{2,1,0:T(8,128)(2,1)S(1)}, u32[]{:S(2)}, u32[]{:S(2)}) collective-permute-start(bf16[2,32,512]{2,1,0:T(8,128)(2,1)S(1)} %get-tuple-element.16), channel_id=1, source_target_pairs={{0,1},{1,0},{2,3},{3,2},{4,5},{5,4},{6,7},{7,6},{8,9},{9,8},{10,11... | collective-permute-start | bytes 196616 | tf_op jit(solution)/shard_map/ppermute | solution.py:250
  8.6 2.2 %stage.1.refs_4_ = bf16[32,512,128]{2,1,0:T(8,128)(2,1)S(1)} custom-call(bf16[32,512,128]{2,1,0:T(8,128)(2,1)} %maps_hbm.1, bf16[2,32,512]{2,1,0:T(8,128)(2,1)S(1)} %get-tuple-element.13.after.refs_0_), custom_call_target="tpu_custom_call" | custom-call | bytes 8388608 | tf_op jit(solution)/shard_map/stage/pallas_call | solution.py:159
  10.8 0.0 collective-permute-done.refs_1_
  10.8 1.1 %collective-permute-done.1.refs_2_ = bf16[2,32,512]{2,1,0:T(8,128)(2,1)S(1)} collective-permute-done((bf16[2,32,512]{2,1,0:T(8,128)(2,1)S(1)}, bf16[2,32,512]{2,1,0:T(8,128)(2,1)S(1)}, u32[]{:S(2)}, u32[]{:S(2)}) %collective-permute-start.1) | collective-permute-done | bytes 65568 | tf_op jit(solution)/shard_map/ppermute | solution.py:250
  11.9 0.3 %collective-permute-done.2.refs_3_ = bf16[2,32,512]{2,1,0:T(8,128)(2,1)S(1)} collective-permute-done((bf16[2,32,512]{2,1,0:T(8,128)(2,1)S(1)}, bf16[2,32,512]{2,1,0:T(8,128)(2,1)S(1)}, u32[]{:S(2)}, u32[]{:S(2)}) %collective-permute-start.2) | collective-permute-done | bytes 65568 | tf_op jit(solution)/shard_map/ppermute | solution.py:250
  12.2 0.9 %project.1 = (bf16[32,2,128]{2,1,0:T(2,128)(2,1)S(1)}, bf16[32,2,128]{2,1,0:T(2,128)(2,1)S(1)}, bf16[32,2,128]{2,1,0:T(2,128)(2,1)S(1)}, bf16[32,2,128]{2,1,0:T(2,128)(2,1)S(1)}) custom-call(bf16[2,32,512]{2,1,0:T(8,128)(2,1)S(1)} %get-tuple-element.13.after.refs_0_, bf16[2,32,512]{2,1,0:T(8,128)(2,1)S(1)} %collective-permute-done.refs_1_, ...), custom_call_target="tpu_custom_call" | custom-call | flops 33554432 | bytes 4194304 | tf_op jit(solution)/shard_map/project/pallas_call | solution.py:205
  13.1 1.6 %collective-permute-start.3 = (bf16[32,2,128]{2,1,0:T(2,128)(2,1)S(1)}, bf16[32,2,128]{2,1,0:T(2,128)(2,1)S(1)}, u32[]{:S(2)}, u32[]{:S(2)}) collective-permute-start(bf16[32,2,128]{2,1,0:T(2,128)(2,1)S(1)} %get-tuple-element.18), channel_id=1, source_target_pairs={{0,3},{1,2},{2,1},{3,0},{4,7},{5,6},{6,5},{7,4},{8,11},{9,10},{10,... | collective-permute-start | bytes 49160 | tf_op jit(solution)/shard_map/ppermute | solution.py:250
  14.7 1.0 %collective-permute-start.4 = (bf16[32,2,128]{2,1,0:T(2,128)(2,1)S(1)}, bf16[32,2,128]{2,1,0:T(2,128)(2,1)S(1)}, u32[]{:S(2)}, u32[]{:S(2)}) collective-permute-start(bf16[32,2,128]{2,1,0:T(2,128)(2,1)S(1)} %get-tuple-element.19), channel_id=1, source_target_pairs={{0,2},{1,3},{2,0},{3,1},{4,6},{5,7},{6,4},{7,5},{8,10},{9,11},{10,... | collective-permute-start | bytes 49160 | tf_op jit(solution)/shard_map/ppermute | solution.py:250
  15.8 0.9 %collective-permute-start.5 = (bf16[32,2,128]{2,1,0:T(2,128)(2,1)S(1)}, bf16[32,2,128]{2,1,0:T(2,128)(2,1)S(1)}, u32[]{:S(2)}, u32[]{:S(2)}) collective-permute-start(bf16[32,2,128]{2,1,0:T(2,128)(2,1)S(1)} %get-tuple-element.20), channel_id=1, source_target_pairs={{0,1},{1,0},{2,3},{3,2},{4,5},{5,4},{6,7},{7,6},{8,9},{9,8},{10,11... | collective-permute-start | bytes 49160 | tf_op jit(solution)/shard_map/ppermute | solution.py:250
  16.6 1.1 %collective-permute-done.3.refs_1_ = bf16[32,2,128]{2,1,0:T(2,128)(2,1)S(1)} collective-permute-done((bf16[32,2,128]{2,1,0:T(2,128)(2,1)S(1)}, bf16[32,2,128]{2,1,0:T(2,128)(2,1)S(1)}, u32[]{:S(2)}, u32[]{:S(2)}) %collective-permute-start.3) | collective-permute-done | bytes 16416 | tf_op jit(solution)/shard_map/ppermute | solution.py:250
  17.8 0.7 %collective-permute-done.4.refs_2_ = bf16[32,2,128]{2,1,0:T(2,128)(2,1)S(1)} collective-permute-done((bf16[32,2,128]{2,1,0:T(2,128)(2,1)S(1)}, bf16[32,2,128]{2,1,0:T(2,128)(2,1)S(1)}, u32[]{:S(2)}, u32[]{:S(2)}) %collective-permute-start.4) | collective-permute-done | bytes 16416 | tf_op jit(solution)/shard_map/ppermute | solution.py:250
  18.5 1.0 %collective-permute-done.5.refs_3_ = bf16[32,2,128]{2,1,0:T(2,128)(2,1)S(1)} collective-permute-done((bf16[32,2,128]{2,1,0:T(2,128)(2,1)S(1)}, bf16[32,2,128]{2,1,0:T(2,128)(2,1)S(1)}, u32[]{:S(2)}, u32[]{:S(2)}) %collective-permute-start.5) | collective-permute-done | bytes 16416 | tf_op jit(solution)/shard_map/ppermute | solution.py:250
  19.5 0.7 %assemble.1 = bf16[4,32,2,128]{3,2,1,0:T(2,128)(2,1)} custom-call(bf16[32,2,128]{2,1,0:T(2,128)(2,1)S(1)} %get-tuple-element.17.refs_0_, bf16[32,2,128]{2,1,0:T(2,128)(2,1)S(1)} %collective-permute-done.3.refs_1_, bf16[32,2,128]{2,1,0:T(2,128)(2,1)S(1)} %collective-permute-done.4.refs_2_, bf16[32,2,128]{2,1,0:T(2,128)(2,1)S(1)} %collective-permute-done.5.refs_3_), custom_call_target="tpu_custom_call" | custom-call | tf_op jit(solution)/shard_map/assemble/pallas_call | solution.py:236
Async XLA Ops:
  5.1 5.8 %collective-permute-start = (bf16[2,32,512]{2,1,0:T(8,128)(2,1)S(1)}, bf16[2,32,512]{2,1,0:T(8,128)(2,1)S(1)}, u32[]{:S(2)}, u32[]{:S(2)}) collective-permute-start(bf16[2,32,512]{2,1,0:T(8,128)(2,1)S(1)} %get-tuple-element.14), channel_id=1, source_target_pairs={{0,3},{1,2},{2,1},{3,0},{4,7},{5,6},{6,5},{7,4},{8,11},{9,10},{10,... | collective-permute-start | bytes 196616 | tf_op jit(solution)/shard_map/ppermute | solution.py:250
  7.0 5.0 %collective-permute-start.1 = (bf16[2,32,512]{2,1,0:T(8,128)(2,1)S(1)}, bf16[2,32,512]{2,1,0:T(8,128)(2,1)S(1)}, u32[]{:S(2)}, u32[]{:S(2)}) collective-permute-start(bf16[2,32,512]{2,1,0:T(8,128)(2,1)S(1)} %get-tuple-element.15), channel_id=1, source_target_pairs={{0,2},{1,3},{2,0},{3,1},{4,6},{5,7},{6,4},{7,5},{8,10},{9,11},{10,... | collective-permute-start | bytes 196616 | tf_op jit(solution)/shard_map/ppermute | solution.py:250
  8.0 4.3 %collective-permute-start.2 = (bf16[2,32,512]{2,1,0:T(8,128)(2,1)S(1)}, bf16[2,32,512]{2,1,0:T(8,128)(2,1)S(1)}, u32[]{:S(2)}, u32[]{:S(2)}) collective-permute-start(bf16[2,32,512]{2,1,0:T(8,128)(2,1)S(1)} %get-tuple-element.16), channel_id=1, source_target_pairs={{0,1},{1,0},{2,3},{3,2},{4,5},{5,4},{6,7},{7,6},{8,9},{9,8},{10,11... | collective-permute-start | bytes 196616 | tf_op jit(solution)/shard_map/ppermute | solution.py:250
  13.1 4.7 %collective-permute-start.3 = (bf16[32,2,128]{2,1,0:T(2,128)(2,1)S(1)}, bf16[32,2,128]{2,1,0:T(2,128)(2,1)S(1)}, u32[]{:S(2)}, u32[]{:S(2)}) collective-permute-start(bf16[32,2,128]{2,1,0:T(2,128)(2,1)S(1)} %get-tuple-element.18), channel_id=1, source_target_pairs={{0,3},{1,2},{2,1},{3,0},{4,7},{5,6},{6,5},{7,4},{8,11},{9,10},{10,... | collective-permute-start | bytes 49160 | tf_op jit(solution)/shard_map/ppermute | solution.py:250
  14.7 3.7 %collective-permute-start.4 = (bf16[32,2,128]{2,1,0:T(2,128)(2,1)S(1)}, bf16[32,2,128]{2,1,0:T(2,128)(2,1)S(1)}, u32[]{:S(2)}, u32[]{:S(2)}) collective-permute-start(bf16[32,2,128]{2,1,0:T(2,128)(2,1)S(1)} %get-tuple-element.19), channel_id=1, source_target_pairs={{0,2},{1,3},{2,0},{3,1},{4,6},{5,7},{6,4},{7,5},{8,10},{9,11},{10,... | collective-permute-start | bytes 49160 | tf_op jit(solution)/shard_map/ppermute | solution.py:250
  15.8 3.7 %collective-permute-start.5 = (bf16[32,2,128]{2,1,0:T(2,128)(2,1)S(1)}, bf16[32,2,128]{2,1,0:T(2,128)(2,1)S(1)}, u32[]{:S(2)}, u32[]{:S(2)}) collective-permute-start(bf16[32,2,128]{2,1,0:T(2,128)(2,1)S(1)} %get-tuple-element.20), channel_id=1, source_target_pairs={{0,1},{1,0},{2,3},{3,2},{4,5},{5,4},{6,7},{7,6},{8,9},{9,8},{10,11... | collective-permute-start | bytes 49160 | tf_op jit(solution)/shard_map/ppermute | solution.py:250

commit v8 on v7

--- a/solution.py
+++ b/solution.py
@@ -149,10 +149,19 @@
     )(*in_hbm(lengths, jnp.swapaxes(query, 1, 2), scales, jnp.swapaxes(cache, 1, 2)))
 
 
-def stage_kernel(maps_hbm, after, maps, sem):
-    copy = pltpu.make_async_copy(maps_hbm, maps, sem)
-    copy.start()
-    copy.wait()
+def stage_kernel(maps_hbm, after, maps, sems):
+    count = sems.shape[0]
+    size = maps.shape[0] // count
+    copies = [
+        pltpu.make_async_copy(
+            maps_hbm.at[pl.ds(i * size, size)], maps.at[pl.ds(i * size, size)], sems.at[i]
+        )
+        for i in range(count)
+    ]
+    for copy in copies:
+        copy.start()
+    for copy in copies:
+        copy.wait()
 
 
 def stage(maps, after):
@@ -161,7 +170,7 @@
         out_shape=jax.ShapeDtypeStruct(maps.shape, maps.dtype),
         in_specs=[pl.BlockSpec(memory_space=pl.ANY)] * 2,
         out_specs=pl.BlockSpec(memory_space=pltpu.VMEM),
-        scratch_shapes=[pltpu.SemaphoreType.DMA(())],
+        scratch_shapes=[pltpu.SemaphoreType.DMA((math.gcd(maps.shape[0], 8),))],
         compiler_params=pltpu.CompilerParams(vmem_limit_bytes=8 * 2**20),
         cost_estimate=pl.CostEstimate(
             flops=0, bytes_accessed=4 * maps.size, transcendentals=0
@@ -170,60 +179,63 @@
     )(*in_hbm(maps), after)
 
 
-def project_kernel(owners, *refs):
-    parts, maps, outs, rows = refs[:owners], refs[owners], refs[owners + 1:-1], refs[-1]
+def project_kernel(count, *refs):
+    parts, maps, outs, rows = refs[:count], refs[count], refs[-1 - count:-1], refs[-1]
     requests, local_heads, rank = parts[0].shape
     width = maps.shape[2]
-    batch = owners * requests
+    batch = count * requests
+    group = min(max(1, 16 // batch), local_heads)
     for b in range(batch):
         for k in range(rank // LANES):
             rows[k, b * local_heads:(b + 1) * local_heads] = parts[b // requests][
                 b % requests, :, k * LANES:(k + 1) * LANES
             ].astype(jnp.float32)
-    for h in range(0, local_heads, 2):
-        pair = jnp.concatenate(
+    for first in range(0, local_heads, group):
+        heads = range(first, first + group)
+        mixed = jnp.concatenate(
             [
                 jnp.concatenate(
-                    [rows[k, pl.ds(h + i, batch, stride=local_heads), :] for i in range(2)], axis=0
+                    [rows[k, pl.ds(h, batch, stride=local_heads), :] for h in heads], axis=0
                 ).astype(jnp.bfloat16)
                 for k in range(rank // LANES)
             ],
             axis=1,
         )
-        both = jnp.concatenate([maps[h], maps[h + 1]], axis=1)
-        values = jnp.dot(pair, both, preferred_element_type=jnp.float32)
-        for i in range(2):
-            mine = values[i * batch:(i + 1) * batch, i * width:(i + 1) * width]
+        wide = jnp.concatenate([maps[h] for h in heads], axis=1)
+        values = jnp.dot(mixed, wide, preferred_element_type=jnp.float32)
+        for i, h in enumerate(heads):
+            own = values[i * batch:(i + 1) * batch, i * width:(i + 1) * width]
             for d, out in enumerate(outs):
-                out[h + i] = mine[d * requests:(d + 1) * requests].astype(jnp.bfloat16)
-
-
-def project(latents, maps):
-    owners = len(latents)
-    requests, local_heads, rank = latents[0].shape
+                out[h] = own[d * requests:(d + 1) * requests].astype(jnp.bfloat16)
+
+
+def project(parts, maps, earlier):
+    count = len(parts)
+    requests, local_heads, rank = parts[0].shape
     width = maps.shape[2]
     return pl.pallas_call(
-        functools.partial(project_kernel, owners),
-        out_shape=[jax.ShapeDtypeStruct((local_heads, requests, width), jnp.bfloat16)] * owners,
-        in_specs=[pl.BlockSpec(memory_space=pltpu.VMEM)] * (owners + 1),
-        out_specs=[pl.BlockSpec(memory_space=pltpu.VMEM)] * owners,
-        scratch_shapes=[pltpu.VMEM((rank // LANES, owners * requests * local_heads, LANES), jnp.float32)],
+        functools.partial(project_kernel, count),
+        out_shape=[jax.ShapeDtypeStruct((local_heads, requests, width), jnp.bfloat16)] * count,
+        in_specs=[pl.BlockSpec(memory_space=pltpu.VMEM)] * (count + 1)
+        + [pl.BlockSpec(memory_space=pl.ANY)] * len(earlier),
+        out_specs=[pl.BlockSpec(memory_space=pltpu.VMEM)] * count,
+        scratch_shapes=[pltpu.VMEM((rank // LANES, count * requests * local_heads, LANES), jnp.float32)],
         compiler_params=pltpu.CompilerParams(vmem_limit_bytes=24 * 2**20),
         cost_estimate=pl.CostEstimate(
-            flops=2 * owners * requests * local_heads * rank * width,
+            flops=2 * count * requests * local_heads * rank * width,
             bytes_accessed=2 * local_heads * rank * width,
             transcendentals=0,
         ),
         name="project",
-    )(*latents, maps)
-
-
-def assemble_kernel(owners, *refs):
-    parts, out, sems = refs[:owners], refs[owners], refs[owners + 1]
+    )(*parts, maps, *earlier)
+
+
+def assemble_kernel(partners, *refs):
+    parts, (out, sems) = refs[:len(partners)], refs[-2:]
     me = lax.axis_index("tp")
     copies = [
-        pltpu.make_async_copy(part, out.at[me ^ k], sems.at[k])
-        for k, part in zip(order(owners), parts)
+        pltpu.make_async_copy(part, out.at[me ^ k], sems.at[i])
+        for i, (k, part) in enumerate(zip(partners, parts))
     ]
     for copy in copies:
         copy.start()
@@ -231,24 +243,24 @@
         copy.wait()
 
 
-def assemble(parts):
-    owners = len(parts)
-    return pl.pallas_call(
-        functools.partial(assemble_kernel, owners),
+def assemble(parts, partners, owners, begun):
+    return pl.pallas_call(
+        functools.partial(assemble_kernel, partners),
         out_shape=pltpu.HBM((owners,) + parts[0].shape, parts[0].dtype),
-        in_specs=[pl.BlockSpec(memory_space=pltpu.VMEM)] * owners,
+        in_specs=[pl.BlockSpec(memory_space=pltpu.VMEM)] * len(parts)
+        + [pl.BlockSpec(memory_space=pltpu.HBM)] * len(begun),
         out_specs=pl.BlockSpec(memory_space=pltpu.HBM),
-        scratch_shapes=[pltpu.SemaphoreType.DMA((owners,))],
+        scratch_shapes=[pltpu.SemaphoreType.DMA((len(parts),))],
+        input_output_aliases={len(parts): 0} if begun else {},
         compiler_params=pltpu.CompilerParams(vmem_limit_bytes=2 * 2**20),
         name="assemble",
-    )(*parts)
-
-
-def exchange(parts):
-    owners = len(parts)
+    )(*parts, *begun)
+
+
+def exchange(parts, partners, owners):
     return [
         lax.ppermute(part, "tp", [(i, i ^ k) for i in range(owners)]) if k else part
-        for k, part in zip(order(owners), parts)
+        for k, part in zip(partners, parts)
     ]
 
 
@@ -256,8 +268,17 @@
     owners = lax.axis_size("tp")
     latents = attend(query, cache, scales, lengths, owners)
     maps = stage(value_up, latents[0])
-    values = exchange(project(exchange(latents), maps))
-    returned = assemble(values)
+    partners = order(owners)
+    received = exchange(latents, partners, owners)
+    groups = [slice(0, owners // 2), slice(owners // 2, owners)]
+    values = []
+    for some in groups:
+        earlier = values[0][:1] if values else []
+        values.append(exchange(project(received[some], maps, earlier), partners[some], owners))
+    begun = []
+    for some, parts in zip(groups, values):
+        begun = [assemble(parts, partners[some], owners, begun)]
+    returned = begun[0]
     _, local_heads, requests, width = returned.shape
     returned = returned.reshape(owners * local_heads, requests, width)
     return jnp.swapaxes(returned, 0, 1).reshape(requests, owners * local_heads * width)

time: 20.4 us -> 20 us (0.980); the launches traced: 20.1 us -> 20.1 us
  starting transfers between devices: 7.12 us -> 9.02 us
  waiting for transfers between devices: 4.24 us -> 3.11 us
  Pallas kernels: 8.75 us -> 7.95 us
    pallas_call x1, Pallas kernels: 5.05 us -> 2.99 us  [attend(): pl.pallas_call(functools.partial(attend_kernel, owners), out_shape=[part]...]
    ppermute x6, starting transfers between devices: 7.12 us -> 9.02 us  [exchange(): lax.ppermute(part, 'tp', [(i, i ^ k) for i in range(owners)])]
    pallas_call x2 -> x4, Pallas kernels: 1.51 us -> 2.75 us  [the longest x2 1.49 us: project(): pl.pallas_call(functools.partial(project_kernel, count), out_shape=[jax.S...]
    ppermute x6, waiting for transfers between devices: 4.24 us -> 3.11 us  [exchange(): lax.ppermute(part, 'tp', [(i, i ^ k) for i in range(owners)])]
  transfers between devices with their start and end apart: 6 -> 6, of which waited for: 5 -> 3; matrix products, arithmetic and copies ran while one was open for 0% -> 0% of each run, Pallas kernels for 11% -> 22%
where the time goes in v8:
time: 20 us; the launch traced here: 20.1 us
  starting transfers between devices  9.02 us (45%)
  Pallas kernels  7.95 us (40%)
  waiting for transfers between devices  3.11 us (16%)
    ppermute x6, starting transfers between devices, exchange(): lax.ppermute(part, 'tp', [(i, i ^ k) for i in range(owners)])  9.02 us
    ppermute x6, waiting for transfers between devices, exchange(): lax.ppermute(part, 'tp', [(i, i ^ k) for i in range(owners)])  3.11 us
    pallas_call x1, Pallas kernels, attend(): pl.pallas_call(functools.partial(attend_kernel, owners), out_shape=[part]...  2.99 us
    pallas_call x1, Pallas kernels, stage(): pl.pallas_call(stage_kernel, out_shape=jax.ShapeDtypeStruct(maps.shape, m...  2.21 us
    pallas_call x2, Pallas kernels, project(): pl.pallas_call(functools.partial(project_kernel, count), out_shape=[jax.S...  1.49 us
    pallas_call x2, Pallas kernels, assemble(): pl.pallas_call(functools.partial(assemble_kernel, partners), out_shape=pl...  1.25 us
  transfers between devices with their start and end apart: 6, of which 3 were waited for; matrix products, arithmetic and copies ran while one was open for 0% of the time, Pallas kernels for 22%

profile of v8, /device:TPU:0, one launch (start us, length us, event | category | flops | bytes accessed | tf_op | source)
XLA Modules:
  0.0 20.1 jit_solution(5596774183487677394)
XLA Ops:
  0.0 3.0 %attend.1 = (bf16[2,32,512]{2,1,0:T(8,128)(2,1)S(1)}, bf16[2,32,512]{2,1,0:T(8,128)(2,1)S(1)}, bf16[2,32,512]{2,1,0:T(8,128)(2,1)S(1)}, bf16[2,32,512]{2,1,0:T(8,128)(2,1)S(1)}) custom-call(s32[2]{0:T(128)} %lengths_hbm.1, bf16[2,576,128]{2,1,0:T(8,128)(2,1)} %bitcast.8, f32[576]{0:T(1024)} %scales_hbm.1, bf16[2,576,1536]{2,1,0:T(8,128)(2,1)} %bitcast.7), custom_call_target="tpu_custom_call" | custom-call | flops 905969664 | bytes 3538944 | tf_op jit(solution)/shard_map/attend/pallas_call | solution.py:125
  3.0 4.5 %collective-permute-start.2 = (bf16[2,32,512]{2,1,0:T(8,128)(2,1)S(1)}, bf16[2,32,512]{2,1,0:T(8,128)(2,1)S(1)}, u32[]{:S(2)}, u32[]{:S(2)}) collective-permute-start(bf16[2,32,512]{2,1,0:T(8,128)(2,1)S(1)} %get-tuple-element.16), channel_id=1, source_target_pairs={{0,3},{1,2},{2,1},{3,0},{4,7},{5,6},{6,5},{7,4},{8,11},{9,10},{10,... | collective-permute-start | bytes 196616 | tf_op jit(solution)/shard_map/ppermute | solution.py:262
  7.5 1.0 %collective-permute-start = (bf16[2,32,512]{2,1,0:T(8,128)(2,1)S(1)}, bf16[2,32,512]{2,1,0:T(8,128)(2,1)S(1)}, u32[]{:S(2)}, u32[]{:S(2)}) collective-permute-start(bf16[2,32,512]{2,1,0:T(8,128)(2,1)S(1)} %get-tuple-element.13), channel_id=1, source_target_pairs={{0,2},{1,3},{2,0},{3,1},{4,6},{5,7},{6,4},{7,5},{8,10},{9,11},{10,... | collective-permute-start | bytes 196616 | tf_op jit(solution)/shard_map/ppermute | solution.py:262
  8.5 0.0 collective-permute-start.1
  8.5 2.2 %stage.1.refs_2_ = bf16[32,512,128]{2,1,0:T(8,128)(2,1)S(1)} custom-call(bf16[32,512,128]{2,1,0:T(8,128)(2,1)} %maps_hbm.1, bf16[2,32,512]{2,1,0:T(8,128)(2,1)S(1)} %get-tuple-element.15.after.refs_0_), custom_call_target="tpu_custom_call" | custom-call | bytes 8388608 | tf_op jit(solution)/shard_map/stage/pallas_call | solution.py:168
  10.7 0.0 collective-permute-done.2.refs_1_
  10.7 0.7 %project.2 = (bf16[32,2,128]{2,1,0:T(2,128)(2,1)S(1)}, bf16[32,2,128]{2,1,0:T(2,128)(2,1)S(1)}) custom-call(bf16[2,32,512]{2,1,0:T(8,128)(2,1)S(1)} %get-tuple-element.15.after.refs_0_, bf16[2,32,512]{2,1,0:T(8,128)(2,1)S(1)} %collective-permute-done.2.refs_1_, bf16[32,512,128]{2,1,0:T(8,128)(2,1)S(1)} %stage.1.refs_2_), custom_call_target="tpu_custom_call" | custom-call | flops 16777216 | bytes 4194304 | tf_op jit(solution)/shard_map/project/pallas_call | solution.py:216
  11.5 2.5 %collective-permute-start.5 = (bf16[32,2,128]{2,1,0:T(2,128)(2,1)S(1)}, bf16[32,2,128]{2,1,0:T(2,128)(2,1)S(1)}, u32[]{:S(2)}, u32[]{:S(2)}) collective-permute-start(bf16[32,2,128]{2,1,0:T(2,128)(2,1)S(1)} %get-tuple-element.20), channel_id=1, source_target_pairs={{0,3},{1,2},{2,1},{3,0},{4,7},{5,6},{6,5},{7,4},{8,11},{9,10},{10,... | collective-permute-start | bytes 49160 | tf_op jit(solution)/shard_map/ppermute | solution.py:262
  14.0 0.0 collective-permute-done.refs_0_
  14.0 0.0 collective-permute-done.1.refs_1_
  14.0 0.7 %project.3 = (bf16[32,2,128]{2,1,0:T(2,128)(2,1)S(1)}, bf16[32,2,128]{2,1,0:T(2,128)(2,1)S(1)}) custom-call(bf16[2,32,512]{2,1,0:T(8,128)(2,1)S(1)} %collective-permute-done.refs_0_, bf16[2,32,512]{2,1,0:T(8,128)(2,1)S(1)} %collective-permute-done.1.refs_1_, bf16[32,512,128]{2,1,0:T(8,128)(2,1)S(1)} %stage.1.refs_2_, ...), custom_call_target="tpu_custom_call" | custom-call | flops 16777216 | bytes 4194304 | tf_op jit(solution)/shard_map/project/pallas_call | solution.py:216
  14.7 1.0 %collective-permute-start.3 = (bf16[32,2,128]{2,1,0:T(2,128)(2,1)S(1)}, bf16[32,2,128]{2,1,0:T(2,128)(2,1)S(1)}, u32[]{:S(2)}, u32[]{:S(2)}) collective-permute-start(bf16[32,2,128]{2,1,0:T(2,128)(2,1)S(1)} %get-tuple-element.18), channel_id=1, source_target_pairs={{0,2},{1,3},{2,0},{3,1},{4,6},{5,7},{6,4},{7,5},{8,10},{9,11},{10,... | collective-permute-start | bytes 49160 | tf_op jit(solution)/shard_map/ppermute | solution.py:262
  15.7 0.0 collective-permute-start.4
  15.8 0.4 %collective-permute-done.5.refs_1_ = bf16[32,2,128]{2,1,0:T(2,128)(2,1)S(1)} collective-permute-done((bf16[32,2,128]{2,1,0:T(2,128)(2,1)S(1)}, bf16[32,2,128]{2,1,0:T(2,128)(2,1)S(1)}, u32[]{:S(2)}, u32[]{:S(2)}) %collective-permute-start.5) | collective-permute-done | bytes 16416 | tf_op jit(solution)/shard_map/ppermute | solution.py:262
  16.1 0.6 %assemble.2.refs_2_ = bf16[4,32,2,128]{3,2,1,0:T(2,128)(2,1)} custom-call(bf16[32,2,128]{2,1,0:T(2,128)(2,1)S(1)} %get-tuple-element.17.refs_3_.refs_0_, bf16[32,2,128]{2,1,0:T(2,128)(2,1)S(1)} %collective-permute-done.5.refs_1_), custom_call_target="tpu_custom_call" | custom-call | tf_op jit(solution)/shard_map/assemble/pallas_call | solution.py:247
  16.8 1.7 %collective-permute-done.3.refs_0_ = bf16[32,2,128]{2,1,0:T(2,128)(2,1)S(1)} collective-permute-done((bf16[32,2,128]{2,1,0:T(2,128)(2,1)S(1)}, bf16[32,2,128]{2,1,0:T(2,128)(2,1)S(1)}, u32[]{:S(2)}, u32[]{:S(2)}) %collective-permute-start.3) | collective-permute-done | bytes 16416 | tf_op jit(solution)/shard_map/ppermute | solution.py:262
  18.5 1.0 %collective-permute-done.4.refs_1_ = bf16[32,2,128]{2,1,0:T(2,128)(2,1)S(1)} collective-permute-done((bf16[32,2,128]{2,1,0:T(2,128)(2,1)S(1)}, bf16[32,2,128]{2,1,0:T(2,128)(2,1)S(1)}, u32[]{:S(2)}, u32[]{:S(2)}) %collective-permute-start.4) | collective-permute-done | bytes 16416 | tf_op jit(solution)/shard_map/ppermute | solution.py:262
  19.5 0.6 %assemble.3 = bf16[4,32,2,128]{3,2,1,0:T(2,128)(2,1)} custom-call(bf16[32,2,128]{2,1,0:T(2,128)(2,1)S(1)} %collective-permute-done.3.refs_0_, bf16[32,2,128]{2,1,0:T(2,128)(2,1)S(1)} %collective-permute-done.4.refs_1_, bf16[4,32,2,128]{3,2,1,0:T(2,128)(2,1)} %assemble.2.refs_2_), custom_call_target="tpu_custom_call", output_to_operand_aliasing={{}: (2, {})} | custom-call | tf_op jit(solution)/shard_map/assemble/pallas_call | solution.py:247
Async XLA Ops:
  3.0 7.7 %collective-permute-start.2 = (bf16[2,32,512]{2,1,0:T(8,128)(2,1)S(1)}, bf16[2,32,512]{2,1,0:T(8,128)(2,1)S(1)}, u32[]{:S(2)}, u32[]{:S(2)}) collective-permute-start(bf16[2,32,512]{2,1,0:T(8,128)(2,1)S(1)} %get-tuple-element.16), channel_id=1, source_target_pairs={{0,3},{1,2},{2,1},{3,0},{4,7},{5,6},{6,5},{7,4},{8,11},{9,10},{10,... | collective-permute-start | bytes 196616 | tf_op jit(solution)/shard_map/ppermute | solution.py:262
  7.5 6.5 %collective-permute-start = (bf16[2,32,512]{2,1,0:T(8,128)(2,1)S(1)}, bf16[2,32,512]{2,1,0:T(8,128)(2,1)S(1)}, u32[]{:S(2)}, u32[]{:S(2)}) collective-permute-start(bf16[2,32,512]{2,1,0:T(8,128)(2,1)S(1)} %get-tuple-element.13), channel_id=1, source_target_pairs={{0,2},{1,3},{2,0},{3,1},{4,6},{5,7},{6,4},{7,5},{8,10},{9,11},{10,... | collective-permute-start | bytes 196616 | tf_op jit(solution)/shard_map/ppermute | solution.py:262
  8.5 5.5 %collective-permute-start.1 = (bf16[2,32,512]{2,1,0:T(8,128)(2,1)S(1)}, bf16[2,32,512]{2,1,0:T(8,128)(2,1)S(1)}, u32[]{:S(2)}, u32[]{:S(2)}) collective-permute-start(bf16[2,32,512]{2,1,0:T(8,128)(2,1)S(1)} %get-tuple-element.14), channel_id=1, source_target_pairs={{0,1},{1,0},{2,3},{3,2},{4,5},{5,4},{6,7},{7,6},{8,9},{9,8},{10,11... | collective-permute-start | bytes 196616 | tf_op jit(solution)/shard_map/ppermute | solution.py:262
  11.5 4.7 %collective-permute-start.5 = (bf16[32,2,128]{2,1,0:T(2,128)(2,1)S(1)}, bf16[32,2,128]{2,1,0:T(2,128)(2,1)S(1)}, u32[]{:S(2)}, u32[]{:S(2)}) collective-permute-start(bf16[32,2,128]{2,1,0:T(2,128)(2,1)S(1)} %get-tuple-element.20), channel_id=1, source_target_pairs={{0,3},{1,2},{2,1},{3,0},{4,7},{5,6},{6,5},{7,4},{8,11},{9,10},{10,... | collective-permute-start | bytes 49160 | tf_op jit(solution)/shard_map/ppermute | solution.py:262
  14.7 3.8 %collective-permute-start.3 = (bf16[32,2,128]{2,1,0:T(2,128)(2,1)S(1)}, bf16[32,2,128]{2,1,0:T(2,128)(2,1)S(1)}, u32[]{:S(2)}, u32[]{:S(2)}) collective-permute-start(bf16[32,2,128]{2,1,0:T(2,128)(2,1)S(1)} %get-tuple-element.18), channel_id=1, source_target_pairs={{0,2},{1,3},{2,0},{3,1},{4,6},{5,7},{6,4},{7,5},{8,10},{9,11},{10,... | collective-permute-start | bytes 49160 | tf_op jit(solution)/shard_map/ppermute | solution.py:262
  15.7 3.7 %collective-permute-start.4 = (bf16[32,2,128]{2,1,0:T(2,128)(2,1)S(1)}, bf16[32,2,128]{2,1,0:T(2,128)(2,1)S(1)}, u32[]{:S(2)}, u32[]{:S(2)}) collective-permute-start(bf16[32,2,128]{2,1,0:T(2,128)(2,1)S(1)} %get-tuple-element.19), channel_id=1, source_target_pairs={{0,1},{1,0},{2,3},{3,2},{4,5},{5,4},{6,7},{7,6},{8,9},{9,8},{10,11... | collective-permute-start | bytes 49160 | tf_op jit(solution)/shard_map/ppermute | solution.py:262

commit v9 on v8

--- a/solution.py
+++ b/solution.py
@@ -19,8 +19,8 @@
     return [0] + list(range(owners - 1, 0, -1))
 
 
-def attend_kernel(owners, lengths_hbm, query_hbm, scales_hbm, cache, *refs):
-    outs, refs = refs[:owners], refs[owners:]
+def attend_kernel(owners, lengths_hbm, query_hbm, scales_hbm, cache, maps_hbm, *refs):
+    outs, maps, refs = refs[:owners], refs[owners], refs[owners + 1:]
     latents, lengths, query, scales, keys, scaled, scores, weights, sems, small_sems = refs
     requests, channels, heads = query.shape
     local_heads, rank = latents.shape[2:]
@@ -41,38 +41,53 @@
     ]
     for copy in small:
         copy.start()
-    for b in range(blocks):
-        for r in range(requests):
-            fetch(r, b).start()
+    for r in range(requests):
+        fetch(r, 0).start()
+    small[0].wait()
+    pairs = []
+    for first in range(0, requests, 2):
+        swap = (lengths[first] < lengths[first + 1]).astype(jnp.int32)
+        pairs.append((first + swap, first + 1 - swap))
+    for r in [r for pair in pairs for r in pair]:
+        for b in range(1, blocks):
+            @pl.when(b * block < lengths[r])
+            def _():
+                fetch(r, b).start()
+    maps_copy = pltpu.make_async_copy(maps_hbm, maps, small_sems.at[3])
+    maps_copy.start()
     small[1].wait()
     small[2].wait()
     scale_row = scales[...].reshape(1, channels)
     for r in range(requests):
         scaled[r] = (query[r].astype(jnp.float32).T * scale_row).astype(jnp.bfloat16)
-    small[0].wait()
+
+    def spread(column):
+        return jnp.broadcast_to(column, (heads, LANES))
 
     def score(slot, r, live):
         top = None
         for b in range(live):
             fetch(r, b).wait()
-            span = slice(b * block, (b + 1) * block)
-            part = jnp.dot(scaled[r], keys[r, :, span], preferred_element_type=jnp.float32)
+            part = jnp.dot(
+                scaled[r], keys[r, :, b * block:(b + 1) * block],
+                preferred_element_type=jnp.float32,
+            )
             if b == live - 1:
                 place = b * block + lax.broadcasted_iota(jnp.int32, part.shape, 1)
                 part = jnp.where(place < lengths[r], part, -jnp.inf)
-            scores[slot, :, span] = part
-            high = jnp.max(part, axis=1, keepdims=True)
-            top = high if top is None else jnp.maximum(top, high)
-        return top
+            for at in range(0, block, LANES):
+                piece = part[:, at:at + LANES]
+                scores[slot, :, b * block + at:b * block + at + LANES] = piece
+                top = piece if top is None else jnp.maximum(top, piece)
+        return spread(jnp.max(top, axis=1, keepdims=True))
 
     def weigh(slot, live, top):
-        total = jnp.zeros_like(top)
-        for b in range(live):
-            span = slice(b * block, (b + 1) * block)
-            weight = jnp.exp2((scores[slot, :, span] - top) * EXP2_SCALE)
-            total += jnp.sum(weight, axis=1, keepdims=True)
-            weights[slot, :, span] = weight.astype(jnp.bfloat16)
-        return total
+        total = None
+        for at in range(0, live * block, LANES):
+            weight = jnp.exp2((scores[slot, :, at:at + LANES] - top) * EXP2_SCALE)
+            total = weight if total is None else total + weight
+            weights[slot, :, at:at + LANES] = weight.astype(jnp.bfloat16)
+        return jnp.sum(total, axis=1, keepdims=True)
 
     def mix(slot, r, live):
         return lax.dot_general(
@@ -94,14 +109,8 @@
         finish(r, mixture_r, total_r)
         mixture_s = mix(1, s, live_s)
         finish(s, mixture_s, total_s)
-        for b in range(live_r, blocks):
-            fetch(r, b).wait()
-        for b in range(live_s, blocks):
-            fetch(s, b).wait()
-
-    for first in range(0, requests, 2):
-        swap = (lengths[first] < lengths[first + 1]).astype(jnp.int32)
-        longer, shorter = first + swap, first + 1 - swap
+
+    for longer, shorter in pairs:
         live = [(lengths[r] + (block - 1)) // block for r in (longer, shorter)]
         for live_r in range(1, blocks + 1):
             for live_s in range(1, live_r + 1):
@@ -111,22 +120,23 @@
 
     for out, k in zip(outs, order(owners)):
         out[...] = latents[me ^ k]
+    maps_copy.wait()
 
 
 def in_hbm(*arrays):
     return [pltpu.with_memory_space_constraint(array, pltpu.HBM) for array in arrays]
 
 
-def attend(query, cache, scales, lengths, owners):
+def attend(query, cache, scales, lengths, maps, owners):
     requests, heads, channels = query.shape
     cache_len = cache.shape[1]
     rank = channels - ROPE_DIM
     part = jax.ShapeDtypeStruct((requests, heads // owners, rank), jnp.bfloat16)
     return pl.pallas_call(
         functools.partial(attend_kernel, owners),
-        out_shape=[part] * owners,
-        in_specs=[pl.BlockSpec(memory_space=pl.ANY)] * 4,
-        out_specs=[pl.BlockSpec(memory_space=pltpu.VMEM)] * owners,
+        out_shape=[part] * owners + [jax.ShapeDtypeStruct(maps.shape, maps.dtype)],
+        in_specs=[pl.BlockSpec(memory_space=pl.ANY)] * 5,
+        out_specs=[pl.BlockSpec(memory_space=pltpu.VMEM)] * (owners + 1),
         scratch_shapes=[
             pltpu.VMEM((owners,) + part.shape, part.dtype),
             pltpu.SMEM((requests,), jnp.int32),
@@ -137,7 +147,7 @@
             pltpu.VMEM((2, heads, cache_len), jnp.float32),
             pltpu.VMEM((2, heads, cache_len), jnp.bfloat16),
             pltpu.SemaphoreType.DMA((requests, cache_len // min(BLOCK, cache_len))),
-            pltpu.SemaphoreType.DMA((3,)),
+            pltpu.SemaphoreType.DMA((4,)),
         ],
         compiler_params=pltpu.CompilerParams(vmem_limit_bytes=24 * 2**20),
         cost_estimate=pl.CostEstimate(
@@ -146,37 +156,7 @@
             transcendentals=requests * heads * cache_len,
         ),
         name="attend",
-    )(*in_hbm(lengths, jnp.swapaxes(query, 1, 2), scales, jnp.swapaxes(cache, 1, 2)))
-
-
-def stage_kernel(maps_hbm, after, maps, sems):
-    count = sems.shape[0]
-    size = maps.shape[0] // count
-    copies = [
-        pltpu.make_async_copy(
-            maps_hbm.at[pl.ds(i * size, size)], maps.at[pl.ds(i * size, size)], sems.at[i]
-        )
-        for i in range(count)
-    ]
-    for copy in copies:
-        copy.start()
-    for copy in copies:
-        copy.wait()
-
-
-def stage(maps, after):
-    return pl.pallas_call(
-        stage_kernel,
-        out_shape=jax.ShapeDtypeStruct(maps.shape, maps.dtype),
-        in_specs=[pl.BlockSpec(memory_space=pl.ANY)] * 2,
-        out_specs=pl.BlockSpec(memory_space=pltpu.VMEM),
-        scratch_shapes=[pltpu.SemaphoreType.DMA((math.gcd(maps.shape[0], 8),))],
-        compiler_params=pltpu.CompilerParams(vmem_limit_bytes=8 * 2**20),
-        cost_estimate=pl.CostEstimate(
-            flops=0, bytes_accessed=4 * maps.size, transcendentals=0
-        ),
-        name="stage",
-    )(*in_hbm(maps), after)
+    )(*in_hbm(lengths, jnp.swapaxes(query, 1, 2), scales, jnp.swapaxes(cache, 1, 2), maps))
 
 
 def project_kernel(count, *refs):
@@ -266,8 +246,7 @@
 
 def on_device(query, cache, scales, lengths, value_up):
     owners = lax.axis_size("tp")
-    latents = attend(query, cache, scales, lengths, owners)
-    maps = stage(value_up, latents[0])
+    *latents, maps = attend(query, cache, scales, lengths, value_up, owners)
     partners = order(owners)
     received = exchange(latents, partners, owners)
     groups = [slice(0, owners // 2), slice(owners // 2, owners)]

time: 20 us -> 21.1 us (1.055); the launches traced: 20.1 us -> 20.9 us
  waiting for transfers between devices: 3.11 us -> 4.65 us
  Pallas kernels: 7.95 us -> 7.07 us
    pallas_call x1 -> x0, Pallas kernels: 2.21 us -> none  [stage(): pl.pallas_call(stage_kernel, out_shape=jax.ShapeDtypeStruct(maps.shape, m...]
    ppermute x6, waiting for transfers between devices: 3.11 us -> 4.65 us  [exchange(): lax.ppermute(part, 'tp', [(i, i ^ k) for i in range(owners)])]
    pallas_call x1, Pallas kernels: 2.99 us -> 4.32 us  [attend(): pl.pallas_call(functools.partial(attend_kernel, owners), out_shape=[part]...]
  transfers between devices with their start and end apart: 6 -> 6, of which waited for: 3 -> 3; matrix products, arithmetic and copies ran while one was open for 0% -> 0% of each run, Pallas kernels for 22% -> 10%
where the time goes in v9:
time: 21.1 us; the launch traced here: 20.9 us
  starting transfers between devices  9.19 us (44%)
  Pallas kernels  7.07 us (34%)
  waiting for transfers between devices  4.65 us (22%)
    ppermute x6, starting transfers between devices, exchange(): lax.ppermute(part, 'tp', [(i, i ^ k) for i in range(owners)])  9.19 us
    ppermute x6, waiting for transfers between devices, exchange(): lax.ppermute(part, 'tp', [(i, i ^ k) for i in range(owners)])  4.65 us
    pallas_call x1, Pallas kernels, attend(): pl.pallas_call(functools.partial(attend_kernel, owners), out_shape=[part]...  4.32 us
    pallas_call x2, Pallas kernels, project(): pl.pallas_call(functools.partial(project_kernel, count), out_shape=[jax.S...  1.49 us
    pallas_call x2, Pallas kernels, assemble(): pl.pallas_call(functools.partial(assemble_kernel, partners), out_shape=pl...  1.25 us
  transfers between devices with their start and end apart: 6, of which 3 were waited for; matrix products, arithmetic and copies ran while one was open for 0% of the time, Pallas kernels for 10%

profile of v9, /device:TPU:0, one launch (start us, length us, event | category | flops | bytes accessed | tf_op | source)
XLA Modules:
  0.0 20.9 jit_solution(15438598777921238761)
XLA Ops:
  0.0 4.3 %attend.1 = (bf16[2,32,512]{2,1,0:T(8,128)(2,1)S(1)}, bf16[2,32,512]{2,1,0:T(8,128)(2,1)S(1)}, bf16[2,32,512]{2,1,0:T(8,128)(2,1)S(1)}, bf16[2,32,512]{2,1,0:T(8,128)(2,1)S(1)}, bf16[32,512,128]{2,1,0:T(8,128)(2,1)S(1)}) custom-call(s32[2]{0:T(128)} %lengths_hbm.1, bf16[2,576,128]{2,1,0:T(8,128)(2,1)} %bitcast.8, f32[576]{0:T(1024)} %scales_hbm.1, ...), custom_call_target="tpu_custom_call" | custom-call | flops 905969664 | bytes 3538944 | tf_op jit(solution)/shard_map/attend/pallas_call | solution.py:135
  4.3 4.0 %collective-permute-start.2 = (bf16[2,32,512]{2,1,0:T(8,128)(2,1)S(1)}, bf16[2,32,512]{2,1,0:T(8,128)(2,1)S(1)}, u32[]{:S(2)}, u32[]{:S(2)}) collective-permute-start(bf16[2,32,512]{2,1,0:T(8,128)(2,1)S(1)} %get-tuple-element.18), channel_id=1, source_target_pairs={{0,3},{1,2},{2,1},{3,0},{4,7},{5,6},{6,5},{7,4},{8,11},{9,10},{10,... | collective-permute-start | bytes 196616 | tf_op jit(solution)/shard_map/ppermute | solution.py:242
  8.3 0.9 %collective-permute-start = (bf16[2,32,512]{2,1,0:T(8,128)(2,1)S(1)}, bf16[2,32,512]{2,1,0:T(8,128)(2,1)S(1)}, u32[]{:S(2)}, u32[]{:S(2)}) collective-permute-start(bf16[2,32,512]{2,1,0:T(8,128)(2,1)S(1)} %get-tuple-element.14), channel_id=1, source_target_pairs={{0,2},{1,3},{2,0},{3,1},{4,6},{5,7},{6,4},{7,5},{8,10},{9,11},{10,... | collective-permute-start | bytes 196616 | tf_op jit(solution)/shard_map/ppermute | solution.py:242
  9.2 0.0 collective-permute-start.1
  9.2 1.5 %collective-permute-done.2.refs_1_ = bf16[2,32,512]{2,1,0:T(8,128)(2,1)S(1)} collective-permute-done((bf16[2,32,512]{2,1,0:T(8,128)(2,1)S(1)}, bf16[2,32,512]{2,1,0:T(8,128)(2,1)S(1)}, u32[]{:S(2)}, u32[]{:S(2)}) %collective-permute-start.2) | collective-permute-done | bytes 65568 | tf_op jit(solution)/shard_map/ppermute | solution.py:242
  10.8 0.7 %project.2 = (bf16[32,2,128]{2,1,0:T(2,128)(2,1)S(1)}, bf16[32,2,128]{2,1,0:T(2,128)(2,1)S(1)}) custom-call(bf16[2,32,512]{2,1,0:T(8,128)(2,1)S(1)} %get-tuple-element.17.refs_0_, bf16[2,32,512]{2,1,0:T(8,128)(2,1)S(1)} %collective-permute-done.2.refs_1_, bf16[32,512,128]{2,1,0:T(8,128)(2,1)S(1)} %get-tuple-element.16.refs_2_), custom_call_target="tpu_custom_call" | custom-call | flops 16777216 | bytes 4194304 | tf_op jit(solution)/shard_map/project/pallas_call | solution.py:196
  11.5 3.4 %collective-permute-start.5 = (bf16[32,2,128]{2,1,0:T(2,128)(2,1)S(1)}, bf16[32,2,128]{2,1,0:T(2,128)(2,1)S(1)}, u32[]{:S(2)}, u32[]{:S(2)}) collective-permute-start(bf16[32,2,128]{2,1,0:T(2,128)(2,1)S(1)} %get-tuple-element.22), channel_id=1, source_target_pairs={{0,3},{1,2},{2,1},{3,0},{4,7},{5,6},{6,5},{7,4},{8,11},{9,10},{10,... | collective-permute-start | bytes 49160 | tf_op jit(solution)/shard_map/ppermute | solution.py:242
  14.9 0.0 collective-permute-done.refs_0_
  14.9 0.0 collective-permute-done.1.refs_1_
  14.9 0.7 %project.3 = (bf16[32,2,128]{2,1,0:T(2,128)(2,1)S(1)}, bf16[32,2,128]{2,1,0:T(2,128)(2,1)S(1)}) custom-call(bf16[2,32,512]{2,1,0:T(8,128)(2,1)S(1)} %collective-permute-done.refs_0_, bf16[2,32,512]{2,1,0:T(8,128)(2,1)S(1)} %collective-permute-done.1.refs_1_, bf16[32,512,128]{2,1,0:T(8,128)(2,1)S(1)} %get-tuple-element.16.refs_2_, ...), custom_call_target="tpu_custom_call" | custom-call | flops 16777216 | bytes 4194304 | tf_op jit(solution)/shard_map/project/pallas_call | solution.py:196
  15.7 0.9 %collective-permute-start.3 = (bf16[32,2,128]{2,1,0:T(2,128)(2,1)S(1)}, bf16[32,2,128]{2,1,0:T(2,128)(2,1)S(1)}, u32[]{:S(2)}, u32[]{:S(2)}) collective-permute-start(bf16[32,2,128]{2,1,0:T(2,128)(2,1)S(1)} %get-tuple-element.20), channel_id=1, source_target_pairs={{0,2},{1,3},{2,0},{3,1},{4,6},{5,7},{6,4},{7,5},{8,10},{9,11},{10,... | collective-permute-start | bytes 49160 | tf_op jit(solution)/shard_map/ppermute | solution.py:242
  16.6 0.0 collective-permute-start.4
  16.6 0.0 collective-permute-done.5.refs_1_
  16.6 0.6 %assemble.2.refs_2_ = bf16[4,32,2,128]{3,2,1,0:T(2,128)(2,1)} custom-call(bf16[32,2,128]{2,1,0:T(2,128)(2,1)S(1)} %get-tuple-element.19.refs_3_.refs_0_, bf16[32,2,128]{2,1,0:T(2,128)(2,1)S(1)} %collective-permute-done.5.refs_1_), custom_call_target="tpu_custom_call" | custom-call | tf_op jit(solution)/shard_map/assemble/pallas_call | solution.py:227
  17.3 2.2 %collective-permute-done.3.refs_0_ = bf16[32,2,128]{2,1,0:T(2,128)(2,1)S(1)} collective-permute-done((bf16[32,2,128]{2,1,0:T(2,128)(2,1)S(1)}, bf16[32,2,128]{2,1,0:T(2,128)(2,1)S(1)}, u32[]{:S(2)}, u32[]{:S(2)}) %collective-permute-start.3) | collective-permute-done | bytes 16416 | tf_op jit(solution)/shard_map/ppermute | solution.py:242
  19.4 0.9 %collective-permute-done.4.refs_1_ = bf16[32,2,128]{2,1,0:T(2,128)(2,1)S(1)} collective-permute-done((bf16[32,2,128]{2,1,0:T(2,128)(2,1)S(1)}, bf16[32,2,128]{2,1,0:T(2,128)(2,1)S(1)}, u32[]{:S(2)}, u32[]{:S(2)}) %collective-permute-start.4) | collective-permute-done | bytes 16416 | tf_op jit(solution)/shard_map/ppermute | solution.py:242
  20.3 0.6 %assemble.3 = bf16[4,32,2,128]{3,2,1,0:T(2,128)(2,1)} custom-call(bf16[32,2,128]{2,1,0:T(2,128)(2,1)S(1)} %collective-permute-done.3.refs_0_, bf16[32,2,128]{2,1,0:T(2,128)(2,1)S(1)} %collective-permute-done.4.refs_1_, bf16[4,32,2,128]{3,2,1,0:T(2,128)(2,1)} %assemble.2.refs_2_), custom_call_target="tpu_custom_call", output_to_operand_aliasing={{}: (2, {})} | custom-call | tf_op jit(solution)/shard_map/assemble/pallas_call | solution.py:227
Async XLA Ops:
  4.3 6.4 %collective-permute-start.2 = (bf16[2,32,512]{2,1,0:T(8,128)(2,1)S(1)}, bf16[2,32,512]{2,1,0:T(8,128)(2,1)S(1)}, u32[]{:S(2)}, u32[]{:S(2)}) collective-permute-start(bf16[2,32,512]{2,1,0:T(8,128)(2,1)S(1)} %get-tuple-element.18), channel_id=1, source_target_pairs={{0,3},{1,2},{2,1},{3,0},{4,7},{5,6},{6,5},{7,4},{8,11},{9,10},{10,... | collective-permute-start | bytes 196616 | tf_op jit(solution)/shard_map/ppermute | solution.py:242
  8.3 6.6 %collective-permute-start = (bf16[2,32,512]{2,1,0:T(8,128)(2,1)S(1)}, bf16[2,32,512]{2,1,0:T(8,128)(2,1)S(1)}, u32[]{:S(2)}, u32[]{:S(2)}) collective-permute-start(bf16[2,32,512]{2,1,0:T(8,128)(2,1)S(1)} %get-tuple-element.14), channel_id=1, source_target_pairs={{0,2},{1,3},{2,0},{3,1},{4,6},{5,7},{6,4},{7,5},{8,10},{9,11},{10,... | collective-permute-start | bytes 196616 | tf_op jit(solution)/shard_map/ppermute | solution.py:242
  9.2 5.7 %collective-permute-start.1 = (bf16[2,32,512]{2,1,0:T(8,128)(2,1)S(1)}, bf16[2,32,512]{2,1,0:T(8,128)(2,1)S(1)}, u32[]{:S(2)}, u32[]{:S(2)}) collective-permute-start(bf16[2,32,512]{2,1,0:T(8,128)(2,1)S(1)} %get-tuple-element.15), channel_id=1, source_target_pairs={{0,1},{1,0},{2,3},{3,2},{4,5},{5,4},{6,7},{7,6},{8,9},{9,8},{10,11... | collective-permute-start | bytes 196616 | tf_op jit(solution)/shard_map/ppermute | solution.py:242
  11.5 5.1 %collective-permute-start.5 = (bf16[32,2,128]{2,1,0:T(2,128)(2,1)S(1)}, bf16[32,2,128]{2,1,0:T(2,128)(2,1)S(1)}, u32[]{:S(2)}, u32[]{:S(2)}) collective-permute-start(bf16[32,2,128]{2,1,0:T(2,128)(2,1)S(1)} %get-tuple-element.22), channel_id=1, source_target_pairs={{0,3},{1,2},{2,1},{3,0},{4,7},{5,6},{6,5},{7,4},{8,11},{9,10},{10,... | collective-permute-start | bytes 49160 | tf_op jit(solution)/shard_map/ppermute | solution.py:242
  15.7 3.8 %collective-permute-start.3 = (bf16[32,2,128]{2,1,0:T(2,128)(2,1)S(1)}, bf16[32,2,128]{2,1,0:T(2,128)(2,1)S(1)}, u32[]{:S(2)}, u32[]{:S(2)}) collective-permute-start(bf16[32,2,128]{2,1,0:T(2,128)(2,1)S(1)} %get-tuple-element.20), channel_id=1, source_target_pairs={{0,2},{1,3},{2,0},{3,1},{4,6},{5,7},{6,4},{7,5},{8,10},{9,11},{10,... | collective-permute-start | bytes 49160 | tf_op jit(solution)/shard_map/ppermute | solution.py:242
  16.6 3.7 %collective-permute-start.4 = (bf16[32,2,128]{2,1,0:T(2,128)(2,1)S(1)}, bf16[32,2,128]{2,1,0:T(2,128)(2,1)S(1)}, u32[]{:S(2)}, u32[]{:S(2)}) collective-permute-start(bf16[32,2,128]{2,1,0:T(2,128)(2,1)S(1)} %get-tuple-element.21), channel_id=1, source_target_pairs={{0,1},{1,0},{2,3},{3,2},{4,5},{5,4},{6,7},{7,6},{8,9},{9,8},{10,11... | collective-permute-start | bytes 49160 | tf_op jit(solution)/shard_map/ppermute | solution.py:242

commit v10 on v3

--- a/solution.py
+++ b/solution.py
@@ -10,18 +10,23 @@
 
 ROPE_DIM = 64
 SOFTMAX_SCALE = (1.0 + 0.1 * math.log(40.0)) ** 2 / math.sqrt(192.0)
+EXP2_SCALE = SOFTMAX_SCALE * math.log2(math.e)
 BLOCK = 512
 LANES = 128
+
+
+def order(owners):
+    return [0] + list(range(owners - 1, 0, -1))
 
 
 def attend_kernel(owners, lengths_hbm, query_hbm, scales_hbm, cache, *refs):
     outs, (latents, lengths, query, scales, keys, sems, small_sems) = refs[:owners], refs[owners:]
     requests, channels, heads = query.shape
     local_heads, rank = latents.shape[2:]
-    me = lax.axis_index("tp")
     cache_len = cache.shape[2]
     block = min(BLOCK, cache_len)
     blocks = cache_len // block
+    me = lax.axis_index("tp")
 
     def fetch(r, b):
         span = pl.ds(b * block, block)
@@ -65,15 +70,16 @@
         for part in parts[1:]:
             top = jnp.maximum(top, jnp.max(part, axis=1, keepdims=True))
         total = jnp.zeros_like(top)
-        mixture = jnp.zeros((heads, rank), jnp.float32)
-        for b, part in enumerate(parts):
-            weights = jnp.exp((part - top) * SOFTMAX_SCALE)
-            total += jnp.sum(weights, axis=1, keepdims=True)
-            mixture += lax.dot_general(
-                weights.astype(jnp.bfloat16), keys[r, :rank, b * block:(b + 1) * block],
-                (((1,), (1,)), ((), ())), preferred_element_type=jnp.float32,
-            )
-        latent = (mixture / total * scale_row[:, :rank]).astype(jnp.bfloat16)
+        weights = []
+        for part in parts:
+            weight = jnp.exp2((part - top) * EXP2_SCALE)
+            total += jnp.sum(weight, axis=1, keepdims=True)
+            weights.append(weight.astype(jnp.bfloat16))
+        mixture = lax.dot_general(
+            jnp.concatenate(weights, axis=1), keys[r, :rank, :live * block],
+            (((1,), (1,)), ((), ())), preferred_element_type=jnp.float32,
+        )
+        latent = (mixture * (1.0 / total) * scale_row[:, :rank]).astype(jnp.bfloat16)
         for d in range(owners):
             latents[d, r] = latent[d * local_heads:(d + 1) * local_heads]
 
@@ -83,21 +89,26 @@
             def _():
                 request(r, live)
 
-    for k, out in enumerate(outs):
+    for out, k in zip(outs, order(owners)):
         out[...] = latents[me ^ k]
+
+
+def in_hbm(*arrays):
+    return [pltpu.with_memory_space_constraint(array, pltpu.HBM) for array in arrays]
 
 
 def attend(query, cache, scales, lengths, owners):
     requests, heads, channels = query.shape
     cache_len = cache.shape[1]
     rank = channels - ROPE_DIM
+    part = jax.ShapeDtypeStruct((requests, heads // owners, rank), jnp.bfloat16)
     return pl.pallas_call(
         functools.partial(attend_kernel, owners),
-        out_shape=[jax.ShapeDtypeStruct((requests, heads // owners, rank), jnp.bfloat16)] * owners,
+        out_shape=[part] * owners,
         in_specs=[pl.BlockSpec(memory_space=pl.ANY)] * 4,
         out_specs=[pl.BlockSpec(memory_space=pltpu.VMEM)] * owners,
         scratch_shapes=[
-            pltpu.VMEM((owners, requests, heads // owners, rank), jnp.bfloat16),
+            pltpu.VMEM((owners,) + part.shape, part.dtype),
             pltpu.SMEM((requests,), jnp.int32),
             pltpu.VMEM((requests, channels, heads), jnp.bfloat16),
             pltpu.VMEM((channels,), jnp.float32),
@@ -112,7 +123,28 @@
             transcendentals=requests * heads * cache_len,
         ),
         name="attend",
-    )(*(pltpu.with_memory_space_constraint(x, pltpu.HBM) for x in (lengths, jnp.swapaxes(query, 1, 2), scales, jnp.swapaxes(cache, 1, 2))))
+    )(*in_hbm(lengths, jnp.swapaxes(query, 1, 2), scales, jnp.swapaxes(cache, 1, 2)))
+
+
+def stage_kernel(maps_hbm, after, maps, sem):
+    copy = pltpu.make_async_copy(maps_hbm, maps, sem)
+    copy.start()
+    copy.wait()
+
+
+def stage(maps, after):
+    return pl.pallas_call(
+        stage_kernel,
+        out_shape=jax.ShapeDtypeStruct(maps.shape, maps.dtype),
+        in_specs=[pl.BlockSpec(memory_space=pl.ANY)] * 2,
+        out_specs=pl.BlockSpec(memory_space=pltpu.VMEM),
+        scratch_shapes=[pltpu.SemaphoreType.DMA(())],
+        compiler_params=pltpu.CompilerParams(vmem_limit_bytes=8 * 2**20),
+        cost_estimate=pl.CostEstimate(
+            flops=0, bytes_accessed=4 * maps.size, transcendentals=0
+        ),
+        name="stage",
+    )(*in_hbm(maps), after)
 
 
 def project_kernel(owners, *refs):
@@ -167,7 +199,8 @@
     parts, out, sems = refs[:owners], refs[owners], refs[owners + 1]
     me = lax.axis_index("tp")
     copies = [
-        pltpu.make_async_copy(part, out.at[me ^ k], sems.at[k]) for k, part in enumerate(parts)
+        pltpu.make_async_copy(part, out.at[me ^ k], sems.at[k])
+        for k, part in zip(order(owners), parts)
     ]
     for copy in copies:
         copy.start()
@@ -180,25 +213,27 @@
     return pl.pallas_call(
         functools.partial(assemble_kernel, owners),
         out_shape=pltpu.HBM((owners,) + parts[0].shape, parts[0].dtype),
-        in_specs=[pl.BlockSpec(memory_space=pl.ANY)] * owners,
+        in_specs=[pl.BlockSpec(memory_space=pltpu.VMEM)] * owners,
         out_specs=pl.BlockSpec(memory_space=pltpu.HBM),
         scratch_shapes=[pltpu.SemaphoreType.DMA((owners,))],
+        compiler_params=pltpu.CompilerParams(vmem_limit_bytes=2 * 2**20),
         name="assemble",
     )(*parts)
 
 
 def exchange(parts):
     owners = len(parts)
-    return [parts[0]] + [
-        lax.ppermute(part, "tp", [(i, i ^ k) for i in range(owners)])
-        for k, part in enumerate(parts) if k
+    return [
+        lax.ppermute(part, "tp", [(i, i ^ k) for i in range(owners)]) if k else part
+        for k, part in zip(order(owners), parts)
     ]
 
 
 def on_device(query, cache, scales, lengths, value_up):
     owners = lax.axis_size("tp")
-    latents = exchange(attend(query, cache, scales, lengths, owners))
-    values = exchange(project(latents, value_up))
+    latents = attend(query, cache, scales, lengths, owners)
+    maps = stage(value_up, latents[0])
+    values = exchange(project(exchange(latents), maps))
     returned = assemble(values)
     _, local_heads, requests, width = returned.shape
     returned = returned.reshape(owners * local_heads, requests, width)

time: 26.2 us -> 20 us (0.76)
  local copies, waits for them, and re-layouts: 3.38 us -> 0 us
  waiting for transfers between devices: 6.87 us -> 3.82 us
  starting transfers between devices: 8.76 us -> 9.34 us
  Pallas kernels: 6.98 us -> 6.7 us
    unnamed x10 -> x0, local copies, waits for them, and re-layouts: 3.38 us -> none
    ppermute x6, waiting for transfers between devices: 6.87 us -> 3.82 us  [exchange(): lax.ppermute(part, 'tp', [(i, i ^ k) for i in range(owners)])]
    pallas_call x1, Pallas kernels: 3.12 us -> 0.66 us  [assemble(): pl.pallas_call(functools.partial(assemble_kernel, owners), out_shape=pltp...]
    pallas_call x1 -> x2, Pallas kernels: 3.01 us -> 5.19 us  [the longest x1 3 us: attend(): pl.pallas_call(functools.partial(attend_kernel, owners), out_shape=[part]...]
    ppermute x6, starting transfers between devices: 8.76 us -> 9.34 us  [exchange(): lax.ppermute(part, 'tp', [(i, i ^ k) for i in range(owners)])]
  transfers between devices with their start and end apart: 6 -> 6, of which waited for: 5 -> 4; matrix products, arithmetic and copies ran while one was open for 0% -> 0% of each run, Pallas kernels for 0% -> 11%
where the time goes in v10:
time: 20 us; the launch traced here: 19.9 us
  starting transfers between devices  9.34 us (47%)
  Pallas kernels  6.7 us (34%)
  waiting for transfers between devices  3.82 us (19%)
    ppermute x6, starting transfers between devices, exchange(): lax.ppermute(part, 'tp', [(i, i ^ k) for i in range(owners)])  9.34 us
    ppermute x6, waiting for transfers between devices, exchange(): lax.ppermute(part, 'tp', [(i, i ^ k) for i in range(owners)])  3.82 us
    pallas_call x1, Pallas kernels, attend(): pl.pallas_call(functools.partial(attend_kernel, owners), out_shape=[part]...  3 us
    pallas_call x1, Pallas kernels, stage(): pl.pallas_call(stage_kernel, out_shape=jax.ShapeDtypeStruct(maps.shape, m...  2.2 us
    pallas_call x1, Pallas kernels, project(): pl.pallas_call(functools.partial(project_kernel, owners), out_shape=[jax....  0.85 us
    pallas_call x1, Pallas kernels, assemble(): pl.pallas_call(functools.partial(assemble_kernel, owners), out_shape=pltp...  0.66 us
  transfers between devices with their start and end apart: 6, of which 4 were waited for; matrix products, arithmetic and copies ran while one was open for 0% of the time, Pallas kernels for 11%

profile of v10, /device:TPU:0, one launch (start us, length us, event | category | flops | bytes accessed | tf_op | source)
XLA Modules:
  0.0 19.9 jit_solution(2693016286537767971)
XLA Ops:
  0.0 3.0 %attend.1 = (bf16[2,32,512]{2,1,0:T(8,128)(2,1)S(1)}, bf16[2,32,512]{2,1,0:T(8,128)(2,1)S(1)}, bf16[2,32,512]{2,1,0:T(8,128)(2,1)S(1)}, bf16[2,32,512]{2,1,0:T(8,128)(2,1)S(1)}) custom-call(s32[2]{0:T(128)} %lengths_hbm.1, bf16[2,576,128]{2,1,0:T(8,128)(2,1)} %bitcast.8, f32[576]{0:T(1024)} %scales_hbm.1, bf16[2,576,1536]{2,1,0:T(8,128)(2,1)} %bitcast.7), custom_call_target="tpu_custom_call" | custom-call | flops 905969664 | bytes 3538944 | tf_op jit(solution)/shard_map/attend/pallas_call | solution.py:105
  3.0 5.2 %collective-permute-start = (bf16[2,32,512]{2,1,0:T(8,128)(2,1)S(1)}, bf16[2,32,512]{2,1,0:T(8,128)(2,1)S(1)}, u32[]{:S(2)}, u32[]{:S(2)}) collective-permute-start(bf16[2,32,512]{2,1,0:T(8,128)(2,1)S(1)} %get-tuple-element.14), channel_id=1, source_target_pairs={{0,3},{1,2},{2,1},{3,0},{4,7},{5,6},{6,5},{7,4},{8,11},{9,10},{10,... | collective-permute-start | bytes 196616 | tf_op jit(solution)/shard_map/ppermute | solution.py:227
  8.2 0.0 collective-permute-start.1
  8.2 0.6 %collective-permute-start.2 = (bf16[2,32,512]{2,1,0:T(8,128)(2,1)S(1)}, bf16[2,32,512]{2,1,0:T(8,128)(2,1)S(1)}, u32[]{:S(2)}, u32[]{:S(2)}) collective-permute-start(bf16[2,32,512]{2,1,0:T(8,128)(2,1)S(1)} %get-tuple-element.16), channel_id=1, source_target_pairs={{0,1},{1,0},{2,3},{3,2},{4,5},{5,4},{6,7},{7,6},{8,9},{9,8},{10,11... | collective-permute-start | bytes 196616 | tf_op jit(solution)/shard_map/ppermute | solution.py:227
  8.8 2.2 %stage.1.refs_4_ = bf16[32,512,128]{2,1,0:T(8,128)(2,1)S(1)} custom-call(bf16[32,512,128]{2,1,0:T(8,128)(2,1)} %maps_hbm.1, bf16[2,32,512]{2,1,0:T(8,128)(2,1)S(1)} %get-tuple-element.13.after.refs_0_), custom_call_target="tpu_custom_call" | custom-call | bytes 8388608 | tf_op jit(solution)/shard_map/stage/pallas_call | solution.py:136
  11.0 0.0 collective-permute-done.refs_1_
  11.0 1.4 %collective-permute-done.1.refs_2_ = bf16[2,32,512]{2,1,0:T(8,128)(2,1)S(1)} collective-permute-done((bf16[2,32,512]{2,1,0:T(8,128)(2,1)S(1)}, bf16[2,32,512]{2,1,0:T(8,128)(2,1)S(1)}, u32[]{:S(2)}, u32[]{:S(2)}) %collective-permute-start.1) | collective-permute-done | bytes 65568 | tf_op jit(solution)/shard_map/ppermute | solution.py:227
  12.4 0.0 collective-permute-done.2.refs_3_
  12.4 0.9 %project.1 = (bf16[32,2,128]{2,1,0:T(2,128)(2,1)S(1)}, bf16[32,2,128]{2,1,0:T(2,128)(2,1)S(1)}, bf16[32,2,128]{2,1,0:T(2,128)(2,1)S(1)}, bf16[32,2,128]{2,1,0:T(2,128)(2,1)S(1)}) custom-call(bf16[2,32,512]{2,1,0:T(8,128)(2,1)S(1)} %get-tuple-element.13.after.refs_0_, bf16[2,32,512]{2,1,0:T(8,128)(2,1)S(1)} %collective-permute-done.refs_1_, ...), custom_call_target="tpu_custom_call" | custom-call | flops 33554432 | bytes 4194304 | tf_op jit(solution)/shard_map/project/pallas_call | solution.py:182
  13.3 1.6 %collective-permute-start.3 = (bf16[32,2,128]{2,1,0:T(2,128)(2,1)S(1)}, bf16[32,2,128]{2,1,0:T(2,128)(2,1)S(1)}, u32[]{:S(2)}, u32[]{:S(2)}) collective-permute-start(bf16[32,2,128]{2,1,0:T(2,128)(2,1)S(1)} %get-tuple-element.18), channel_id=1, source_target_pairs={{0,3},{1,2},{2,1},{3,0},{4,7},{5,6},{6,5},{7,4},{8,11},{9,10},{10,... | collective-permute-start | bytes 49160 | tf_op jit(solution)/shard_map/ppermute | solution.py:227
  14.9 0.6 %collective-permute-start.4 = (bf16[32,2,128]{2,1,0:T(2,128)(2,1)S(1)}, bf16[32,2,128]{2,1,0:T(2,128)(2,1)S(1)}, u32[]{:S(2)}, u32[]{:S(2)}) collective-permute-start(bf16[32,2,128]{2,1,0:T(2,128)(2,1)S(1)} %get-tuple-element.19), channel_id=1, source_target_pairs={{0,2},{1,3},{2,0},{3,1},{4,6},{5,7},{6,4},{7,5},{8,10},{9,11},{10,... | collective-permute-start | bytes 49160 | tf_op jit(solution)/shard_map/ppermute | solution.py:227
  15.5 1.3 %collective-permute-start.5 = (bf16[32,2,128]{2,1,0:T(2,128)(2,1)S(1)}, bf16[32,2,128]{2,1,0:T(2,128)(2,1)S(1)}, u32[]{:S(2)}, u32[]{:S(2)}) collective-permute-start(bf16[32,2,128]{2,1,0:T(2,128)(2,1)S(1)} %get-tuple-element.20), channel_id=1, source_target_pairs={{0,1},{1,0},{2,3},{3,2},{4,5},{5,4},{6,7},{7,6},{8,9},{9,8},{10,11... | collective-permute-start | bytes 49160 | tf_op jit(solution)/shard_map/ppermute | solution.py:227
  16.8 1.1 %collective-permute-done.3.refs_1_ = bf16[32,2,128]{2,1,0:T(2,128)(2,1)S(1)} collective-permute-done((bf16[32,2,128]{2,1,0:T(2,128)(2,1)S(1)}, bf16[32,2,128]{2,1,0:T(2,128)(2,1)S(1)}, u32[]{:S(2)}, u32[]{:S(2)}) %collective-permute-start.3) | collective-permute-done | bytes 16416 | tf_op jit(solution)/shard_map/ppermute | solution.py:227
  18.0 0.7 %collective-permute-done.4.refs_2_ = bf16[32,2,128]{2,1,0:T(2,128)(2,1)S(1)} collective-permute-done((bf16[32,2,128]{2,1,0:T(2,128)(2,1)S(1)}, bf16[32,2,128]{2,1,0:T(2,128)(2,1)S(1)}, u32[]{:S(2)}, u32[]{:S(2)}) %collective-permute-start.4) | collective-permute-done | bytes 16416 | tf_op jit(solution)/shard_map/ppermute | solution.py:227
  18.7 0.6 %collective-permute-done.5.refs_3_ = bf16[32,2,128]{2,1,0:T(2,128)(2,1)S(1)} collective-permute-done((bf16[32,2,128]{2,1,0:T(2,128)(2,1)S(1)}, bf16[32,2,128]{2,1,0:T(2,128)(2,1)S(1)}, u32[]{:S(2)}, u32[]{:S(2)}) %collective-permute-start.5) | collective-permute-done | bytes 16416 | tf_op jit(solution)/shard_map/ppermute | solution.py:227
  19.2 0.7 %assemble.1 = bf16[4,32,2,128]{3,2,1,0:T(2,128)(2,1)} custom-call(bf16[32,2,128]{2,1,0:T(2,128)(2,1)S(1)} %get-tuple-element.17.refs_0_, bf16[32,2,128]{2,1,0:T(2,128)(2,1)S(1)} %collective-permute-done.3.refs_1_, bf16[32,2,128]{2,1,0:T(2,128)(2,1)S(1)} %collective-permute-done.4.refs_2_, bf16[32,2,128]{2,1,0:T(2,128)(2,1)S(1)} %collective-permute-done.5.refs_3_), custom_call_target="tpu_custom_call" | custom-call | tf_op jit(solution)/shard_map/assemble/pallas_call | solution.py:213
Async XLA Ops:
  3.0 8.0 %collective-permute-start = (bf16[2,32,512]{2,1,0:T(8,128)(2,1)S(1)}, bf16[2,32,512]{2,1,0:T(8,128)(2,1)S(1)}, u32[]{:S(2)}, u32[]{:S(2)}) collective-permute-start(bf16[2,32,512]{2,1,0:T(8,128)(2,1)S(1)} %get-tuple-element.14), channel_id=1, source_target_pairs={{0,3},{1,2},{2,1},{3,0},{4,7},{5,6},{6,5},{7,4},{8,11},{9,10},{10,... | collective-permute-start | bytes 196616 | tf_op jit(solution)/shard_map/ppermute | solution.py:227
  8.2 4.3 %collective-permute-start.1 = (bf16[2,32,512]{2,1,0:T(8,128)(2,1)S(1)}, bf16[2,32,512]{2,1,0:T(8,128)(2,1)S(1)}, u32[]{:S(2)}, u32[]{:S(2)}) collective-permute-start(bf16[2,32,512]{2,1,0:T(8,128)(2,1)S(1)} %get-tuple-element.15), channel_id=1, source_target_pairs={{0,2},{1,3},{2,0},{3,1},{4,6},{5,7},{6,4},{7,5},{8,10},{9,11},{10,... | collective-permute-start | bytes 196616 | tf_op jit(solution)/shard_map/ppermute | solution.py:227
  8.2 4.3 %collective-permute-start.2 = (bf16[2,32,512]{2,1,0:T(8,128)(2,1)S(1)}, bf16[2,32,512]{2,1,0:T(8,128)(2,1)S(1)}, u32[]{:S(2)}, u32[]{:S(2)}) collective-permute-start(bf16[2,32,512]{2,1,0:T(8,128)(2,1)S(1)} %get-tuple-element.16), channel_id=1, source_target_pairs={{0,1},{1,0},{2,3},{3,2},{4,5},{5,4},{6,7},{7,6},{8,9},{9,8},{10,11... | collective-permute-start | bytes 196616 | tf_op jit(solution)/shard_map/ppermute | solution.py:227
  13.3 4.7 %collective-permute-start.3 = (bf16[32,2,128]{2,1,0:T(2,128)(2,1)S(1)}, bf16[32,2,128]{2,1,0:T(2,128)(2,1)S(1)}, u32[]{:S(2)}, u32[]{:S(2)}) collective-permute-start(bf16[32,2,128]{2,1,0:T(2,128)(2,1)S(1)} %get-tuple-element.18), channel_id=1, source_target_pairs={{0,3},{1,2},{2,1},{3,0},{4,7},{5,6},{6,5},{7,4},{8,11},{9,10},{10,... | collective-permute-start | bytes 49160 | tf_op jit(solution)/shard_map/ppermute | solution.py:227
  14.9 3.7 %collective-permute-start.4 = (bf16[32,2,128]{2,1,0:T(2,128)(2,1)S(1)}, bf16[32,2,128]{2,1,0:T(2,128)(2,1)S(1)}, u32[]{:S(2)}, u32[]{:S(2)}) collective-permute-start(bf16[32,2,128]{2,1,0:T(2,128)(2,1)S(1)} %get-tuple-element.19), channel_id=1, source_target_pairs={{0,2},{1,3},{2,0},{3,1},{4,6},{5,7},{6,4},{7,5},{8,10},{9,11},{10,... | collective-permute-start | bytes 49160 | tf_op jit(solution)/shard_map/ppermute | solution.py:227
  15.5 3.7 %collective-permute-start.5 = (bf16[32,2,128]{2,1,0:T(2,128)(2,1)S(1)}, bf16[32,2,128]{2,1,0:T(2,128)(2,1)S(1)}, u32[]{:S(2)}, u32[]{:S(2)}) collective-permute-start(bf16[32,2,128]{2,1,0:T(2,128)(2,1)S(1)} %get-tuple-element.20), channel_id=1, source_target_pairs={{0,1},{1,0},{2,3},{3,2},{4,5},{5,4},{6,7},{7,6},{8,9},{9,8},{10,11... | collective-permute-start | bytes 49160 | tf_op jit(solution)/shard_map/ppermute | solution.py:227

commit v11 on v10

--- a/solution.py
+++ b/solution.py
@@ -13,6 +13,7 @@
 EXP2_SCALE = SOFTMAX_SCALE * math.log2(math.e)
 BLOCK = 512
 LANES = 128
+GROUP_ROWS = 16
 
 
 def order(owners):
@@ -22,7 +23,7 @@
 def attend_kernel(owners, lengths_hbm, query_hbm, scales_hbm, cache, *refs):
     outs, (latents, lengths, query, scales, keys, sems, small_sems) = refs[:owners], refs[owners:]
     requests, channels, heads = query.shape
-    local_heads, rank = latents.shape[2:]
+    rows, rank = outs[0].shape
     cache_len = cache.shape[2]
     block = min(BLOCK, cache_len)
     blocks = cache_len // block
@@ -79,9 +80,9 @@
             jnp.concatenate(weights, axis=1), keys[r, :rank, :live * block],
             (((1,), (1,)), ((), ())), preferred_element_type=jnp.float32,
         )
-        latent = (mixture * (1.0 / total) * scale_row[:, :rank]).astype(jnp.bfloat16)
-        for d in range(owners):
-            latents[d, r] = latent[d * local_heads:(d + 1) * local_heads]
+        latent = mixture * (1.0 / total) * scale_row[:, :rank]
+        for at in range(0, rank, LANES):
+            latents[at // LANES, pl.ds(r, heads, stride=requests), :] = latent[:, at:at + LANES]
 
     for r in range(requests):
         for live in range(1, blocks + 1):
@@ -90,7 +91,9 @@
                 request(r, live)
 
     for out, k in zip(outs, order(owners)):
-        out[...] = latents[me ^ k]
+        mine = pl.ds(pl.multiple_of((me ^ k) * rows, rows), rows)
+        for at in range(0, rank, LANES):
+            out[:, at:at + LANES] = latents[at // LANES, mine, :].astype(jnp.bfloat16)
 
 
 def in_hbm(*arrays):
@@ -101,14 +104,14 @@
     requests, heads, channels = query.shape
     cache_len = cache.shape[1]
     rank = channels - ROPE_DIM
-    part = jax.ShapeDtypeStruct((requests, heads // owners, rank), jnp.bfloat16)
+    part = jax.ShapeDtypeStruct((heads // owners * requests, rank), jnp.bfloat16)
     return pl.pallas_call(
         functools.partial(attend_kernel, owners),
         out_shape=[part] * owners,
         in_specs=[pl.BlockSpec(memory_space=pl.ANY)] * 4,
         out_specs=[pl.BlockSpec(memory_space=pltpu.VMEM)] * owners,
         scratch_shapes=[
-            pltpu.VMEM((owners,) + part.shape, part.dtype),
+            pltpu.VMEM((rank // LANES, heads * requests, LANES), jnp.float32),
             pltpu.SMEM((requests,), jnp.int32),
             pltpu.VMEM((requests, channels, heads), jnp.bfloat16),
             pltpu.VMEM((channels,), jnp.float32),
@@ -147,52 +150,41 @@
     )(*in_hbm(maps), after)
 
 
-def project_kernel(owners, *refs):
-    parts, maps, outs, rows = refs[:owners], refs[owners], refs[owners + 1:-1], refs[-1]
-    requests, local_heads, rank = parts[0].shape
-    width = maps.shape[2]
-    batch = owners * requests
-    for b in range(batch):
-        for k in range(rank // LANES):
-            rows[k, b * local_heads:(b + 1) * local_heads] = parts[b // requests][
-                b % requests, :, k * LANES:(k + 1) * LANES
-            ].astype(jnp.float32)
-    for h in range(0, local_heads, 2):
-        pair = jnp.concatenate(
-            [
-                jnp.concatenate(
-                    [rows[k, pl.ds(h + i, batch, stride=local_heads), :] for i in range(2)], axis=0
-                ).astype(jnp.bfloat16)
-                for k in range(rank // LANES)
-            ],
-            axis=1,
-        )
-        both = jnp.concatenate([maps[h], maps[h + 1]], axis=1)
-        values = jnp.dot(pair, both, preferred_element_type=jnp.float32)
-        for i in range(2):
-            mine = values[i * batch:(i + 1) * batch, i * width:(i + 1) * width]
-            for d, out in enumerate(outs):
-                out[h + i] = mine[d * requests:(d + 1) * requests].astype(jnp.bfloat16)
-
-
-def project(latents, maps):
-    owners = len(latents)
-    requests, local_heads, rank = latents[0].shape
-    width = maps.shape[2]
-    return pl.pallas_call(
-        functools.partial(project_kernel, owners),
-        out_shape=[jax.ShapeDtypeStruct((local_heads, requests, width), jnp.bfloat16)] * owners,
-        in_specs=[pl.BlockSpec(memory_space=pltpu.VMEM)] * (owners + 1),
-        out_specs=[pl.BlockSpec(memory_space=pltpu.VMEM)] * owners,
-        scratch_shapes=[pltpu.VMEM((rank // LANES, owners * requests * local_heads, LANES), jnp.float32)],
+def project_kernel(count, *refs):
+    parts, maps, outs = refs[:count], refs[count], refs[count + 1:]
+    local_heads, requests, width = outs[0].shape
+    group = min(GROUP_ROWS // requests, local_heads)
+    rows = group * requests
+    for first in range(0, local_heads, group):
+        here = slice(first * requests, first * requests + rows)
+        mixed = jnp.concatenate([part[here, :] for part in parts], axis=0)
+        wide = jnp.concatenate([maps[first + i] for i in range(group)], axis=1)
+        values = jnp.dot(mixed, wide, preferred_element_type=jnp.float32)
+        head = lax.broadcasted_iota(jnp.int32, (rows, width), 0) // requests
+        for d, out in enumerate(outs):
+            block = values[d * rows:(d + 1) * rows]
+            own = block[:, :width]
+            for i in range(1, group):
+                own = jnp.where(head == i, block[:, i * width:(i + 1) * width], own)
+            out[first:first + group] = own.astype(jnp.bfloat16).reshape(group, requests, width)
+
+
+def project(parts, maps, requests):
+    count = len(parts)
+    local_heads, rank, width = maps.shape
+    return pl.pallas_call(
+        functools.partial(project_kernel, count),
+        out_shape=[jax.ShapeDtypeStruct((local_heads, requests, width), jnp.bfloat16)] * count,
+        in_specs=[pl.BlockSpec(memory_space=pltpu.VMEM)] * (count + 1),
+        out_specs=[pl.BlockSpec(memory_space=pltpu.VMEM)] * count,
         compiler_params=pltpu.CompilerParams(vmem_limit_bytes=24 * 2**20),
         cost_estimate=pl.CostEstimate(
-            flops=2 * owners * requests * local_heads * rank * width,
+            flops=2 * count * requests * local_heads * rank * width,
             bytes_accessed=2 * local_heads * rank * width,
             transcendentals=0,
         ),
         name="project",
-    )(*latents, maps)
+    )(*parts, maps)
 
 
 def assemble_kernel(owners, *refs):
@@ -233,7 +225,7 @@
     owners = lax.axis_size("tp")
     latents = attend(query, cache, scales, lengths, owners)
     maps = stage(value_up, latents[0])
-    values = exchange(project(exchange(latents), maps))
+    values = exchange(project(exchange(latents), maps, query.shape[0]))
     returned = assemble(values)
     _, local_heads, requests, width = returned.shape
     returned = returned.reshape(owners * local_heads, requests, width)

time: 20 us -> 19.9 us (level)
  starting transfers between devices: 9.34 us -> 7.25 us
  waiting for transfers between devices: 3.82 us -> 4.93 us
  Pallas kernels: 6.7 us -> 7.5 us
    ppermute x6, starting transfers between devices: 9.34 us -> 7.25 us  [exchange(): lax.ppermute(part, 'tp', [(i, i ^ k) for i in range(owners)])]
    ppermute x6, waiting for transfers between devices: 3.82 us -> 4.93 us  [exchange(): lax.ppermute(part, 'tp', [(i, i ^ k) for i in range(owners)])]
    pallas_call x1, Pallas kernels: 3 us -> 3.79 us  [attend(): pl.pallas_call(functools.partial(attend_kernel, owners), out_shape=[part]...]
  transfers between devices with their start and end apart: 6 -> 6, of which waited for: 4 -> 5; matrix products, arithmetic and copies ran while one was open for 0% -> 0% of each run, Pallas kernels for 11% -> 11%
where the time goes in v11:
time: 19.9 us; the launch traced here: 19.7 us
  Pallas kernels  7.5 us (38%)
  starting transfers between devices  7.25 us (36%)
  waiting for transfers between devices  4.93 us (25%)
    ppermute x6, starting transfers between devices, exchange(): lax.ppermute(part, 'tp', [(i, i ^ k) for i in range(owners)])  7.25 us
    ppermute x6, waiting for transfers between devices, exchange(): lax.ppermute(part, 'tp', [(i, i ^ k) for i in range(owners)])  4.93 us
    pallas_call x1, Pallas kernels, attend(): pl.pallas_call(functools.partial(attend_kernel, owners), out_shape=[part]...  3.79 us
    pallas_call x1, Pallas kernels, stage(): pl.pallas_call(stage_kernel, out_shape=jax.ShapeDtypeStruct(maps.shape, m...  2.2 us
    pallas_call x1, Pallas kernels, project(): pl.pallas_call(functools.partial(project_kernel, count), out_shape=[jax.S...  0.86 us
    pallas_call x1, Pallas kernels, assemble(): pl.pallas_call(functools.partial(assemble_kernel, owners), out_shape=pltp...  0.66 us
  transfers between devices with their start and end apart: 6, of which 5 were waited for; matrix products, arithmetic and copies ran while one was open for 0% of the time, Pallas kernels for 11%

profile of v11, /device:TPU:0, one launch (start us, length us, event | category | flops | bytes accessed | tf_op | source)
XLA Modules:
  0.0 19.7 jit_solution(568769023055250126)
XLA Ops:
  0.0 3.8 %attend.1 = (bf16[64,512]{1,0:T(8,128)(2,1)S(1)}, bf16[64,512]{1,0:T(8,128)(2,1)S(1)}, bf16[64,512]{1,0:T(8,128)(2,1)S(1)}, bf16[64,512]{1,0:T(8,128)(2,1)S(1)}) custom-call(s32[2]{0:T(128)} %lengths_hbm.1, bf16[2,576,128]{2,1,0:T(8,128)(2,1)} %bitcast.8, f32[576]{0:T(1024)} %scales_hbm.1, bf16[2,576,1536]{2,1,0:T(8,128)(2,1)} %bitcast.7), custom_call_target="tpu_custom_call" | custom-call | flops 905969664 | bytes 3538944 | tf_op jit(solution)/shard_map/attend/pallas_call | solution.py:108
  3.8 2.8 %collective-permute-start = (bf16[64,512]{1,0:T(8,128)(2,1)S(1)}, bf16[64,512]{1,0:T(8,128)(2,1)S(1)}, u32[]{:S(2)}, u32[]{:S(2)}) collective-permute-start(bf16[64,512]{1,0:T(8,128)(2,1)S(1)} %get-tuple-element.14), channel_id=1, source_target_pairs={{0,3},{1,2},{2,1},{3,0},{4,7},{5,6},{6,5},{7,4},{8,11},{9,10},{10,... | collective-permute-start | bytes 196616 | tf_op jit(solution)/shard_map/ppermute | solution.py:219
  6.6 0.9 %collective-permute-start.1 = (bf16[64,512]{1,0:T(8,128)(2,1)S(1)}, bf16[64,512]{1,0:T(8,128)(2,1)S(1)}, u32[]{:S(2)}, u32[]{:S(2)}) collective-permute-start(bf16[64,512]{1,0:T(8,128)(2,1)S(1)} %get-tuple-element.15), channel_id=1, source_target_pairs={{0,2},{1,3},{2,0},{3,1},{4,6},{5,7},{6,4},{7,5},{8,10},{9,11},{10,... | collective-permute-start | bytes 196616 | tf_op jit(solution)/shard_map/ppermute | solution.py:219
  7.5 0.0 collective-permute-start.2
  7.5 2.2 %stage.1.refs_4_ = bf16[32,512,128]{2,1,0:T(8,128)(2,1)S(1)} custom-call(bf16[32,512,128]{2,1,0:T(8,128)(2,1)} %maps_hbm.1, bf16[64,512]{1,0:T(8,128)(2,1)S(1)} %get-tuple-element.13.after.refs_0_), custom_call_target="tpu_custom_call" | custom-call | bytes 8388608 | tf_op jit(solution)/shard_map/stage/pallas_call | solution.py:139
  9.7 0.0 collective-permute-done.refs_1_
  9.7 1.6 %collective-permute-done.1.refs_2_ = bf16[64,512]{1,0:T(8,128)(2,1)S(1)} collective-permute-done((bf16[64,512]{1,0:T(8,128)(2,1)S(1)}, bf16[64,512]{1,0:T(8,128)(2,1)S(1)}, u32[]{:S(2)}, u32[]{:S(2)}) %collective-permute-start.1) | collective-permute-done | bytes 65568 | tf_op jit(solution)/shard_map/ppermute | solution.py:219
  11.3 0.5 %collective-permute-done.2.refs_3_ = bf16[64,512]{1,0:T(8,128)(2,1)S(1)} collective-permute-done((bf16[64,512]{1,0:T(8,128)(2,1)S(1)}, bf16[64,512]{1,0:T(8,128)(2,1)S(1)}, u32[]{:S(2)}, u32[]{:S(2)}) %collective-permute-start.2) | collective-permute-done | bytes 65568 | tf_op jit(solution)/shard_map/ppermute | solution.py:219
  11.8 0.9 %project.1 = (bf16[32,2,128]{2,1,0:T(2,128)(2,1)S(1)}, bf16[32,2,128]{2,1,0:T(2,128)(2,1)S(1)}, bf16[32,2,128]{2,1,0:T(2,128)(2,1)S(1)}, bf16[32,2,128]{2,1,0:T(2,128)(2,1)S(1)}) custom-call(bf16[64,512]{1,0:T(8,128)(2,1)S(1)} %get-tuple-element.13.after.refs_0_, bf16[64,512]{1,0:T(8,128)(2,1)S(1)} %collective-permute-done.refs_1_, ...), custom_call_target="tpu_custom_call" | custom-call | flops 33554432 | bytes 4194304 | tf_op jit(solution)/shard_map/project/pallas_call | solution.py:175
  12.6 1.4 %collective-permute-start.3 = (bf16[32,2,128]{2,1,0:T(2,128)(2,1)S(1)}, bf16[32,2,128]{2,1,0:T(2,128)(2,1)S(1)}, u32[]{:S(2)}, u32[]{:S(2)}) collective-permute-start(bf16[32,2,128]{2,1,0:T(2,128)(2,1)S(1)} %get-tuple-element.18), channel_id=1, source_target_pairs={{0,3},{1,2},{2,1},{3,0},{4,7},{5,6},{6,5},{7,4},{8,11},{9,10},{10,... | collective-permute-start | bytes 49160 | tf_op jit(solution)/shard_map/ppermute | solution.py:219
  14.0 1.3 %collective-permute-start.4 = (bf16[32,2,128]{2,1,0:T(2,128)(2,1)S(1)}, bf16[32,2,128]{2,1,0:T(2,128)(2,1)S(1)}, u32[]{:S(2)}, u32[]{:S(2)}) collective-permute-start(bf16[32,2,128]{2,1,0:T(2,128)(2,1)S(1)} %get-tuple-element.19), channel_id=1, source_target_pairs={{0,2},{1,3},{2,0},{3,1},{4,6},{5,7},{6,4},{7,5},{8,10},{9,11},{10,... | collective-permute-start | bytes 49160 | tf_op jit(solution)/shard_map/ppermute | solution.py:219
  15.3 0.9 %collective-permute-start.5 = (bf16[32,2,128]{2,1,0:T(2,128)(2,1)S(1)}, bf16[32,2,128]{2,1,0:T(2,128)(2,1)S(1)}, u32[]{:S(2)}, u32[]{:S(2)}) collective-permute-start(bf16[32,2,128]{2,1,0:T(2,128)(2,1)S(1)} %get-tuple-element.20), channel_id=1, source_target_pairs={{0,1},{1,0},{2,3},{3,2},{4,5},{5,4},{6,7},{7,6},{8,9},{9,8},{10,11... | collective-permute-start | bytes 49160 | tf_op jit(solution)/shard_map/ppermute | solution.py:219
  16.2 1.1 %collective-permute-done.3.refs_1_ = bf16[32,2,128]{2,1,0:T(2,128)(2,1)S(1)} collective-permute-done((bf16[32,2,128]{2,1,0:T(2,128)(2,1)S(1)}, bf16[32,2,128]{2,1,0:T(2,128)(2,1)S(1)}, u32[]{:S(2)}, u32[]{:S(2)}) %collective-permute-start.3) | collective-permute-done | bytes 16416 | tf_op jit(solution)/shard_map/ppermute | solution.py:219
  17.3 0.4 %collective-permute-done.4.refs_2_ = bf16[32,2,128]{2,1,0:T(2,128)(2,1)S(1)} collective-permute-done((bf16[32,2,128]{2,1,0:T(2,128)(2,1)S(1)}, bf16[32,2,128]{2,1,0:T(2,128)(2,1)S(1)}, u32[]{:S(2)}, u32[]{:S(2)}) %collective-permute-start.4) | collective-permute-done | bytes 16416 | tf_op jit(solution)/shard_map/ppermute | solution.py:219
  17.7 1.3 %collective-permute-done.5.refs_3_ = bf16[32,2,128]{2,1,0:T(2,128)(2,1)S(1)} collective-permute-done((bf16[32,2,128]{2,1,0:T(2,128)(2,1)S(1)}, bf16[32,2,128]{2,1,0:T(2,128)(2,1)S(1)}, u32[]{:S(2)}, u32[]{:S(2)}) %collective-permute-start.5) | collective-permute-done | bytes 16416 | tf_op jit(solution)/shard_map/ppermute | solution.py:219
  19.1 0.7 %assemble.1 = bf16[4,32,2,128]{3,2,1,0:T(2,128)(2,1)} custom-call(bf16[32,2,128]{2,1,0:T(2,128)(2,1)S(1)} %get-tuple-element.17.refs_0_, bf16[32,2,128]{2,1,0:T(2,128)(2,1)S(1)} %collective-permute-done.3.refs_1_, bf16[32,2,128]{2,1,0:T(2,128)(2,1)S(1)} %collective-permute-done.4.refs_2_, bf16[32,2,128]{2,1,0:T(2,128)(2,1)S(1)} %collective-permute-done.5.refs_3_), custom_call_target="tpu_custom_call" | custom-call | tf_op jit(solution)/shard_map/assemble/pallas_call | solution.py:205
Async XLA Ops:
  3.8 5.9 %collective-permute-start = (bf16[64,512]{1,0:T(8,128)(2,1)S(1)}, bf16[64,512]{1,0:T(8,128)(2,1)S(1)}, u32[]{:S(2)}, u32[]{:S(2)}) collective-permute-start(bf16[64,512]{1,0:T(8,128)(2,1)S(1)} %get-tuple-element.14), channel_id=1, source_target_pairs={{0,3},{1,2},{2,1},{3,0},{4,7},{5,6},{6,5},{7,4},{8,11},{9,10},{10,... | collective-permute-start | bytes 196616 | tf_op jit(solution)/shard_map/ppermute | solution.py:219
  6.6 4.7 %collective-permute-start.1 = (bf16[64,512]{1,0:T(8,128)(2,1)S(1)}, bf16[64,512]{1,0:T(8,128)(2,1)S(1)}, u32[]{:S(2)}, u32[]{:S(2)}) collective-permute-start(bf16[64,512]{1,0:T(8,128)(2,1)S(1)} %get-tuple-element.15), channel_id=1, source_target_pairs={{0,2},{1,3},{2,0},{3,1},{4,6},{5,7},{6,4},{7,5},{8,10},{9,11},{10,... | collective-permute-start | bytes 196616 | tf_op jit(solution)/shard_map/ppermute | solution.py:219
  7.5 4.3 %collective-permute-start.2 = (bf16[64,512]{1,0:T(8,128)(2,1)S(1)}, bf16[64,512]{1,0:T(8,128)(2,1)S(1)}, u32[]{:S(2)}, u32[]{:S(2)}) collective-permute-start(bf16[64,512]{1,0:T(8,128)(2,1)S(1)} %get-tuple-element.16), channel_id=1, source_target_pairs={{0,1},{1,0},{2,3},{3,2},{4,5},{5,4},{6,7},{7,6},{8,9},{9,8},{10,11... | collective-permute-start | bytes 196616 | tf_op jit(solution)/shard_map/ppermute | solution.py:219
  12.6 4.7 %collective-permute-start.3 = (bf16[32,2,128]{2,1,0:T(2,128)(2,1)S(1)}, bf16[32,2,128]{2,1,0:T(2,128)(2,1)S(1)}, u32[]{:S(2)}, u32[]{:S(2)}) collective-permute-start(bf16[32,2,128]{2,1,0:T(2,128)(2,1)S(1)} %get-tuple-element.18), channel_id=1, source_target_pairs={{0,3},{1,2},{2,1},{3,0},{4,7},{5,6},{6,5},{7,4},{8,11},{9,10},{10,... | collective-permute-start | bytes 49160 | tf_op jit(solution)/shard_map/ppermute | solution.py:219
  14.0 3.7 %collective-permute-start.4 = (bf16[32,2,128]{2,1,0:T(2,128)(2,1)S(1)}, bf16[32,2,128]{2,1,0:T(2,128)(2,1)S(1)}, u32[]{:S(2)}, u32[]{:S(2)}) collective-permute-start(bf16[32,2,128]{2,1,0:T(2,128)(2,1)S(1)} %get-tuple-element.19), channel_id=1, source_target_pairs={{0,2},{1,3},{2,0},{3,1},{4,6},{5,7},{6,4},{7,5},{8,10},{9,11},{10,... | collective-permute-start | bytes 49160 | tf_op jit(solution)/shard_map/ppermute | solution.py:219
  15.3 3.7 %collective-permute-start.5 = (bf16[32,2,128]{2,1,0:T(2,128)(2,1)S(1)}, bf16[32,2,128]{2,1,0:T(2,128)(2,1)S(1)}, u32[]{:S(2)}, u32[]{:S(2)}) collective-permute-start(bf16[32,2,128]{2,1,0:T(2,128)(2,1)S(1)} %get-tuple-element.20), channel_id=1, source_target_pairs={{0,1},{1,0},{2,3},{3,2},{4,5},{5,4},{6,7},{7,6},{8,9},{9,8},{10,11... | collective-permute-start | bytes 49160 | tf_op jit(solution)/shard_map/ppermute | solution.py:219

commit v12 on v11

--- a/solution.py
+++ b/solution.py
@@ -1,4 +1,5 @@
 import functools
+import itertools
 import math
 
 import jax
@@ -41,54 +42,72 @@
     ]
     for copy in small:
         copy.start()
-    fetch(0, 0).start()
+    for r in range(requests):
+        fetch(r, 0).start()
     small[0].wait()
     for r in range(requests):
-        for b in range(blocks):
-            if (r, b) != (0, 0):
-                @pl.when(b * block < lengths[r])
-                def _():
-                    fetch(r, b).start()
+        for b in range(1, blocks):
+            @pl.when(b * block < lengths[r])
+            def _():
+                fetch(r, b).start()
     small[1].wait()
     small[2].wait()
 
     scale_row = scales[...].reshape(1, channels)
 
-    def request(r, live):
-        scaled = (query[r].astype(jnp.float32).T * scale_row).astype(jnp.bfloat16)
-        parts = []
-        for b in range(live):
-            fetch(r, b).wait()
-            part = jnp.dot(
-                scaled, keys[r, :, b * block:(b + 1) * block],
-                preferred_element_type=jnp.float32,
-            )
-            if b == live - 1:
-                place = b * block + lax.broadcasted_iota(jnp.int32, part.shape, 1)
-                part = jnp.where(place < lengths[r], part, -jnp.inf)
-            parts.append(part)
-        top = jnp.max(parts[0], axis=1, keepdims=True)
-        for part in parts[1:]:
-            top = jnp.maximum(top, jnp.max(part, axis=1, keepdims=True))
-        total = jnp.zeros_like(top)
-        weights = []
-        for part in parts:
-            weight = jnp.exp2((part - top) * EXP2_SCALE)
-            total += jnp.sum(weight, axis=1, keepdims=True)
-            weights.append(weight.astype(jnp.bfloat16))
+    def score(scaled, r, b, live):
+        fetch(r, b).wait()
+        part = jnp.dot(
+            scaled[r], keys[r, :, b * block:(b + 1) * block], preferred_element_type=jnp.float32
+        )
+        if b == live - 1:
+            place = b * block + lax.broadcasted_iota(jnp.int32, part.shape, 1)
+            part = jnp.where(place < lengths[r], part, -jnp.inf)
+        return part
+
+    def weigh(part, r, b):
+        top = jnp.max(part, axis=1, keepdims=True)
+        weight = jnp.exp2((part - top) * EXP2_SCALE)
+        total = jnp.sum(weight, axis=1, keepdims=True)
         mixture = lax.dot_general(
-            jnp.concatenate(weights, axis=1), keys[r, :rank, :live * block],
+            weight.astype(jnp.bfloat16), keys[r, :rank, b * block:(b + 1) * block],
             (((1,), (1,)), ((), ())), preferred_element_type=jnp.float32,
         )
+        return top, total, mixture
+
+    def merge(one, two):
+        top = jnp.maximum(one[0], two[0])
+        first = jnp.exp2((one[0] - top) * EXP2_SCALE)
+        second = jnp.exp2((two[0] - top) * EXP2_SCALE)
+        return (top,) + tuple(x * first + y * second for x, y in zip(one[1:], two[1:]))
+
+    def finish(r, total, mixture):
         latent = mixture * (1.0 / total) * scale_row[:, :rank]
         for at in range(0, rank, LANES):
             latents[at // LANES, pl.ds(r, heads, stride=requests), :] = latent[:, at:at + LANES]
 
-    for r in range(requests):
-        for live in range(1, blocks + 1):
-            @pl.when((lengths[r] > (live - 1) * block) & (lengths[r] <= live * block))
+    def several(group, live):
+        scaled = {
+            r: (query[r].astype(jnp.float32).T * scale_row).astype(jnp.bfloat16) for r in group
+        }
+        units = [(r, b, n) for r, n in zip(group, live) for b in range(n)]
+        part = score(scaled, *units[0])
+        state = None
+        for i, (r, b, n) in enumerate(units):
+            ahead = score(scaled, *units[i + 1]) if i + 1 < len(units) else None
+            done = weigh(part, r, b)
+            state = done if b == 0 else merge(state, done)
+            if b == n - 1:
+                finish(r, *state[1:])
+            part = ahead
+
+    for first in range(0, requests, 2):
+        group = tuple(range(first, min(first + 2, requests)))
+        count = [(lengths[r] + (block - 1)) // block for r in group]
+        for live in itertools.product(range(1, blocks + 1), repeat=len(group)):
+            @pl.when(functools.reduce(jnp.logical_and, [c == n for c, n in zip(count, live)]))
             def _():
-                request(r, live)
+                several(group, live)
 
     for out, k in zip(outs, order(owners)):
         mine = pl.ds(pl.multiple_of((me ^ k) * rows, rows), rows)

time: 19.9 us -> 19.5 us (0.980)
  starting transfers between devices: 7.25 us -> 9.22 us
  Pallas kernels: 7.5 us -> 5.98 us
  waiting for transfers between devices: 4.93 us -> 4.17 us
    ppermute x6, starting transfers between devices: 7.25 us -> 9.22 us  [exchange(): lax.ppermute(part, 'tp', [(i, i ^ k) for i in range(owners)])]
    pallas_call x1, Pallas kernels: 3.79 us -> 2.26 us  [attend(): pl.pallas_call(functools.partial(attend_kernel, owners), out_shape=[part]...]
    ppermute x6, waiting for transfers between devices: 4.93 us -> 4.17 us  [exchange(): lax.ppermute(part, 'tp', [(i, i ^ k) for i in range(owners)])]
  transfers between devices with their start and end apart: 6 -> 6, of which waited for: 5 -> 4; matrix products, arithmetic and copies ran while one was open for 0% -> 0% of each run, Pallas kernels for 11% -> 11%
where the time goes in v12:
time: 19.5 us; the launch traced here: 19.4 us
  starting transfers between devices  9.22 us (47%)
  Pallas kernels  5.98 us (31%)
  waiting for transfers between devices  4.17 us (21%)
    ppermute x6, starting transfers between devices, exchange(): lax.ppermute(part, 'tp', [(i, i ^ k) for i in range(owners)])  9.22 us
    ppermute x6, waiting for transfers between devices, exchange(): lax.ppermute(part, 'tp', [(i, i ^ k) for i in range(owners)])  4.17 us
    pallas_call x1, Pallas kernels, attend(): pl.pallas_call(functools.partial(attend_kernel, owners), out_shape=[part]...  2.26 us
    pallas_call x1, Pallas kernels, stage(): pl.pallas_call(stage_kernel, out_shape=jax.ShapeDtypeStruct(maps.shape, m...  2.2 us
    pallas_call x1, Pallas kernels, project(): pl.pallas_call(functools.partial(project_kernel, count), out_shape=[jax.S...  0.86 us
    pallas_call x1, Pallas kernels, assemble(): pl.pallas_call(functools.partial(assemble_kernel, owners), out_shape=pltp...  0.66 us
  transfers between devices with their start and end apart: 6, of which 4 were waited for; matrix products, arithmetic and copies ran while one was open for 0% of the time, Pallas kernels for 11%

profile of v12, /device:TPU:0, one launch (start us, length us, event | category | flops | bytes accessed | tf_op | source)
XLA Modules:
  0.0 19.4 jit_solution(14934879967115892065)
XLA Ops:
  0.0 2.3 %attend.1 = (bf16[64,512]{1,0:T(8,128)(2,1)S(1)}, bf16[64,512]{1,0:T(8,128)(2,1)S(1)}, bf16[64,512]{1,0:T(8,128)(2,1)S(1)}, bf16[64,512]{1,0:T(8,128)(2,1)S(1)}) custom-call(s32[2]{0:T(128)} %lengths_hbm.1, bf16[2,576,128]{2,1,0:T(8,128)(2,1)} %bitcast.8, f32[576]{0:T(1024)} %scales_hbm.1, bf16[2,576,1536]{2,1,0:T(8,128)(2,1)} %bitcast.7), custom_call_target="tpu_custom_call" | custom-call | flops 905969664 | bytes 3538944 | tf_op jit(solution)/shard_map/attend/pallas_call | solution.py:127
  2.3 4.4 %collective-permute-start = (bf16[64,512]{1,0:T(8,128)(2,1)S(1)}, bf16[64,512]{1,0:T(8,128)(2,1)S(1)}, u32[]{:S(2)}, u32[]{:S(2)}) collective-permute-start(bf16[64,512]{1,0:T(8,128)(2,1)S(1)} %get-tuple-element.14), channel_id=1, source_target_pairs={{0,3},{1,2},{2,1},{3,0},{4,7},{5,6},{6,5},{7,4},{8,11},{9,10},{10,... | collective-permute-start | bytes 196616 | tf_op jit(solution)/shard_map/ppermute | solution.py:238
  6.7 1.3 %collective-permute-start.1 = (bf16[64,512]{1,0:T(8,128)(2,1)S(1)}, bf16[64,512]{1,0:T(8,128)(2,1)S(1)}, u32[]{:S(2)}, u32[]{:S(2)}) collective-permute-start(bf16[64,512]{1,0:T(8,128)(2,1)S(1)} %get-tuple-element.15), channel_id=1, source_target_pairs={{0,2},{1,3},{2,0},{3,1},{4,6},{5,7},{6,4},{7,5},{8,10},{9,11},{10,... | collective-permute-start | bytes 196616 | tf_op jit(solution)/shard_map/ppermute | solution.py:238
  7.9 0.0 collective-permute-start.2
  7.9 2.2 %stage.1.refs_4_ = bf16[32,512,128]{2,1,0:T(8,128)(2,1)S(1)} custom-call(bf16[32,512,128]{2,1,0:T(8,128)(2,1)} %maps_hbm.1, bf16[64,512]{1,0:T(8,128)(2,1)S(1)} %get-tuple-element.13.after.refs_0_), custom_call_target="tpu_custom_call" | custom-call | bytes 8388608 | tf_op jit(solution)/shard_map/stage/pallas_call | solution.py:158
  10.1 0.0 collective-permute-done.refs_1_
  10.2 0.8 %collective-permute-done.1.refs_2_ = bf16[64,512]{1,0:T(8,128)(2,1)S(1)} collective-permute-done((bf16[64,512]{1,0:T(8,128)(2,1)S(1)}, bf16[64,512]{1,0:T(8,128)(2,1)S(1)}, u32[]{:S(2)}, u32[]{:S(2)}) %collective-permute-start.1) | collective-permute-done | bytes 65568 | tf_op jit(solution)/shard_map/ppermute | solution.py:238
  10.9 1.3 %collective-permute-done.2.refs_3_ = bf16[64,512]{1,0:T(8,128)(2,1)S(1)} collective-permute-done((bf16[64,512]{1,0:T(8,128)(2,1)S(1)}, bf16[64,512]{1,0:T(8,128)(2,1)S(1)}, u32[]{:S(2)}, u32[]{:S(2)}) %collective-permute-start.2) | collective-permute-done | bytes 65568 | tf_op jit(solution)/shard_map/ppermute | solution.py:238
  12.2 0.9 %project.1 = (bf16[32,2,128]{2,1,0:T(2,128)(2,1)S(1)}, bf16[32,2,128]{2,1,0:T(2,128)(2,1)S(1)}, bf16[32,2,128]{2,1,0:T(2,128)(2,1)S(1)}, bf16[32,2,128]{2,1,0:T(2,128)(2,1)S(1)}) custom-call(bf16[64,512]{1,0:T(8,128)(2,1)S(1)} %get-tuple-element.13.after.refs_0_, bf16[64,512]{1,0:T(8,128)(2,1)S(1)} %collective-permute-done.refs_1_, ...), custom_call_target="tpu_custom_call" | custom-call | flops 33554432 | bytes 4194304 | tf_op jit(solution)/shard_map/project/pallas_call | solution.py:194
  13.1 0.9 %collective-permute-start.3 = (bf16[32,2,128]{2,1,0:T(2,128)(2,1)S(1)}, bf16[32,2,128]{2,1,0:T(2,128)(2,1)S(1)}, u32[]{:S(2)}, u32[]{:S(2)}) collective-permute-start(bf16[32,2,128]{2,1,0:T(2,128)(2,1)S(1)} %get-tuple-element.18), channel_id=1, source_target_pairs={{0,3},{1,2},{2,1},{3,0},{4,7},{5,6},{6,5},{7,4},{8,11},{9,10},{10,... | collective-permute-start | bytes 49160 | tf_op jit(solution)/shard_map/ppermute | solution.py:238
  14.0 1.0 %collective-permute-start.4 = (bf16[32,2,128]{2,1,0:T(2,128)(2,1)S(1)}, bf16[32,2,128]{2,1,0:T(2,128)(2,1)S(1)}, u32[]{:S(2)}, u32[]{:S(2)}) collective-permute-start(bf16[32,2,128]{2,1,0:T(2,128)(2,1)S(1)} %get-tuple-element.19), channel_id=1, source_target_pairs={{0,2},{1,3},{2,0},{3,1},{4,6},{5,7},{6,4},{7,5},{8,10},{9,11},{10,... | collective-permute-start | bytes 49160 | tf_op jit(solution)/shard_map/ppermute | solution.py:238
  15.0 1.6 %collective-permute-start.5 = (bf16[32,2,128]{2,1,0:T(2,128)(2,1)S(1)}, bf16[32,2,128]{2,1,0:T(2,128)(2,1)S(1)}, u32[]{:S(2)}, u32[]{:S(2)}) collective-permute-start(bf16[32,2,128]{2,1,0:T(2,128)(2,1)S(1)} %get-tuple-element.20), channel_id=1, source_target_pairs={{0,1},{1,0},{2,3},{3,2},{4,5},{5,4},{6,7},{7,6},{8,9},{9,8},{10,11... | collective-permute-start | bytes 49160 | tf_op jit(solution)/shard_map/ppermute | solution.py:238
  16.6 1.3 %collective-permute-done.3.refs_1_ = bf16[32,2,128]{2,1,0:T(2,128)(2,1)S(1)} collective-permute-done((bf16[32,2,128]{2,1,0:T(2,128)(2,1)S(1)}, bf16[32,2,128]{2,1,0:T(2,128)(2,1)S(1)}, u32[]{:S(2)}, u32[]{:S(2)}) %collective-permute-start.3) | collective-permute-done | bytes 16416 | tf_op jit(solution)/shard_map/ppermute | solution.py:238
  17.9 0.0 collective-permute-done.4.refs_2_
  17.9 0.9 %collective-permute-done.5.refs_3_ = bf16[32,2,128]{2,1,0:T(2,128)(2,1)S(1)} collective-permute-done((bf16[32,2,128]{2,1,0:T(2,128)(2,1)S(1)}, bf16[32,2,128]{2,1,0:T(2,128)(2,1)S(1)}, u32[]{:S(2)}, u32[]{:S(2)}) %collective-permute-start.5) | collective-permute-done | bytes 16416 | tf_op jit(solution)/shard_map/ppermute | solution.py:238
  18.7 0.7 %assemble.1 = bf16[4,32,2,128]{3,2,1,0:T(2,128)(2,1)} custom-call(bf16[32,2,128]{2,1,0:T(2,128)(2,1)S(1)} %get-tuple-element.17.refs_0_, bf16[32,2,128]{2,1,0:T(2,128)(2,1)S(1)} %collective-permute-done.3.refs_1_, bf16[32,2,128]{2,1,0:T(2,128)(2,1)S(1)} %collective-permute-done.4.refs_2_, bf16[32,2,128]{2,1,0:T(2,128)(2,1)S(1)} %collective-permute-done.5.refs_3_), custom_call_target="tpu_custom_call" | custom-call | tf_op jit(solution)/shard_map/assemble/pallas_call | solution.py:224
Async XLA Ops:
  2.3 7.9 %collective-permute-start = (bf16[64,512]{1,0:T(8,128)(2,1)S(1)}, bf16[64,512]{1,0:T(8,128)(2,1)S(1)}, u32[]{:S(2)}, u32[]{:S(2)}) collective-permute-start(bf16[64,512]{1,0:T(8,128)(2,1)S(1)} %get-tuple-element.14), channel_id=1, source_target_pairs={{0,3},{1,2},{2,1},{3,0},{4,7},{5,6},{6,5},{7,4},{8,11},{9,10},{10,... | collective-permute-start | bytes 196616 | tf_op jit(solution)/shard_map/ppermute | solution.py:238
  6.7 4.3 %collective-permute-start.1 = (bf16[64,512]{1,0:T(8,128)(2,1)S(1)}, bf16[64,512]{1,0:T(8,128)(2,1)S(1)}, u32[]{:S(2)}, u32[]{:S(2)}) collective-permute-start(bf16[64,512]{1,0:T(8,128)(2,1)S(1)} %get-tuple-element.15), channel_id=1, source_target_pairs={{0,2},{1,3},{2,0},{3,1},{4,6},{5,7},{6,4},{7,5},{8,10},{9,11},{10,... | collective-permute-start | bytes 196616 | tf_op jit(solution)/shard_map/ppermute | solution.py:238
  7.9 4.3 %collective-permute-start.2 = (bf16[64,512]{1,0:T(8,128)(2,1)S(1)}, bf16[64,512]{1,0:T(8,128)(2,1)S(1)}, u32[]{:S(2)}, u32[]{:S(2)}) collective-permute-start(bf16[64,512]{1,0:T(8,128)(2,1)S(1)} %get-tuple-element.16), channel_id=1, source_target_pairs={{0,1},{1,0},{2,3},{3,2},{4,5},{5,4},{6,7},{7,6},{8,9},{9,8},{10,11... | collective-permute-start | bytes 196616 | tf_op jit(solution)/shard_map/ppermute | solution.py:238
  13.1 4.8 %collective-permute-start.3 = (bf16[32,2,128]{2,1,0:T(2,128)(2,1)S(1)}, bf16[32,2,128]{2,1,0:T(2,128)(2,1)S(1)}, u32[]{:S(2)}, u32[]{:S(2)}) collective-permute-start(bf16[32,2,128]{2,1,0:T(2,128)(2,1)S(1)} %get-tuple-element.18), channel_id=1, source_target_pairs={{0,3},{1,2},{2,1},{3,0},{4,7},{5,6},{6,5},{7,4},{8,11},{9,10},{10,... | collective-permute-start | bytes 49160 | tf_op jit(solution)/shard_map/ppermute | solution.py:238
  14.0 3.9 %collective-permute-start.4 = (bf16[32,2,128]{2,1,0:T(2,128)(2,1)S(1)}, bf16[32,2,128]{2,1,0:T(2,128)(2,1)S(1)}, u32[]{:S(2)}, u32[]{:S(2)}) collective-permute-start(bf16[32,2,128]{2,1,0:T(2,128)(2,1)S(1)} %get-tuple-element.19), channel_id=1, source_target_pairs={{0,2},{1,3},{2,0},{3,1},{4,6},{5,7},{6,4},{7,5},{8,10},{9,11},{10,... | collective-permute-start | bytes 49160 | tf_op jit(solution)/shard_map/ppermute | solution.py:238
  15.0 3.7 %collective-permute-start.5 = (bf16[32,2,128]{2,1,0:T(2,128)(2,1)S(1)}, bf16[32,2,128]{2,1,0:T(2,128)(2,1)S(1)}, u32[]{:S(2)}, u32[]{:S(2)}) collective-permute-start(bf16[32,2,128]{2,1,0:T(2,128)(2,1)S(1)} %get-tuple-element.20), channel_id=1, source_target_pairs={{0,1},{1,0},{2,3},{3,2},{4,5},{5,4},{6,7},{7,6},{8,9},{9,8},{10,11... | collective-permute-start | bytes 49160 | tf_op jit(solution)/shard_map/ppermute | solution.py:238

commit v13 on v12

--- a/solution.py
+++ b/solution.py
@@ -13,6 +13,7 @@
 SOFTMAX_SCALE = (1.0 + 0.1 * math.log(40.0)) ** 2 / math.sqrt(192.0)
 EXP2_SCALE = SOFTMAX_SCALE * math.log2(math.e)
 BLOCK = 512
+EAGER = 2
 LANES = 128
 GROUP_ROWS = 16
 
@@ -42,11 +43,13 @@
     ]
     for copy in small:
         copy.start()
-    for r in range(requests):
-        fetch(r, 0).start()
+    eager = min(EAGER, blocks)
+    for b in range(eager):
+        for r in range(requests):
+            fetch(r, b).start()
     small[0].wait()
     for r in range(requests):
-        for b in range(1, blocks):
+        for b in range(eager, blocks):
             @pl.when(b * block < lengths[r])
             def _():
                 fetch(r, b).start()
@@ -100,6 +103,9 @@
             if b == n - 1:
                 finish(r, *state[1:])
             part = ahead
+        for r, n in zip(group, live):
+            for b in range(n, eager):
+                fetch(r, b).wait()
 
     for first in range(0, requests, 2):
         group = tuple(range(first, min(first + 2, requests)))

time: 19.5 us -> 20 us (1.026)
  waiting for transfers between devices: 4.17 us -> 4.54 us
  Pallas kernels: 5.98 us -> 6.25 us
  starting transfers between devices: 9.22 us -> 9.01 us
    ppermute x6, waiting for transfers between devices: 4.17 us -> 4.54 us  [exchange(): lax.ppermute(part, 'tp', [(i, i ^ k) for i in range(owners)])]
    pallas_call x1, Pallas kernels: 2.26 us -> 2.54 us  [attend(): pl.pallas_call(functools.partial(attend_kernel, owners), out_shape=[part]...]
    ppermute x6, starting transfers between devices: 9.22 us -> 9.01 us  [exchange(): lax.ppermute(part, 'tp', [(i, i ^ k) for i in range(owners)])]
where the time goes in v13:
time: 20 us; the launch traced here: 19.8 us
  starting transfers between devices  9.01 us (45%)
  Pallas kernels  6.25 us (31%)
  waiting for transfers between devices  4.54 us (23%)
    ppermute x6, starting transfers between devices, exchange(): lax.ppermute(part, 'tp', [(i, i ^ k) for i in range(owners)])  9.01 us
    ppermute x6, waiting for transfers between devices, exchange(): lax.ppermute(part, 'tp', [(i, i ^ k) for i in range(owners)])  4.54 us
    pallas_call x1, Pallas kernels, attend(): pl.pallas_call(functools.partial(attend_kernel, owners), out_shape=[part]...  2.54 us
    pallas_call x1, Pallas kernels, stage(): pl.pallas_call(stage_kernel, out_shape=jax.ShapeDtypeStruct(maps.shape, m...  2.2 us
    pallas_call x1, Pallas kernels, project(): pl.pallas_call(functools.partial(project_kernel, count), out_shape=[jax.S...  0.86 us
    pallas_call x1, Pallas kernels, assemble(): pl.pallas_call(functools.partial(assemble_kernel, owners), out_shape=pltp...  0.66 us
  transfers between devices with their start and end apart: 6, of which 4 were waited for; matrix products, arithmetic and copies ran while one was open for 0% of the time, Pallas kernels for 11%

profile of v13, /device:TPU:0, one launch (start us, length us, event | category | flops | bytes accessed | tf_op | source)
XLA Modules:
  0.0 19.8 jit_solution(11471442169585680173)
XLA Ops:
  0.0 2.5 %attend.1 = (bf16[64,512]{1,0:T(8,128)(2,1)S(1)}, bf16[64,512]{1,0:T(8,128)(2,1)S(1)}, bf16[64,512]{1,0:T(8,128)(2,1)S(1)}, bf16[64,512]{1,0:T(8,128)(2,1)S(1)}) custom-call(s32[2]{0:T(128)} %lengths_hbm.1, bf16[2,576,128]{2,1,0:T(8,128)(2,1)} %bitcast.8, f32[576]{0:T(1024)} %scales_hbm.1, bf16[2,576,1536]{2,1,0:T(8,128)(2,1)} %bitcast.7), custom_call_target="tpu_custom_call" | custom-call | flops 905969664 | bytes 3538944 | tf_op jit(solution)/shard_map/attend/pallas_call | solution.py:133
  2.5 4.8 %collective-permute-start = (bf16[64,512]{1,0:T(8,128)(2,1)S(1)}, bf16[64,512]{1,0:T(8,128)(2,1)S(1)}, u32[]{:S(2)}, u32[]{:S(2)}) collective-permute-start(bf16[64,512]{1,0:T(8,128)(2,1)S(1)} %get-tuple-element.14), channel_id=1, source_target_pairs={{0,3},{1,2},{2,1},{3,0},{4,7},{5,6},{6,5},{7,4},{8,11},{9,10},{10,... | collective-permute-start | bytes 196616 | tf_op jit(solution)/shard_map/ppermute | solution.py:244
  7.4 0.0 collective-permute-start.1
  7.4 0.6 %collective-permute-start.2 = (bf16[64,512]{1,0:T(8,128)(2,1)S(1)}, bf16[64,512]{1,0:T(8,128)(2,1)S(1)}, u32[]{:S(2)}, u32[]{:S(2)}) collective-permute-start(bf16[64,512]{1,0:T(8,128)(2,1)S(1)} %get-tuple-element.16), channel_id=1, source_target_pairs={{0,1},{1,0},{2,3},{3,2},{4,5},{5,4},{6,7},{7,6},{8,9},{9,8},{10,11... | collective-permute-start | bytes 196616 | tf_op jit(solution)/shard_map/ppermute | solution.py:244
  8.0 2.2 %stage.1.refs_4_ = bf16[32,512,128]{2,1,0:T(8,128)(2,1)S(1)} custom-call(bf16[32,512,128]{2,1,0:T(8,128)(2,1)} %maps_hbm.1, bf16[64,512]{1,0:T(8,128)(2,1)S(1)} %get-tuple-element.13.after.refs_0_), custom_call_target="tpu_custom_call" | custom-call | bytes 8388608 | tf_op jit(solution)/shard_map/stage/pallas_call | solution.py:164
  10.2 0.0 collective-permute-done.refs_1_
  10.2 1.4 %collective-permute-done.1.refs_2_ = bf16[64,512]{1,0:T(8,128)(2,1)S(1)} collective-permute-done((bf16[64,512]{1,0:T(8,128)(2,1)S(1)}, bf16[64,512]{1,0:T(8,128)(2,1)S(1)}, u32[]{:S(2)}, u32[]{:S(2)}) %collective-permute-start.1) | collective-permute-done | bytes 65568 | tf_op jit(solution)/shard_map/ppermute | solution.py:244
  11.6 0.0 collective-permute-done.2.refs_3_
  11.6 0.9 %project.1 = (bf16[32,2,128]{2,1,0:T(2,128)(2,1)S(1)}, bf16[32,2,128]{2,1,0:T(2,128)(2,1)S(1)}, bf16[32,2,128]{2,1,0:T(2,128)(2,1)S(1)}, bf16[32,2,128]{2,1,0:T(2,128)(2,1)S(1)}) custom-call(bf16[64,512]{1,0:T(8,128)(2,1)S(1)} %get-tuple-element.13.after.refs_0_, bf16[64,512]{1,0:T(8,128)(2,1)S(1)} %collective-permute-done.refs_1_, ...), custom_call_target="tpu_custom_call" | custom-call | flops 33554432 | bytes 4194304 | tf_op jit(solution)/shard_map/project/pallas_call | solution.py:200
  12.5 1.6 %collective-permute-start.3 = (bf16[32,2,128]{2,1,0:T(2,128)(2,1)S(1)}, bf16[32,2,128]{2,1,0:T(2,128)(2,1)S(1)}, u32[]{:S(2)}, u32[]{:S(2)}) collective-permute-start(bf16[32,2,128]{2,1,0:T(2,128)(2,1)S(1)} %get-tuple-element.18), channel_id=1, source_target_pairs={{0,3},{1,2},{2,1},{3,0},{4,7},{5,6},{6,5},{7,4},{8,11},{9,10},{10,... | collective-permute-start | bytes 49160 | tf_op jit(solution)/shard_map/ppermute | solution.py:244
  14.1 1.3 %collective-permute-start.4 = (bf16[32,2,128]{2,1,0:T(2,128)(2,1)S(1)}, bf16[32,2,128]{2,1,0:T(2,128)(2,1)S(1)}, u32[]{:S(2)}, u32[]{:S(2)}) collective-permute-start(bf16[32,2,128]{2,1,0:T(2,128)(2,1)S(1)} %get-tuple-element.19), channel_id=1, source_target_pairs={{0,2},{1,3},{2,0},{3,1},{4,6},{5,7},{6,4},{7,5},{8,10},{9,11},{10,... | collective-permute-start | bytes 49160 | tf_op jit(solution)/shard_map/ppermute | solution.py:244
  15.4 0.6 %collective-permute-start.5 = (bf16[32,2,128]{2,1,0:T(2,128)(2,1)S(1)}, bf16[32,2,128]{2,1,0:T(2,128)(2,1)S(1)}, u32[]{:S(2)}, u32[]{:S(2)}) collective-permute-start(bf16[32,2,128]{2,1,0:T(2,128)(2,1)S(1)} %get-tuple-element.20), channel_id=1, source_target_pairs={{0,1},{1,0},{2,3},{3,2},{4,5},{5,4},{6,7},{7,6},{8,9},{9,8},{10,11... | collective-permute-start | bytes 49160 | tf_op jit(solution)/shard_map/ppermute | solution.py:244
  16.1 1.3 %collective-permute-done.3.refs_1_ = bf16[32,2,128]{2,1,0:T(2,128)(2,1)S(1)} collective-permute-done((bf16[32,2,128]{2,1,0:T(2,128)(2,1)S(1)}, bf16[32,2,128]{2,1,0:T(2,128)(2,1)S(1)}, u32[]{:S(2)}, u32[]{:S(2)}) %collective-permute-start.3) | collective-permute-done | bytes 16416 | tf_op jit(solution)/shard_map/ppermute | solution.py:244
  17.3 0.5 %collective-permute-done.4.refs_2_ = bf16[32,2,128]{2,1,0:T(2,128)(2,1)S(1)} collective-permute-done((bf16[32,2,128]{2,1,0:T(2,128)(2,1)S(1)}, bf16[32,2,128]{2,1,0:T(2,128)(2,1)S(1)}, u32[]{:S(2)}, u32[]{:S(2)}) %collective-permute-start.4) | collective-permute-done | bytes 16416 | tf_op jit(solution)/shard_map/ppermute | solution.py:244
  17.9 1.3 %collective-permute-done.5.refs_3_ = bf16[32,2,128]{2,1,0:T(2,128)(2,1)S(1)} collective-permute-done((bf16[32,2,128]{2,1,0:T(2,128)(2,1)S(1)}, bf16[32,2,128]{2,1,0:T(2,128)(2,1)S(1)}, u32[]{:S(2)}, u32[]{:S(2)}) %collective-permute-start.5) | collective-permute-done | bytes 16416 | tf_op jit(solution)/shard_map/ppermute | solution.py:244
  19.2 0.7 %assemble.1 = bf16[4,32,2,128]{3,2,1,0:T(2,128)(2,1)} custom-call(bf16[32,2,128]{2,1,0:T(2,128)(2,1)S(1)} %get-tuple-element.17.refs_0_, bf16[32,2,128]{2,1,0:T(2,128)(2,1)S(1)} %collective-permute-done.3.refs_1_, bf16[32,2,128]{2,1,0:T(2,128)(2,1)S(1)} %collective-permute-done.4.refs_2_, bf16[32,2,128]{2,1,0:T(2,128)(2,1)S(1)} %collective-permute-done.5.refs_3_), custom_call_target="tpu_custom_call" | custom-call | tf_op jit(solution)/shard_map/assemble/pallas_call | solution.py:230
Async XLA Ops:
  2.5 7.7 %collective-permute-start = (bf16[64,512]{1,0:T(8,128)(2,1)S(1)}, bf16[64,512]{1,0:T(8,128)(2,1)S(1)}, u32[]{:S(2)}, u32[]{:S(2)}) collective-permute-start(bf16[64,512]{1,0:T(8,128)(2,1)S(1)} %get-tuple-element.14), channel_id=1, source_target_pairs={{0,3},{1,2},{2,1},{3,0},{4,7},{5,6},{6,5},{7,4},{8,11},{9,10},{10,... | collective-permute-start | bytes 196616 | tf_op jit(solution)/shard_map/ppermute | solution.py:244
  7.4 4.3 %collective-permute-start.1 = (bf16[64,512]{1,0:T(8,128)(2,1)S(1)}, bf16[64,512]{1,0:T(8,128)(2,1)S(1)}, u32[]{:S(2)}, u32[]{:S(2)}) collective-permute-start(bf16[64,512]{1,0:T(8,128)(2,1)S(1)} %get-tuple-element.15), channel_id=1, source_target_pairs={{0,2},{1,3},{2,0},{3,1},{4,6},{5,7},{6,4},{7,5},{8,10},{9,11},{10,... | collective-permute-start | bytes 196616 | tf_op jit(solution)/shard_map/ppermute | solution.py:244
  7.4 4.3 %collective-permute-start.2 = (bf16[64,512]{1,0:T(8,128)(2,1)S(1)}, bf16[64,512]{1,0:T(8,128)(2,1)S(1)}, u32[]{:S(2)}, u32[]{:S(2)}) collective-permute-start(bf16[64,512]{1,0:T(8,128)(2,1)S(1)} %get-tuple-element.16), channel_id=1, source_target_pairs={{0,1},{1,0},{2,3},{3,2},{4,5},{5,4},{6,7},{7,6},{8,9},{9,8},{10,11... | collective-permute-start | bytes 196616 | tf_op jit(solution)/shard_map/ppermute | solution.py:244
  12.5 4.8 %collective-permute-start.3 = (bf16[32,2,128]{2,1,0:T(2,128)(2,1)S(1)}, bf16[32,2,128]{2,1,0:T(2,128)(2,1)S(1)}, u32[]{:S(2)}, u32[]{:S(2)}) collective-permute-start(bf16[32,2,128]{2,1,0:T(2,128)(2,1)S(1)} %get-tuple-element.18), channel_id=1, source_target_pairs={{0,3},{1,2},{2,1},{3,0},{4,7},{5,6},{6,5},{7,4},{8,11},{9,10},{10,... | collective-permute-start | bytes 49160 | tf_op jit(solution)/shard_map/ppermute | solution.py:244
  14.1 3.7 %collective-permute-start.4 = (bf16[32,2,128]{2,1,0:T(2,128)(2,1)S(1)}, bf16[32,2,128]{2,1,0:T(2,128)(2,1)S(1)}, u32[]{:S(2)}, u32[]{:S(2)}) collective-permute-start(bf16[32,2,128]{2,1,0:T(2,128)(2,1)S(1)} %get-tuple-element.19), channel_id=1, source_target_pairs={{0,2},{1,3},{2,0},{3,1},{4,6},{5,7},{6,4},{7,5},{8,10},{9,11},{10,... | collective-permute-start | bytes 49160 | tf_op jit(solution)/shard_map/ppermute | solution.py:244
  15.4 3.7 %collective-permute-start.5 = (bf16[32,2,128]{2,1,0:T(2,128)(2,1)S(1)}, bf16[32,2,128]{2,1,0:T(2,128)(2,1)S(1)}, u32[]{:S(2)}, u32[]{:S(2)}) collective-permute-start(bf16[32,2,128]{2,1,0:T(2,128)(2,1)S(1)} %get-tuple-element.20), channel_id=1, source_target_pairs={{0,1},{1,0},{2,3},{3,2},{4,5},{5,4},{6,7},{7,6},{8,9},{9,8},{10,11... | collective-permute-start | bytes 49160 | tf_op jit(solution)/shard_map/ppermute | solution.py:244

commit v14 on v12

--- a/solution.py
+++ b/solution.py
@@ -34,31 +34,38 @@
         span = pl.ds(b * block, block)
         return pltpu.make_async_copy(cache.at[r, :, span], keys.at[r, :, span], sems.at[r, b])
 
-    small = [
-        pltpu.make_async_copy(source, target, small_sems.at[i])
-        for i, (source, target) in enumerate(
-            [(lengths_hbm, lengths), (query_hbm, query), (scales_hbm, scales)]
-        )
-    ]
-    for copy in small:
-        copy.start()
+    def ask(r):
+        return pltpu.make_async_copy(query_hbm.at[r], query.at[r], small_sems.at[2 + r])
+
+    lengths_copy = pltpu.make_async_copy(lengths_hbm, lengths, small_sems.at[0])
+    scales_copy = pltpu.make_async_copy(scales_hbm, scales, small_sems.at[1])
+    lengths_copy.start()
+    scales_copy.start()
     for r in range(requests):
+        ask(r).start()
         fetch(r, 0).start()
-    small[0].wait()
+    lengths_copy.wait()
     for r in range(requests):
         for b in range(1, blocks):
             @pl.when(b * block < lengths[r])
             def _():
                 fetch(r, b).start()
-    small[1].wait()
-    small[2].wait()
-
+    scales_copy.wait()
     scale_row = scales[...].reshape(1, channels)
 
+    def scale(r):
+        ask(r).wait()
+        return (query[r].astype(jnp.float32).T * scale_row).astype(jnp.bfloat16)
+
     def score(scaled, r, b, live):
+        if r not in scaled:
+            scaled[r] = scale(r)
         fetch(r, b).wait()
+        span = slice(b * block, (b + 1) * block)
         part = jnp.dot(
-            scaled[r], keys[r, :, b * block:(b + 1) * block], preferred_element_type=jnp.float32
+            scaled[r][:, :rank], keys[r, :rank, span], preferred_element_type=jnp.float32
+        ) + jnp.dot(
+            scaled[r][:, rank:], keys[r, rank:, span], preferred_element_type=jnp.float32
         )
         if b == live - 1:
             place = b * block + lax.broadcasted_iota(jnp.int32, part.shape, 1)
@@ -87,9 +94,7 @@
             latents[at // LANES, pl.ds(r, heads, stride=requests), :] = latent[:, at:at + LANES]
 
     def several(group, live):
-        scaled = {
-            r: (query[r].astype(jnp.float32).T * scale_row).astype(jnp.bfloat16) for r in group
-        }
+        scaled = {}
         units = [(r, b, n) for r, n in zip(group, live) for b in range(n)]
         part = score(scaled, *units[0])
         state = None
@@ -136,7 +141,7 @@
             pltpu.VMEM((channels,), jnp.float32),
             pltpu.VMEM((requests, channels, cache_len), jnp.bfloat16),
             pltpu.SemaphoreType.DMA((requests, cache_len // min(BLOCK, cache_len))),
-            pltpu.SemaphoreType.DMA((3,)),
+            pltpu.SemaphoreType.DMA((2 + requests,)),
         ],
         compiler_params=pltpu.CompilerParams(vmem_limit_bytes=24 * 2**20),
         cost_estimate=pl.CostEstimate(

time: 19.5 us -> 19.3 us (0.990)
  Pallas kernels: 5.98 us -> 6.44 us
  starting transfers between devices: 9.22 us -> 8.87 us
  waiting for transfers between devices: 4.17 us -> 3.86 us
    pallas_call x1, Pallas kernels: 2.26 us -> 2.73 us  [attend(): pl.pallas_call(functools.partial(attend_kernel, owners), out_shape=[part]...]
    ppermute x6, starting transfers between devices: 9.22 us -> 8.87 us  [exchange(): lax.ppermute(part, 'tp', [(i, i ^ k) for i in range(owners)])]
    ppermute x6, waiting for transfers between devices: 4.17 us -> 3.86 us  [exchange(): lax.ppermute(part, 'tp', [(i, i ^ k) for i in range(owners)])]
  transfers between devices with their start and end apart: 6 -> 6, of which waited for: 4 -> 5; matrix products, arithmetic and copies ran while one was open for 0% -> 0% of each run, Pallas kernels for 11% -> 11%
where the time goes in v14:
time: 19.3 us; the launch traced here: 19.2 us
  starting transfers between devices  8.87 us (46%)
  Pallas kernels  6.44 us (33%)
  waiting for transfers between devices  3.86 us (20%)
    ppermute x6, starting transfers between devices, exchange(): lax.ppermute(part, 'tp', [(i, i ^ k) for i in range(owners)])  8.87 us
    ppermute x6, waiting for transfers between devices, exchange(): lax.ppermute(part, 'tp', [(i, i ^ k) for i in range(owners)])  3.86 us
    pallas_call x1, Pallas kernels, attend(): pl.pallas_call(functools.partial(attend_kernel, owners), out_shape=[part]...  2.73 us
    pallas_call x1, Pallas kernels, stage(): pl.pallas_call(stage_kernel, out_shape=jax.ShapeDtypeStruct(maps.shape, m...  2.2 us
    pallas_call x1, Pallas kernels, project(): pl.pallas_call(functools.partial(project_kernel, count), out_shape=[jax.S...  0.86 us
    pallas_call x1, Pallas kernels, assemble(): pl.pallas_call(functools.partial(assemble_kernel, owners), out_shape=pltp...  0.66 us
  transfers between devices with their start and end apart: 6, of which 5 were waited for; matrix products, arithmetic and copies ran while one was open for 0% of the time, Pallas kernels for 11%

profile of v14, /device:TPU:0, one launch (start us, length us, event | category | flops | bytes accessed | tf_op | source)
XLA Modules:
  0.0 19.2 jit_solution(12021391503396631008)
XLA Ops:
  0.0 2.7 %attend.1 = (bf16[64,512]{1,0:T(8,128)(2,1)S(1)}, bf16[64,512]{1,0:T(8,128)(2,1)S(1)}, bf16[64,512]{1,0:T(8,128)(2,1)S(1)}, bf16[64,512]{1,0:T(8,128)(2,1)S(1)}) custom-call(s32[2]{0:T(128)} %lengths_hbm.1, bf16[2,576,128]{2,1,0:T(8,128)(2,1)} %bitcast.8, f32[576]{0:T(1024)} %scales_hbm.1, bf16[2,576,1536]{2,1,0:T(8,128)(2,1)} %bitcast.7), custom_call_target="tpu_custom_call" | custom-call | flops 905969664 | bytes 3538944 | tf_op jit(solution)/shard_map/attend/pallas_call | solution.py:132
  2.7 4.4 %collective-permute-start = (bf16[64,512]{1,0:T(8,128)(2,1)S(1)}, bf16[64,512]{1,0:T(8,128)(2,1)S(1)}, u32[]{:S(2)}, u32[]{:S(2)}) collective-permute-start(bf16[64,512]{1,0:T(8,128)(2,1)S(1)} %get-tuple-element.14), channel_id=1, source_target_pairs={{0,3},{1,2},{2,1},{3,0},{4,7},{5,6},{6,5},{7,4},{8,11},{9,10},{10,... | collective-permute-start | bytes 196616 | tf_op jit(solution)/shard_map/ppermute | solution.py:243
  7.1 0.5 %collective-permute-start.1 = (bf16[64,512]{1,0:T(8,128)(2,1)S(1)}, bf16[64,512]{1,0:T(8,128)(2,1)S(1)}, u32[]{:S(2)}, u32[]{:S(2)}) collective-permute-start(bf16[64,512]{1,0:T(8,128)(2,1)S(1)} %get-tuple-element.15), channel_id=1, source_target_pairs={{0,2},{1,3},{2,0},{3,1},{4,6},{5,7},{6,4},{7,5},{8,10},{9,11},{10,... | collective-permute-start | bytes 196616 | tf_op jit(solution)/shard_map/ppermute | solution.py:243
  7.6 0.4 %collective-permute-start.2 = (bf16[64,512]{1,0:T(8,128)(2,1)S(1)}, bf16[64,512]{1,0:T(8,128)(2,1)S(1)}, u32[]{:S(2)}, u32[]{:S(2)}) collective-permute-start(bf16[64,512]{1,0:T(8,128)(2,1)S(1)} %get-tuple-element.16), channel_id=1, source_target_pairs={{0,1},{1,0},{2,3},{3,2},{4,5},{5,4},{6,7},{7,6},{8,9},{9,8},{10,11... | collective-permute-start | bytes 196616 | tf_op jit(solution)/shard_map/ppermute | solution.py:243
  8.1 2.2 %stage.1.refs_4_ = bf16[32,512,128]{2,1,0:T(8,128)(2,1)S(1)} custom-call(bf16[32,512,128]{2,1,0:T(8,128)(2,1)} %maps_hbm.1, bf16[64,512]{1,0:T(8,128)(2,1)S(1)} %get-tuple-element.13.after.refs_0_), custom_call_target="tpu_custom_call" | custom-call | bytes 8388608 | tf_op jit(solution)/shard_map/stage/pallas_call | solution.py:163
  10.3 0.0 collective-permute-done.refs_1_
  10.3 1.1 %collective-permute-done.1.refs_2_ = bf16[64,512]{1,0:T(8,128)(2,1)S(1)} collective-permute-done((bf16[64,512]{1,0:T(8,128)(2,1)S(1)}, bf16[64,512]{1,0:T(8,128)(2,1)S(1)}, u32[]{:S(2)}, u32[]{:S(2)}) %collective-permute-start.1) | collective-permute-done | bytes 65568 | tf_op jit(solution)/shard_map/ppermute | solution.py:243
  11.4 0.5 %collective-permute-done.2.refs_3_ = bf16[64,512]{1,0:T(8,128)(2,1)S(1)} collective-permute-done((bf16[64,512]{1,0:T(8,128)(2,1)S(1)}, bf16[64,512]{1,0:T(8,128)(2,1)S(1)}, u32[]{:S(2)}, u32[]{:S(2)}) %collective-permute-start.2) | collective-permute-done | bytes 65568 | tf_op jit(solution)/shard_map/ppermute | solution.py:243
  11.9 0.9 %project.1 = (bf16[32,2,128]{2,1,0:T(2,128)(2,1)S(1)}, bf16[32,2,128]{2,1,0:T(2,128)(2,1)S(1)}, bf16[32,2,128]{2,1,0:T(2,128)(2,1)S(1)}, bf16[32,2,128]{2,1,0:T(2,128)(2,1)S(1)}) custom-call(bf16[64,512]{1,0:T(8,128)(2,1)S(1)} %get-tuple-element.13.after.refs_0_, bf16[64,512]{1,0:T(8,128)(2,1)S(1)} %collective-permute-done.refs_1_, ...), custom_call_target="tpu_custom_call" | custom-call | flops 33554432 | bytes 4194304 | tf_op jit(solution)/shard_map/project/pallas_call | solution.py:199
  12.8 2.0 %collective-permute-start.3 = (bf16[32,2,128]{2,1,0:T(2,128)(2,1)S(1)}, bf16[32,2,128]{2,1,0:T(2,128)(2,1)S(1)}, u32[]{:S(2)}, u32[]{:S(2)}) collective-permute-start(bf16[32,2,128]{2,1,0:T(2,128)(2,1)S(1)} %get-tuple-element.18), channel_id=1, source_target_pairs={{0,3},{1,2},{2,1},{3,0},{4,7},{5,6},{6,5},{7,4},{8,11},{9,10},{10,... | collective-permute-start | bytes 49160 | tf_op jit(solution)/shard_map/ppermute | solution.py:243
  14.7 0.1 collective-permute-start.4
  14.8 1.5 %collective-permute-start.5 = (bf16[32,2,128]{2,1,0:T(2,128)(2,1)S(1)}, bf16[32,2,128]{2,1,0:T(2,128)(2,1)S(1)}, u32[]{:S(2)}, u32[]{:S(2)}) collective-permute-start(bf16[32,2,128]{2,1,0:T(2,128)(2,1)S(1)} %get-tuple-element.20), channel_id=1, source_target_pairs={{0,1},{1,0},{2,3},{3,2},{4,5},{5,4},{6,7},{7,6},{8,9},{9,8},{10,11... | collective-permute-start | bytes 49160 | tf_op jit(solution)/shard_map/ppermute | solution.py:243
  16.3 1.1 %collective-permute-done.3.refs_1_ = bf16[32,2,128]{2,1,0:T(2,128)(2,1)S(1)} collective-permute-done((bf16[32,2,128]{2,1,0:T(2,128)(2,1)S(1)}, bf16[32,2,128]{2,1,0:T(2,128)(2,1)S(1)}, u32[]{:S(2)}, u32[]{:S(2)}) %collective-permute-start.3) | collective-permute-done | bytes 16416 | tf_op jit(solution)/shard_map/ppermute | solution.py:243
  17.5 1.0 %collective-permute-done.4.refs_2_ = bf16[32,2,128]{2,1,0:T(2,128)(2,1)S(1)} collective-permute-done((bf16[32,2,128]{2,1,0:T(2,128)(2,1)S(1)}, bf16[32,2,128]{2,1,0:T(2,128)(2,1)S(1)}, u32[]{:S(2)}, u32[]{:S(2)}) %collective-permute-start.4) | collective-permute-done | bytes 16416 | tf_op jit(solution)/shard_map/ppermute | solution.py:243
  18.5 0.1 collective-permute-done.5.refs_3_
  18.6 0.7 %assemble.1 = bf16[4,32,2,128]{3,2,1,0:T(2,128)(2,1)} custom-call(bf16[32,2,128]{2,1,0:T(2,128)(2,1)S(1)} %get-tuple-element.17.refs_0_, bf16[32,2,128]{2,1,0:T(2,128)(2,1)S(1)} %collective-permute-done.3.refs_1_, bf16[32,2,128]{2,1,0:T(2,128)(2,1)S(1)} %collective-permute-done.4.refs_2_, bf16[32,2,128]{2,1,0:T(2,128)(2,1)S(1)} %collective-permute-done.5.refs_3_), custom_call_target="tpu_custom_call" | custom-call | tf_op jit(solution)/shard_map/assemble/pallas_call | solution.py:229
Async XLA Ops:
  2.7 7.5 %collective-permute-start = (bf16[64,512]{1,0:T(8,128)(2,1)S(1)}, bf16[64,512]{1,0:T(8,128)(2,1)S(1)}, u32[]{:S(2)}, u32[]{:S(2)}) collective-permute-start(bf16[64,512]{1,0:T(8,128)(2,1)S(1)} %get-tuple-element.14), channel_id=1, source_target_pairs={{0,3},{1,2},{2,1},{3,0},{4,7},{5,6},{6,5},{7,4},{8,11},{9,10},{10,... | collective-permute-start | bytes 196616 | tf_op jit(solution)/shard_map/ppermute | solution.py:243
  7.1 4.3 %collective-permute-start.1 = (bf16[64,512]{1,0:T(8,128)(2,1)S(1)}, bf16[64,512]{1,0:T(8,128)(2,1)S(1)}, u32[]{:S(2)}, u32[]{:S(2)}) collective-permute-start(bf16[64,512]{1,0:T(8,128)(2,1)S(1)} %get-tuple-element.15), channel_id=1, source_target_pairs={{0,2},{1,3},{2,0},{3,1},{4,6},{5,7},{6,4},{7,5},{8,10},{9,11},{10,... | collective-permute-start | bytes 196616 | tf_op jit(solution)/shard_map/ppermute | solution.py:243
  7.6 4.3 %collective-permute-start.2 = (bf16[64,512]{1,0:T(8,128)(2,1)S(1)}, bf16[64,512]{1,0:T(8,128)(2,1)S(1)}, u32[]{:S(2)}, u32[]{:S(2)}) collective-permute-start(bf16[64,512]{1,0:T(8,128)(2,1)S(1)} %get-tuple-element.16), channel_id=1, source_target_pairs={{0,1},{1,0},{2,3},{3,2},{4,5},{5,4},{6,7},{7,6},{8,9},{9,8},{10,11... | collective-permute-start | bytes 196616 | tf_op jit(solution)/shard_map/ppermute | solution.py:243
  12.8 4.7 %collective-permute-start.3 = (bf16[32,2,128]{2,1,0:T(2,128)(2,1)S(1)}, bf16[32,2,128]{2,1,0:T(2,128)(2,1)S(1)}, u32[]{:S(2)}, u32[]{:S(2)}) collective-permute-start(bf16[32,2,128]{2,1,0:T(2,128)(2,1)S(1)} %get-tuple-element.18), channel_id=1, source_target_pairs={{0,3},{1,2},{2,1},{3,0},{4,7},{5,6},{6,5},{7,4},{8,11},{9,10},{10,... | collective-permute-start | bytes 49160 | tf_op jit(solution)/shard_map/ppermute | solution.py:243
  14.7 3.7 %collective-permute-start.4 = (bf16[32,2,128]{2,1,0:T(2,128)(2,1)S(1)}, bf16[32,2,128]{2,1,0:T(2,128)(2,1)S(1)}, u32[]{:S(2)}, u32[]{:S(2)}) collective-permute-start(bf16[32,2,128]{2,1,0:T(2,128)(2,1)S(1)} %get-tuple-element.19), channel_id=1, source_target_pairs={{0,2},{1,3},{2,0},{3,1},{4,6},{5,7},{6,4},{7,5},{8,10},{9,11},{10,... | collective-permute-start | bytes 49160 | tf_op jit(solution)/shard_map/ppermute | solution.py:243
  14.8 3.7 %collective-permute-start.5 = (bf16[32,2,128]{2,1,0:T(2,128)(2,1)S(1)}, bf16[32,2,128]{2,1,0:T(2,128)(2,1)S(1)}, u32[]{:S(2)}, u32[]{:S(2)}) collective-permute-start(bf16[32,2,128]{2,1,0:T(2,128)(2,1)S(1)} %get-tuple-element.20), channel_id=1, source_target_pairs={{0,1},{1,0},{2,3},{3,2},{4,5},{5,4},{6,7},{7,6},{8,9},{9,8},{10,11... | collective-permute-start | bytes 49160 | tf_op jit(solution)/shard_map/ppermute | solution.py:243

commit v15 on v14

--- a/solution.py
+++ b/solution.py
@@ -62,11 +62,7 @@
             scaled[r] = scale(r)
         fetch(r, b).wait()
         span = slice(b * block, (b + 1) * block)
-        part = jnp.dot(
-            scaled[r][:, :rank], keys[r, :rank, span], preferred_element_type=jnp.float32
-        ) + jnp.dot(
-            scaled[r][:, rank:], keys[r, rank:, span], preferred_element_type=jnp.float32
-        )
+        part = jnp.dot(scaled[r], keys[r, :, span], preferred_element_type=jnp.float32)
         if b == live - 1:
             place = b * block + lax.broadcasted_iota(jnp.int32, part.shape, 1)
             part = jnp.where(place < lengths[r], part, -jnp.inf)
@@ -95,15 +91,16 @@
 
     def several(group, live):
         scaled = {}
-        units = [(r, b, n) for r, n in zip(group, live) for b in range(n)]
+        units = [(r, 0, n) for r, n in zip(group, live)]
+        units += [(r, b, n) for r, n in zip(group, live) for b in range(1, n)]
         part = score(scaled, *units[0])
-        state = None
+        state = {}
         for i, (r, b, n) in enumerate(units):
             ahead = score(scaled, *units[i + 1]) if i + 1 < len(units) else None
             done = weigh(part, r, b)
-            state = done if b == 0 else merge(state, done)
+            state[r] = merge(state[r], done) if b else done
             if b == n - 1:
-                finish(r, *state[1:])
+                finish(r, *state[r][1:])
             part = ahead
 
     for first in range(0, requests, 2):

time: 19.3 us -> 19.6 us (1.016); the launches traced: 19.2 us -> 19.2 us
  starting transfers between devices: 8.87 us -> 9.36 us
  Pallas kernels: 6.44 us -> 6.05 us
    ppermute x6, starting transfers between devices: 8.87 us -> 9.36 us  [exchange(): lax.ppermute(part, 'tp', [(i, i ^ k) for i in range(owners)])]
    pallas_call x1, Pallas kernels: 2.73 us -> 2.34 us  [attend(): pl.pallas_call(functools.partial(attend_kernel, owners), out_shape=[part]...]
  transfers between devices with their start and end apart: 6 -> 6, of which waited for: 5 -> 4; matrix products, arithmetic and copies ran while one was open for 0% -> 0% of each run, Pallas kernels for 11% -> 11%
where the time goes in v15:
time: 19.6 us; the launch traced here: 19.2 us
  starting transfers between devices  9.36 us (48%)
  Pallas kernels  6.05 us (31%)
  waiting for transfers between devices  3.77 us (19%)
    ppermute x6, starting transfers between devices, exchange(): lax.ppermute(part, 'tp', [(i, i ^ k) for i in range(owners)])  9.36 us
    ppermute x6, waiting for transfers between devices, exchange(): lax.ppermute(part, 'tp', [(i, i ^ k) for i in range(owners)])  3.77 us
    pallas_call x1, Pallas kernels, attend(): pl.pallas_call(functools.partial(attend_kernel, owners), out_shape=[part]...  2.34 us
    pallas_call x1, Pallas kernels, stage(): pl.pallas_call(stage_kernel, out_shape=jax.ShapeDtypeStruct(maps.shape, m...  2.2 us
    pallas_call x1, Pallas kernels, project(): pl.pallas_call(functools.partial(project_kernel, count), out_shape=[jax.S...  0.86 us
    pallas_call x1, Pallas kernels, assemble(): pl.pallas_call(functools.partial(assemble_kernel, owners), out_shape=pltp...  0.66 us
  transfers between devices with their start and end apart: 6, of which 4 were waited for; matrix products, arithmetic and copies ran while one was open for 0% of the time, Pallas kernels for 11%

profile of v15, /device:TPU:0, one launch (start us, length us, event | category | flops | bytes accessed | tf_op | source)
XLA Modules:
  0.0 19.2 jit_solution(10601539918424129898)
XLA Ops:
  0.0 2.3 %attend.1 = (bf16[64,512]{1,0:T(8,128)(2,1)S(1)}, bf16[64,512]{1,0:T(8,128)(2,1)S(1)}, bf16[64,512]{1,0:T(8,128)(2,1)S(1)}, bf16[64,512]{1,0:T(8,128)(2,1)S(1)}) custom-call(s32[2]{0:T(128)} %lengths_hbm.1, bf16[2,576,128]{2,1,0:T(8,128)(2,1)} %bitcast.8, f32[576]{0:T(1024)} %scales_hbm.1, bf16[2,576,1536]{2,1,0:T(8,128)(2,1)} %bitcast.7), custom_call_target="tpu_custom_call" | custom-call | flops 905969664 | bytes 3538944 | tf_op jit(solution)/shard_map/attend/pallas_call | solution.py:129
  2.3 4.4 %collective-permute-start = (bf16[64,512]{1,0:T(8,128)(2,1)S(1)}, bf16[64,512]{1,0:T(8,128)(2,1)S(1)}, u32[]{:S(2)}, u32[]{:S(2)}) collective-permute-start(bf16[64,512]{1,0:T(8,128)(2,1)S(1)} %get-tuple-element.14), channel_id=1, source_target_pairs={{0,3},{1,2},{2,1},{3,0},{4,7},{5,6},{6,5},{7,4},{8,11},{9,10},{10,... | collective-permute-start | bytes 196616 | tf_op jit(solution)/shard_map/ppermute | solution.py:240
  6.8 0.1 collective-permute-start.1
  6.8 1.3 %collective-permute-start.2 = (bf16[64,512]{1,0:T(8,128)(2,1)S(1)}, bf16[64,512]{1,0:T(8,128)(2,1)S(1)}, u32[]{:S(2)}, u32[]{:S(2)}) collective-permute-start(bf16[64,512]{1,0:T(8,128)(2,1)S(1)} %get-tuple-element.16), channel_id=1, source_target_pairs={{0,1},{1,0},{2,3},{3,2},{4,5},{5,4},{6,7},{7,6},{8,9},{9,8},{10,11... | collective-permute-start | bytes 196616 | tf_op jit(solution)/shard_map/ppermute | solution.py:240
  8.2 2.2 %stage.1.refs_4_ = bf16[32,512,128]{2,1,0:T(8,128)(2,1)S(1)} custom-call(bf16[32,512,128]{2,1,0:T(8,128)(2,1)} %maps_hbm.1, bf16[64,512]{1,0:T(8,128)(2,1)S(1)} %get-tuple-element.13.after.refs_0_), custom_call_target="tpu_custom_call" | custom-call | bytes 8388608 | tf_op jit(solution)/shard_map/stage/pallas_call | solution.py:160
  10.4 0.0 collective-permute-done.refs_1_
  10.4 0.6 %collective-permute-done.1.refs_2_ = bf16[64,512]{1,0:T(8,128)(2,1)S(1)} collective-permute-done((bf16[64,512]{1,0:T(8,128)(2,1)S(1)}, bf16[64,512]{1,0:T(8,128)(2,1)S(1)}, u32[]{:S(2)}, u32[]{:S(2)}) %collective-permute-start.1) | collective-permute-done | bytes 65568 | tf_op jit(solution)/shard_map/ppermute | solution.py:240
  11.0 0.2 %collective-permute-done.2.refs_3_ = bf16[64,512]{1,0:T(8,128)(2,1)S(1)} collective-permute-done((bf16[64,512]{1,0:T(8,128)(2,1)S(1)}, bf16[64,512]{1,0:T(8,128)(2,1)S(1)}, u32[]{:S(2)}, u32[]{:S(2)}) %collective-permute-start.2) | collective-permute-done | bytes 65568 | tf_op jit(solution)/shard_map/ppermute | solution.py:240
  11.2 0.9 %project.1 = (bf16[32,2,128]{2,1,0:T(2,128)(2,1)S(1)}, bf16[32,2,128]{2,1,0:T(2,128)(2,1)S(1)}, bf16[32,2,128]{2,1,0:T(2,128)(2,1)S(1)}, bf16[32,2,128]{2,1,0:T(2,128)(2,1)S(1)}) custom-call(bf16[64,512]{1,0:T(8,128)(2,1)S(1)} %get-tuple-element.13.after.refs_0_, bf16[64,512]{1,0:T(8,128)(2,1)S(1)} %collective-permute-done.refs_1_, ...), custom_call_target="tpu_custom_call" | custom-call | flops 33554432 | bytes 4194304 | tf_op jit(solution)/shard_map/project/pallas_call | solution.py:196
  12.1 2.7 %collective-permute-start.3 = (bf16[32,2,128]{2,1,0:T(2,128)(2,1)S(1)}, bf16[32,2,128]{2,1,0:T(2,128)(2,1)S(1)}, u32[]{:S(2)}, u32[]{:S(2)}) collective-permute-start(bf16[32,2,128]{2,1,0:T(2,128)(2,1)S(1)} %get-tuple-element.18), channel_id=1, source_target_pairs={{0,3},{1,2},{2,1},{3,0},{4,7},{5,6},{6,5},{7,4},{8,11},{9,10},{10,... | collective-permute-start | bytes 49160 | tf_op jit(solution)/shard_map/ppermute | solution.py:240
  14.8 0.0 collective-permute-start.4
  14.8 0.8 %collective-permute-start.5 = (bf16[32,2,128]{2,1,0:T(2,128)(2,1)S(1)}, bf16[32,2,128]{2,1,0:T(2,128)(2,1)S(1)}, u32[]{:S(2)}, u32[]{:S(2)}) collective-permute-start(bf16[32,2,128]{2,1,0:T(2,128)(2,1)S(1)} %get-tuple-element.20), channel_id=1, source_target_pairs={{0,1},{1,0},{2,3},{3,2},{4,5},{5,4},{6,7},{7,6},{8,9},{9,8},{10,11... | collective-permute-start | bytes 49160 | tf_op jit(solution)/shard_map/ppermute | solution.py:240
  15.6 1.1 %collective-permute-done.3.refs_1_ = bf16[32,2,128]{2,1,0:T(2,128)(2,1)S(1)} collective-permute-done((bf16[32,2,128]{2,1,0:T(2,128)(2,1)S(1)}, bf16[32,2,128]{2,1,0:T(2,128)(2,1)S(1)}, u32[]{:S(2)}, u32[]{:S(2)}) %collective-permute-start.3) | collective-permute-done | bytes 16416 | tf_op jit(solution)/shard_map/ppermute | solution.py:240
  16.8 1.8 %collective-permute-done.4.refs_2_ = bf16[32,2,128]{2,1,0:T(2,128)(2,1)S(1)} collective-permute-done((bf16[32,2,128]{2,1,0:T(2,128)(2,1)S(1)}, bf16[32,2,128]{2,1,0:T(2,128)(2,1)S(1)}, u32[]{:S(2)}, u32[]{:S(2)}) %collective-permute-start.4) | collective-permute-done | bytes 16416 | tf_op jit(solution)/shard_map/ppermute | solution.py:240
  18.5 0.0 collective-permute-done.5.refs_3_
  18.6 0.7 %assemble.1 = bf16[4,32,2,128]{3,2,1,0:T(2,128)(2,1)} custom-call(bf16[32,2,128]{2,1,0:T(2,128)(2,1)S(1)} %get-tuple-element.17.refs_0_, bf16[32,2,128]{2,1,0:T(2,128)(2,1)S(1)} %collective-permute-done.3.refs_1_, bf16[32,2,128]{2,1,0:T(2,128)(2,1)S(1)} %collective-permute-done.4.refs_2_, bf16[32,2,128]{2,1,0:T(2,128)(2,1)S(1)} %collective-permute-done.5.refs_3_), custom_call_target="tpu_custom_call" | custom-call | tf_op jit(solution)/shard_map/assemble/pallas_call | solution.py:226
Async XLA Ops:
  2.3 8.0 %collective-permute-start = (bf16[64,512]{1,0:T(8,128)(2,1)S(1)}, bf16[64,512]{1,0:T(8,128)(2,1)S(1)}, u32[]{:S(2)}, u32[]{:S(2)}) collective-permute-start(bf16[64,512]{1,0:T(8,128)(2,1)S(1)} %get-tuple-element.14), channel_id=1, source_target_pairs={{0,3},{1,2},{2,1},{3,0},{4,7},{5,6},{6,5},{7,4},{8,11},{9,10},{10,... | collective-permute-start | bytes 196616 | tf_op jit(solution)/shard_map/ppermute | solution.py:240
  6.8 4.3 %collective-permute-start.1 = (bf16[64,512]{1,0:T(8,128)(2,1)S(1)}, bf16[64,512]{1,0:T(8,128)(2,1)S(1)}, u32[]{:S(2)}, u32[]{:S(2)}) collective-permute-start(bf16[64,512]{1,0:T(8,128)(2,1)S(1)} %get-tuple-element.15), channel_id=1, source_target_pairs={{0,2},{1,3},{2,0},{3,1},{4,6},{5,7},{6,4},{7,5},{8,10},{9,11},{10,... | collective-permute-start | bytes 196616 | tf_op jit(solution)/shard_map/ppermute | solution.py:240
  6.8 4.4 %collective-permute-start.2 = (bf16[64,512]{1,0:T(8,128)(2,1)S(1)}, bf16[64,512]{1,0:T(8,128)(2,1)S(1)}, u32[]{:S(2)}, u32[]{:S(2)}) collective-permute-start(bf16[64,512]{1,0:T(8,128)(2,1)S(1)} %get-tuple-element.16), channel_id=1, source_target_pairs={{0,1},{1,0},{2,3},{3,2},{4,5},{5,4},{6,7},{7,6},{8,9},{9,8},{10,11... | collective-permute-start | bytes 196616 | tf_op jit(solution)/shard_map/ppermute | solution.py:240
  12.1 4.7 %collective-permute-start.3 = (bf16[32,2,128]{2,1,0:T(2,128)(2,1)S(1)}, bf16[32,2,128]{2,1,0:T(2,128)(2,1)S(1)}, u32[]{:S(2)}, u32[]{:S(2)}) collective-permute-start(bf16[32,2,128]{2,1,0:T(2,128)(2,1)S(1)} %get-tuple-element.18), channel_id=1, source_target_pairs={{0,3},{1,2},{2,1},{3,0},{4,7},{5,6},{6,5},{7,4},{8,11},{9,10},{10,... | collective-permute-start | bytes 49160 | tf_op jit(solution)/shard_map/ppermute | solution.py:240
  14.8 3.7 %collective-permute-start.4 = (bf16[32,2,128]{2,1,0:T(2,128)(2,1)S(1)}, bf16[32,2,128]{2,1,0:T(2,128)(2,1)S(1)}, u32[]{:S(2)}, u32[]{:S(2)}) collective-permute-start(bf16[32,2,128]{2,1,0:T(2,128)(2,1)S(1)} %get-tuple-element.19), channel_id=1, source_target_pairs={{0,2},{1,3},{2,0},{3,1},{4,6},{5,7},{6,4},{7,5},{8,10},{9,11},{10,... | collective-permute-start | bytes 49160 | tf_op jit(solution)/shard_map/ppermute | solution.py:240
  14.8 3.7 %collective-permute-start.5 = (bf16[32,2,128]{2,1,0:T(2,128)(2,1)S(1)}, bf16[32,2,128]{2,1,0:T(2,128)(2,1)S(1)}, u32[]{:S(2)}, u32[]{:S(2)}) collective-permute-start(bf16[32,2,128]{2,1,0:T(2,128)(2,1)S(1)} %get-tuple-element.20), channel_id=1, source_target_pairs={{0,1},{1,0},{2,3},{3,2},{4,5},{5,4},{6,7},{7,6},{8,9},{9,8},{10,11... | collective-permute-start | bytes 49160 | tf_op jit(solution)/shard_map/ppermute | solution.py:240

commit v16 on v15

--- a/solution.py
+++ b/solution.py
@@ -63,18 +63,19 @@
         fetch(r, b).wait()
         span = slice(b * block, (b + 1) * block)
         part = jnp.dot(scaled[r], keys[r, :, span], preferred_element_type=jnp.float32)
+        part = part.T
         if b == live - 1:
-            place = b * block + lax.broadcasted_iota(jnp.int32, part.shape, 1)
+            place = b * block + lax.broadcasted_iota(jnp.int32, part.shape, 0)
             part = jnp.where(place < lengths[r], part, -jnp.inf)
         return part
 
     def weigh(part, r, b):
-        top = jnp.max(part, axis=1, keepdims=True)
+        top = jnp.max(part, axis=0, keepdims=True)
         weight = jnp.exp2((part - top) * EXP2_SCALE)
-        total = jnp.sum(weight, axis=1, keepdims=True)
-        mixture = lax.dot_general(
-            weight.astype(jnp.bfloat16), keys[r, :rank, b * block:(b + 1) * block],
-            (((1,), (1,)), ((), ())), preferred_element_type=jnp.float32,
+        total = jnp.sum(weight, axis=0, keepdims=True)
+        mixture = jnp.dot(
+            keys[r, :rank, b * block:(b + 1) * block], weight.astype(jnp.bfloat16),
+            preferred_element_type=jnp.float32,
         )
         return top, total, mixture
 
@@ -85,7 +86,7 @@
         return (top,) + tuple(x * first + y * second for x, y in zip(one[1:], two[1:]))
 
     def finish(r, total, mixture):
-        latent = mixture * (1.0 / total) * scale_row[:, :rank]
+        latent = (mixture * (1.0 / total)).T * scale_row[:, :rank]
         for at in range(0, rank, LANES):
             latents[at // LANES, pl.ds(r, heads, stride=requests), :] = latent[:, at:at + LANES]
 

time: 19.6 us -> 20.7 us (1.056)
  Pallas kernels: 6.05 us -> 6.62 us
  starting transfers between devices: 9.36 us -> 9.89 us
    pallas_call x1, Pallas kernels: 2.34 us -> 2.91 us  [attend(): pl.pallas_call(functools.partial(attend_kernel, owners), out_shape=[part]...]
    ppermute x6, starting transfers between devices: 9.36 us -> 9.89 us  [exchange(): lax.ppermute(part, 'tp', [(i, i ^ k) for i in range(owners)])]
  transfers between devices with their start and end apart: 6 -> 6, of which waited for: 4 -> 3; matrix products, arithmetic and copies ran while one was open for 0% -> 0% of each run, Pallas kernels for 11% -> 11%
where the time goes in v16:
time: 20.7 us; the launch traced here: 20.5 us
  starting transfers between devices  9.89 us (48%)
  Pallas kernels  6.62 us (32%)
  waiting for transfers between devices  3.77 us (18%)
    ppermute x6, starting transfers between devices, exchange(): lax.ppermute(part, 'tp', [(i, i ^ k) for i in range(owners)])  9.89 us
    ppermute x6, waiting for transfers between devices, exchange(): lax.ppermute(part, 'tp', [(i, i ^ k) for i in range(owners)])  3.77 us
    pallas_call x1, Pallas kernels, attend(): pl.pallas_call(functools.partial(attend_kernel, owners), out_shape=[part]...  2.91 us
    pallas_call x1, Pallas kernels, stage(): pl.pallas_call(stage_kernel, out_shape=jax.ShapeDtypeStruct(maps.shape, m...  2.2 us
    pallas_call x1, Pallas kernels, project(): pl.pallas_call(functools.partial(project_kernel, count), out_shape=[jax.S...  0.86 us
    pallas_call x1, Pallas kernels, assemble(): pl.pallas_call(functools.partial(assemble_kernel, owners), out_shape=pltp...  0.66 us
  transfers between devices with their start and end apart: 6, of which 3 were waited for; matrix products, arithmetic and copies ran while one was open for 0% of the time, Pallas kernels for 11%

profile of v16, /device:TPU:0, one launch (start us, length us, event | category | flops | bytes accessed | tf_op | source)
XLA Modules:
  0.0 20.5 jit_solution(4204468890317490481)
XLA Ops:
  0.0 2.9 %attend.1 = (bf16[64,512]{1,0:T(8,128)(2,1)S(1)}, bf16[64,512]{1,0:T(8,128)(2,1)S(1)}, bf16[64,512]{1,0:T(8,128)(2,1)S(1)}, bf16[64,512]{1,0:T(8,128)(2,1)S(1)}) custom-call(s32[2]{0:T(128)} %lengths_hbm.1, bf16[2,576,128]{2,1,0:T(8,128)(2,1)} %bitcast.8, f32[576]{0:T(1024)} %scales_hbm.1, bf16[2,576,1536]{2,1,0:T(8,128)(2,1)} %bitcast.7), custom_call_target="tpu_custom_call" | custom-call | flops 905969664 | bytes 3538944 | tf_op jit(solution)/shard_map/attend/pallas_call | solution.py:130
  2.9 4.0 %collective-permute-start = (bf16[64,512]{1,0:T(8,128)(2,1)S(1)}, bf16[64,512]{1,0:T(8,128)(2,1)S(1)}, u32[]{:S(2)}, u32[]{:S(2)}) collective-permute-start(bf16[64,512]{1,0:T(8,128)(2,1)S(1)} %get-tuple-element.14), channel_id=1, source_target_pairs={{0,3},{1,2},{2,1},{3,0},{4,7},{5,6},{6,5},{7,4},{8,11},{9,10},{10,... | collective-permute-start | bytes 196616 | tf_op jit(solution)/shard_map/ppermute | solution.py:241
  6.9 2.4 %collective-permute-start.1 = (bf16[64,512]{1,0:T(8,128)(2,1)S(1)}, bf16[64,512]{1,0:T(8,128)(2,1)S(1)}, u32[]{:S(2)}, u32[]{:S(2)}) collective-permute-start(bf16[64,512]{1,0:T(8,128)(2,1)S(1)} %get-tuple-element.15), channel_id=1, source_target_pairs={{0,2},{1,3},{2,0},{3,1},{4,6},{5,7},{6,4},{7,5},{8,10},{9,11},{10,... | collective-permute-start | bytes 196616 | tf_op jit(solution)/shard_map/ppermute | solution.py:241
  9.2 0.0 collective-permute-start.2
  9.3 2.2 %stage.1.refs_4_ = bf16[32,512,128]{2,1,0:T(8,128)(2,1)S(1)} custom-call(bf16[32,512,128]{2,1,0:T(8,128)(2,1)} %maps_hbm.1, bf16[64,512]{1,0:T(8,128)(2,1)S(1)} %get-tuple-element.13.after.refs_0_), custom_call_target="tpu_custom_call" | custom-call | bytes 8388608 | tf_op jit(solution)/shard_map/stage/pallas_call | solution.py:161
  11.5 0.0 collective-permute-done.refs_1_
  11.5 0.0 collective-permute-done.1.refs_2_
  11.5 2.0 %collective-permute-done.2.refs_3_ = bf16[64,512]{1,0:T(8,128)(2,1)S(1)} collective-permute-done((bf16[64,512]{1,0:T(8,128)(2,1)S(1)}, bf16[64,512]{1,0:T(8,128)(2,1)S(1)}, u32[]{:S(2)}, u32[]{:S(2)}) %collective-permute-start.2) | collective-permute-done | bytes 65568 | tf_op jit(solution)/shard_map/ppermute | solution.py:241
  13.5 0.9 %project.1 = (bf16[32,2,128]{2,1,0:T(2,128)(2,1)S(1)}, bf16[32,2,128]{2,1,0:T(2,128)(2,1)S(1)}, bf16[32,2,128]{2,1,0:T(2,128)(2,1)S(1)}, bf16[32,2,128]{2,1,0:T(2,128)(2,1)S(1)}) custom-call(bf16[64,512]{1,0:T(8,128)(2,1)S(1)} %get-tuple-element.13.after.refs_0_, bf16[64,512]{1,0:T(8,128)(2,1)S(1)} %collective-permute-done.refs_1_, ...), custom_call_target="tpu_custom_call" | custom-call | flops 33554432 | bytes 4194304 | tf_op jit(solution)/shard_map/project/pallas_call | solution.py:197
  14.4 0.2 %collective-permute-start.3 = (bf16[32,2,128]{2,1,0:T(2,128)(2,1)S(1)}, bf16[32,2,128]{2,1,0:T(2,128)(2,1)S(1)}, u32[]{:S(2)}, u32[]{:S(2)}) collective-permute-start(bf16[32,2,128]{2,1,0:T(2,128)(2,1)S(1)} %get-tuple-element.18), channel_id=1, source_target_pairs={{0,3},{1,2},{2,1},{3,0},{4,7},{5,6},{6,5},{7,4},{8,11},{9,10},{10,... | collective-permute-start | bytes 49160 | tf_op jit(solution)/shard_map/ppermute | solution.py:241
  14.6 1.3 %collective-permute-start.4 = (bf16[32,2,128]{2,1,0:T(2,128)(2,1)S(1)}, bf16[32,2,128]{2,1,0:T(2,128)(2,1)S(1)}, u32[]{:S(2)}, u32[]{:S(2)}) collective-permute-start(bf16[32,2,128]{2,1,0:T(2,128)(2,1)S(1)} %get-tuple-element.19), channel_id=1, source_target_pairs={{0,2},{1,3},{2,0},{3,1},{4,6},{5,7},{6,4},{7,5},{8,10},{9,11},{10,... | collective-permute-start | bytes 49160 | tf_op jit(solution)/shard_map/ppermute | solution.py:241
  15.9 2.0 %collective-permute-start.5 = (bf16[32,2,128]{2,1,0:T(2,128)(2,1)S(1)}, bf16[32,2,128]{2,1,0:T(2,128)(2,1)S(1)}, u32[]{:S(2)}, u32[]{:S(2)}) collective-permute-start(bf16[32,2,128]{2,1,0:T(2,128)(2,1)S(1)} %get-tuple-element.20), channel_id=1, source_target_pairs={{0,1},{1,0},{2,3},{3,2},{4,5},{5,4},{6,7},{7,6},{8,9},{9,8},{10,11... | collective-permute-start | bytes 49160 | tf_op jit(solution)/shard_map/ppermute | solution.py:241
  17.9 1.1 %collective-permute-done.3.refs_1_ = bf16[32,2,128]{2,1,0:T(2,128)(2,1)S(1)} collective-permute-done((bf16[32,2,128]{2,1,0:T(2,128)(2,1)S(1)}, bf16[32,2,128]{2,1,0:T(2,128)(2,1)S(1)}, u32[]{:S(2)}, u32[]{:S(2)}) %collective-permute-start.3) | collective-permute-done | bytes 16416 | tf_op jit(solution)/shard_map/ppermute | solution.py:241
  19.1 0.0 collective-permute-done.4.refs_2_
  19.1 0.6 %collective-permute-done.5.refs_3_ = bf16[32,2,128]{2,1,0:T(2,128)(2,1)S(1)} collective-permute-done((bf16[32,2,128]{2,1,0:T(2,128)(2,1)S(1)}, bf16[32,2,128]{2,1,0:T(2,128)(2,1)S(1)}, u32[]{:S(2)}, u32[]{:S(2)}) %collective-permute-start.5) | collective-permute-done | bytes 16416 | tf_op jit(solution)/shard_map/ppermute | solution.py:241
  19.6 0.7 %assemble.1 = bf16[4,32,2,128]{3,2,1,0:T(2,128)(2,1)} custom-call(bf16[32,2,128]{2,1,0:T(2,128)(2,1)S(1)} %get-tuple-element.17.refs_0_, bf16[32,2,128]{2,1,0:T(2,128)(2,1)S(1)} %collective-permute-done.3.refs_1_, bf16[32,2,128]{2,1,0:T(2,128)(2,1)S(1)} %collective-permute-done.4.refs_2_, bf16[32,2,128]{2,1,0:T(2,128)(2,1)S(1)} %collective-permute-done.5.refs_3_), custom_call_target="tpu_custom_call" | custom-call | tf_op jit(solution)/shard_map/assemble/pallas_call | solution.py:227
Async XLA Ops:
  2.9 8.5 %collective-permute-start = (bf16[64,512]{1,0:T(8,128)(2,1)S(1)}, bf16[64,512]{1,0:T(8,128)(2,1)S(1)}, u32[]{:S(2)}, u32[]{:S(2)}) collective-permute-start(bf16[64,512]{1,0:T(8,128)(2,1)S(1)} %get-tuple-element.14), channel_id=1, source_target_pairs={{0,3},{1,2},{2,1},{3,0},{4,7},{5,6},{6,5},{7,4},{8,11},{9,10},{10,... | collective-permute-start | bytes 196616 | tf_op jit(solution)/shard_map/ppermute | solution.py:241
  6.9 4.6 %collective-permute-start.1 = (bf16[64,512]{1,0:T(8,128)(2,1)S(1)}, bf16[64,512]{1,0:T(8,128)(2,1)S(1)}, u32[]{:S(2)}, u32[]{:S(2)}) collective-permute-start(bf16[64,512]{1,0:T(8,128)(2,1)S(1)} %get-tuple-element.15), channel_id=1, source_target_pairs={{0,2},{1,3},{2,0},{3,1},{4,6},{5,7},{6,4},{7,5},{8,10},{9,11},{10,... | collective-permute-start | bytes 196616 | tf_op jit(solution)/shard_map/ppermute | solution.py:241
  9.2 4.3 %collective-permute-start.2 = (bf16[64,512]{1,0:T(8,128)(2,1)S(1)}, bf16[64,512]{1,0:T(8,128)(2,1)S(1)}, u32[]{:S(2)}, u32[]{:S(2)}) collective-permute-start(bf16[64,512]{1,0:T(8,128)(2,1)S(1)} %get-tuple-element.16), channel_id=1, source_target_pairs={{0,1},{1,0},{2,3},{3,2},{4,5},{5,4},{6,7},{7,6},{8,9},{9,8},{10,11... | collective-permute-start | bytes 196616 | tf_op jit(solution)/shard_map/ppermute | solution.py:241
  14.4 4.7 %collective-permute-start.3 = (bf16[32,2,128]{2,1,0:T(2,128)(2,1)S(1)}, bf16[32,2,128]{2,1,0:T(2,128)(2,1)S(1)}, u32[]{:S(2)}, u32[]{:S(2)}) collective-permute-start(bf16[32,2,128]{2,1,0:T(2,128)(2,1)S(1)} %get-tuple-element.18), channel_id=1, source_target_pairs={{0,3},{1,2},{2,1},{3,0},{4,7},{5,6},{6,5},{7,4},{8,11},{9,10},{10,... | collective-permute-start | bytes 49160 | tf_op jit(solution)/shard_map/ppermute | solution.py:241
  14.6 4.5 %collective-permute-start.4 = (bf16[32,2,128]{2,1,0:T(2,128)(2,1)S(1)}, bf16[32,2,128]{2,1,0:T(2,128)(2,1)S(1)}, u32[]{:S(2)}, u32[]{:S(2)}) collective-permute-start(bf16[32,2,128]{2,1,0:T(2,128)(2,1)S(1)} %get-tuple-element.19), channel_id=1, source_target_pairs={{0,2},{1,3},{2,0},{3,1},{4,6},{5,7},{6,4},{7,5},{8,10},{9,11},{10,... | collective-permute-start | bytes 49160 | tf_op jit(solution)/shard_map/ppermute | solution.py:241
  15.9 3.7 %collective-permute-start.5 = (bf16[32,2,128]{2,1,0:T(2,128)(2,1)S(1)}, bf16[32,2,128]{2,1,0:T(2,128)(2,1)S(1)}, u32[]{:S(2)}, u32[]{:S(2)}) collective-permute-start(bf16[32,2,128]{2,1,0:T(2,128)(2,1)S(1)} %get-tuple-element.20), channel_id=1, source_target_pairs={{0,1},{1,0},{2,3},{3,2},{4,5},{5,4},{6,7},{7,6},{8,9},{9,8},{10,11... | collective-permute-start | bytes 49160 | tf_op jit(solution)/shard_map/ppermute | solution.py:241

commit v17 on v15

--- a/solution.py
+++ b/solution.py
@@ -1,5 +1,4 @@
 import functools
-import itertools
 import math
 
 import jax
@@ -22,7 +21,8 @@
 
 
 def attend_kernel(owners, lengths_hbm, query_hbm, scales_hbm, cache, *refs):
-    outs, (latents, lengths, query, scales, keys, sems, small_sems) = refs[:owners], refs[owners:]
+    outs, refs = refs[:owners], refs[owners:]
+    latents, lengths, query, scales, keys, scaled, tops, totals, mixtures, sems, small_sems = refs
     requests, channels, heads = query.shape
     rows, rank = outs[0].shape
     cache_len = cache.shape[2]
@@ -53,63 +53,49 @@
     scales_copy.wait()
     scale_row = scales[...].reshape(1, channels)
 
-    def scale(r):
+    count = [(lengths[r] + (block - 1)) // block for r in range(requests)]
+
+    @pl.loop(0, requests)
+    def _(r):
         ask(r).wait()
-        return (query[r].astype(jnp.float32).T * scale_row).astype(jnp.bfloat16)
-
-    def score(scaled, r, b, live):
-        if r not in scaled:
-            scaled[r] = scale(r)
+        scaled[r] = (query[r].astype(jnp.float32).T * scale_row).astype(jnp.bfloat16)
+        tops[r] = jnp.full(tops.shape[1:], -jnp.inf, jnp.float32)
+        totals[r] = jnp.zeros(totals.shape[1:], jnp.float32)
+        mixtures[r] = jnp.zeros(mixtures.shape[1:], jnp.float32)
+
+    def step(r, b):
         fetch(r, b).wait()
-        span = slice(b * block, (b + 1) * block)
+        span = pl.ds(pl.multiple_of(b * block, block), block)
         part = jnp.dot(scaled[r], keys[r, :, span], preferred_element_type=jnp.float32)
-        if b == live - 1:
-            place = b * block + lax.broadcasted_iota(jnp.int32, part.shape, 1)
-            part = jnp.where(place < lengths[r], part, -jnp.inf)
-        return part
-
-    def weigh(part, r, b):
-        top = jnp.max(part, axis=1, keepdims=True)
-        weight = jnp.exp2((part - top) * EXP2_SCALE)
-        total = jnp.sum(weight, axis=1, keepdims=True)
-        mixture = lax.dot_general(
-            weight.astype(jnp.bfloat16), keys[r, :rank, b * block:(b + 1) * block],
+        place = b * block + lax.broadcasted_iota(jnp.int32, part.shape, 1)
+        part = jnp.where(place < lengths[r], part, -jnp.inf)
+        before = tops[r]
+        top = jnp.maximum(before, jnp.max(part, axis=1, keepdims=True))
+        fade = jnp.exp2((before - top) * EXP2_SCALE)
+        weight = jnp.exp2((part - top[:, :1]) * EXP2_SCALE)
+        tops[r] = top
+        totals[r] = totals[r] * fade + jnp.sum(weight, axis=1, keepdims=True)
+        mixtures[r] = mixtures[r] * fade[:, :1] + lax.dot_general(
+            weight.astype(jnp.bfloat16), keys[r, :rank, span],
             (((1,), (1,)), ((), ())), preferred_element_type=jnp.float32,
         )
-        return top, total, mixture
-
-    def merge(one, two):
-        top = jnp.maximum(one[0], two[0])
-        first = jnp.exp2((one[0] - top) * EXP2_SCALE)
-        second = jnp.exp2((two[0] - top) * EXP2_SCALE)
-        return (top,) + tuple(x * first + y * second for x, y in zip(one[1:], two[1:]))
-
-    def finish(r, total, mixture):
-        latent = mixture * (1.0 / total) * scale_row[:, :rank]
+
+    for first in range(0, requests, 2):
+        pair = [first, min(first + 1, requests - 1)]
+        extra = count[pair[0]] - 1
+
+        @pl.loop(0, count[pair[0]] + count[pair[1]])
+        def _(u):
+            late = (u - 2 >= extra).astype(jnp.int32)
+            r = jnp.where(u < 2, u, late)
+            b = jnp.where(u < 2, 0, u - 1 - late * extra)
+            step(first + r, b)
+
+    @pl.loop(0, requests)
+    def _(r):
+        latent = mixtures[r] * (1.0 / totals[r][:, :1]) * scale_row[:, :rank]
         for at in range(0, rank, LANES):
             latents[at // LANES, pl.ds(r, heads, stride=requests), :] = latent[:, at:at + LANES]
-
-    def several(group, live):
-        scaled = {}
-        units = [(r, 0, n) for r, n in zip(group, live)]
-        units += [(r, b, n) for r, n in zip(group, live) for b in range(1, n)]
-        part = score(scaled, *units[0])
-        state = {}
-        for i, (r, b, n) in enumerate(units):
-            ahead = score(scaled, *units[i + 1]) if i + 1 < len(units) else None
-            done = weigh(part, r, b)
-            state[r] = merge(state[r], done) if b else done
-            if b == n - 1:
-                finish(r, *state[r][1:])
-            part = ahead
-
-    for first in range(0, requests, 2):
-        group = tuple(range(first, min(first + 2, requests)))
-        count = [(lengths[r] + (block - 1)) // block for r in group]
-        for live in itertools.product(range(1, blocks + 1), repeat=len(group)):
-            @pl.when(functools.reduce(jnp.logical_and, [c == n for c, n in zip(count, live)]))
-            def _():
-                several(group, live)
 
     for out, k in zip(outs, order(owners)):
         mine = pl.ds(pl.multiple_of((me ^ k) * rows, rows), rows)
@@ -137,6 +123,10 @@
             pltpu.VMEM((requests, channels, heads), jnp.bfloat16),
             pltpu.VMEM((channels,), jnp.float32),
             pltpu.VMEM((requests, channels, cache_len), jnp.bfloat16),
+            pltpu.VMEM((requests, heads, channels), jnp.bfloat16),
+            pltpu.VMEM((requests, heads, LANES), jnp.float32),
+            pltpu.VMEM((requests, heads, LANES), jnp.float32),
+            pltpu.VMEM((requests, heads, rank), jnp.float32),
             pltpu.SemaphoreType.DMA((requests, cache_len // min(BLOCK, cache_len))),
             pltpu.SemaphoreType.DMA((2 + requests,)),
         ],

time: 19.6 us -> 20.5 us (1.046)
  Pallas kernels: 6.05 us -> 7.38 us
  starting transfers between devices: 9.36 us -> 8.84 us
  waiting for transfers between devices: 3.77 us -> 4.03 us
    pallas_call x1, Pallas kernels: 2.34 us -> 3.67 us  [attend(): pl.pallas_call(functools.partial(attend_kernel, owners), out_shape=[part]...]
    ppermute x6, starting transfers between devices: 9.36 us -> 8.84 us  [exchange(): lax.ppermute(part, 'tp', [(i, i ^ k) for i in range(owners)])]
    ppermute x6, waiting for transfers between devices: 3.77 us -> 4.03 us  [exchange(): lax.ppermute(part, 'tp', [(i, i ^ k) for i in range(owners)])]
where the time goes in v17:
time: 20.5 us; the launch traced here: 20.3 us
  starting transfers between devices  8.84 us (43%)
  Pallas kernels  7.38 us (36%)
  waiting for transfers between devices  4.03 us (20%)
    ppermute x6, starting transfers between devices, exchange(): lax.ppermute(part, 'tp', [(i, i ^ k) for i in range(owners)])  8.84 us
    ppermute x6, waiting for transfers between devices, exchange(): lax.ppermute(part, 'tp', [(i, i ^ k) for i in range(owners)])  4.03 us
    pallas_call x1, Pallas kernels, attend(): pl.pallas_call(functools.partial(attend_kernel, owners), out_shape=[part]...  3.67 us
    pallas_call x1, Pallas kernels, stage(): pl.pallas_call(stage_kernel, out_shape=jax.ShapeDtypeStruct(maps.shape, m...  2.2 us
    pallas_call x1, Pallas kernels, project(): pl.pallas_call(functools.partial(project_kernel, count), out_shape=[jax.S...  0.86 us
    pallas_call x1, Pallas kernels, assemble(): pl.pallas_call(functools.partial(assemble_kernel, owners), out_shape=pltp...  0.66 us
  transfers between devices with their start and end apart: 6, of which 4 were waited for; matrix products, arithmetic and copies ran while one was open for 0% of the time, Pallas kernels for 11%

profile of v17, /device:TPU:0, one launch (start us, length us, event | category | flops | bytes accessed | tf_op | source)
XLA Modules:
  0.0 20.3 jit_solution(3953188696609024824)
XLA Ops:
  0.0 3.7 %attend.1 = (bf16[64,512]{1,0:T(8,128)(2,1)S(1)}, bf16[64,512]{1,0:T(8,128)(2,1)S(1)}, bf16[64,512]{1,0:T(8,128)(2,1)S(1)}, bf16[64,512]{1,0:T(8,128)(2,1)S(1)}) custom-call(s32[2]{0:T(128)} %lengths_hbm.1, bf16[2,576,128]{2,1,0:T(8,128)(2,1)} %bitcast.8, f32[576]{0:T(1024)} %scales_hbm.1, bf16[2,576,1536]{2,1,0:T(8,128)(2,1)} %bitcast.7), custom_call_target="tpu_custom_call" | custom-call | flops 905969664 | bytes 3538944 | tf_op jit(solution)/shard_map/attend/pallas_call | solution.py:115
  3.7 4.6 %collective-permute-start = (bf16[64,512]{1,0:T(8,128)(2,1)S(1)}, bf16[64,512]{1,0:T(8,128)(2,1)S(1)}, u32[]{:S(2)}, u32[]{:S(2)}) collective-permute-start(bf16[64,512]{1,0:T(8,128)(2,1)S(1)} %get-tuple-element.14), channel_id=1, source_target_pairs={{0,3},{1,2},{2,1},{3,0},{4,7},{5,6},{6,5},{7,4},{8,11},{9,10},{10,... | collective-permute-start | bytes 196616 | tf_op jit(solution)/shard_map/ppermute | solution.py:230
  8.3 0.0 collective-permute-start.1
  8.3 0.6 %collective-permute-start.2 = (bf16[64,512]{1,0:T(8,128)(2,1)S(1)}, bf16[64,512]{1,0:T(8,128)(2,1)S(1)}, u32[]{:S(2)}, u32[]{:S(2)}) collective-permute-start(bf16[64,512]{1,0:T(8,128)(2,1)S(1)} %get-tuple-element.16), channel_id=1, source_target_pairs={{0,1},{1,0},{2,3},{3,2},{4,5},{5,4},{6,7},{7,6},{8,9},{9,8},{10,11... | collective-permute-start | bytes 196616 | tf_op jit(solution)/shard_map/ppermute | solution.py:230
  9.0 2.2 %stage.1.refs_4_ = bf16[32,512,128]{2,1,0:T(8,128)(2,1)S(1)} custom-call(bf16[32,512,128]{2,1,0:T(8,128)(2,1)} %maps_hbm.1, bf16[64,512]{1,0:T(8,128)(2,1)S(1)} %get-tuple-element.13.after.refs_0_), custom_call_target="tpu_custom_call" | custom-call | bytes 8388608 | tf_op jit(solution)/shard_map/stage/pallas_call | solution.py:150
  11.2 0.0 collective-permute-done.refs_1_
  11.2 1.4 %collective-permute-done.1.refs_2_ = bf16[64,512]{1,0:T(8,128)(2,1)S(1)} collective-permute-done((bf16[64,512]{1,0:T(8,128)(2,1)S(1)}, bf16[64,512]{1,0:T(8,128)(2,1)S(1)}, u32[]{:S(2)}, u32[]{:S(2)}) %collective-permute-start.1) | collective-permute-done | bytes 65568 | tf_op jit(solution)/shard_map/ppermute | solution.py:230
  12.6 0.0 collective-permute-done.2.refs_3_
  12.6 0.9 %project.1 = (bf16[32,2,128]{2,1,0:T(2,128)(2,1)S(1)}, bf16[32,2,128]{2,1,0:T(2,128)(2,1)S(1)}, bf16[32,2,128]{2,1,0:T(2,128)(2,1)S(1)}, bf16[32,2,128]{2,1,0:T(2,128)(2,1)S(1)}) custom-call(bf16[64,512]{1,0:T(8,128)(2,1)S(1)} %get-tuple-element.13.after.refs_0_, bf16[64,512]{1,0:T(8,128)(2,1)S(1)} %collective-permute-done.refs_1_, ...), custom_call_target="tpu_custom_call" | custom-call | flops 33554432 | bytes 4194304 | tf_op jit(solution)/shard_map/project/pallas_call | solution.py:186
  13.4 1.5 %collective-permute-start.3 = (bf16[32,2,128]{2,1,0:T(2,128)(2,1)S(1)}, bf16[32,2,128]{2,1,0:T(2,128)(2,1)S(1)}, u32[]{:S(2)}, u32[]{:S(2)}) collective-permute-start(bf16[32,2,128]{2,1,0:T(2,128)(2,1)S(1)} %get-tuple-element.18), channel_id=1, source_target_pairs={{0,3},{1,2},{2,1},{3,0},{4,7},{5,6},{6,5},{7,4},{8,11},{9,10},{10,... | collective-permute-start | bytes 49160 | tf_op jit(solution)/shard_map/ppermute | solution.py:230
  15.0 0.9 %collective-permute-start.4 = (bf16[32,2,128]{2,1,0:T(2,128)(2,1)S(1)}, bf16[32,2,128]{2,1,0:T(2,128)(2,1)S(1)}, u32[]{:S(2)}, u32[]{:S(2)}) collective-permute-start(bf16[32,2,128]{2,1,0:T(2,128)(2,1)S(1)} %get-tuple-element.19), channel_id=1, source_target_pairs={{0,2},{1,3},{2,0},{3,1},{4,6},{5,7},{6,4},{7,5},{8,10},{9,11},{10,... | collective-permute-start | bytes 49160 | tf_op jit(solution)/shard_map/ppermute | solution.py:230
  15.9 1.1 %collective-permute-start.5 = (bf16[32,2,128]{2,1,0:T(2,128)(2,1)S(1)}, bf16[32,2,128]{2,1,0:T(2,128)(2,1)S(1)}, u32[]{:S(2)}, u32[]{:S(2)}) collective-permute-start(bf16[32,2,128]{2,1,0:T(2,128)(2,1)S(1)} %get-tuple-element.20), channel_id=1, source_target_pairs={{0,1},{1,0},{2,3},{3,2},{4,5},{5,4},{6,7},{7,6},{8,9},{9,8},{10,11... | collective-permute-start | bytes 49160 | tf_op jit(solution)/shard_map/ppermute | solution.py:230
  17.0 1.1 %collective-permute-done.3.refs_1_ = bf16[32,2,128]{2,1,0:T(2,128)(2,1)S(1)} collective-permute-done((bf16[32,2,128]{2,1,0:T(2,128)(2,1)S(1)}, bf16[32,2,128]{2,1,0:T(2,128)(2,1)S(1)}, u32[]{:S(2)}, u32[]{:S(2)}) %collective-permute-start.3) | collective-permute-done | bytes 16416 | tf_op jit(solution)/shard_map/ppermute | solution.py:230
  18.2 0.6 %collective-permute-done.4.refs_2_ = bf16[32,2,128]{2,1,0:T(2,128)(2,1)S(1)} collective-permute-done((bf16[32,2,128]{2,1,0:T(2,128)(2,1)S(1)}, bf16[32,2,128]{2,1,0:T(2,128)(2,1)S(1)}, u32[]{:S(2)}, u32[]{:S(2)}) %collective-permute-start.4) | collective-permute-done | bytes 16416 | tf_op jit(solution)/shard_map/ppermute | solution.py:230
  18.7 0.9 %collective-permute-done.5.refs_3_ = bf16[32,2,128]{2,1,0:T(2,128)(2,1)S(1)} collective-permute-done((bf16[32,2,128]{2,1,0:T(2,128)(2,1)S(1)}, bf16[32,2,128]{2,1,0:T(2,128)(2,1)S(1)}, u32[]{:S(2)}, u32[]{:S(2)}) %collective-permute-start.5) | collective-permute-done | bytes 16416 | tf_op jit(solution)/shard_map/ppermute | solution.py:230
  19.6 0.7 %assemble.1 = bf16[4,32,2,128]{3,2,1,0:T(2,128)(2,1)} custom-call(bf16[32,2,128]{2,1,0:T(2,128)(2,1)S(1)} %get-tuple-element.17.refs_0_, bf16[32,2,128]{2,1,0:T(2,128)(2,1)S(1)} %collective-permute-done.3.refs_1_, bf16[32,2,128]{2,1,0:T(2,128)(2,1)S(1)} %collective-permute-done.4.refs_2_, bf16[32,2,128]{2,1,0:T(2,128)(2,1)S(1)} %collective-permute-done.5.refs_3_), custom_call_target="tpu_custom_call" | custom-call | tf_op jit(solution)/shard_map/assemble/pallas_call | solution.py:216
Async XLA Ops:
  3.7 7.5 %collective-permute-start = (bf16[64,512]{1,0:T(8,128)(2,1)S(1)}, bf16[64,512]{1,0:T(8,128)(2,1)S(1)}, u32[]{:S(2)}, u32[]{:S(2)}) collective-permute-start(bf16[64,512]{1,0:T(8,128)(2,1)S(1)} %get-tuple-element.14), channel_id=1, source_target_pairs={{0,3},{1,2},{2,1},{3,0},{4,7},{5,6},{6,5},{7,4},{8,11},{9,10},{10,... | collective-permute-start | bytes 196616 | tf_op jit(solution)/shard_map/ppermute | solution.py:230
  8.3 4.3 %collective-permute-start.1 = (bf16[64,512]{1,0:T(8,128)(2,1)S(1)}, bf16[64,512]{1,0:T(8,128)(2,1)S(1)}, u32[]{:S(2)}, u32[]{:S(2)}) collective-permute-start(bf16[64,512]{1,0:T(8,128)(2,1)S(1)} %get-tuple-element.15), channel_id=1, source_target_pairs={{0,2},{1,3},{2,0},{3,1},{4,6},{5,7},{6,4},{7,5},{8,10},{9,11},{10,... | collective-permute-start | bytes 196616 | tf_op jit(solution)/shard_map/ppermute | solution.py:230
  8.3 4.3 %collective-permute-start.2 = (bf16[64,512]{1,0:T(8,128)(2,1)S(1)}, bf16[64,512]{1,0:T(8,128)(2,1)S(1)}, u32[]{:S(2)}, u32[]{:S(2)}) collective-permute-start(bf16[64,512]{1,0:T(8,128)(2,1)S(1)} %get-tuple-element.16), channel_id=1, source_target_pairs={{0,1},{1,0},{2,3},{3,2},{4,5},{5,4},{6,7},{7,6},{8,9},{9,8},{10,11... | collective-permute-start | bytes 196616 | tf_op jit(solution)/shard_map/ppermute | solution.py:230
  13.4 4.7 %collective-permute-start.3 = (bf16[32,2,128]{2,1,0:T(2,128)(2,1)S(1)}, bf16[32,2,128]{2,1,0:T(2,128)(2,1)S(1)}, u32[]{:S(2)}, u32[]{:S(2)}) collective-permute-start(bf16[32,2,128]{2,1,0:T(2,128)(2,1)S(1)} %get-tuple-element.18), channel_id=1, source_target_pairs={{0,3},{1,2},{2,1},{3,0},{4,7},{5,6},{6,5},{7,4},{8,11},{9,10},{10,... | collective-permute-start | bytes 49160 | tf_op jit(solution)/shard_map/ppermute | solution.py:230
  15.0 3.7 %collective-permute-start.4 = (bf16[32,2,128]{2,1,0:T(2,128)(2,1)S(1)}, bf16[32,2,128]{2,1,0:T(2,128)(2,1)S(1)}, u32[]{:S(2)}, u32[]{:S(2)}) collective-permute-start(bf16[32,2,128]{2,1,0:T(2,128)(2,1)S(1)} %get-tuple-element.19), channel_id=1, source_target_pairs={{0,2},{1,3},{2,0},{3,1},{4,6},{5,7},{6,4},{7,5},{8,10},{9,11},{10,... | collective-permute-start | bytes 49160 | tf_op jit(solution)/shard_map/ppermute | solution.py:230
  15.9 3.7 %collective-permute-start.5 = (bf16[32,2,128]{2,1,0:T(2,128)(2,1)S(1)}, bf16[32,2,128]{2,1,0:T(2,128)(2,1)S(1)}, u32[]{:S(2)}, u32[]{:S(2)}) collective-permute-start(bf16[32,2,128]{2,1,0:T(2,128)(2,1)S(1)} %get-tuple-element.20), channel_id=1, source_target_pairs={{0,1},{1,0},{2,3},{3,2},{4,5},{5,4},{6,7},{7,6},{8,9},{9,8},{10,11... | collective-permute-start | bytes 49160 | tf_op jit(solution)/shard_map/ppermute | solution.py:230

commit v18 on v15

--- a/solution.py
+++ b/solution.py
@@ -68,21 +68,19 @@
             part = jnp.where(place < lengths[r], part, -jnp.inf)
         return part
 
-    def weigh(part, r, b):
-        top = jnp.max(part, axis=1, keepdims=True)
-        weight = jnp.exp2((part - top) * EXP2_SCALE)
-        total = jnp.sum(weight, axis=1, keepdims=True)
-        mixture = lax.dot_general(
-            weight.astype(jnp.bfloat16), keys[r, :rank, b * block:(b + 1) * block],
+    def weigh(parts):
+        top = functools.reduce(
+            jnp.maximum, [jnp.max(part, axis=1, keepdims=True) for part in parts]
+        )
+        weights = [jnp.exp2((part - top) * EXP2_SCALE) for part in parts]
+        total = sum(jnp.sum(weight, axis=1, keepdims=True) for weight in weights)
+        return total, jnp.concatenate([weight.astype(jnp.bfloat16) for weight in weights], axis=1)
+
+    def mix(weights, r):
+        return lax.dot_general(
+            weights, keys[r, :rank, :weights.shape[1]],
             (((1,), (1,)), ((), ())), preferred_element_type=jnp.float32,
         )
-        return top, total, mixture
-
-    def merge(one, two):
-        top = jnp.maximum(one[0], two[0])
-        first = jnp.exp2((one[0] - top) * EXP2_SCALE)
-        second = jnp.exp2((two[0] - top) * EXP2_SCALE)
-        return (top,) + tuple(x * first + y * second for x, y in zip(one[1:], two[1:]))
 
     def finish(r, total, mixture):
         latent = mixture * (1.0 / total) * scale_row[:, :rank]
@@ -93,15 +91,12 @@
         scaled = {}
         units = [(r, 0, n) for r, n in zip(group, live)]
         units += [(r, b, n) for r, n in zip(group, live) for b in range(1, n)]
-        part = score(scaled, *units[0])
-        state = {}
-        for i, (r, b, n) in enumerate(units):
-            ahead = score(scaled, *units[i + 1]) if i + 1 < len(units) else None
-            done = weigh(part, r, b)
-            state[r] = merge(state[r], done) if b else done
-            if b == n - 1:
-                finish(r, *state[r][1:])
-            part = ahead
+        parts = {r: [] for r in group}
+        for r, b, n in units:
+            parts[r].append(score(scaled, r, b, n))
+        for r in group:
+            total, weights = weigh(parts[r])
+            finish(r, total, mix(weights, r))
 
     for first in range(0, requests, 2):
         group = tuple(range(first, min(first + 2, requests)))

time: 19.6 us -> 19.2 us (0.980); the launches traced: 19.2 us -> 19.1 us
  starting transfers between devices: 9.36 us -> 9.02 us
  waiting for transfers between devices: 3.77 us -> 4.04 us
    ppermute x6, starting transfers between devices: 9.36 us -> 9.02 us  [exchange(): lax.ppermute(part, 'tp', [(i, i ^ k) for i in range(owners)])]
    ppermute x6, waiting for transfers between devices: 3.77 us -> 4.04 us  [exchange(): lax.ppermute(part, 'tp', [(i, i ^ k) for i in range(owners)])]
where the time goes in v18:
time: 19.2 us; the launch traced here: 19.1 us
  starting transfers between devices  9.02 us (47%)
  Pallas kernels  6.05 us (32%)
  waiting for transfers between devices  4.04 us (21%)
    ppermute x6, starting transfers between devices, exchange(): lax.ppermute(part, 'tp', [(i, i ^ k) for i in range(owners)])  9.02 us
    ppermute x6, waiting for transfers between devices, exchange(): lax.ppermute(part, 'tp', [(i, i ^ k) for i in range(owners)])  4.04 us
    pallas_call x1, Pallas kernels, attend(): pl.pallas_call(functools.partial(attend_kernel, owners), out_shape=[part]...  2.34 us
    pallas_call x1, Pallas kernels, stage(): pl.pallas_call(stage_kernel, out_shape=jax.ShapeDtypeStruct(maps.shape, m...  2.2 us
    pallas_call x1, Pallas kernels, project(): pl.pallas_call(functools.partial(project_kernel, count), out_shape=[jax.S...  0.86 us
    pallas_call x1, Pallas kernels, assemble(): pl.pallas_call(functools.partial(assemble_kernel, owners), out_shape=pltp...  0.66 us
  transfers between devices with their start and end apart: 6, of which 4 were waited for; matrix products, arithmetic and copies ran while one was open for 0% of the time, Pallas kernels for 11%

profile of v18, /device:TPU:0, one launch (start us, length us, event | category | flops | bytes accessed | tf_op | source)
XLA Modules:
  0.0 19.1 jit_solution(5265548698468171262)
XLA Ops:
  0.0 2.3 %attend.1 = (bf16[64,512]{1,0:T(8,128)(2,1)S(1)}, bf16[64,512]{1,0:T(8,128)(2,1)S(1)}, bf16[64,512]{1,0:T(8,128)(2,1)S(1)}, bf16[64,512]{1,0:T(8,128)(2,1)S(1)}) custom-call(s32[2]{0:T(128)} %lengths_hbm.1, bf16[2,576,128]{2,1,0:T(8,128)(2,1)} %bitcast.8, f32[576]{0:T(1024)} %scales_hbm.1, bf16[2,576,1536]{2,1,0:T(8,128)(2,1)} %bitcast.7), custom_call_target="tpu_custom_call" | custom-call | flops 905969664 | bytes 3538944 | tf_op jit(solution)/shard_map/attend/pallas_call | solution.py:124
  2.3 4.8 %collective-permute-start = (bf16[64,512]{1,0:T(8,128)(2,1)S(1)}, bf16[64,512]{1,0:T(8,128)(2,1)S(1)}, u32[]{:S(2)}, u32[]{:S(2)}) collective-permute-start(bf16[64,512]{1,0:T(8,128)(2,1)S(1)} %get-tuple-element.14), channel_id=1, source_target_pairs={{0,3},{1,2},{2,1},{3,0},{4,7},{5,6},{6,5},{7,4},{8,11},{9,10},{10,... | collective-permute-start | bytes 196616 | tf_op jit(solution)/shard_map/ppermute | solution.py:235
  7.2 0.0 collective-permute-start.1
  7.2 0.6 %collective-permute-start.2 = (bf16[64,512]{1,0:T(8,128)(2,1)S(1)}, bf16[64,512]{1,0:T(8,128)(2,1)S(1)}, u32[]{:S(2)}, u32[]{:S(2)}) collective-permute-start(bf16[64,512]{1,0:T(8,128)(2,1)S(1)} %get-tuple-element.16), channel_id=1, source_target_pairs={{0,1},{1,0},{2,3},{3,2},{4,5},{5,4},{6,7},{7,6},{8,9},{9,8},{10,11... | collective-permute-start | bytes 196616 | tf_op jit(solution)/shard_map/ppermute | solution.py:235
  7.8 2.2 %stage.1.refs_4_ = bf16[32,512,128]{2,1,0:T(8,128)(2,1)S(1)} custom-call(bf16[32,512,128]{2,1,0:T(8,128)(2,1)} %maps_hbm.1, bf16[64,512]{1,0:T(8,128)(2,1)S(1)} %get-tuple-element.13.after.refs_0_), custom_call_target="tpu_custom_call" | custom-call | bytes 8388608 | tf_op jit(solution)/shard_map/stage/pallas_call | solution.py:155
  10.0 0.0 collective-permute-done.refs_1_
  10.0 1.4 %collective-permute-done.1.refs_2_ = bf16[64,512]{1,0:T(8,128)(2,1)S(1)} collective-permute-done((bf16[64,512]{1,0:T(8,128)(2,1)S(1)}, bf16[64,512]{1,0:T(8,128)(2,1)S(1)}, u32[]{:S(2)}, u32[]{:S(2)}) %collective-permute-start.1) | collective-permute-done | bytes 65568 | tf_op jit(solution)/shard_map/ppermute | solution.py:235
  11.4 0.0 collective-permute-done.2.refs_3_
  11.4 0.9 %project.1 = (bf16[32,2,128]{2,1,0:T(2,128)(2,1)S(1)}, bf16[32,2,128]{2,1,0:T(2,128)(2,1)S(1)}, bf16[32,2,128]{2,1,0:T(2,128)(2,1)S(1)}, bf16[32,2,128]{2,1,0:T(2,128)(2,1)S(1)}) custom-call(bf16[64,512]{1,0:T(8,128)(2,1)S(1)} %get-tuple-element.13.after.refs_0_, bf16[64,512]{1,0:T(8,128)(2,1)S(1)} %collective-permute-done.refs_1_, ...), custom_call_target="tpu_custom_call" | custom-call | flops 33554432 | bytes 4194304 | tf_op jit(solution)/shard_map/project/pallas_call | solution.py:191
  12.3 1.6 %collective-permute-start.3 = (bf16[32,2,128]{2,1,0:T(2,128)(2,1)S(1)}, bf16[32,2,128]{2,1,0:T(2,128)(2,1)S(1)}, u32[]{:S(2)}, u32[]{:S(2)}) collective-permute-start(bf16[32,2,128]{2,1,0:T(2,128)(2,1)S(1)} %get-tuple-element.18), channel_id=1, source_target_pairs={{0,3},{1,2},{2,1},{3,0},{4,7},{5,6},{6,5},{7,4},{8,11},{9,10},{10,... | collective-permute-start | bytes 49160 | tf_op jit(solution)/shard_map/ppermute | solution.py:235
  13.9 0.8 %collective-permute-start.4 = (bf16[32,2,128]{2,1,0:T(2,128)(2,1)S(1)}, bf16[32,2,128]{2,1,0:T(2,128)(2,1)S(1)}, u32[]{:S(2)}, u32[]{:S(2)}) collective-permute-start(bf16[32,2,128]{2,1,0:T(2,128)(2,1)S(1)} %get-tuple-element.19), channel_id=1, source_target_pairs={{0,2},{1,3},{2,0},{3,1},{4,6},{5,7},{6,4},{7,5},{8,10},{9,11},{10,... | collective-permute-start | bytes 49160 | tf_op jit(solution)/shard_map/ppermute | solution.py:235
  14.8 1.1 %collective-permute-start.5 = (bf16[32,2,128]{2,1,0:T(2,128)(2,1)S(1)}, bf16[32,2,128]{2,1,0:T(2,128)(2,1)S(1)}, u32[]{:S(2)}, u32[]{:S(2)}) collective-permute-start(bf16[32,2,128]{2,1,0:T(2,128)(2,1)S(1)} %get-tuple-element.20), channel_id=1, source_target_pairs={{0,1},{1,0},{2,3},{3,2},{4,5},{5,4},{6,7},{7,6},{8,9},{9,8},{10,11... | collective-permute-start | bytes 49160 | tf_op jit(solution)/shard_map/ppermute | solution.py:235
  15.9 1.1 %collective-permute-done.3.refs_1_ = bf16[32,2,128]{2,1,0:T(2,128)(2,1)S(1)} collective-permute-done((bf16[32,2,128]{2,1,0:T(2,128)(2,1)S(1)}, bf16[32,2,128]{2,1,0:T(2,128)(2,1)S(1)}, u32[]{:S(2)}, u32[]{:S(2)}) %collective-permute-start.3) | collective-permute-done | bytes 16416 | tf_op jit(solution)/shard_map/ppermute | solution.py:235
  17.0 0.7 %collective-permute-done.4.refs_2_ = bf16[32,2,128]{2,1,0:T(2,128)(2,1)S(1)} collective-permute-done((bf16[32,2,128]{2,1,0:T(2,128)(2,1)S(1)}, bf16[32,2,128]{2,1,0:T(2,128)(2,1)S(1)}, u32[]{:S(2)}, u32[]{:S(2)}) %collective-permute-start.4) | collective-permute-done | bytes 16416 | tf_op jit(solution)/shard_map/ppermute | solution.py:235
  17.7 0.8 %collective-permute-done.5.refs_3_ = bf16[32,2,128]{2,1,0:T(2,128)(2,1)S(1)} collective-permute-done((bf16[32,2,128]{2,1,0:T(2,128)(2,1)S(1)}, bf16[32,2,128]{2,1,0:T(2,128)(2,1)S(1)}, u32[]{:S(2)}, u32[]{:S(2)}) %collective-permute-start.5) | collective-permute-done | bytes 16416 | tf_op jit(solution)/shard_map/ppermute | solution.py:235
  18.5 0.7 %assemble.1 = bf16[4,32,2,128]{3,2,1,0:T(2,128)(2,1)} custom-call(bf16[32,2,128]{2,1,0:T(2,128)(2,1)S(1)} %get-tuple-element.17.refs_0_, bf16[32,2,128]{2,1,0:T(2,128)(2,1)S(1)} %collective-permute-done.3.refs_1_, bf16[32,2,128]{2,1,0:T(2,128)(2,1)S(1)} %collective-permute-done.4.refs_2_, bf16[32,2,128]{2,1,0:T(2,128)(2,1)S(1)} %collective-permute-done.5.refs_3_), custom_call_target="tpu_custom_call" | custom-call | tf_op jit(solution)/shard_map/assemble/pallas_call | solution.py:221
Async XLA Ops:
  2.3 7.7 %collective-permute-start = (bf16[64,512]{1,0:T(8,128)(2,1)S(1)}, bf16[64,512]{1,0:T(8,128)(2,1)S(1)}, u32[]{:S(2)}, u32[]{:S(2)}) collective-permute-start(bf16[64,512]{1,0:T(8,128)(2,1)S(1)} %get-tuple-element.14), channel_id=1, source_target_pairs={{0,3},{1,2},{2,1},{3,0},{4,7},{5,6},{6,5},{7,4},{8,11},{9,10},{10,... | collective-permute-start | bytes 196616 | tf_op jit(solution)/shard_map/ppermute | solution.py:235
  7.2 4.3 %collective-permute-start.1 = (bf16[64,512]{1,0:T(8,128)(2,1)S(1)}, bf16[64,512]{1,0:T(8,128)(2,1)S(1)}, u32[]{:S(2)}, u32[]{:S(2)}) collective-permute-start(bf16[64,512]{1,0:T(8,128)(2,1)S(1)} %get-tuple-element.15), channel_id=1, source_target_pairs={{0,2},{1,3},{2,0},{3,1},{4,6},{5,7},{6,4},{7,5},{8,10},{9,11},{10,... | collective-permute-start | bytes 196616 | tf_op jit(solution)/shard_map/ppermute | solution.py:235
  7.2 4.3 %collective-permute-start.2 = (bf16[64,512]{1,0:T(8,128)(2,1)S(1)}, bf16[64,512]{1,0:T(8,128)(2,1)S(1)}, u32[]{:S(2)}, u32[]{:S(2)}) collective-permute-start(bf16[64,512]{1,0:T(8,128)(2,1)S(1)} %get-tuple-element.16), channel_id=1, source_target_pairs={{0,1},{1,0},{2,3},{3,2},{4,5},{5,4},{6,7},{7,6},{8,9},{9,8},{10,11... | collective-permute-start | bytes 196616 | tf_op jit(solution)/shard_map/ppermute | solution.py:235
  12.3 4.7 %collective-permute-start.3 = (bf16[32,2,128]{2,1,0:T(2,128)(2,1)S(1)}, bf16[32,2,128]{2,1,0:T(2,128)(2,1)S(1)}, u32[]{:S(2)}, u32[]{:S(2)}) collective-permute-start(bf16[32,2,128]{2,1,0:T(2,128)(2,1)S(1)} %get-tuple-element.18), channel_id=1, source_target_pairs={{0,3},{1,2},{2,1},{3,0},{4,7},{5,6},{6,5},{7,4},{8,11},{9,10},{10,... | collective-permute-start | bytes 49160 | tf_op jit(solution)/shard_map/ppermute | solution.py:235
  13.9 3.7 %collective-permute-start.4 = (bf16[32,2,128]{2,1,0:T(2,128)(2,1)S(1)}, bf16[32,2,128]{2,1,0:T(2,128)(2,1)S(1)}, u32[]{:S(2)}, u32[]{:S(2)}) collective-permute-start(bf16[32,2,128]{2,1,0:T(2,128)(2,1)S(1)} %get-tuple-element.19), channel_id=1, source_target_pairs={{0,2},{1,3},{2,0},{3,1},{4,6},{5,7},{6,4},{7,5},{8,10},{9,11},{10,... | collective-permute-start | bytes 49160 | tf_op jit(solution)/shard_map/ppermute | solution.py:235
  14.8 3.7 %collective-permute-start.5 = (bf16[32,2,128]{2,1,0:T(2,128)(2,1)S(1)}, bf16[32,2,128]{2,1,0:T(2,128)(2,1)S(1)}, u32[]{:S(2)}, u32[]{:S(2)}) collective-permute-start(bf16[32,2,128]{2,1,0:T(2,128)(2,1)S(1)} %get-tuple-element.20), channel_id=1, source_target_pairs={{0,1},{1,0},{2,3},{3,2},{4,5},{5,4},{6,7},{7,6},{8,9},{9,8},{10,11... | collective-permute-start | bytes 49160 | tf_op jit(solution)/shard_map/ppermute | solution.py:235

commit v19 on v18

--- a/solution.py
+++ b/solution.py
@@ -14,6 +14,8 @@
 EXP2_SCALE = SOFTMAX_SCALE * math.log2(math.e)
 BLOCK = 512
 LANES = 128
+TILE = 256
+UNITS = 2
 GROUP_ROWS = 16
 
 
@@ -22,7 +24,8 @@
 
 
 def attend_kernel(owners, lengths_hbm, query_hbm, scales_hbm, cache, *refs):
-    outs, (latents, lengths, query, scales, keys, sems, small_sems) = refs[:owners], refs[owners:]
+    outs, refs = refs[:owners], refs[owners:]
+    latents, lengths, query, scales, keys, sems, small_sems = refs
     requests, channels, heads = query.shape
     rows, rank = outs[0].shape
     cache_len = cache.shape[2]
@@ -55,14 +58,31 @@
 
     def scale(r):
         ask(r).wait()
-        return (query[r].astype(jnp.float32).T * scale_row).astype(jnp.bfloat16)
-
-    def score(scaled, r, b, live):
+        rows = (query[r].astype(jnp.float32).T * scale_row).astype(jnp.bfloat16)
+        return jnp.concatenate(
+            [rows, jnp.zeros((heads, -channels % TILE), jnp.bfloat16)], axis=1
+        )
+
+    def tile(r, k, at):
+        rows = keys[r, k * TILE:min((k + 1) * TILE, channels), at:at + TILE]
+        if rows.shape[0] == TILE:
+            return rows
+        return jnp.concatenate(
+            [rows, jnp.zeros((TILE - rows.shape[0], TILE), jnp.bfloat16)], axis=0
+        )
+
+    def score(sums, scaled, r, b, live):
         if r not in scaled:
             scaled[r] = scale(r)
         fetch(r, b).wait()
-        span = slice(b * block, (b + 1) * block)
-        part = jnp.dot(scaled[r], keys[r, :, span], preferred_element_type=jnp.float32)
+        for k in range(-(-channels // TILE)):
+            for unit in range(UNITS):
+                pltpu.matmul_push_rhs(tile(r, k, b * block + unit * TILE), k % 2, unit)
+            for unit in range(UNITS):
+                pltpu.matmul_acc_lhs(
+                    sums[unit], scaled[r][:, k * TILE:(k + 1) * TILE], load_staged_rhs=k % 2
+                )
+        part = jnp.concatenate([pltpu.matmul_pop(sums[unit]) for unit in range(UNITS)], axis=1)
         if b == live - 1:
             place = b * block + lax.broadcasted_iota(jnp.int32, part.shape, 1)
             part = jnp.where(place < lengths[r], part, -jnp.inf)
@@ -76,11 +96,16 @@
         total = sum(jnp.sum(weight, axis=1, keepdims=True) for weight in weights)
         return total, jnp.concatenate([weight.astype(jnp.bfloat16) for weight in weights], axis=1)
 
-    def mix(weights, r):
-        return lax.dot_general(
-            weights, keys[r, :rank, :weights.shape[1]],
-            (((1,), (1,)), ((), ())), preferred_element_type=jnp.float32,
-        )
+    def mix(sums, weights, r):
+        for k in range(weights.shape[1] // TILE):
+            span = slice(k * TILE, (k + 1) * TILE)
+            for unit in range(UNITS):
+                pltpu.matmul_push_rhs(
+                    keys[r, unit * TILE:(unit + 1) * TILE, span], k % 2, unit, transpose=True
+                )
+            for unit in range(UNITS):
+                pltpu.matmul_acc_lhs(sums[unit], weights[:, span], load_staged_rhs=k % 2)
+        return jnp.concatenate([pltpu.matmul_pop(sums[unit]) for unit in range(UNITS)], axis=1)
 
     def finish(r, total, mixture):
         latent = mixture * (1.0 / total) * scale_row[:, :rank]
@@ -91,12 +116,20 @@
         scaled = {}
         units = [(r, 0, n) for r, n in zip(group, live)]
         units += [(r, b, n) for r, n in zip(group, live) for b in range(1, n)]
-        parts = {r: [] for r in group}
-        for r, b, n in units:
-            parts[r].append(score(scaled, r, b, n))
-        for r in group:
-            total, weights = weigh(parts[r])
-            finish(r, total, mix(weights, r))
+
+        def work(*sums):
+            sums = [sums[i:i + UNITS] for i in range(0, len(sums), UNITS)]
+            parts = {r: [] for r in group}
+            for i, (r, b, n) in enumerate(units):
+                parts[r].append(score(sums[i % 2], scaled, r, b, n))
+            for r in group:
+                total, weights = weigh(parts[r])
+                finish(r, total, mix(sums[2], weights, r))
+
+        pl.run_scoped(
+            work,
+            *[pltpu.ACC(unit)((heads, TILE), jnp.float32) for _ in range(3) for unit in range(UNITS)],
+        )
 
     for first in range(0, requests, 2):
         group = tuple(range(first, min(first + 2, requests)))

time: 19.2 us -> 19.7 us (1.026)
  starting transfers between devices: 9.02 us -> 7.63 us
  Pallas kernels: 6.05 us -> 7.35 us
  waiting for transfers between devices: 4.04 us -> 4.67 us
    ppermute x6, starting transfers between devices: 9.02 us -> 7.63 us  [exchange(): lax.ppermute(part, 'tp', [(i, i ^ k) for i in range(owners)])]
    pallas_call x1, Pallas kernels: 2.34 us -> 3.64 us  [attend(): pl.pallas_call(functools.partial(attend_kernel, owners), out_shape=[part]...]
    ppermute x6, waiting for transfers between devices: 4.04 us -> 4.67 us  [exchange(): lax.ppermute(part, 'tp', [(i, i ^ k) for i in range(owners)])]
  transfers between devices with their start and end apart: 6 -> 6, of which waited for: 4 -> 5; matrix products, arithmetic and copies ran while one was open for 0% -> 0% of each run, Pallas kernels for 11% -> 11%
where the time goes in v19:
time: 19.7 us
  starting transfers between devices  7.63 us (39%)
  Pallas kernels  7.35 us (37%)
  waiting for transfers between devices  4.67 us (24%)
    ppermute x6, starting transfers between devices, exchange(): lax.ppermute(part, 'tp', [(i, i ^ k) for i in range(owners)])  7.63 us
    ppermute x6, waiting for transfers between devices, exchange(): lax.ppermute(part, 'tp', [(i, i ^ k) for i in range(owners)])  4.67 us
    pallas_call x1, Pallas kernels, attend(): pl.pallas_call(functools.partial(attend_kernel, owners), out_shape=[part]...  3.64 us
    pallas_call x1, Pallas kernels, stage(): pl.pallas_call(stage_kernel, out_shape=jax.ShapeDtypeStruct(maps.shape, m...  2.2 us
    pallas_call x1, Pallas kernels, project(): pl.pallas_call(functools.partial(project_kernel, count), out_shape=[jax.S...  0.86 us
    pallas_call x1, Pallas kernels, assemble(): pl.pallas_call(functools.partial(assemble_kernel, owners), out_shape=pltp...  0.66 us
  transfers between devices with their start and end apart: 6, of which 5 were waited for; matrix products, arithmetic and copies ran while one was open for 0% of the time, Pallas kernels for 11%

profile of v19, /device:TPU:0, one launch (start us, length us, event | category | flops | bytes accessed | tf_op | source)
XLA Modules:
  0.0 19.7 jit_solution(978131005660289924)
XLA Ops:
  0.0 3.6 %attend.1 = (bf16[64,512]{1,0:T(8,128)(2,1)S(1)}, bf16[64,512]{1,0:T(8,128)(2,1)S(1)}, bf16[64,512]{1,0:T(8,128)(2,1)S(1)}, bf16[64,512]{1,0:T(8,128)(2,1)S(1)}) custom-call(s32[2]{0:T(128)} %lengths_hbm.1, bf16[2,576,128]{2,1,0:T(8,128)(2,1)} %bitcast.8, f32[576]{0:T(1024)} %scales_hbm.1, bf16[2,576,1536]{2,1,0:T(8,128)(2,1)} %bitcast.7), custom_call_target="tpu_custom_call" | custom-call | flops 905969664 | bytes 3538944 | tf_op jit(solution)/shard_map/attend/pallas_call | solution.py:157
  3.6 3.2 %collective-permute-start = (bf16[64,512]{1,0:T(8,128)(2,1)S(1)}, bf16[64,512]{1,0:T(8,128)(2,1)S(1)}, u32[]{:S(2)}, u32[]{:S(2)}) collective-permute-start(bf16[64,512]{1,0:T(8,128)(2,1)S(1)} %get-tuple-element.14), channel_id=1, source_target_pairs={{0,3},{1,2},{2,1},{3,0},{4,7},{5,6},{6,5},{7,4},{8,11},{9,10},{10,... | collective-permute-start | bytes 196616 | tf_op jit(solution)/shard_map/ppermute | solution.py:268
  6.8 0.0 collective-permute-start.1
  6.8 0.9 %collective-permute-start.2 = (bf16[64,512]{1,0:T(8,128)(2,1)S(1)}, bf16[64,512]{1,0:T(8,128)(2,1)S(1)}, u32[]{:S(2)}, u32[]{:S(2)}) collective-permute-start(bf16[64,512]{1,0:T(8,128)(2,1)S(1)} %get-tuple-element.16), channel_id=1, source_target_pairs={{0,1},{1,0},{2,3},{3,2},{4,5},{5,4},{6,7},{7,6},{8,9},{9,8},{10,11... | collective-permute-start | bytes 196616 | tf_op jit(solution)/shard_map/ppermute | solution.py:268
  7.7 2.2 %stage.1.refs_4_ = bf16[32,512,128]{2,1,0:T(8,128)(2,1)S(1)} custom-call(bf16[32,512,128]{2,1,0:T(8,128)(2,1)} %maps_hbm.1, bf16[64,512]{1,0:T(8,128)(2,1)S(1)} %get-tuple-element.13.after.refs_0_), custom_call_target="tpu_custom_call" | custom-call | bytes 8388608 | tf_op jit(solution)/shard_map/stage/pallas_call | solution.py:188
  9.9 0.0 collective-permute-done.refs_1_
  9.9 1.2 %collective-permute-done.1.refs_2_ = bf16[64,512]{1,0:T(8,128)(2,1)S(1)} collective-permute-done((bf16[64,512]{1,0:T(8,128)(2,1)S(1)}, bf16[64,512]{1,0:T(8,128)(2,1)S(1)}, u32[]{:S(2)}, u32[]{:S(2)}) %collective-permute-start.1) | collective-permute-done | bytes 65568 | tf_op jit(solution)/shard_map/ppermute | solution.py:268
  11.2 0.2 collective-permute-done.2.refs_3_
  11.4 0.9 %project.1 = (bf16[32,2,128]{2,1,0:T(2,128)(2,1)S(1)}, bf16[32,2,128]{2,1,0:T(2,128)(2,1)S(1)}, bf16[32,2,128]{2,1,0:T(2,128)(2,1)S(1)}, bf16[32,2,128]{2,1,0:T(2,128)(2,1)S(1)}) custom-call(bf16[64,512]{1,0:T(8,128)(2,1)S(1)} %get-tuple-element.13.after.refs_0_, bf16[64,512]{1,0:T(8,128)(2,1)S(1)} %collective-permute-done.refs_1_, ...), custom_call_target="tpu_custom_call" | custom-call | flops 33554432 | bytes 4194304 | tf_op jit(solution)/shard_map/project/pallas_call | solution.py:224
  12.2 2.1 %collective-permute-start.3 = (bf16[32,2,128]{2,1,0:T(2,128)(2,1)S(1)}, bf16[32,2,128]{2,1,0:T(2,128)(2,1)S(1)}, u32[]{:S(2)}, u32[]{:S(2)}) collective-permute-start(bf16[32,2,128]{2,1,0:T(2,128)(2,1)S(1)} %get-tuple-element.18), channel_id=1, source_target_pairs={{0,3},{1,2},{2,1},{3,0},{4,7},{5,6},{6,5},{7,4},{8,11},{9,10},{10,... | collective-permute-start | bytes 49160 | tf_op jit(solution)/shard_map/ppermute | solution.py:268
  14.4 0.9 %collective-permute-start.4 = (bf16[32,2,128]{2,1,0:T(2,128)(2,1)S(1)}, bf16[32,2,128]{2,1,0:T(2,128)(2,1)S(1)}, u32[]{:S(2)}, u32[]{:S(2)}) collective-permute-start(bf16[32,2,128]{2,1,0:T(2,128)(2,1)S(1)} %get-tuple-element.19), channel_id=1, source_target_pairs={{0,2},{1,3},{2,0},{3,1},{4,6},{5,7},{6,4},{7,5},{8,10},{9,11},{10,... | collective-permute-start | bytes 49160 | tf_op jit(solution)/shard_map/ppermute | solution.py:268
  15.3 0.5 %collective-permute-start.5 = (bf16[32,2,128]{2,1,0:T(2,128)(2,1)S(1)}, bf16[32,2,128]{2,1,0:T(2,128)(2,1)S(1)}, u32[]{:S(2)}, u32[]{:S(2)}) collective-permute-start(bf16[32,2,128]{2,1,0:T(2,128)(2,1)S(1)} %get-tuple-element.20), channel_id=1, source_target_pairs={{0,1},{1,0},{2,3},{3,2},{4,5},{5,4},{6,7},{7,6},{8,9},{9,8},{10,11... | collective-permute-start | bytes 49160 | tf_op jit(solution)/shard_map/ppermute | solution.py:268
  15.8 1.2 %collective-permute-done.3.refs_1_ = bf16[32,2,128]{2,1,0:T(2,128)(2,1)S(1)} collective-permute-done((bf16[32,2,128]{2,1,0:T(2,128)(2,1)S(1)}, bf16[32,2,128]{2,1,0:T(2,128)(2,1)S(1)}, u32[]{:S(2)}, u32[]{:S(2)}) %collective-permute-start.3) | collective-permute-done | bytes 16416 | tf_op jit(solution)/shard_map/ppermute | solution.py:268
  17.0 1.1 %collective-permute-done.4.refs_2_ = bf16[32,2,128]{2,1,0:T(2,128)(2,1)S(1)} collective-permute-done((bf16[32,2,128]{2,1,0:T(2,128)(2,1)S(1)}, bf16[32,2,128]{2,1,0:T(2,128)(2,1)S(1)}, u32[]{:S(2)}, u32[]{:S(2)}) %collective-permute-start.4) | collective-permute-done | bytes 16416 | tf_op jit(solution)/shard_map/ppermute | solution.py:268
  18.1 0.9 %collective-permute-done.5.refs_3_ = bf16[32,2,128]{2,1,0:T(2,128)(2,1)S(1)} collective-permute-done((bf16[32,2,128]{2,1,0:T(2,128)(2,1)S(1)}, bf16[32,2,128]{2,1,0:T(2,128)(2,1)S(1)}, u32[]{:S(2)}, u32[]{:S(2)}) %collective-permute-start.5) | collective-permute-done | bytes 16416 | tf_op jit(solution)/shard_map/ppermute | solution.py:268
  19.0 0.7 %assemble.1 = bf16[4,32,2,128]{3,2,1,0:T(2,128)(2,1)} custom-call(bf16[32,2,128]{2,1,0:T(2,128)(2,1)S(1)} %get-tuple-element.17.refs_0_, bf16[32,2,128]{2,1,0:T(2,128)(2,1)S(1)} %collective-permute-done.3.refs_1_, bf16[32,2,128]{2,1,0:T(2,128)(2,1)S(1)} %collective-permute-done.4.refs_2_, bf16[32,2,128]{2,1,0:T(2,128)(2,1)S(1)} %collective-permute-done.5.refs_3_), custom_call_target="tpu_custom_call" | custom-call | tf_op jit(solution)/shard_map/assemble/pallas_call | solution.py:254
Async XLA Ops:
  3.6 6.3 %collective-permute-start = (bf16[64,512]{1,0:T(8,128)(2,1)S(1)}, bf16[64,512]{1,0:T(8,128)(2,1)S(1)}, u32[]{:S(2)}, u32[]{:S(2)}) collective-permute-start(bf16[64,512]{1,0:T(8,128)(2,1)S(1)} %get-tuple-element.14), channel_id=1, source_target_pairs={{0,3},{1,2},{2,1},{3,0},{4,7},{5,6},{6,5},{7,4},{8,11},{9,10},{10,... | collective-permute-start | bytes 196616 | tf_op jit(solution)/shard_map/ppermute | solution.py:268
  6.8 4.4 %collective-permute-start.1 = (bf16[64,512]{1,0:T(8,128)(2,1)S(1)}, bf16[64,512]{1,0:T(8,128)(2,1)S(1)}, u32[]{:S(2)}, u32[]{:S(2)}) collective-permute-start(bf16[64,512]{1,0:T(8,128)(2,1)S(1)} %get-tuple-element.15), channel_id=1, source_target_pairs={{0,2},{1,3},{2,0},{3,1},{4,6},{5,7},{6,4},{7,5},{8,10},{9,11},{10,... | collective-permute-start | bytes 196616 | tf_op jit(solution)/shard_map/ppermute | solution.py:268
  6.8 4.5 %collective-permute-start.2 = (bf16[64,512]{1,0:T(8,128)(2,1)S(1)}, bf16[64,512]{1,0:T(8,128)(2,1)S(1)}, u32[]{:S(2)}, u32[]{:S(2)}) collective-permute-start(bf16[64,512]{1,0:T(8,128)(2,1)S(1)} %get-tuple-element.16), channel_id=1, source_target_pairs={{0,1},{1,0},{2,3},{3,2},{4,5},{5,4},{6,7},{7,6},{8,9},{9,8},{10,11... | collective-permute-start | bytes 196616 | tf_op jit(solution)/shard_map/ppermute | solution.py:268
  12.2 4.8 %collective-permute-start.3 = (bf16[32,2,128]{2,1,0:T(2,128)(2,1)S(1)}, bf16[32,2,128]{2,1,0:T(2,128)(2,1)S(1)}, u32[]{:S(2)}, u32[]{:S(2)}) collective-permute-start(bf16[32,2,128]{2,1,0:T(2,128)(2,1)S(1)} %get-tuple-element.18), channel_id=1, source_target_pairs={{0,3},{1,2},{2,1},{3,0},{4,7},{5,6},{6,5},{7,4},{8,11},{9,10},{10,... | collective-permute-start | bytes 49160 | tf_op jit(solution)/shard_map/ppermute | solution.py:268
  14.4 3.7 %collective-permute-start.4 = (bf16[32,2,128]{2,1,0:T(2,128)(2,1)S(1)}, bf16[32,2,128]{2,1,0:T(2,128)(2,1)S(1)}, u32[]{:S(2)}, u32[]{:S(2)}) collective-permute-start(bf16[32,2,128]{2,1,0:T(2,128)(2,1)S(1)} %get-tuple-element.19), channel_id=1, source_target_pairs={{0,2},{1,3},{2,0},{3,1},{4,6},{5,7},{6,4},{7,5},{8,10},{9,11},{10,... | collective-permute-start | bytes 49160 | tf_op jit(solution)/shard_map/ppermute | solution.py:268
  15.3 3.7 %collective-permute-start.5 = (bf16[32,2,128]{2,1,0:T(2,128)(2,1)S(1)}, bf16[32,2,128]{2,1,0:T(2,128)(2,1)S(1)}, u32[]{:S(2)}, u32[]{:S(2)}) collective-permute-start(bf16[32,2,128]{2,1,0:T(2,128)(2,1)S(1)} %get-tuple-element.20), channel_id=1, source_target_pairs={{0,1},{1,0},{2,3},{3,2},{4,5},{5,4},{6,7},{7,6},{8,9},{9,8},{10,11... | collective-permute-start | bytes 49160 | tf_op jit(solution)/shard_map/ppermute | solution.py:268

commit v20 on v19

--- a/solution.py
+++ b/solution.py
@@ -15,6 +15,7 @@
 BLOCK = 512
 LANES = 128
 TILE = 256
+CHUNK = 32
 UNITS = 2
 GROUP_ROWS = 16
 
@@ -71,41 +72,54 @@
             [rows, jnp.zeros((TILE - rows.shape[0], TILE), jnp.bfloat16)], axis=0
         )
 
-    def score(sums, scaled, r, b, live):
-        if r not in scaled:
-            scaled[r] = scale(r)
-        fetch(r, b).wait()
-        for k in range(-(-channels // TILE)):
+    def score_steps(sums, scaled, r, b):
+        def step(k):
             for unit in range(UNITS):
                 pltpu.matmul_push_rhs(tile(r, k, b * block + unit * TILE), k % 2, unit)
             for unit in range(UNITS):
                 pltpu.matmul_acc_lhs(
                     sums[unit], scaled[r][:, k * TILE:(k + 1) * TILE], load_staged_rhs=k % 2
                 )
+
+        return [functools.partial(step, k) for k in range(-(-channels // TILE))]
+
+    def scores(sums, r, b, live):
         part = jnp.concatenate([pltpu.matmul_pop(sums[unit]) for unit in range(UNITS)], axis=1)
         if b == live - 1:
             place = b * block + lax.broadcasted_iota(jnp.int32, part.shape, 1)
             part = jnp.where(place < lengths[r], part, -jnp.inf)
         return part
 
-    def weigh(parts):
-        top = functools.reduce(
-            jnp.maximum, [jnp.max(part, axis=1, keepdims=True) for part in parts]
-        )
-        weights = [jnp.exp2((part - top) * EXP2_SCALE) for part in parts]
-        total = sum(jnp.sum(weight, axis=1, keepdims=True) for weight in weights)
-        return total, jnp.concatenate([weight.astype(jnp.bfloat16) for weight in weights], axis=1)
-
-    def mix(sums, weights, r):
-        for k in range(weights.shape[1] // TILE):
-            span = slice(k * TILE, (k + 1) * TILE)
+    def weigh_steps(part, top, weights, totals):
+        def step(at):
+            rows = slice(at, at + CHUNK)
+            weight = jnp.exp2((part[rows] - top[rows]) * EXP2_SCALE)
+            totals.append(jnp.sum(weight, axis=1, keepdims=True))
+            weights.append(weight.astype(jnp.bfloat16))
+
+        return [functools.partial(step, at) for at in range(0, heads, CHUNK)]
+
+    def mix_steps(sums, weights, r, b):
+        def step(k):
+            at = b * block + k * TILE
             for unit in range(UNITS):
                 pltpu.matmul_push_rhs(
-                    keys[r, unit * TILE:(unit + 1) * TILE, span], k % 2, unit, transpose=True
+                    keys[r, unit * TILE:(unit + 1) * TILE, at:at + TILE], k % 2, unit,
+                    transpose=True,
                 )
             for unit in range(UNITS):
-                pltpu.matmul_acc_lhs(sums[unit], weights[:, span], load_staged_rhs=k % 2)
-        return jnp.concatenate([pltpu.matmul_pop(sums[unit]) for unit in range(UNITS)], axis=1)
+                pltpu.matmul_acc_lhs(
+                    sums[unit], weights[:, k * TILE:(k + 1) * TILE], load_staged_rhs=k % 2
+                )
+
+        return [functools.partial(step, k) for k in range(block // TILE)]
+
+    def interleave(one, two):
+        total = max(len(one), len(two))
+        for i in range(total):
+            for steps in (one, two):
+                for at in range(i * len(steps) // total, (i + 1) * len(steps) // total):
+                    steps[at]()
 
     def finish(r, total, mixture):
         latent = mixture * (1.0 / total) * scale_row[:, :rank]
@@ -114,21 +128,72 @@
 
     def several(group, live):
         scaled = {}
-        units = [(r, 0, n) for r, n in zip(group, live)]
-        units += [(r, b, n) for r, n in zip(group, live) for b in range(1, n)]
 
         def work(*sums):
             sums = [sums[i:i + UNITS] for i in range(0, len(sums), UNITS)]
             parts = {r: [] for r in group}
-            for i, (r, b, n) in enumerate(units):
-                parts[r].append(score(sums[i % 2], scaled, r, b, n))
-            for r in group:
-                total, weights = weigh(parts[r])
-                finish(r, total, mix(sums[2], weights, r))
+            weights = {(r, b): [] for r, n in zip(group, live) for b in range(n)}
+            totals = {(r, b): [] for r, b in weights}
+            tops = {}
+
+            def weigh(r, b):
+                return weigh_steps(parts[r][b], tops[r], weights[r, b], totals[r, b])
+
+            def column(pieces):
+                return jnp.concatenate(pieces, axis=0)
+
+            def top_of(r):
+                return functools.reduce(
+                    jnp.maximum, [jnp.max(part, axis=1, keepdims=True) for part in parts[r]]
+                )
+
+            def mix_all(r, then=()):
+                pool = sums[2 + r % 2]
+                for b in range(size[r]):
+                    ahead = weigh(r, b + 1) if b + 1 < size[r] else then
+                    interleave(mix_steps(pool, column(weights[r, b]), r, b), ahead)
+                total = sum(column(totals[r, b]) for b in range(size[r]))
+                finish(r, total, jnp.concatenate([pltpu.matmul_pop(x) for x in pool], axis=1))
+
+            size = dict(zip(group, live))
+            short, *rest = sorted(group, key=size.get)
+            turns = [(r, 0) for r in (short, *rest)]
+            turns += [(r, b) for r in (short, *rest) for b in range(1, size[r])]
+            pending = []
+            mixed = False
+            for i, (r, b) in enumerate(turns):
+                if r not in scaled:
+                    scaled[r] = scale(r)
+                fetch(r, b).wait()
+                interleave(score_steps(sums[i % 2], scaled, r, b), pending)
+                parts[r].append(scores(sums[i % 2], r, b, size[r]))
+                if len(parts[short]) < size[short]:
+                    continue
+                if short not in tops:
+                    tops[short] = top_of(short)
+                    pending = weigh(short, 0)
+                elif not mixed and i + 1 < len(turns):
+                    pending, mixed = [], True
+                    mix_all(short)
+                else:
+                    pending = []
+            for step in pending:
+                step()
+            for r in rest:
+                tops[r] = top_of(r)
+                ahead = weigh(r, 0)
+                if mixed:
+                    for step in ahead:
+                        step()
+                else:
+                    mix_all(short, ahead)
+                mix_all(r)
+            if not rest:
+                mix_all(short)
 
         pl.run_scoped(
             work,
-            *[pltpu.ACC(unit)((heads, TILE), jnp.float32) for _ in range(3) for unit in range(UNITS)],
+            *[pltpu.ACC(unit)((heads, TILE), jnp.float32) for _ in range(4) for unit in range(UNITS)],
         )
 
     for first in range(0, requests, 2):

time: 19.7 us -> 19.6 us (level); the launches traced: 19.7 us -> 19.3 us
  waiting for transfers between devices: 4.67 us -> 3.77 us
  starting transfers between devices: 7.63 us -> 8.51 us
  Pallas kernels: 7.35 us -> 7 us
    ppermute x6, waiting for transfers between devices: 4.67 us -> 3.77 us  [exchange(): lax.ppermute(part, 'tp', [(i, i ^ k) for i in range(owners)])]
    ppermute x6, starting transfers between devices: 7.63 us -> 8.51 us  [exchange(): lax.ppermute(part, 'tp', [(i, i ^ k) for i in range(owners)])]
    pallas_call x1, Pallas kernels: 3.64 us -> 3.29 us  [attend(): pl.pallas_call(functools.partial(attend_kernel, owners), out_shape=[part]...]
  transfers between devices with their start and end apart: 6 -> 6, of which waited for: 5 -> 4; matrix products, arithmetic and copies ran while one was open for 0% -> 0% of each run, Pallas kernels for 11% -> 11%
where the time goes in v20:
time: 19.6 us; the launch traced here: 19.3 us
  starting transfers between devices  8.51 us (43%)
  Pallas kernels  7 us (36%)
  waiting for transfers between devices  3.77 us (19%)
    ppermute x6, starting transfers between devices, exchange(): lax.ppermute(part, 'tp', [(i, i ^ k) for i in range(owners)])  8.51 us
    ppermute x6, waiting for transfers between devices, exchange(): lax.ppermute(part, 'tp', [(i, i ^ k) for i in range(owners)])  3.77 us
    pallas_call x1, Pallas kernels, attend(): pl.pallas_call(functools.partial(attend_kernel, owners), out_shape=[part]...  3.29 us
    pallas_call x1, Pallas kernels, stage(): pl.pallas_call(stage_kernel, out_shape=jax.ShapeDtypeStruct(maps.shape, m...  2.2 us
    pallas_call x1, Pallas kernels, project(): pl.pallas_call(functools.partial(project_kernel, count), out_shape=[jax.S...  0.86 us
    pallas_call x1, Pallas kernels, assemble(): pl.pallas_call(functools.partial(assemble_kernel, owners), out_shape=pltp...  0.66 us
  transfers between devices with their start and end apart: 6, of which 4 were waited for; matrix products, arithmetic and copies ran while one was open for 0% of the time, Pallas kernels for 11%

profile of v20, /device:TPU:0, one launch (start us, length us, event | category | flops | bytes accessed | tf_op | source)
XLA Modules:
  0.0 19.3 jit_solution(13651360502685220397)
XLA Ops:
  0.0 3.3 %attend.1 = (bf16[64,512]{1,0:T(8,128)(2,1)S(1)}, bf16[64,512]{1,0:T(8,128)(2,1)S(1)}, bf16[64,512]{1,0:T(8,128)(2,1)S(1)}, bf16[64,512]{1,0:T(8,128)(2,1)S(1)}) custom-call(s32[2]{0:T(128)} %lengths_hbm.1, bf16[2,576,128]{2,1,0:T(8,128)(2,1)} %bitcast.8, f32[576]{0:T(1024)} %scales_hbm.1, bf16[2,576,1536]{2,1,0:T(8,128)(2,1)} %bitcast.7), custom_call_target="tpu_custom_call" | custom-call | flops 905969664 | bytes 3538944 | tf_op jit(solution)/shard_map/attend/pallas_call | solution.py:222
  3.3 3.1 %collective-permute-start = (bf16[64,512]{1,0:T(8,128)(2,1)S(1)}, bf16[64,512]{1,0:T(8,128)(2,1)S(1)}, u32[]{:S(2)}, u32[]{:S(2)}) collective-permute-start(bf16[64,512]{1,0:T(8,128)(2,1)S(1)} %get-tuple-element.14), channel_id=1, source_target_pairs={{0,3},{1,2},{2,1},{3,0},{4,7},{5,6},{6,5},{7,4},{8,11},{9,10},{10,... | collective-permute-start | bytes 196616 | tf_op jit(solution)/shard_map/ppermute | solution.py:333
  6.4 1.0 %collective-permute-start.1 = (bf16[64,512]{1,0:T(8,128)(2,1)S(1)}, bf16[64,512]{1,0:T(8,128)(2,1)S(1)}, u32[]{:S(2)}, u32[]{:S(2)}) collective-permute-start(bf16[64,512]{1,0:T(8,128)(2,1)S(1)} %get-tuple-element.15), channel_id=1, source_target_pairs={{0,2},{1,3},{2,0},{3,1},{4,6},{5,7},{6,4},{7,5},{8,10},{9,11},{10,... | collective-permute-start | bytes 196616 | tf_op jit(solution)/shard_map/ppermute | solution.py:333
  7.4 0.9 %collective-permute-start.2 = (bf16[64,512]{1,0:T(8,128)(2,1)S(1)}, bf16[64,512]{1,0:T(8,128)(2,1)S(1)}, u32[]{:S(2)}, u32[]{:S(2)}) collective-permute-start(bf16[64,512]{1,0:T(8,128)(2,1)S(1)} %get-tuple-element.16), channel_id=1, source_target_pairs={{0,1},{1,0},{2,3},{3,2},{4,5},{5,4},{6,7},{7,6},{8,9},{9,8},{10,11... | collective-permute-start | bytes 196616 | tf_op jit(solution)/shard_map/ppermute | solution.py:333
  8.3 2.2 %stage.1.refs_4_ = bf16[32,512,128]{2,1,0:T(8,128)(2,1)S(1)} custom-call(bf16[32,512,128]{2,1,0:T(8,128)(2,1)} %maps_hbm.1, bf16[64,512]{1,0:T(8,128)(2,1)S(1)} %get-tuple-element.13.after.refs_0_), custom_call_target="tpu_custom_call" | custom-call | bytes 8388608 | tf_op jit(solution)/shard_map/stage/pallas_call | solution.py:253
  10.5 0.0 collective-permute-done.refs_1_
  10.5 0.2 collective-permute-done.1.refs_2_
  10.7 1.0 %collective-permute-done.2.refs_3_ = bf16[64,512]{1,0:T(8,128)(2,1)S(1)} collective-permute-done((bf16[64,512]{1,0:T(8,128)(2,1)S(1)}, bf16[64,512]{1,0:T(8,128)(2,1)S(1)}, u32[]{:S(2)}, u32[]{:S(2)}) %collective-permute-start.2) | collective-permute-done | bytes 65568 | tf_op jit(solution)/shard_map/ppermute | solution.py:333
  11.6 0.9 %project.1 = (bf16[32,2,128]{2,1,0:T(2,128)(2,1)S(1)}, bf16[32,2,128]{2,1,0:T(2,128)(2,1)S(1)}, bf16[32,2,128]{2,1,0:T(2,128)(2,1)S(1)}, bf16[32,2,128]{2,1,0:T(2,128)(2,1)S(1)}) custom-call(bf16[64,512]{1,0:T(8,128)(2,1)S(1)} %get-tuple-element.13.after.refs_0_, bf16[64,512]{1,0:T(8,128)(2,1)S(1)} %collective-permute-done.refs_1_, ...), custom_call_target="tpu_custom_call" | custom-call | flops 33554432 | bytes 4194304 | tf_op jit(solution)/shard_map/project/pallas_call | solution.py:289
  12.5 2.4 %collective-permute-start.3 = (bf16[32,2,128]{2,1,0:T(2,128)(2,1)S(1)}, bf16[32,2,128]{2,1,0:T(2,128)(2,1)S(1)}, u32[]{:S(2)}, u32[]{:S(2)}) collective-permute-start(bf16[32,2,128]{2,1,0:T(2,128)(2,1)S(1)} %get-tuple-element.18), channel_id=1, source_target_pairs={{0,3},{1,2},{2,1},{3,0},{4,7},{5,6},{6,5},{7,4},{8,11},{9,10},{10,... | collective-permute-start | bytes 49160 | tf_op jit(solution)/shard_map/ppermute | solution.py:333
  14.9 0.0 collective-permute-start.4
  14.9 1.1 %collective-permute-start.5 = (bf16[32,2,128]{2,1,0:T(2,128)(2,1)S(1)}, bf16[32,2,128]{2,1,0:T(2,128)(2,1)S(1)}, u32[]{:S(2)}, u32[]{:S(2)}) collective-permute-start(bf16[32,2,128]{2,1,0:T(2,128)(2,1)S(1)} %get-tuple-element.20), channel_id=1, source_target_pairs={{0,1},{1,0},{2,3},{3,2},{4,5},{5,4},{6,7},{7,6},{8,9},{9,8},{10,11... | collective-permute-start | bytes 49160 | tf_op jit(solution)/shard_map/ppermute | solution.py:333
  16.0 1.1 %collective-permute-done.3.refs_1_ = bf16[32,2,128]{2,1,0:T(2,128)(2,1)S(1)} collective-permute-done((bf16[32,2,128]{2,1,0:T(2,128)(2,1)S(1)}, bf16[32,2,128]{2,1,0:T(2,128)(2,1)S(1)}, u32[]{:S(2)}, u32[]{:S(2)}) %collective-permute-start.3) | collective-permute-done | bytes 16416 | tf_op jit(solution)/shard_map/ppermute | solution.py:333
  17.2 1.5 %collective-permute-done.4.refs_2_ = bf16[32,2,128]{2,1,0:T(2,128)(2,1)S(1)} collective-permute-done((bf16[32,2,128]{2,1,0:T(2,128)(2,1)S(1)}, bf16[32,2,128]{2,1,0:T(2,128)(2,1)S(1)}, u32[]{:S(2)}, u32[]{:S(2)}) %collective-permute-start.4) | collective-permute-done | bytes 16416 | tf_op jit(solution)/shard_map/ppermute | solution.py:333
  18.6 0.0 collective-permute-done.5.refs_3_
  18.7 0.7 %assemble.1 = bf16[4,32,2,128]{3,2,1,0:T(2,128)(2,1)} custom-call(bf16[32,2,128]{2,1,0:T(2,128)(2,1)S(1)} %get-tuple-element.17.refs_0_, bf16[32,2,128]{2,1,0:T(2,128)(2,1)S(1)} %collective-permute-done.3.refs_1_, bf16[32,2,128]{2,1,0:T(2,128)(2,1)S(1)} %collective-permute-done.4.refs_2_, bf16[32,2,128]{2,1,0:T(2,128)(2,1)S(1)} %collective-permute-done.5.refs_3_), custom_call_target="tpu_custom_call" | custom-call | tf_op jit(solution)/shard_map/assemble/pallas_call | solution.py:319
Async XLA Ops:
  3.3 7.2 %collective-permute-start = (bf16[64,512]{1,0:T(8,128)(2,1)S(1)}, bf16[64,512]{1,0:T(8,128)(2,1)S(1)}, u32[]{:S(2)}, u32[]{:S(2)}) collective-permute-start(bf16[64,512]{1,0:T(8,128)(2,1)S(1)} %get-tuple-element.14), channel_id=1, source_target_pairs={{0,3},{1,2},{2,1},{3,0},{4,7},{5,6},{6,5},{7,4},{8,11},{9,10},{10,... | collective-permute-start | bytes 196616 | tf_op jit(solution)/shard_map/ppermute | solution.py:333
  6.4 4.3 %collective-permute-start.1 = (bf16[64,512]{1,0:T(8,128)(2,1)S(1)}, bf16[64,512]{1,0:T(8,128)(2,1)S(1)}, u32[]{:S(2)}, u32[]{:S(2)}) collective-permute-start(bf16[64,512]{1,0:T(8,128)(2,1)S(1)} %get-tuple-element.15), channel_id=1, source_target_pairs={{0,2},{1,3},{2,0},{3,1},{4,6},{5,7},{6,4},{7,5},{8,10},{9,11},{10,... | collective-permute-start | bytes 196616 | tf_op jit(solution)/shard_map/ppermute | solution.py:333
  7.4 4.3 %collective-permute-start.2 = (bf16[64,512]{1,0:T(8,128)(2,1)S(1)}, bf16[64,512]{1,0:T(8,128)(2,1)S(1)}, u32[]{:S(2)}, u32[]{:S(2)}) collective-permute-start(bf16[64,512]{1,0:T(8,128)(2,1)S(1)} %get-tuple-element.16), channel_id=1, source_target_pairs={{0,1},{1,0},{2,3},{3,2},{4,5},{5,4},{6,7},{7,6},{8,9},{9,8},{10,11... | collective-permute-start | bytes 196616 | tf_op jit(solution)/shard_map/ppermute | solution.py:333
  12.5 4.7 %collective-permute-start.3 = (bf16[32,2,128]{2,1,0:T(2,128)(2,1)S(1)}, bf16[32,2,128]{2,1,0:T(2,128)(2,1)S(1)}, u32[]{:S(2)}, u32[]{:S(2)}) collective-permute-start(bf16[32,2,128]{2,1,0:T(2,128)(2,1)S(1)} %get-tuple-element.18), channel_id=1, source_target_pairs={{0,3},{1,2},{2,1},{3,0},{4,7},{5,6},{6,5},{7,4},{8,11},{9,10},{10,... | collective-permute-start | bytes 49160 | tf_op jit(solution)/shard_map/ppermute | solution.py:333
  14.9 3.7 %collective-permute-start.4 = (bf16[32,2,128]{2,1,0:T(2,128)(2,1)S(1)}, bf16[32,2,128]{2,1,0:T(2,128)(2,1)S(1)}, u32[]{:S(2)}, u32[]{:S(2)}) collective-permute-start(bf16[32,2,128]{2,1,0:T(2,128)(2,1)S(1)} %get-tuple-element.19), channel_id=1, source_target_pairs={{0,2},{1,3},{2,0},{3,1},{4,6},{5,7},{6,4},{7,5},{8,10},{9,11},{10,... | collective-permute-start | bytes 49160 | tf_op jit(solution)/shard_map/ppermute | solution.py:333
  14.9 3.7 %collective-permute-start.5 = (bf16[32,2,128]{2,1,0:T(2,128)(2,1)S(1)}, bf16[32,2,128]{2,1,0:T(2,128)(2,1)S(1)}, u32[]{:S(2)}, u32[]{:S(2)}) collective-permute-start(bf16[32,2,128]{2,1,0:T(2,128)(2,1)S(1)} %get-tuple-element.20), channel_id=1, source_target_pairs={{0,1},{1,0},{2,3},{3,2},{4,5},{5,4},{6,7},{7,6},{8,9},{9,8},{10,11... | collective-permute-start | bytes 49160 | tf_op jit(solution)/shard_map/ppermute | solution.py:333

commit v21 on v18

--- a/solution.py
+++ b/solution.py
@@ -19,6 +19,17 @@
 
 def order(owners):
     return [0] + list(range(owners - 1, 0, -1))
+
+
+def choose(count, cases, act):
+    if len(cases) == 1:
+        act(cases[0])
+        return
+    lax.cond(
+        functools.reduce(jnp.logical_and, [c == n for c, n in zip(count, cases[0])]),
+        lambda: act(cases[0]),
+        lambda: choose(count, cases[1:], act),
+    )
 
 
 def attend_kernel(owners, lengths_hbm, query_hbm, scales_hbm, cache, *refs):
@@ -101,10 +112,9 @@
     for first in range(0, requests, 2):
         group = tuple(range(first, min(first + 2, requests)))
         count = [(lengths[r] + (block - 1)) // block for r in group]
-        for live in itertools.product(range(1, blocks + 1), repeat=len(group)):
-            @pl.when(functools.reduce(jnp.logical_and, [c == n for c, n in zip(count, live)]))
-            def _():
-                several(group, live)
+        cases = list(itertools.product(range(1, blocks + 1), repeat=len(group)))
+        cases.sort(key=lambda live: (sum(live) <= blocks, sum(live), -max(live)))
+        choose(count, cases, functools.partial(several, group))
 
     for out, k in zip(outs, order(owners)):
         mine = pl.ds(pl.multiple_of((me ^ k) * rows, rows), rows)

time: 19.2 us -> 19.6 us (1.021); the launches traced: 19.1 us -> 19.3 us
  starting transfers between devices: 9.02 us -> 8.05 us
  Pallas kernels: 6.05 us -> 6.89 us
  waiting for transfers between devices: 4.04 us -> 4.35 us
    ppermute x6, starting transfers between devices: 9.02 us -> 8.05 us  [exchange(): lax.ppermute(part, 'tp', [(i, i ^ k) for i in range(owners)])]
    pallas_call x1, Pallas kernels: 2.34 us -> 3.19 us  [attend(): pl.pallas_call(functools.partial(attend_kernel, owners), out_shape=[part]...]
    ppermute x6, waiting for transfers between devices: 4.04 us -> 4.35 us  [exchange(): lax.ppermute(part, 'tp', [(i, i ^ k) for i in range(owners)])]
  transfers between devices with their start and end apart: 6 -> 6, of which waited for: 4 -> 5; matrix products, arithmetic and copies ran while one was open for 0% -> 0% of each run, Pallas kernels for 11% -> 11%
where the time goes in v21:
time: 19.6 us; the launch traced here: 19.3 us
  starting transfers between devices  8.05 us (41%)
  Pallas kernels  6.89 us (35%)
  waiting for transfers between devices  4.35 us (22%)
    ppermute x6, starting transfers between devices, exchange(): lax.ppermute(part, 'tp', [(i, i ^ k) for i in range(owners)])  8.05 us
    ppermute x6, waiting for transfers between devices, exchange(): lax.ppermute(part, 'tp', [(i, i ^ k) for i in range(owners)])  4.35 us
    pallas_call x1, Pallas kernels, attend(): pl.pallas_call(functools.partial(attend_kernel, owners), out_shape=[part]...  3.19 us
    pallas_call x1, Pallas kernels, stage(): pl.pallas_call(stage_kernel, out_shape=jax.ShapeDtypeStruct(maps.shape, m...  2.2 us
    pallas_call x1, Pallas kernels, project(): pl.pallas_call(functools.partial(project_kernel, count), out_shape=[jax.S...  0.86 us
    pallas_call x1, Pallas kernels, assemble(): pl.pallas_call(functools.partial(assemble_kernel, owners), out_shape=pltp...  0.66 us
  transfers between devices with their start and end apart: 6, of which 5 were waited for; matrix products, arithmetic and copies ran while one was open for 0% of the time, Pallas kernels for 11%

profile of v21, /device:TPU:0, one launch (start us, length us, event | category | flops | bytes accessed | tf_op | source)
XLA Modules:
  0.0 19.3 jit_solution(1228775163366146639)
XLA Ops:
  0.0 3.2 %attend.1 = (bf16[64,512]{1,0:T(8,128)(2,1)S(1)}, bf16[64,512]{1,0:T(8,128)(2,1)S(1)}, bf16[64,512]{1,0:T(8,128)(2,1)S(1)}, bf16[64,512]{1,0:T(8,128)(2,1)S(1)}) custom-call(s32[2]{0:T(128)} %lengths_hbm.1, bf16[2,576,128]{2,1,0:T(8,128)(2,1)} %bitcast.8, f32[576]{0:T(1024)} %scales_hbm.1, bf16[2,576,1536]{2,1,0:T(8,128)(2,1)} %bitcast.7), custom_call_target="tpu_custom_call" | custom-call | flops 905969664 | bytes 3538944 | tf_op jit(solution)/shard_map/attend/pallas_call | solution.py:134
  3.2 3.5 %collective-permute-start = (bf16[64,512]{1,0:T(8,128)(2,1)S(1)}, bf16[64,512]{1,0:T(8,128)(2,1)S(1)}, u32[]{:S(2)}, u32[]{:S(2)}) collective-permute-start(bf16[64,512]{1,0:T(8,128)(2,1)S(1)} %get-tuple-element.14), channel_id=1, source_target_pairs={{0,3},{1,2},{2,1},{3,0},{4,7},{5,6},{6,5},{7,4},{8,11},{9,10},{10,... | collective-permute-start | bytes 196616 | tf_op jit(solution)/shard_map/ppermute | solution.py:245
  6.7 1.0 %collective-permute-start.1 = (bf16[64,512]{1,0:T(8,128)(2,1)S(1)}, bf16[64,512]{1,0:T(8,128)(2,1)S(1)}, u32[]{:S(2)}, u32[]{:S(2)}) collective-permute-start(bf16[64,512]{1,0:T(8,128)(2,1)S(1)} %get-tuple-element.15), channel_id=1, source_target_pairs={{0,2},{1,3},{2,0},{3,1},{4,6},{5,7},{6,4},{7,5},{8,10},{9,11},{10,... | collective-permute-start | bytes 196616 | tf_op jit(solution)/shard_map/ppermute | solution.py:245
  7.7 0.0 collective-permute-start.2
  7.7 2.2 %stage.1.refs_4_ = bf16[32,512,128]{2,1,0:T(8,128)(2,1)S(1)} custom-call(bf16[32,512,128]{2,1,0:T(8,128)(2,1)} %maps_hbm.1, bf16[64,512]{1,0:T(8,128)(2,1)S(1)} %get-tuple-element.13.after.refs_0_), custom_call_target="tpu_custom_call" | custom-call | bytes 8388608 | tf_op jit(solution)/shard_map/stage/pallas_call | solution.py:165
  9.9 0.0 collective-permute-done.refs_1_
  9.9 1.1 %collective-permute-done.1.refs_2_ = bf16[64,512]{1,0:T(8,128)(2,1)S(1)} collective-permute-done((bf16[64,512]{1,0:T(8,128)(2,1)S(1)}, bf16[64,512]{1,0:T(8,128)(2,1)S(1)}, u32[]{:S(2)}, u32[]{:S(2)}) %collective-permute-start.1) | collective-permute-done | bytes 65568 | tf_op jit(solution)/shard_map/ppermute | solution.py:245
  11.0 1.0 %collective-permute-done.2.refs_3_ = bf16[64,512]{1,0:T(8,128)(2,1)S(1)} collective-permute-done((bf16[64,512]{1,0:T(8,128)(2,1)S(1)}, bf16[64,512]{1,0:T(8,128)(2,1)S(1)}, u32[]{:S(2)}, u32[]{:S(2)}) %collective-permute-start.2) | collective-permute-done | bytes 65568 | tf_op jit(solution)/shard_map/ppermute | solution.py:245
  11.9 0.9 %project.1 = (bf16[32,2,128]{2,1,0:T(2,128)(2,1)S(1)}, bf16[32,2,128]{2,1,0:T(2,128)(2,1)S(1)}, bf16[32,2,128]{2,1,0:T(2,128)(2,1)S(1)}, bf16[32,2,128]{2,1,0:T(2,128)(2,1)S(1)}) custom-call(bf16[64,512]{1,0:T(8,128)(2,1)S(1)} %get-tuple-element.13.after.refs_0_, bf16[64,512]{1,0:T(8,128)(2,1)S(1)} %collective-permute-done.refs_1_, ...), custom_call_target="tpu_custom_call" | custom-call | flops 33554432 | bytes 4194304 | tf_op jit(solution)/shard_map/project/pallas_call | solution.py:201
  12.8 1.6 %collective-permute-start.3 = (bf16[32,2,128]{2,1,0:T(2,128)(2,1)S(1)}, bf16[32,2,128]{2,1,0:T(2,128)(2,1)S(1)}, u32[]{:S(2)}, u32[]{:S(2)}) collective-permute-start(bf16[32,2,128]{2,1,0:T(2,128)(2,1)S(1)} %get-tuple-element.18), channel_id=1, source_target_pairs={{0,3},{1,2},{2,1},{3,0},{4,7},{5,6},{6,5},{7,4},{8,11},{9,10},{10,... | collective-permute-start | bytes 49160 | tf_op jit(solution)/shard_map/ppermute | solution.py:245
  14.3 0.6 %collective-permute-start.4 = (bf16[32,2,128]{2,1,0:T(2,128)(2,1)S(1)}, bf16[32,2,128]{2,1,0:T(2,128)(2,1)S(1)}, u32[]{:S(2)}, u32[]{:S(2)}) collective-permute-start(bf16[32,2,128]{2,1,0:T(2,128)(2,1)S(1)} %get-tuple-element.19), channel_id=1, source_target_pairs={{0,2},{1,3},{2,0},{3,1},{4,6},{5,7},{6,4},{7,5},{8,10},{9,11},{10,... | collective-permute-start | bytes 49160 | tf_op jit(solution)/shard_map/ppermute | solution.py:245
  14.9 1.4 %collective-permute-start.5 = (bf16[32,2,128]{2,1,0:T(2,128)(2,1)S(1)}, bf16[32,2,128]{2,1,0:T(2,128)(2,1)S(1)}, u32[]{:S(2)}, u32[]{:S(2)}) collective-permute-start(bf16[32,2,128]{2,1,0:T(2,128)(2,1)S(1)} %get-tuple-element.20), channel_id=1, source_target_pairs={{0,1},{1,0},{2,3},{3,2},{4,5},{5,4},{6,7},{7,6},{8,9},{9,8},{10,11... | collective-permute-start | bytes 49160 | tf_op jit(solution)/shard_map/ppermute | solution.py:245
  16.3 1.1 %collective-permute-done.3.refs_1_ = bf16[32,2,128]{2,1,0:T(2,128)(2,1)S(1)} collective-permute-done((bf16[32,2,128]{2,1,0:T(2,128)(2,1)S(1)}, bf16[32,2,128]{2,1,0:T(2,128)(2,1)S(1)}, u32[]{:S(2)}, u32[]{:S(2)}) %collective-permute-start.3) | collective-permute-done | bytes 16416 | tf_op jit(solution)/shard_map/ppermute | solution.py:245
  17.5 0.6 %collective-permute-done.4.refs_2_ = bf16[32,2,128]{2,1,0:T(2,128)(2,1)S(1)} collective-permute-done((bf16[32,2,128]{2,1,0:T(2,128)(2,1)S(1)}, bf16[32,2,128]{2,1,0:T(2,128)(2,1)S(1)}, u32[]{:S(2)}, u32[]{:S(2)}) %collective-permute-start.4) | collective-permute-done | bytes 16416 | tf_op jit(solution)/shard_map/ppermute | solution.py:245
  18.1 0.6 %collective-permute-done.5.refs_3_ = bf16[32,2,128]{2,1,0:T(2,128)(2,1)S(1)} collective-permute-done((bf16[32,2,128]{2,1,0:T(2,128)(2,1)S(1)}, bf16[32,2,128]{2,1,0:T(2,128)(2,1)S(1)}, u32[]{:S(2)}, u32[]{:S(2)}) %collective-permute-start.5) | collective-permute-done | bytes 16416 | tf_op jit(solution)/shard_map/ppermute | solution.py:245
  18.7 0.7 %assemble.1 = bf16[4,32,2,128]{3,2,1,0:T(2,128)(2,1)} custom-call(bf16[32,2,128]{2,1,0:T(2,128)(2,1)S(1)} %get-tuple-element.17.refs_0_, bf16[32,2,128]{2,1,0:T(2,128)(2,1)S(1)} %collective-permute-done.3.refs_1_, bf16[32,2,128]{2,1,0:T(2,128)(2,1)S(1)} %collective-permute-done.4.refs_2_, bf16[32,2,128]{2,1,0:T(2,128)(2,1)S(1)} %collective-permute-done.5.refs_3_), custom_call_target="tpu_custom_call" | custom-call | tf_op jit(solution)/shard_map/assemble/pallas_call | solution.py:231
Async XLA Ops:
  3.2 6.7 %collective-permute-start = (bf16[64,512]{1,0:T(8,128)(2,1)S(1)}, bf16[64,512]{1,0:T(8,128)(2,1)S(1)}, u32[]{:S(2)}, u32[]{:S(2)}) collective-permute-start(bf16[64,512]{1,0:T(8,128)(2,1)S(1)} %get-tuple-element.14), channel_id=1, source_target_pairs={{0,3},{1,2},{2,1},{3,0},{4,7},{5,6},{6,5},{7,4},{8,11},{9,10},{10,... | collective-permute-start | bytes 196616 | tf_op jit(solution)/shard_map/ppermute | solution.py:245
  6.7 4.3 %collective-permute-start.1 = (bf16[64,512]{1,0:T(8,128)(2,1)S(1)}, bf16[64,512]{1,0:T(8,128)(2,1)S(1)}, u32[]{:S(2)}, u32[]{:S(2)}) collective-permute-start(bf16[64,512]{1,0:T(8,128)(2,1)S(1)} %get-tuple-element.15), channel_id=1, source_target_pairs={{0,2},{1,3},{2,0},{3,1},{4,6},{5,7},{6,4},{7,5},{8,10},{9,11},{10,... | collective-permute-start | bytes 196616 | tf_op jit(solution)/shard_map/ppermute | solution.py:245
  7.7 4.3 %collective-permute-start.2 = (bf16[64,512]{1,0:T(8,128)(2,1)S(1)}, bf16[64,512]{1,0:T(8,128)(2,1)S(1)}, u32[]{:S(2)}, u32[]{:S(2)}) collective-permute-start(bf16[64,512]{1,0:T(8,128)(2,1)S(1)} %get-tuple-element.16), channel_id=1, source_target_pairs={{0,1},{1,0},{2,3},{3,2},{4,5},{5,4},{6,7},{7,6},{8,9},{9,8},{10,11... | collective-permute-start | bytes 196616 | tf_op jit(solution)/shard_map/ppermute | solution.py:245
  12.8 4.7 %collective-permute-start.3 = (bf16[32,2,128]{2,1,0:T(2,128)(2,1)S(1)}, bf16[32,2,128]{2,1,0:T(2,128)(2,1)S(1)}, u32[]{:S(2)}, u32[]{:S(2)}) collective-permute-start(bf16[32,2,128]{2,1,0:T(2,128)(2,1)S(1)} %get-tuple-element.18), channel_id=1, source_target_pairs={{0,3},{1,2},{2,1},{3,0},{4,7},{5,6},{6,5},{7,4},{8,11},{9,10},{10,... | collective-permute-start | bytes 49160 | tf_op jit(solution)/shard_map/ppermute | solution.py:245
  14.3 3.7 %collective-permute-start.4 = (bf16[32,2,128]{2,1,0:T(2,128)(2,1)S(1)}, bf16[32,2,128]{2,1,0:T(2,128)(2,1)S(1)}, u32[]{:S(2)}, u32[]{:S(2)}) collective-permute-start(bf16[32,2,128]{2,1,0:T(2,128)(2,1)S(1)} %get-tuple-element.19), channel_id=1, source_target_pairs={{0,2},{1,3},{2,0},{3,1},{4,6},{5,7},{6,4},{7,5},{8,10},{9,11},{10,... | collective-permute-start | bytes 49160 | tf_op jit(solution)/shard_map/ppermute | solution.py:245
  14.9 3.7 %collective-permute-start.5 = (bf16[32,2,128]{2,1,0:T(2,128)(2,1)S(1)}, bf16[32,2,128]{2,1,0:T(2,128)(2,1)S(1)}, u32[]{:S(2)}, u32[]{:S(2)}) collective-permute-start(bf16[32,2,128]{2,1,0:T(2,128)(2,1)S(1)} %get-tuple-element.20), channel_id=1, source_target_pairs={{0,1},{1,0},{2,3},{3,2},{4,5},{5,4},{6,7},{7,6},{8,9},{9,8},{10,11... | collective-permute-start | bytes 49160 | tf_op jit(solution)/shard_map/ppermute | solution.py:245

commit v22 on v15

--- a/solution.py
+++ b/solution.py
@@ -236,8 +236,16 @@
 
 def exchange(parts):
     owners = len(parts)
+    groups = lax.axis_size("grp")
+
+    def pairs(k):
+        return [
+            (g * owners + i, (g ^ 1) * owners + (i ^ k))
+            for g in range(groups) for i in range(owners)
+        ]
+
     return [
-        lax.ppermute(part, "tp", [(i, i ^ k) for i in range(owners)]) if k else part
+        lax.ppermute(part, ("grp", "tp"), pairs(k)) if k else part
         for k, part in zip(order(owners), parts)
     ]
 

time: 19.6 us -> 18.7 us (0.954); the launches traced: 19.2 us -> 18.9 us
  starting transfers between devices: 9.36 us -> 8.21 us
  waiting for transfers between devices: 3.77 us -> 4.65 us
    ppermute x6, starting transfers between devices: 9.36 us -> 8.21 us  [exchange(): lax.ppermute(part, ('grp', 'tp'), pairs(k))]
    ppermute x6, waiting for transfers between devices: 3.77 us -> 4.65 us  [exchange(): lax.ppermute(part, ('grp', 'tp'), pairs(k))]
  transfers between devices with their start and end apart: 6 -> 6, of which waited for: 4 -> 5; matrix products, arithmetic and copies ran while one was open for 0% -> 0% of each run, Pallas kernels for 11% -> 12%
where the time goes in v22:
time: 18.7 us; the launch traced here: 18.9 us
  starting transfers between devices  8.21 us (44%)
  Pallas kernels  6.05 us (32%)
  waiting for transfers between devices  4.65 us (25%)
    ppermute x6, starting transfers between devices, exchange(): lax.ppermute(part, ('grp', 'tp'), pairs(k))  8.21 us
    ppermute x6, waiting for transfers between devices, exchange(): lax.ppermute(part, ('grp', 'tp'), pairs(k))  4.65 us
    pallas_call x1, Pallas kernels, attend(): pl.pallas_call(functools.partial(attend_kernel, owners), out_shape=[part]...  2.34 us
    pallas_call x1, Pallas kernels, stage(): pl.pallas_call(stage_kernel, out_shape=jax.ShapeDtypeStruct(maps.shape, m...  2.2 us
    pallas_call x1, Pallas kernels, project(): pl.pallas_call(functools.partial(project_kernel, count), out_shape=[jax.S...  0.86 us
    pallas_call x1, Pallas kernels, assemble(): pl.pallas_call(functools.partial(assemble_kernel, owners), out_shape=pltp...  0.66 us
  transfers between devices with their start and end apart: 6, of which 5 were waited for; matrix products, arithmetic and copies ran while one was open for 0% of the time, Pallas kernels for 12%

profile of v22, /device:TPU:0, one launch (start us, length us, event | category | flops | bytes accessed | tf_op | source)
XLA Modules:
  0.0 18.9 jit_solution(13000877785972094066)
XLA Ops:
  0.0 2.3 %attend.1 = (bf16[64,512]{1,0:T(8,128)(2,1)S(1)}, bf16[64,512]{1,0:T(8,128)(2,1)S(1)}, bf16[64,512]{1,0:T(8,128)(2,1)S(1)}, bf16[64,512]{1,0:T(8,128)(2,1)S(1)}) custom-call(s32[2]{0:T(128)} %lengths_hbm.1, bf16[2,576,128]{2,1,0:T(8,128)(2,1)} %bitcast.8, f32[576]{0:T(1024)} %scales_hbm.1, bf16[2,576,1536]{2,1,0:T(8,128)(2,1)} %bitcast.7), custom_call_target="tpu_custom_call" | custom-call | flops 905969664 | bytes 3538944 | tf_op jit(solution)/shard_map/attend/pallas_call | solution.py:129
  2.3 4.3 %collective-permute-start = (bf16[64,512]{1,0:T(8,128)(2,1)S(1)}, bf16[64,512]{1,0:T(8,128)(2,1)S(1)}, u32[]{:S(2)}, u32[]{:S(2)}) collective-permute-start(bf16[64,512]{1,0:T(8,128)(2,1)S(1)} %get-tuple-element.14), channel_id=1, source_target_pairs={{0,7},{1,6},{2,5},{3,4},{4,3},{5,2},{6,1},{7,0},{8,15},{9,14},{10,... | collective-permute-start | bytes 196616 | tf_op jit(solution)/shard_map/ppermute | solution.py:248
  6.6 0.8 %collective-permute-start.1 = (bf16[64,512]{1,0:T(8,128)(2,1)S(1)}, bf16[64,512]{1,0:T(8,128)(2,1)S(1)}, u32[]{:S(2)}, u32[]{:S(2)}) collective-permute-start(bf16[64,512]{1,0:T(8,128)(2,1)S(1)} %get-tuple-element.15), channel_id=1, source_target_pairs={{0,6},{1,7},{2,4},{3,5},{4,2},{5,3},{6,0},{7,1},{8,14},{9,15},{10,... | collective-permute-start | bytes 196616 | tf_op jit(solution)/shard_map/ppermute | solution.py:248
  7.4 0.1 collective-permute-start.2
  7.5 2.2 %stage.1.refs_4_ = bf16[32,512,128]{2,1,0:T(8,128)(2,1)S(1)} custom-call(bf16[32,512,128]{2,1,0:T(8,128)(2,1)} %maps_hbm.1, bf16[64,512]{1,0:T(8,128)(2,1)S(1)} %get-tuple-element.13.after.refs_0_), custom_call_target="tpu_custom_call" | custom-call | bytes 8388608 | tf_op jit(solution)/shard_map/stage/pallas_call | solution.py:160
  9.7 0.0 collective-permute-done.refs_1_
  9.8 0.6 %collective-permute-done.1.refs_2_ = bf16[64,512]{1,0:T(8,128)(2,1)S(1)} collective-permute-done((bf16[64,512]{1,0:T(8,128)(2,1)S(1)}, bf16[64,512]{1,0:T(8,128)(2,1)S(1)}, u32[]{:S(2)}, u32[]{:S(2)}) %collective-permute-start.1) | collective-permute-done | bytes 65568 | tf_op jit(solution)/shard_map/ppermute | solution.py:248
  10.3 1.4 %collective-permute-done.2.refs_3_ = bf16[64,512]{1,0:T(8,128)(2,1)S(1)} collective-permute-done((bf16[64,512]{1,0:T(8,128)(2,1)S(1)}, bf16[64,512]{1,0:T(8,128)(2,1)S(1)}, u32[]{:S(2)}, u32[]{:S(2)}) %collective-permute-start.2) | collective-permute-done | bytes 65568 | tf_op jit(solution)/shard_map/ppermute | solution.py:248
  11.7 0.9 %project.1 = (bf16[32,2,128]{2,1,0:T(2,128)(2,1)S(1)}, bf16[32,2,128]{2,1,0:T(2,128)(2,1)S(1)}, bf16[32,2,128]{2,1,0:T(2,128)(2,1)S(1)}, bf16[32,2,128]{2,1,0:T(2,128)(2,1)S(1)}) custom-call(bf16[64,512]{1,0:T(8,128)(2,1)S(1)} %get-tuple-element.13.after.refs_0_, bf16[64,512]{1,0:T(8,128)(2,1)S(1)} %collective-permute-done.refs_1_, ...), custom_call_target="tpu_custom_call" | custom-call | flops 33554432 | bytes 4194304 | tf_op jit(solution)/shard_map/project/pallas_call | solution.py:196
  12.6 1.1 %collective-permute-start.3 = (bf16[32,2,128]{2,1,0:T(2,128)(2,1)S(1)}, bf16[32,2,128]{2,1,0:T(2,128)(2,1)S(1)}, u32[]{:S(2)}, u32[]{:S(2)}) collective-permute-start(bf16[32,2,128]{2,1,0:T(2,128)(2,1)S(1)} %get-tuple-element.18), channel_id=1, source_target_pairs={{0,7},{1,6},{2,5},{3,4},{4,3},{5,2},{6,1},{7,0},{8,15},{9,14},{10,... | collective-permute-start | bytes 49160 | tf_op jit(solution)/shard_map/ppermute | solution.py:248
  13.7 1.5 %collective-permute-start.4 = (bf16[32,2,128]{2,1,0:T(2,128)(2,1)S(1)}, bf16[32,2,128]{2,1,0:T(2,128)(2,1)S(1)}, u32[]{:S(2)}, u32[]{:S(2)}) collective-permute-start(bf16[32,2,128]{2,1,0:T(2,128)(2,1)S(1)} %get-tuple-element.19), channel_id=1, source_target_pairs={{0,6},{1,7},{2,4},{3,5},{4,2},{5,3},{6,0},{7,1},{8,14},{9,15},{10,... | collective-permute-start | bytes 49160 | tf_op jit(solution)/shard_map/ppermute | solution.py:248
  15.1 0.5 %collective-permute-start.5 = (bf16[32,2,128]{2,1,0:T(2,128)(2,1)S(1)}, bf16[32,2,128]{2,1,0:T(2,128)(2,1)S(1)}, u32[]{:S(2)}, u32[]{:S(2)}) collective-permute-start(bf16[32,2,128]{2,1,0:T(2,128)(2,1)S(1)} %get-tuple-element.20), channel_id=1, source_target_pairs={{0,5},{1,4},{2,7},{3,6},{4,1},{5,0},{6,3},{7,2},{8,13},{9,12},{10,... | collective-permute-start | bytes 49160 | tf_op jit(solution)/shard_map/ppermute | solution.py:248
  15.6 1.1 %collective-permute-done.3.refs_1_ = bf16[32,2,128]{2,1,0:T(2,128)(2,1)S(1)} collective-permute-done((bf16[32,2,128]{2,1,0:T(2,128)(2,1)S(1)}, bf16[32,2,128]{2,1,0:T(2,128)(2,1)S(1)}, u32[]{:S(2)}, u32[]{:S(2)}) %collective-permute-start.3) | collective-permute-done | bytes 16416 | tf_op jit(solution)/shard_map/ppermute | solution.py:248
  16.7 0.4 %collective-permute-done.4.refs_2_ = bf16[32,2,128]{2,1,0:T(2,128)(2,1)S(1)} collective-permute-done((bf16[32,2,128]{2,1,0:T(2,128)(2,1)S(1)}, bf16[32,2,128]{2,1,0:T(2,128)(2,1)S(1)}, u32[]{:S(2)}, u32[]{:S(2)}) %collective-permute-start.4) | collective-permute-done | bytes 16416 | tf_op jit(solution)/shard_map/ppermute | solution.py:248
  17.0 1.2 %collective-permute-done.5.refs_3_ = bf16[32,2,128]{2,1,0:T(2,128)(2,1)S(1)} collective-permute-done((bf16[32,2,128]{2,1,0:T(2,128)(2,1)S(1)}, bf16[32,2,128]{2,1,0:T(2,128)(2,1)S(1)}, u32[]{:S(2)}, u32[]{:S(2)}) %collective-permute-start.5) | collective-permute-done | bytes 16416 | tf_op jit(solution)/shard_map/ppermute | solution.py:248
  18.3 0.7 %assemble.1 = bf16[4,32,2,128]{3,2,1,0:T(2,128)(2,1)} custom-call(bf16[32,2,128]{2,1,0:T(2,128)(2,1)S(1)} %get-tuple-element.17.refs_0_, bf16[32,2,128]{2,1,0:T(2,128)(2,1)S(1)} %collective-permute-done.3.refs_1_, bf16[32,2,128]{2,1,0:T(2,128)(2,1)S(1)} %collective-permute-done.4.refs_2_, bf16[32,2,128]{2,1,0:T(2,128)(2,1)S(1)} %collective-permute-done.5.refs_3_), custom_call_target="tpu_custom_call" | custom-call | tf_op jit(solution)/shard_map/assemble/pallas_call | solution.py:226
Async XLA Ops:
  2.3 7.4 %collective-permute-start = (bf16[64,512]{1,0:T(8,128)(2,1)S(1)}, bf16[64,512]{1,0:T(8,128)(2,1)S(1)}, u32[]{:S(2)}, u32[]{:S(2)}) collective-permute-start(bf16[64,512]{1,0:T(8,128)(2,1)S(1)} %get-tuple-element.14), channel_id=1, source_target_pairs={{0,7},{1,6},{2,5},{3,4},{4,3},{5,2},{6,1},{7,0},{8,15},{9,14},{10,... | collective-permute-start | bytes 196616 | tf_op jit(solution)/shard_map/ppermute | solution.py:248
  6.6 3.7 %collective-permute-start.1 = (bf16[64,512]{1,0:T(8,128)(2,1)S(1)}, bf16[64,512]{1,0:T(8,128)(2,1)S(1)}, u32[]{:S(2)}, u32[]{:S(2)}) collective-permute-start(bf16[64,512]{1,0:T(8,128)(2,1)S(1)} %get-tuple-element.15), channel_id=1, source_target_pairs={{0,6},{1,7},{2,4},{3,5},{4,2},{5,3},{6,0},{7,1},{8,14},{9,15},{10,... | collective-permute-start | bytes 196616 | tf_op jit(solution)/shard_map/ppermute | solution.py:248
  7.4 4.3 %collective-permute-start.2 = (bf16[64,512]{1,0:T(8,128)(2,1)S(1)}, bf16[64,512]{1,0:T(8,128)(2,1)S(1)}, u32[]{:S(2)}, u32[]{:S(2)}) collective-permute-start(bf16[64,512]{1,0:T(8,128)(2,1)S(1)} %get-tuple-element.16), channel_id=1, source_target_pairs={{0,5},{1,4},{2,7},{3,6},{4,1},{5,0},{6,3},{7,2},{8,13},{9,12},{10,... | collective-permute-start | bytes 196616 | tf_op jit(solution)/shard_map/ppermute | solution.py:248
  12.6 4.1 %collective-permute-start.3 = (bf16[32,2,128]{2,1,0:T(2,128)(2,1)S(1)}, bf16[32,2,128]{2,1,0:T(2,128)(2,1)S(1)}, u32[]{:S(2)}, u32[]{:S(2)}) collective-permute-start(bf16[32,2,128]{2,1,0:T(2,128)(2,1)S(1)} %get-tuple-element.18), channel_id=1, source_target_pairs={{0,7},{1,6},{2,5},{3,4},{4,3},{5,2},{6,1},{7,0},{8,15},{9,14},{10,... | collective-permute-start | bytes 49160 | tf_op jit(solution)/shard_map/ppermute | solution.py:248
  13.7 3.4 %collective-permute-start.4 = (bf16[32,2,128]{2,1,0:T(2,128)(2,1)S(1)}, bf16[32,2,128]{2,1,0:T(2,128)(2,1)S(1)}, u32[]{:S(2)}, u32[]{:S(2)}) collective-permute-start(bf16[32,2,128]{2,1,0:T(2,128)(2,1)S(1)} %get-tuple-element.19), channel_id=1, source_target_pairs={{0,6},{1,7},{2,4},{3,5},{4,2},{5,3},{6,0},{7,1},{8,14},{9,15},{10,... | collective-permute-start | bytes 49160 | tf_op jit(solution)/shard_map/ppermute | solution.py:248
  15.1 3.2 %collective-permute-start.5 = (bf16[32,2,128]{2,1,0:T(2,128)(2,1)S(1)}, bf16[32,2,128]{2,1,0:T(2,128)(2,1)S(1)}, u32[]{:S(2)}, u32[]{:S(2)}) collective-permute-start(bf16[32,2,128]{2,1,0:T(2,128)(2,1)S(1)} %get-tuple-element.20), channel_id=1, source_target_pairs={{0,5},{1,4},{2,7},{3,6},{4,1},{5,0},{6,3},{7,2},{8,13},{9,12},{10,... | collective-permute-start | bytes 49160 | tf_op jit(solution)/shard_map/ppermute | solution.py:248

commit v23 on v22

--- a/solution.py
+++ b/solution.py
@@ -14,6 +14,7 @@
 EXP2_SCALE = SOFTMAX_SCALE * math.log2(math.e)
 BLOCK = 512
 LANES = 128
+PIECES = 4
 GROUP_ROWS = 16
 
 
@@ -22,7 +23,7 @@
 
 
 def attend_kernel(owners, lengths_hbm, query_hbm, scales_hbm, cache, *refs):
-    outs, (latents, lengths, query, scales, keys, sems, small_sems) = refs[:owners], refs[owners:]
+    outs, (latents, lengths, query, scales, keys, sems, small_sems, first_sems) = refs[:owners], refs[owners:]
     requests, channels, heads = query.shape
     rows, rank = outs[0].shape
     cache_len = cache.shape[2]
@@ -30,9 +31,26 @@
     blocks = cache_len // block
     me = lax.axis_index("tp")
 
+    def pieces(r, b):
+        span = pl.ds(b * block, block)
+        if (r, b) != (0, 0):
+            return [pltpu.make_async_copy(cache.at[r, :, span], keys.at[r, :, span], sems.at[r, b])]
+        size = channels // PIECES
+        return [
+            pltpu.make_async_copy(
+                cache.at[r, pl.ds(i * size, size), span], keys.at[r, pl.ds(i * size, size), span],
+                first_sems.at[i],
+            )
+            for i in range(PIECES)
+        ]
+
     def fetch(r, b):
-        span = pl.ds(b * block, block)
-        return pltpu.make_async_copy(cache.at[r, :, span], keys.at[r, :, span], sems.at[r, b])
+        for copy in pieces(r, b):
+            copy.start()
+
+    def arrive(r, b):
+        for copy in pieces(r, b):
+            copy.wait()
 
     def ask(r):
         return pltpu.make_async_copy(query_hbm.at[r], query.at[r], small_sems.at[2 + r])
@@ -43,13 +61,13 @@
     scales_copy.start()
     for r in range(requests):
         ask(r).start()
-        fetch(r, 0).start()
+        fetch(r, 0)
     lengths_copy.wait()
     for r in range(requests):
         for b in range(1, blocks):
             @pl.when(b * block < lengths[r])
             def _():
-                fetch(r, b).start()
+                fetch(r, b)
     scales_copy.wait()
     scale_row = scales[...].reshape(1, channels)
 
@@ -60,7 +78,7 @@
     def score(scaled, r, b, live):
         if r not in scaled:
             scaled[r] = scale(r)
-        fetch(r, b).wait()
+        arrive(r, b)
         span = slice(b * block, (b + 1) * block)
         part = jnp.dot(scaled[r], keys[r, :, span], preferred_element_type=jnp.float32)
         if b == live - 1:
@@ -139,6 +157,7 @@
             pltpu.VMEM((requests, channels, cache_len), jnp.bfloat16),
             pltpu.SemaphoreType.DMA((requests, cache_len // min(BLOCK, cache_len))),
             pltpu.SemaphoreType.DMA((2 + requests,)),
+            pltpu.SemaphoreType.DMA((PIECES,)),
         ],
         compiler_params=pltpu.CompilerParams(vmem_limit_bytes=24 * 2**20),
         cost_estimate=pl.CostEstimate(
@@ -237,10 +256,11 @@
 def exchange(parts):
     owners = len(parts)
     groups = lax.axis_size("grp")
+    flip = 1 - groups % 2
 
     def pairs(k):
         return [
-            (g * owners + i, (g ^ 1) * owners + (i ^ k))
+            (g * owners + i, (g ^ flip) * owners + (i ^ k))
             for g in range(groups) for i in range(owners)
         ]
 

time: 18.7 us -> 18.9 us (1.011); the launches traced: 18.9 us -> 18.7 us
  Pallas kernels: 6.05 us -> 7.07 us
  waiting for transfers between devices: 4.65 us -> 4.01 us
  starting transfers between devices: 8.21 us -> 7.59 us
    pallas_call x1, Pallas kernels: 2.34 us -> 3.36 us  [attend(): pl.pallas_call(functools.partial(attend_kernel, owners), out_shape=[part]...]
    ppermute x6, waiting for transfers between devices: 4.65 us -> 4.01 us  [exchange(): lax.ppermute(part, ('grp', 'tp'), pairs(k))]
    ppermute x6, starting transfers between devices: 8.21 us -> 7.59 us  [exchange(): lax.ppermute(part, ('grp', 'tp'), pairs(k))]
where the time goes in v23:
time: 18.9 us; the launch traced here: 18.7 us
  starting transfers between devices  7.59 us (40%)
  Pallas kernels  7.07 us (37%)
  waiting for transfers between devices  4.01 us (21%)
    ppermute x6, starting transfers between devices, exchange(): lax.ppermute(part, ('grp', 'tp'), pairs(k))  7.59 us
    ppermute x6, waiting for transfers between devices, exchange(): lax.ppermute(part, ('grp', 'tp'), pairs(k))  4.01 us
    pallas_call x1, Pallas kernels, attend(): pl.pallas_call(functools.partial(attend_kernel, owners), out_shape=[part]...  3.36 us
    pallas_call x1, Pallas kernels, stage(): pl.pallas_call(stage_kernel, out_shape=jax.ShapeDtypeStruct(maps.shape, m...  2.2 us
    pallas_call x1, Pallas kernels, project(): pl.pallas_call(functools.partial(project_kernel, count), out_shape=[jax.S...  0.86 us
    pallas_call x1, Pallas kernels, assemble(): pl.pallas_call(functools.partial(assemble_kernel, owners), out_shape=pltp...  0.66 us
  transfers between devices with their start and end apart: 6, of which 5 were waited for; matrix products, arithmetic and copies ran while one was open for 0% of the time, Pallas kernels for 12%

profile of v23, /device:TPU:0, one launch (start us, length us, event | category | flops | bytes accessed | tf_op | source)
XLA Modules:
  0.0 18.7 jit_solution(18166255797263730740)
XLA Ops:
  0.0 3.4 %attend.1 = (bf16[64,512]{1,0:T(8,128)(2,1)S(1)}, bf16[64,512]{1,0:T(8,128)(2,1)S(1)}, bf16[64,512]{1,0:T(8,128)(2,1)S(1)}, bf16[64,512]{1,0:T(8,128)(2,1)S(1)}) custom-call(s32[2]{0:T(128)} %lengths_hbm.1, bf16[2,576,128]{2,1,0:T(8,128)(2,1)} %bitcast.8, f32[576]{0:T(1024)} %scales_hbm.1, bf16[2,576,1536]{2,1,0:T(8,128)(2,1)} %bitcast.7), custom_call_target="tpu_custom_call" | custom-call | flops 905969664 | bytes 3538944 | tf_op jit(solution)/shard_map/attend/pallas_call | solution.py:147
  3.4 3.0 %collective-permute-start = (bf16[64,512]{1,0:T(8,128)(2,1)S(1)}, bf16[64,512]{1,0:T(8,128)(2,1)S(1)}, u32[]{:S(2)}, u32[]{:S(2)}) collective-permute-start(bf16[64,512]{1,0:T(8,128)(2,1)S(1)} %get-tuple-element.14), channel_id=1, source_target_pairs={{0,7},{1,6},{2,5},{3,4},{4,3},{5,2},{6,1},{7,0},{8,15},{9,14},{10,... | collective-permute-start | bytes 196616 | tf_op jit(solution)/shard_map/ppermute | solution.py:268
  6.3 0.8 %collective-permute-start.1 = (bf16[64,512]{1,0:T(8,128)(2,1)S(1)}, bf16[64,512]{1,0:T(8,128)(2,1)S(1)}, u32[]{:S(2)}, u32[]{:S(2)}) collective-permute-start(bf16[64,512]{1,0:T(8,128)(2,1)S(1)} %get-tuple-element.15), channel_id=1, source_target_pairs={{0,6},{1,7},{2,4},{3,5},{4,2},{5,3},{6,0},{7,1},{8,14},{9,15},{10,... | collective-permute-start | bytes 196616 | tf_op jit(solution)/shard_map/ppermute | solution.py:268
  7.1 0.6 %collective-permute-start.2 = (bf16[64,512]{1,0:T(8,128)(2,1)S(1)}, bf16[64,512]{1,0:T(8,128)(2,1)S(1)}, u32[]{:S(2)}, u32[]{:S(2)}) collective-permute-start(bf16[64,512]{1,0:T(8,128)(2,1)S(1)} %get-tuple-element.16), channel_id=1, source_target_pairs={{0,5},{1,4},{2,7},{3,6},{4,1},{5,0},{6,3},{7,2},{8,13},{9,12},{10,... | collective-permute-start | bytes 196616 | tf_op jit(solution)/shard_map/ppermute | solution.py:268
  7.7 2.2 %stage.1.refs_4_ = bf16[32,512,128]{2,1,0:T(8,128)(2,1)S(1)} custom-call(bf16[32,512,128]{2,1,0:T(8,128)(2,1)} %maps_hbm.1, bf16[64,512]{1,0:T(8,128)(2,1)S(1)} %get-tuple-element.13.after.refs_0_), custom_call_target="tpu_custom_call" | custom-call | bytes 8388608 | tf_op jit(solution)/shard_map/stage/pallas_call | solution.py:179
  9.9 0.0 collective-permute-done.refs_1_
  9.9 0.4 %collective-permute-done.1.refs_2_ = bf16[64,512]{1,0:T(8,128)(2,1)S(1)} collective-permute-done((bf16[64,512]{1,0:T(8,128)(2,1)S(1)}, bf16[64,512]{1,0:T(8,128)(2,1)S(1)}, u32[]{:S(2)}, u32[]{:S(2)}) %collective-permute-start.1) | collective-permute-done | bytes 65568 | tf_op jit(solution)/shard_map/ppermute | solution.py:268
  10.3 0.8 %collective-permute-done.2.refs_3_ = bf16[64,512]{1,0:T(8,128)(2,1)S(1)} collective-permute-done((bf16[64,512]{1,0:T(8,128)(2,1)S(1)}, bf16[64,512]{1,0:T(8,128)(2,1)S(1)}, u32[]{:S(2)}, u32[]{:S(2)}) %collective-permute-start.2) | collective-permute-done | bytes 65568 | tf_op jit(solution)/shard_map/ppermute | solution.py:268
  11.1 0.9 %project.1 = (bf16[32,2,128]{2,1,0:T(2,128)(2,1)S(1)}, bf16[32,2,128]{2,1,0:T(2,128)(2,1)S(1)}, bf16[32,2,128]{2,1,0:T(2,128)(2,1)S(1)}, bf16[32,2,128]{2,1,0:T(2,128)(2,1)S(1)}) custom-call(bf16[64,512]{1,0:T(8,128)(2,1)S(1)} %get-tuple-element.13.after.refs_0_, bf16[64,512]{1,0:T(8,128)(2,1)S(1)} %collective-permute-done.refs_1_, ...), custom_call_target="tpu_custom_call" | custom-call | flops 33554432 | bytes 4194304 | tf_op jit(solution)/shard_map/project/pallas_call | solution.py:215
  11.9 2.1 %collective-permute-start.3 = (bf16[32,2,128]{2,1,0:T(2,128)(2,1)S(1)}, bf16[32,2,128]{2,1,0:T(2,128)(2,1)S(1)}, u32[]{:S(2)}, u32[]{:S(2)}) collective-permute-start(bf16[32,2,128]{2,1,0:T(2,128)(2,1)S(1)} %get-tuple-element.18), channel_id=1, source_target_pairs={{0,7},{1,6},{2,5},{3,4},{4,3},{5,2},{6,1},{7,0},{8,15},{9,14},{10,... | collective-permute-start | bytes 49160 | tf_op jit(solution)/shard_map/ppermute | solution.py:268
  14.0 0.9 %collective-permute-start.4 = (bf16[32,2,128]{2,1,0:T(2,128)(2,1)S(1)}, bf16[32,2,128]{2,1,0:T(2,128)(2,1)S(1)}, u32[]{:S(2)}, u32[]{:S(2)}) collective-permute-start(bf16[32,2,128]{2,1,0:T(2,128)(2,1)S(1)} %get-tuple-element.19), channel_id=1, source_target_pairs={{0,6},{1,7},{2,4},{3,5},{4,2},{5,3},{6,0},{7,1},{8,14},{9,15},{10,... | collective-permute-start | bytes 49160 | tf_op jit(solution)/shard_map/ppermute | solution.py:268
  14.9 0.3 %collective-permute-start.5 = (bf16[32,2,128]{2,1,0:T(2,128)(2,1)S(1)}, bf16[32,2,128]{2,1,0:T(2,128)(2,1)S(1)}, u32[]{:S(2)}, u32[]{:S(2)}) collective-permute-start(bf16[32,2,128]{2,1,0:T(2,128)(2,1)S(1)} %get-tuple-element.20), channel_id=1, source_target_pairs={{0,5},{1,4},{2,7},{3,6},{4,1},{5,0},{6,3},{7,2},{8,13},{9,12},{10,... | collective-permute-start | bytes 49160 | tf_op jit(solution)/shard_map/ppermute | solution.py:268
  15.2 0.9 %collective-permute-done.3.refs_1_ = bf16[32,2,128]{2,1,0:T(2,128)(2,1)S(1)} collective-permute-done((bf16[32,2,128]{2,1,0:T(2,128)(2,1)S(1)}, bf16[32,2,128]{2,1,0:T(2,128)(2,1)S(1)}, u32[]{:S(2)}, u32[]{:S(2)}) %collective-permute-start.3) | collective-permute-done | bytes 16416 | tf_op jit(solution)/shard_map/ppermute | solution.py:268
  16.1 1.1 %collective-permute-done.4.refs_2_ = bf16[32,2,128]{2,1,0:T(2,128)(2,1)S(1)} collective-permute-done((bf16[32,2,128]{2,1,0:T(2,128)(2,1)S(1)}, bf16[32,2,128]{2,1,0:T(2,128)(2,1)S(1)}, u32[]{:S(2)}, u32[]{:S(2)}) %collective-permute-start.4) | collective-permute-done | bytes 16416 | tf_op jit(solution)/shard_map/ppermute | solution.py:268
  17.2 0.9 %collective-permute-done.5.refs_3_ = bf16[32,2,128]{2,1,0:T(2,128)(2,1)S(1)} collective-permute-done((bf16[32,2,128]{2,1,0:T(2,128)(2,1)S(1)}, bf16[32,2,128]{2,1,0:T(2,128)(2,1)S(1)}, u32[]{:S(2)}, u32[]{:S(2)}) %collective-permute-start.5) | collective-permute-done | bytes 16416 | tf_op jit(solution)/shard_map/ppermute | solution.py:268
  18.0 0.7 %assemble.1 = bf16[4,32,2,128]{3,2,1,0:T(2,128)(2,1)} custom-call(bf16[32,2,128]{2,1,0:T(2,128)(2,1)S(1)} %get-tuple-element.17.refs_0_, bf16[32,2,128]{2,1,0:T(2,128)(2,1)S(1)} %collective-permute-done.3.refs_1_, bf16[32,2,128]{2,1,0:T(2,128)(2,1)S(1)} %collective-permute-done.4.refs_2_, bf16[32,2,128]{2,1,0:T(2,128)(2,1)S(1)} %collective-permute-done.5.refs_3_), custom_call_target="tpu_custom_call" | custom-call | tf_op jit(solution)/shard_map/assemble/pallas_call | solution.py:245
Async XLA Ops:
  3.4 6.6 %collective-permute-start = (bf16[64,512]{1,0:T(8,128)(2,1)S(1)}, bf16[64,512]{1,0:T(8,128)(2,1)S(1)}, u32[]{:S(2)}, u32[]{:S(2)}) collective-permute-start(bf16[64,512]{1,0:T(8,128)(2,1)S(1)} %get-tuple-element.14), channel_id=1, source_target_pairs={{0,7},{1,6},{2,5},{3,4},{4,3},{5,2},{6,1},{7,0},{8,15},{9,14},{10,... | collective-permute-start | bytes 196616 | tf_op jit(solution)/shard_map/ppermute | solution.py:268
  6.3 4.0 %collective-permute-start.1 = (bf16[64,512]{1,0:T(8,128)(2,1)S(1)}, bf16[64,512]{1,0:T(8,128)(2,1)S(1)}, u32[]{:S(2)}, u32[]{:S(2)}) collective-permute-start(bf16[64,512]{1,0:T(8,128)(2,1)S(1)} %get-tuple-element.15), channel_id=1, source_target_pairs={{0,6},{1,7},{2,4},{3,5},{4,2},{5,3},{6,0},{7,1},{8,14},{9,15},{10,... | collective-permute-start | bytes 196616 | tf_op jit(solution)/shard_map/ppermute | solution.py:268
  7.1 3.9 %collective-permute-start.2 = (bf16[64,512]{1,0:T(8,128)(2,1)S(1)}, bf16[64,512]{1,0:T(8,128)(2,1)S(1)}, u32[]{:S(2)}, u32[]{:S(2)}) collective-permute-start(bf16[64,512]{1,0:T(8,128)(2,1)S(1)} %get-tuple-element.16), channel_id=1, source_target_pairs={{0,5},{1,4},{2,7},{3,6},{4,1},{5,0},{6,3},{7,2},{8,13},{9,12},{10,... | collective-permute-start | bytes 196616 | tf_op jit(solution)/shard_map/ppermute | solution.py:268
  11.9 4.1 %collective-permute-start.3 = (bf16[32,2,128]{2,1,0:T(2,128)(2,1)S(1)}, bf16[32,2,128]{2,1,0:T(2,128)(2,1)S(1)}, u32[]{:S(2)}, u32[]{:S(2)}) collective-permute-start(bf16[32,2,128]{2,1,0:T(2,128)(2,1)S(1)} %get-tuple-element.18), channel_id=1, source_target_pairs={{0,7},{1,6},{2,5},{3,4},{4,3},{5,2},{6,1},{7,0},{8,15},{9,14},{10,... | collective-permute-start | bytes 49160 | tf_op jit(solution)/shard_map/ppermute | solution.py:268
  14.0 3.2 %collective-permute-start.4 = (bf16[32,2,128]{2,1,0:T(2,128)(2,1)S(1)}, bf16[32,2,128]{2,1,0:T(2,128)(2,1)S(1)}, u32[]{:S(2)}, u32[]{:S(2)}) collective-permute-start(bf16[32,2,128]{2,1,0:T(2,128)(2,1)S(1)} %get-tuple-element.19), channel_id=1, source_target_pairs={{0,6},{1,7},{2,4},{3,5},{4,2},{5,3},{6,0},{7,1},{8,14},{9,15},{10,... | collective-permute-start | bytes 49160 | tf_op jit(solution)/shard_map/ppermute | solution.py:268
  14.9 3.2 %collective-permute-start.5 = (bf16[32,2,128]{2,1,0:T(2,128)(2,1)S(1)}, bf16[32,2,128]{2,1,0:T(2,128)(2,1)S(1)}, u32[]{:S(2)}, u32[]{:S(2)}) collective-permute-start(bf16[32,2,128]{2,1,0:T(2,128)(2,1)S(1)} %get-tuple-element.20), channel_id=1, source_target_pairs={{0,5},{1,4},{2,7},{3,6},{4,1},{5,0},{6,3},{7,2},{8,13},{9,12},{10,... | collective-permute-start | bytes 49160 | tf_op jit(solution)/shard_map/ppermute | solution.py:268

commit v24 on v22

--- a/solution.py
+++ b/solution.py
@@ -18,7 +18,7 @@
 
 
 def order(owners):
-    return [0] + list(range(owners - 1, 0, -1))
+    return [0, owners - 1] + list(range(1, owners - 1))
 
 
 def attend_kernel(owners, lengths_hbm, query_hbm, scales_hbm, cache, *refs):
@@ -34,15 +34,13 @@
         span = pl.ds(b * block, block)
         return pltpu.make_async_copy(cache.at[r, :, span], keys.at[r, :, span], sems.at[r, b])
 
-    def ask(r):
-        return pltpu.make_async_copy(query_hbm.at[r], query.at[r], small_sems.at[2 + r])
-
     lengths_copy = pltpu.make_async_copy(lengths_hbm, lengths, small_sems.at[0])
     scales_copy = pltpu.make_async_copy(scales_hbm, scales, small_sems.at[1])
+    query_copy = pltpu.make_async_copy(query_hbm, query, small_sems.at[2])
     lengths_copy.start()
+    query_copy.start()
     scales_copy.start()
     for r in range(requests):
-        ask(r).start()
         fetch(r, 0).start()
     lengths_copy.wait()
     for r in range(requests):
@@ -50,11 +48,11 @@
             @pl.when(b * block < lengths[r])
             def _():
                 fetch(r, b).start()
+    query_copy.wait()
     scales_copy.wait()
     scale_row = scales[...].reshape(1, channels)
 
     def scale(r):
-        ask(r).wait()
         return (query[r].astype(jnp.float32).T * scale_row).astype(jnp.bfloat16)
 
     def score(scaled, r, b, live):
@@ -138,7 +136,7 @@
             pltpu.VMEM((channels,), jnp.float32),
             pltpu.VMEM((requests, channels, cache_len), jnp.bfloat16),
             pltpu.SemaphoreType.DMA((requests, cache_len // min(BLOCK, cache_len))),
-            pltpu.SemaphoreType.DMA((2 + requests,)),
+            pltpu.SemaphoreType.DMA((3,)),
         ],
         compiler_params=pltpu.CompilerParams(vmem_limit_bytes=24 * 2**20),
         cost_estimate=pl.CostEstimate(
@@ -237,10 +235,11 @@
 def exchange(parts):
     owners = len(parts)
     groups = lax.axis_size("grp")
+    flip = 1 - groups % 2
 
     def pairs(k):
         return [
-            (g * owners + i, (g ^ 1) * owners + (i ^ k))
+            (g * owners + i, (g ^ flip) * owners + (i ^ k))
             for g in range(groups) for i in range(owners)
         ]
 

time: 18.7 us -> 18.3 us (0.979)
  waiting for transfers between devices: 4.65 us -> 3.49 us
  starting transfers between devices: 8.21 us -> 8.93 us
    ppermute x6, waiting for transfers between devices: 4.65 us -> 3.49 us  [exchange(): lax.ppermute(part, ('grp', 'tp'), pairs(k))]
    ppermute x6, starting transfers between devices: 8.21 us -> 8.93 us  [exchange(): lax.ppermute(part, ('grp', 'tp'), pairs(k))]
  transfers between devices with their start and end apart: 6 -> 6, of which waited for: 5 -> 4; matrix products, arithmetic and copies ran while one was open for 0% -> 0% of each run, Pallas kernels for 12% -> 12%
where the time goes in v24:
time: 18.3 us; the launch traced here: 18.4 us
  starting transfers between devices  8.93 us (49%)
  Pallas kernels  5.95 us (33%)
  waiting for transfers between devices  3.49 us (19%)
    ppermute x6, starting transfers between devices, exchange(): lax.ppermute(part, ('grp', 'tp'), pairs(k))  8.93 us
    ppermute x6, waiting for transfers between devices, exchange(): lax.ppermute(part, ('grp', 'tp'), pairs(k))  3.49 us
    pallas_call x1, Pallas kernels, attend(): pl.pallas_call(functools.partial(attend_kernel, owners), out_shape=[part]...  2.24 us
    pallas_call x1, Pallas kernels, stage(): pl.pallas_call(stage_kernel, out_shape=jax.ShapeDtypeStruct(maps.shape, m...  2.2 us
    pallas_call x1, Pallas kernels, project(): pl.pallas_call(functools.partial(project_kernel, count), out_shape=[jax.S...  0.86 us
    pallas_call x1, Pallas kernels, assemble(): pl.pallas_call(functools.partial(assemble_kernel, owners), out_shape=pltp...  0.66 us
  transfers between devices with their start and end apart: 6, of which 4 were waited for; matrix products, arithmetic and copies ran while one was open for 0% of the time, Pallas kernels for 12%

profile of v24, /device:TPU:0, one launch (start us, length us, event | category | flops | bytes accessed | tf_op | source)
XLA Modules:
  0.0 18.4 jit_solution(6403494912885434215)
XLA Ops:
  0.0 2.2 %attend.1 = (bf16[64,512]{1,0:T(8,128)(2,1)S(1)}, bf16[64,512]{1,0:T(8,128)(2,1)S(1)}, bf16[64,512]{1,0:T(8,128)(2,1)S(1)}, bf16[64,512]{1,0:T(8,128)(2,1)S(1)}) custom-call(s32[2]{0:T(128)} %lengths_hbm.1, bf16[2,576,128]{2,1,0:T(8,128)(2,1)} %bitcast.8, f32[576]{0:T(1024)} %scales_hbm.1, bf16[2,576,1536]{2,1,0:T(8,128)(2,1)} %bitcast.7), custom_call_target="tpu_custom_call" | custom-call | flops 905969664 | bytes 3538944 | tf_op jit(solution)/shard_map/attend/pallas_call | solution.py:127
  2.2 4.3 %collective-permute-start = (bf16[64,512]{1,0:T(8,128)(2,1)S(1)}, bf16[64,512]{1,0:T(8,128)(2,1)S(1)}, u32[]{:S(2)}, u32[]{:S(2)}) collective-permute-start(bf16[64,512]{1,0:T(8,128)(2,1)S(1)} %get-tuple-element.14), channel_id=1, source_target_pairs={{0,7},{1,6},{2,5},{3,4},{4,3},{5,2},{6,1},{7,0},{8,15},{9,14},{10,... | collective-permute-start | bytes 196616 | tf_op jit(solution)/shard_map/ppermute | solution.py:247
  6.5 0.8 %collective-permute-start.1 = (bf16[64,512]{1,0:T(8,128)(2,1)S(1)}, bf16[64,512]{1,0:T(8,128)(2,1)S(1)}, u32[]{:S(2)}, u32[]{:S(2)}) collective-permute-start(bf16[64,512]{1,0:T(8,128)(2,1)S(1)} %get-tuple-element.15), channel_id=1, source_target_pairs={{0,5},{1,4},{2,7},{3,6},{4,1},{5,0},{6,3},{7,2},{8,13},{9,12},{10,... | collective-permute-start | bytes 196616 | tf_op jit(solution)/shard_map/ppermute | solution.py:247
  7.4 0.8 %collective-permute-start.2 = (bf16[64,512]{1,0:T(8,128)(2,1)S(1)}, bf16[64,512]{1,0:T(8,128)(2,1)S(1)}, u32[]{:S(2)}, u32[]{:S(2)}) collective-permute-start(bf16[64,512]{1,0:T(8,128)(2,1)S(1)} %get-tuple-element.16), channel_id=1, source_target_pairs={{0,6},{1,7},{2,4},{3,5},{4,2},{5,3},{6,0},{7,1},{8,14},{9,15},{10,... | collective-permute-start | bytes 196616 | tf_op jit(solution)/shard_map/ppermute | solution.py:247
  8.2 2.2 %stage.1.refs_4_ = bf16[32,512,128]{2,1,0:T(8,128)(2,1)S(1)} custom-call(bf16[32,512,128]{2,1,0:T(8,128)(2,1)} %maps_hbm.1, bf16[64,512]{1,0:T(8,128)(2,1)S(1)} %get-tuple-element.13.after.refs_0_), custom_call_target="tpu_custom_call" | custom-call | bytes 8388608 | tf_op jit(solution)/shard_map/stage/pallas_call | solution.py:158
  10.4 0.0 collective-permute-done.refs_1_
  10.4 1.0 %collective-permute-done.1.refs_2_ = bf16[64,512]{1,0:T(8,128)(2,1)S(1)} collective-permute-done((bf16[64,512]{1,0:T(8,128)(2,1)S(1)}, bf16[64,512]{1,0:T(8,128)(2,1)S(1)}, u32[]{:S(2)}, u32[]{:S(2)}) %collective-permute-start.1) | collective-permute-done | bytes 65568 | tf_op jit(solution)/shard_map/ppermute | solution.py:247
  11.4 0.4 %collective-permute-done.2.refs_3_ = bf16[64,512]{1,0:T(8,128)(2,1)S(1)} collective-permute-done((bf16[64,512]{1,0:T(8,128)(2,1)S(1)}, bf16[64,512]{1,0:T(8,128)(2,1)S(1)}, u32[]{:S(2)}, u32[]{:S(2)}) %collective-permute-start.2) | collective-permute-done | bytes 65568 | tf_op jit(solution)/shard_map/ppermute | solution.py:247
  11.7 0.9 %project.1 = (bf16[32,2,128]{2,1,0:T(2,128)(2,1)S(1)}, bf16[32,2,128]{2,1,0:T(2,128)(2,1)S(1)}, bf16[32,2,128]{2,1,0:T(2,128)(2,1)S(1)}, bf16[32,2,128]{2,1,0:T(2,128)(2,1)S(1)}) custom-call(bf16[64,512]{1,0:T(8,128)(2,1)S(1)} %get-tuple-element.13.after.refs_0_, bf16[64,512]{1,0:T(8,128)(2,1)S(1)} %collective-permute-done.refs_1_, ...), custom_call_target="tpu_custom_call" | custom-call | flops 33554432 | bytes 4194304 | tf_op jit(solution)/shard_map/project/pallas_call | solution.py:194
  12.6 0.5 %collective-permute-start.3 = (bf16[32,2,128]{2,1,0:T(2,128)(2,1)S(1)}, bf16[32,2,128]{2,1,0:T(2,128)(2,1)S(1)}, u32[]{:S(2)}, u32[]{:S(2)}) collective-permute-start(bf16[32,2,128]{2,1,0:T(2,128)(2,1)S(1)} %get-tuple-element.18), channel_id=1, source_target_pairs={{0,7},{1,6},{2,5},{3,4},{4,3},{5,2},{6,1},{7,0},{8,15},{9,14},{10,... | collective-permute-start | bytes 49160 | tf_op jit(solution)/shard_map/ppermute | solution.py:247
  13.0 1.5 %collective-permute-start.4 = (bf16[32,2,128]{2,1,0:T(2,128)(2,1)S(1)}, bf16[32,2,128]{2,1,0:T(2,128)(2,1)S(1)}, u32[]{:S(2)}, u32[]{:S(2)}) collective-permute-start(bf16[32,2,128]{2,1,0:T(2,128)(2,1)S(1)} %get-tuple-element.19), channel_id=1, source_target_pairs={{0,5},{1,4},{2,7},{3,6},{4,1},{5,0},{6,3},{7,2},{8,13},{9,12},{10,... | collective-permute-start | bytes 49160 | tf_op jit(solution)/shard_map/ppermute | solution.py:247
  14.6 1.0 %collective-permute-start.5 = (bf16[32,2,128]{2,1,0:T(2,128)(2,1)S(1)}, bf16[32,2,128]{2,1,0:T(2,128)(2,1)S(1)}, u32[]{:S(2)}, u32[]{:S(2)}) collective-permute-start(bf16[32,2,128]{2,1,0:T(2,128)(2,1)S(1)} %get-tuple-element.20), channel_id=1, source_target_pairs={{0,6},{1,7},{2,4},{3,5},{4,2},{5,3},{6,0},{7,1},{8,14},{9,15},{10,... | collective-permute-start | bytes 49160 | tf_op jit(solution)/shard_map/ppermute | solution.py:247
  15.6 1.1 %collective-permute-done.3.refs_1_ = bf16[32,2,128]{2,1,0:T(2,128)(2,1)S(1)} collective-permute-done((bf16[32,2,128]{2,1,0:T(2,128)(2,1)S(1)}, bf16[32,2,128]{2,1,0:T(2,128)(2,1)S(1)}, u32[]{:S(2)}, u32[]{:S(2)}) %collective-permute-start.3) | collective-permute-done | bytes 16416 | tf_op jit(solution)/shard_map/ppermute | solution.py:247
  16.7 0.0 collective-permute-done.4.refs_2_
  16.7 1.0 %collective-permute-done.5.refs_3_ = bf16[32,2,128]{2,1,0:T(2,128)(2,1)S(1)} collective-permute-done((bf16[32,2,128]{2,1,0:T(2,128)(2,1)S(1)}, bf16[32,2,128]{2,1,0:T(2,128)(2,1)S(1)}, u32[]{:S(2)}, u32[]{:S(2)}) %collective-permute-start.5) | collective-permute-done | bytes 16416 | tf_op jit(solution)/shard_map/ppermute | solution.py:247
  17.7 0.7 %assemble.1 = bf16[4,32,2,128]{3,2,1,0:T(2,128)(2,1)} custom-call(bf16[32,2,128]{2,1,0:T(2,128)(2,1)S(1)} %get-tuple-element.17.refs_0_, bf16[32,2,128]{2,1,0:T(2,128)(2,1)S(1)} %collective-permute-done.3.refs_1_, bf16[32,2,128]{2,1,0:T(2,128)(2,1)S(1)} %collective-permute-done.4.refs_2_, bf16[32,2,128]{2,1,0:T(2,128)(2,1)S(1)} %collective-permute-done.5.refs_3_), custom_call_target="tpu_custom_call" | custom-call | tf_op jit(solution)/shard_map/assemble/pallas_call | solution.py:224
Async XLA Ops:
  2.2 8.1 %collective-permute-start = (bf16[64,512]{1,0:T(8,128)(2,1)S(1)}, bf16[64,512]{1,0:T(8,128)(2,1)S(1)}, u32[]{:S(2)}, u32[]{:S(2)}) collective-permute-start(bf16[64,512]{1,0:T(8,128)(2,1)S(1)} %get-tuple-element.14), channel_id=1, source_target_pairs={{0,7},{1,6},{2,5},{3,4},{4,3},{5,2},{6,1},{7,0},{8,15},{9,14},{10,... | collective-permute-start | bytes 196616 | tf_op jit(solution)/shard_map/ppermute | solution.py:247
  6.5 4.8 %collective-permute-start.1 = (bf16[64,512]{1,0:T(8,128)(2,1)S(1)}, bf16[64,512]{1,0:T(8,128)(2,1)S(1)}, u32[]{:S(2)}, u32[]{:S(2)}) collective-permute-start(bf16[64,512]{1,0:T(8,128)(2,1)S(1)} %get-tuple-element.15), channel_id=1, source_target_pairs={{0,5},{1,4},{2,7},{3,6},{4,1},{5,0},{6,3},{7,2},{8,13},{9,12},{10,... | collective-permute-start | bytes 196616 | tf_op jit(solution)/shard_map/ppermute | solution.py:247
  7.4 4.4 %collective-permute-start.2 = (bf16[64,512]{1,0:T(8,128)(2,1)S(1)}, bf16[64,512]{1,0:T(8,128)(2,1)S(1)}, u32[]{:S(2)}, u32[]{:S(2)}) collective-permute-start(bf16[64,512]{1,0:T(8,128)(2,1)S(1)} %get-tuple-element.16), channel_id=1, source_target_pairs={{0,6},{1,7},{2,4},{3,5},{4,2},{5,3},{6,0},{7,1},{8,14},{9,15},{10,... | collective-permute-start | bytes 196616 | tf_op jit(solution)/shard_map/ppermute | solution.py:247
  12.6 4.1 %collective-permute-start.3 = (bf16[32,2,128]{2,1,0:T(2,128)(2,1)S(1)}, bf16[32,2,128]{2,1,0:T(2,128)(2,1)S(1)}, u32[]{:S(2)}, u32[]{:S(2)}) collective-permute-start(bf16[32,2,128]{2,1,0:T(2,128)(2,1)S(1)} %get-tuple-element.18), channel_id=1, source_target_pairs={{0,7},{1,6},{2,5},{3,4},{4,3},{5,2},{6,1},{7,0},{8,15},{9,14},{10,... | collective-permute-start | bytes 49160 | tf_op jit(solution)/shard_map/ppermute | solution.py:247
  13.0 3.7 %collective-permute-start.4 = (bf16[32,2,128]{2,1,0:T(2,128)(2,1)S(1)}, bf16[32,2,128]{2,1,0:T(2,128)(2,1)S(1)}, u32[]{:S(2)}, u32[]{:S(2)}) collective-permute-start(bf16[32,2,128]{2,1,0:T(2,128)(2,1)S(1)} %get-tuple-element.19), channel_id=1, source_target_pairs={{0,5},{1,4},{2,7},{3,6},{4,1},{5,0},{6,3},{7,2},{8,13},{9,12},{10,... | collective-permute-start | bytes 49160 | tf_op jit(solution)/shard_map/ppermute | solution.py:247
  14.6 3.2 %collective-permute-start.5 = (bf16[32,2,128]{2,1,0:T(2,128)(2,1)S(1)}, bf16[32,2,128]{2,1,0:T(2,128)(2,1)S(1)}, u32[]{:S(2)}, u32[]{:S(2)}) collective-permute-start(bf16[32,2,128]{2,1,0:T(2,128)(2,1)S(1)} %get-tuple-element.20), channel_id=1, source_target_pairs={{0,6},{1,7},{2,4},{3,5},{4,2},{5,3},{6,0},{7,1},{8,14},{9,15},{10,... | collective-permute-start | bytes 49160 | tf_op jit(solution)/shard_map/ppermute | solution.py:247

commit v25 on v24

--- a/solution.py
+++ b/solution.py
@@ -22,7 +22,8 @@
 
 
 def attend_kernel(owners, lengths_hbm, query_hbm, scales_hbm, cache, *refs):
-    outs, (latents, lengths, query, scales, keys, sems, small_sems) = refs[:owners], refs[owners:]
+    outs, refs = refs[:owners], refs[owners:]
+    latents, lengths, query, scales, keys, scaled, sems, small_sems = refs
     requests, channels, heads = query.shape
     rows, rank = outs[0].shape
     cache_len = cache.shape[2]
@@ -34,14 +35,14 @@
         span = pl.ds(b * block, block)
         return pltpu.make_async_copy(cache.at[r, :, span], keys.at[r, :, span], sems.at[r, b])
 
+    first_copy = pltpu.make_async_copy(
+        cache.at[:, :, pl.ds(0, block)], keys.at[:, :, pl.ds(0, block)], small_sems.at[3]
+    )
+    query_copy = pltpu.make_async_copy(query_hbm, query, small_sems.at[2])
     lengths_copy = pltpu.make_async_copy(lengths_hbm, lengths, small_sems.at[0])
     scales_copy = pltpu.make_async_copy(scales_hbm, scales, small_sems.at[1])
-    query_copy = pltpu.make_async_copy(query_hbm, query, small_sems.at[2])
-    lengths_copy.start()
-    query_copy.start()
-    scales_copy.start()
-    for r in range(requests):
-        fetch(r, 0).start()
+    for copy in (query_copy, first_copy, lengths_copy, scales_copy):
+        copy.start()
     lengths_copy.wait()
     for r in range(requests):
         for b in range(1, blocks):
@@ -51,14 +52,13 @@
     query_copy.wait()
     scales_copy.wait()
     scale_row = scales[...].reshape(1, channels)
-
-    def scale(r):
-        return (query[r].astype(jnp.float32).T * scale_row).astype(jnp.bfloat16)
-
-    def score(scaled, r, b, live):
-        if r not in scaled:
-            scaled[r] = scale(r)
-        fetch(r, b).wait()
+    for r in range(requests):
+        scaled[r] = (query[r].astype(jnp.float32).T * scale_row).astype(jnp.bfloat16)
+    first_copy.wait()
+
+    def score(r, b, live):
+        if b:
+            fetch(r, b).wait()
         span = slice(b * block, (b + 1) * block)
         part = jnp.dot(scaled[r], keys[r, :, span], preferred_element_type=jnp.float32)
         if b == live - 1:
@@ -88,13 +88,12 @@
             latents[at // LANES, pl.ds(r, heads, stride=requests), :] = latent[:, at:at + LANES]
 
     def several(group, live):
-        scaled = {}
         units = [(r, 0, n) for r, n in zip(group, live)]
         units += [(r, b, n) for r, n in zip(group, live) for b in range(1, n)]
-        part = score(scaled, *units[0])
+        part = score(*units[0])
         state = {}
         for i, (r, b, n) in enumerate(units):
-            ahead = score(scaled, *units[i + 1]) if i + 1 < len(units) else None
+            ahead = score(*units[i + 1]) if i + 1 < len(units) else None
             done = weigh(part, r, b)
             state[r] = merge(state[r], done) if b else done
             if b == n - 1:
@@ -135,8 +134,9 @@
             pltpu.VMEM((requests, channels, heads), jnp.bfloat16),
             pltpu.VMEM((channels,), jnp.float32),
             pltpu.VMEM((requests, channels, cache_len), jnp.bfloat16),
+            pltpu.VMEM((requests, heads, channels), jnp.bfloat16),
             pltpu.SemaphoreType.DMA((requests, cache_len // min(BLOCK, cache_len))),
-            pltpu.SemaphoreType.DMA((3,)),
+            pltpu.SemaphoreType.DMA((4,)),
         ],
         compiler_params=pltpu.CompilerParams(vmem_limit_bytes=24 * 2**20),
         cost_estimate=pl.CostEstimate(

time: 18.3 us -> 18.3 us (level)
  starting transfers between devices: 8.93 us -> 8.16 us
  waiting for transfers between devices: 3.49 us -> 4.12 us
    ppermute x6, starting transfers between devices: 8.93 us -> 8.16 us  [exchange(): lax.ppermute(part, ('grp', 'tp'), pairs(k))]
    ppermute x6, waiting for transfers between devices: 3.49 us -> 4.12 us  [exchange(): lax.ppermute(part, ('grp', 'tp'), pairs(k))]
  transfers between devices with their start and end apart: 6 -> 6, of which waited for: 4 -> 5; matrix products, arithmetic and copies ran while one was open for 0% -> 0% of each run, Pallas kernels for 12% -> 12%
where the time goes in v25:
time: 18.3 us
  starting transfers between devices  8.16 us (45%)
  Pallas kernels  6.01 us (33%)
  waiting for transfers between devices  4.12 us (23%)
    ppermute x6, starting transfers between devices, exchange(): lax.ppermute(part, ('grp', 'tp'), pairs(k))  8.16 us
    ppermute x6, waiting for transfers between devices, exchange(): lax.ppermute(part, ('grp', 'tp'), pairs(k))  4.12 us
    pallas_call x1, Pallas kernels, attend(): pl.pallas_call(functools.partial(attend_kernel, owners), out_shape=[part]...  2.3 us
    pallas_call x1, Pallas kernels, stage(): pl.pallas_call(stage_kernel, out_shape=jax.ShapeDtypeStruct(maps.shape, m...  2.2 us
    pallas_call x1, Pallas kernels, project(): pl.pallas_call(functools.partial(project_kernel, count), out_shape=[jax.S...  0.86 us
    pallas_call x1, Pallas kernels, assemble(): pl.pallas_call(functools.partial(assemble_kernel, owners), out_shape=pltp...  0.66 us
  transfers between devices with their start and end apart: 6, of which 5 were waited for; matrix products, arithmetic and copies ran while one was open for 0% of the time, Pallas kernels for 12%

profile of v25, /device:TPU:0, one launch (start us, length us, event | category | flops | bytes accessed | tf_op | source)
XLA Modules:
  0.0 18.3 jit_solution(3767164548619826354)
XLA Ops:
  0.0 2.3 %attend.1 = (bf16[64,512]{1,0:T(8,128)(2,1)S(1)}, bf16[64,512]{1,0:T(8,128)(2,1)S(1)}, bf16[64,512]{1,0:T(8,128)(2,1)S(1)}, bf16[64,512]{1,0:T(8,128)(2,1)S(1)}) custom-call(s32[2]{0:T(128)} %lengths_hbm.1, bf16[2,576,128]{2,1,0:T(8,128)(2,1)} %bitcast.8, f32[576]{0:T(1024)} %scales_hbm.1, bf16[2,576,1536]{2,1,0:T(8,128)(2,1)} %bitcast.7), custom_call_target="tpu_custom_call" | custom-call | flops 905969664 | bytes 3538944 | tf_op jit(solution)/shard_map/attend/pallas_call | solution.py:126
  2.3 3.8 %collective-permute-start = (bf16[64,512]{1,0:T(8,128)(2,1)S(1)}, bf16[64,512]{1,0:T(8,128)(2,1)S(1)}, u32[]{:S(2)}, u32[]{:S(2)}) collective-permute-start(bf16[64,512]{1,0:T(8,128)(2,1)S(1)} %get-tuple-element.14), channel_id=1, source_target_pairs={{0,7},{1,6},{2,5},{3,4},{4,3},{5,2},{6,1},{7,0},{8,15},{9,14},{10,... | collective-permute-start | bytes 196616 | tf_op jit(solution)/shard_map/ppermute | solution.py:247
  6.2 0.8 %collective-permute-start.1 = (bf16[64,512]{1,0:T(8,128)(2,1)S(1)}, bf16[64,512]{1,0:T(8,128)(2,1)S(1)}, u32[]{:S(2)}, u32[]{:S(2)}) collective-permute-start(bf16[64,512]{1,0:T(8,128)(2,1)S(1)} %get-tuple-element.15), channel_id=1, source_target_pairs={{0,5},{1,4},{2,7},{3,6},{4,1},{5,0},{6,3},{7,2},{8,13},{9,12},{10,... | collective-permute-start | bytes 196616 | tf_op jit(solution)/shard_map/ppermute | solution.py:247
  7.0 0.4 %collective-permute-start.2 = (bf16[64,512]{1,0:T(8,128)(2,1)S(1)}, bf16[64,512]{1,0:T(8,128)(2,1)S(1)}, u32[]{:S(2)}, u32[]{:S(2)}) collective-permute-start(bf16[64,512]{1,0:T(8,128)(2,1)S(1)} %get-tuple-element.16), channel_id=1, source_target_pairs={{0,6},{1,7},{2,4},{3,5},{4,2},{5,3},{6,0},{7,1},{8,14},{9,15},{10,... | collective-permute-start | bytes 196616 | tf_op jit(solution)/shard_map/ppermute | solution.py:247
  7.4 2.2 %stage.1.refs_4_ = bf16[32,512,128]{2,1,0:T(8,128)(2,1)S(1)} custom-call(bf16[32,512,128]{2,1,0:T(8,128)(2,1)} %maps_hbm.1, bf16[64,512]{1,0:T(8,128)(2,1)S(1)} %get-tuple-element.13.after.refs_0_), custom_call_target="tpu_custom_call" | custom-call | bytes 8388608 | tf_op jit(solution)/shard_map/stage/pallas_call | solution.py:158
  9.6 0.0 collective-permute-done.refs_1_
  9.6 1.0 %collective-permute-done.1.refs_2_ = bf16[64,512]{1,0:T(8,128)(2,1)S(1)} collective-permute-done((bf16[64,512]{1,0:T(8,128)(2,1)S(1)}, bf16[64,512]{1,0:T(8,128)(2,1)S(1)}, u32[]{:S(2)}, u32[]{:S(2)}) %collective-permute-start.1) | collective-permute-done | bytes 65568 | tf_op jit(solution)/shard_map/ppermute | solution.py:247
  10.6 0.4 %collective-permute-done.2.refs_3_ = bf16[64,512]{1,0:T(8,128)(2,1)S(1)} collective-permute-done((bf16[64,512]{1,0:T(8,128)(2,1)S(1)}, bf16[64,512]{1,0:T(8,128)(2,1)S(1)}, u32[]{:S(2)}, u32[]{:S(2)}) %collective-permute-start.2) | collective-permute-done | bytes 65568 | tf_op jit(solution)/shard_map/ppermute | solution.py:247
  11.0 0.9 %project.1 = (bf16[32,2,128]{2,1,0:T(2,128)(2,1)S(1)}, bf16[32,2,128]{2,1,0:T(2,128)(2,1)S(1)}, bf16[32,2,128]{2,1,0:T(2,128)(2,1)S(1)}, bf16[32,2,128]{2,1,0:T(2,128)(2,1)S(1)}) custom-call(bf16[64,512]{1,0:T(8,128)(2,1)S(1)} %get-tuple-element.13.after.refs_0_, bf16[64,512]{1,0:T(8,128)(2,1)S(1)} %collective-permute-done.refs_1_, ...), custom_call_target="tpu_custom_call" | custom-call | flops 33554432 | bytes 4194304 | tf_op jit(solution)/shard_map/project/pallas_call | solution.py:194
  11.8 2.2 %collective-permute-start.3 = (bf16[32,2,128]{2,1,0:T(2,128)(2,1)S(1)}, bf16[32,2,128]{2,1,0:T(2,128)(2,1)S(1)}, u32[]{:S(2)}, u32[]{:S(2)}) collective-permute-start(bf16[32,2,128]{2,1,0:T(2,128)(2,1)S(1)} %get-tuple-element.18), channel_id=1, source_target_pairs={{0,7},{1,6},{2,5},{3,4},{4,3},{5,2},{6,1},{7,0},{8,15},{9,14},{10,... | collective-permute-start | bytes 49160 | tf_op jit(solution)/shard_map/ppermute | solution.py:247
  14.0 0.5 %collective-permute-start.4 = (bf16[32,2,128]{2,1,0:T(2,128)(2,1)S(1)}, bf16[32,2,128]{2,1,0:T(2,128)(2,1)S(1)}, u32[]{:S(2)}, u32[]{:S(2)}) collective-permute-start(bf16[32,2,128]{2,1,0:T(2,128)(2,1)S(1)} %get-tuple-element.19), channel_id=1, source_target_pairs={{0,5},{1,4},{2,7},{3,6},{4,1},{5,0},{6,3},{7,2},{8,13},{9,12},{10,... | collective-permute-start | bytes 49160 | tf_op jit(solution)/shard_map/ppermute | solution.py:247
  14.5 0.4 %collective-permute-start.5 = (bf16[32,2,128]{2,1,0:T(2,128)(2,1)S(1)}, bf16[32,2,128]{2,1,0:T(2,128)(2,1)S(1)}, u32[]{:S(2)}, u32[]{:S(2)}) collective-permute-start(bf16[32,2,128]{2,1,0:T(2,128)(2,1)S(1)} %get-tuple-element.20), channel_id=1, source_target_pairs={{0,6},{1,7},{2,4},{3,5},{4,2},{5,3},{6,0},{7,1},{8,14},{9,15},{10,... | collective-permute-start | bytes 49160 | tf_op jit(solution)/shard_map/ppermute | solution.py:247
  14.9 1.0 %collective-permute-done.3.refs_1_ = bf16[32,2,128]{2,1,0:T(2,128)(2,1)S(1)} collective-permute-done((bf16[32,2,128]{2,1,0:T(2,128)(2,1)S(1)}, bf16[32,2,128]{2,1,0:T(2,128)(2,1)S(1)}, u32[]{:S(2)}, u32[]{:S(2)}) %collective-permute-start.3) | collective-permute-done | bytes 16416 | tf_op jit(solution)/shard_map/ppermute | solution.py:247
  16.0 1.2 %collective-permute-done.4.refs_2_ = bf16[32,2,128]{2,1,0:T(2,128)(2,1)S(1)} collective-permute-done((bf16[32,2,128]{2,1,0:T(2,128)(2,1)S(1)}, bf16[32,2,128]{2,1,0:T(2,128)(2,1)S(1)}, u32[]{:S(2)}, u32[]{:S(2)}) %collective-permute-start.4) | collective-permute-done | bytes 16416 | tf_op jit(solution)/shard_map/ppermute | solution.py:247
  17.2 0.5 %collective-permute-done.5.refs_3_ = bf16[32,2,128]{2,1,0:T(2,128)(2,1)S(1)} collective-permute-done((bf16[32,2,128]{2,1,0:T(2,128)(2,1)S(1)}, bf16[32,2,128]{2,1,0:T(2,128)(2,1)S(1)}, u32[]{:S(2)}, u32[]{:S(2)}) %collective-permute-start.5) | collective-permute-done | bytes 16416 | tf_op jit(solution)/shard_map/ppermute | solution.py:247
  17.7 0.7 %assemble.1 = bf16[4,32,2,128]{3,2,1,0:T(2,128)(2,1)} custom-call(bf16[32,2,128]{2,1,0:T(2,128)(2,1)S(1)} %get-tuple-element.17.refs_0_, bf16[32,2,128]{2,1,0:T(2,128)(2,1)S(1)} %collective-permute-done.3.refs_1_, bf16[32,2,128]{2,1,0:T(2,128)(2,1)S(1)} %collective-permute-done.4.refs_2_, bf16[32,2,128]{2,1,0:T(2,128)(2,1)S(1)} %collective-permute-done.5.refs_3_), custom_call_target="tpu_custom_call" | custom-call | tf_op jit(solution)/shard_map/assemble/pallas_call | solution.py:224
Async XLA Ops:
  2.3 7.3 %collective-permute-start = (bf16[64,512]{1,0:T(8,128)(2,1)S(1)}, bf16[64,512]{1,0:T(8,128)(2,1)S(1)}, u32[]{:S(2)}, u32[]{:S(2)}) collective-permute-start(bf16[64,512]{1,0:T(8,128)(2,1)S(1)} %get-tuple-element.14), channel_id=1, source_target_pairs={{0,7},{1,6},{2,5},{3,4},{4,3},{5,2},{6,1},{7,0},{8,15},{9,14},{10,... | collective-permute-start | bytes 196616 | tf_op jit(solution)/shard_map/ppermute | solution.py:247
  6.2 4.4 %collective-permute-start.1 = (bf16[64,512]{1,0:T(8,128)(2,1)S(1)}, bf16[64,512]{1,0:T(8,128)(2,1)S(1)}, u32[]{:S(2)}, u32[]{:S(2)}) collective-permute-start(bf16[64,512]{1,0:T(8,128)(2,1)S(1)} %get-tuple-element.15), channel_id=1, source_target_pairs={{0,5},{1,4},{2,7},{3,6},{4,1},{5,0},{6,3},{7,2},{8,13},{9,12},{10,... | collective-permute-start | bytes 196616 | tf_op jit(solution)/shard_map/ppermute | solution.py:247
  7.0 4.0 %collective-permute-start.2 = (bf16[64,512]{1,0:T(8,128)(2,1)S(1)}, bf16[64,512]{1,0:T(8,128)(2,1)S(1)}, u32[]{:S(2)}, u32[]{:S(2)}) collective-permute-start(bf16[64,512]{1,0:T(8,128)(2,1)S(1)} %get-tuple-element.16), channel_id=1, source_target_pairs={{0,6},{1,7},{2,4},{3,5},{4,2},{5,3},{6,0},{7,1},{8,14},{9,15},{10,... | collective-permute-start | bytes 196616 | tf_op jit(solution)/shard_map/ppermute | solution.py:247
  11.8 4.1 %collective-permute-start.3 = (bf16[32,2,128]{2,1,0:T(2,128)(2,1)S(1)}, bf16[32,2,128]{2,1,0:T(2,128)(2,1)S(1)}, u32[]{:S(2)}, u32[]{:S(2)}) collective-permute-start(bf16[32,2,128]{2,1,0:T(2,128)(2,1)S(1)} %get-tuple-element.18), channel_id=1, source_target_pairs={{0,7},{1,6},{2,5},{3,4},{4,3},{5,2},{6,1},{7,0},{8,15},{9,14},{10,... | collective-permute-start | bytes 49160 | tf_op jit(solution)/shard_map/ppermute | solution.py:247
  14.0 3.2 %collective-permute-start.4 = (bf16[32,2,128]{2,1,0:T(2,128)(2,1)S(1)}, bf16[32,2,128]{2,1,0:T(2,128)(2,1)S(1)}, u32[]{:S(2)}, u32[]{:S(2)}) collective-permute-start(bf16[32,2,128]{2,1,0:T(2,128)(2,1)S(1)} %get-tuple-element.19), channel_id=1, source_target_pairs={{0,5},{1,4},{2,7},{3,6},{4,1},{5,0},{6,3},{7,2},{8,13},{9,12},{10,... | collective-permute-start | bytes 49160 | tf_op jit(solution)/shard_map/ppermute | solution.py:247
  14.5 3.2 %collective-permute-start.5 = (bf16[32,2,128]{2,1,0:T(2,128)(2,1)S(1)}, bf16[32,2,128]{2,1,0:T(2,128)(2,1)S(1)}, u32[]{:S(2)}, u32[]{:S(2)}) collective-permute-start(bf16[32,2,128]{2,1,0:T(2,128)(2,1)S(1)} %get-tuple-element.20), channel_id=1, source_target_pairs={{0,6},{1,7},{2,4},{3,5},{4,2},{5,3},{6,0},{7,1},{8,14},{9,15},{10,... | collective-permute-start | bytes 49160 | tf_op jit(solution)/shard_map/ppermute | solution.py:247

commit v26 on v24

--- a/solution.py
+++ b/solution.py
@@ -171,7 +171,8 @@
 
 def project_kernel(count, *refs):
     parts, maps, outs = refs[:count], refs[count], refs[count + 1:]
-    local_heads, requests, width = outs[0].shape
+    local_heads, width = maps.shape[0], maps.shape[2]
+    requests = outs[0].shape[0] // local_heads
     group = min(GROUP_ROWS // requests, local_heads)
     rows = group * requests
     for first in range(0, local_heads, group):
@@ -185,7 +186,7 @@
             own = block[:, :width]
             for i in range(1, group):
                 own = jnp.where(head == i, block[:, i * width:(i + 1) * width], own)
-            out[first:first + group] = own.astype(jnp.bfloat16).reshape(group, requests, width)
+            out[here, :] = own.astype(jnp.bfloat16)
 
 
 def project(parts, maps, requests):
@@ -193,7 +194,7 @@
     local_heads, rank, width = maps.shape
     return pl.pallas_call(
         functools.partial(project_kernel, count),
-        out_shape=[jax.ShapeDtypeStruct((local_heads, requests, width), jnp.bfloat16)] * count,
+        out_shape=[jax.ShapeDtypeStruct((local_heads * requests, width), jnp.bfloat16)] * count,
         in_specs=[pl.BlockSpec(memory_space=pltpu.VMEM)] * (count + 1),
         out_specs=[pl.BlockSpec(memory_space=pltpu.VMEM)] * count,
         compiler_params=pltpu.CompilerParams(vmem_limit_bytes=24 * 2**20),
@@ -207,26 +208,25 @@
 
 
 def assemble_kernel(owners, *refs):
-    parts, out, sems = refs[:owners], refs[owners], refs[owners + 1]
+    parts, (out, blocks, sem) = refs[:owners], refs[owners:]
     me = lax.axis_index("tp")
-    copies = [
-        pltpu.make_async_copy(part, out.at[me ^ k], sems.at[k])
-        for k, part in zip(order(owners), parts)
-    ]
-    for copy in copies:
-        copy.start()
-    for copy in copies:
-        copy.wait()
-
-
-def assemble(parts):
+    for k, part in zip(order(owners), parts):
+        blocks[me ^ k] = part[...].reshape(blocks.shape[1:])
+    copy = pltpu.make_async_copy(blocks, out, sem)
+    copy.start()
+    copy.wait()
+
+
+def assemble(parts, requests):
     owners = len(parts)
+    rows, width = parts[0].shape
+    shape = (owners, rows // requests, requests, width)
     return pl.pallas_call(
         functools.partial(assemble_kernel, owners),
-        out_shape=pltpu.HBM((owners,) + parts[0].shape, parts[0].dtype),
+        out_shape=pltpu.HBM(shape, parts[0].dtype),
         in_specs=[pl.BlockSpec(memory_space=pltpu.VMEM)] * owners,
         out_specs=pl.BlockSpec(memory_space=pltpu.HBM),
-        scratch_shapes=[pltpu.SemaphoreType.DMA((owners,))],
+        scratch_shapes=[pltpu.VMEM(shape, parts[0].dtype), pltpu.SemaphoreType.DMA(())],
         compiler_params=pltpu.CompilerParams(vmem_limit_bytes=2 * 2**20),
         name="assemble",
     )(*parts)
@@ -254,7 +254,7 @@
     latents = attend(query, cache, scales, lengths, owners)
     maps = stage(value_up, latents[0])
     values = exchange(project(exchange(latents), maps, query.shape[0]))
-    returned = assemble(values)
+    returned = assemble(values, query.shape[0])
     _, local_heads, requests, width = returned.shape
     returned = returned.reshape(owners * local_heads, requests, width)
     return jnp.swapaxes(returned, 0, 1).reshape(requests, owners * local_heads * width)

time: 18.3 us -> 18.2 us (level); the launches traced: 18.4 us -> 17.9 us
  waiting for transfers between devices: 3.49 us -> 2.36 us
  Pallas kernels: 5.95 us -> 6.84 us
  starting transfers between devices: 8.93 us -> 8.64 us
    ppermute x6, waiting for transfers between devices: 3.49 us -> 2.36 us  [exchange(): lax.ppermute(part, ('grp', 'tp'), pairs(k))]
    pallas_call x1, Pallas kernels: 2.24 us -> 3.13 us  [attend(): pl.pallas_call(functools.partial(attend_kernel, owners), out_shape=[part]...]
    ppermute x6, starting transfers between devices: 8.93 us -> 8.64 us  [exchange(): lax.ppermute(part, ('grp', 'tp'), pairs(k))]
  transfers between devices with their start and end apart: 6 -> 6, of which waited for: 4 -> 3; matrix products, arithmetic and copies ran while one was open for 0% -> 0% of each run, Pallas kernels for 12% -> 12%
where the time goes in v26:
time: 18.2 us; the launch traced here: 17.9 us
  starting transfers between devices  8.64 us (47%)
  Pallas kernels  6.84 us (38%)
  waiting for transfers between devices  2.36 us (13%)
    ppermute x6, starting transfers between devices, exchange(): lax.ppermute(part, ('grp', 'tp'), pairs(k))  8.64 us
    pallas_call x1, Pallas kernels, attend(): pl.pallas_call(functools.partial(attend_kernel, owners), out_shape=[part]...  3.13 us
    ppermute x6, waiting for transfers between devices, exchange(): lax.ppermute(part, ('grp', 'tp'), pairs(k))  2.36 us
    pallas_call x1, Pallas kernels, stage(): pl.pallas_call(stage_kernel, out_shape=jax.ShapeDtypeStruct(maps.shape, m...  2.2 us
    pallas_call x1, Pallas kernels, project(): pl.pallas_call(functools.partial(project_kernel, count), out_shape=[jax.S...  0.83 us
    pallas_call x1, Pallas kernels, assemble(): pl.pallas_call(functools.partial(assemble_kernel, owners), out_shape=pltp...  0.69 us
  transfers between devices with their start and end apart: 6, of which 3 were waited for; matrix products, arithmetic and copies ran while one was open for 0% of the time, Pallas kernels for 12%

profile of v26, /device:TPU:0, one launch (start us, length us, event | category | flops | bytes accessed | tf_op | source)
XLA Modules:
  0.0 17.9 jit_solution(3683712058211622962)
XLA Ops:
  0.0 3.1 %attend.1 = (bf16[64,512]{1,0:T(8,128)(2,1)S(1)}, bf16[64,512]{1,0:T(8,128)(2,1)S(1)}, bf16[64,512]{1,0:T(8,128)(2,1)S(1)}, bf16[64,512]{1,0:T(8,128)(2,1)S(1)}) custom-call(s32[2]{0:T(128)} %lengths_hbm.1, bf16[2,576,128]{2,1,0:T(8,128)(2,1)} %bitcast.8, f32[576]{0:T(1024)} %scales_hbm.1, bf16[2,576,1536]{2,1,0:T(8,128)(2,1)} %bitcast.7), custom_call_target="tpu_custom_call" | custom-call | flops 905969664 | bytes 3538944 | tf_op jit(solution)/shard_map/attend/pallas_call | solution.py:127
  3.1 2.9 %collective-permute-start = (bf16[64,512]{1,0:T(8,128)(2,1)S(1)}, bf16[64,512]{1,0:T(8,128)(2,1)S(1)}, u32[]{:S(2)}, u32[]{:S(2)}) collective-permute-start(bf16[64,512]{1,0:T(8,128)(2,1)S(1)} %get-tuple-element.14), channel_id=1, source_target_pairs={{0,7},{1,6},{2,5},{3,4},{4,3},{5,2},{6,1},{7,0},{8,15},{9,14},{10,... | collective-permute-start | bytes 196616 | tf_op jit(solution)/shard_map/ppermute | solution.py:247
  6.1 1.3 %collective-permute-start.1 = (bf16[64,512]{1,0:T(8,128)(2,1)S(1)}, bf16[64,512]{1,0:T(8,128)(2,1)S(1)}, u32[]{:S(2)}, u32[]{:S(2)}) collective-permute-start(bf16[64,512]{1,0:T(8,128)(2,1)S(1)} %get-tuple-element.15), channel_id=1, source_target_pairs={{0,5},{1,4},{2,7},{3,6},{4,1},{5,0},{6,3},{7,2},{8,13},{9,12},{10,... | collective-permute-start | bytes 196616 | tf_op jit(solution)/shard_map/ppermute | solution.py:247
  7.4 1.0 %collective-permute-start.2 = (bf16[64,512]{1,0:T(8,128)(2,1)S(1)}, bf16[64,512]{1,0:T(8,128)(2,1)S(1)}, u32[]{:S(2)}, u32[]{:S(2)}) collective-permute-start(bf16[64,512]{1,0:T(8,128)(2,1)S(1)} %get-tuple-element.16), channel_id=1, source_target_pairs={{0,6},{1,7},{2,4},{3,5},{4,2},{5,3},{6,0},{7,1},{8,14},{9,15},{10,... | collective-permute-start | bytes 196616 | tf_op jit(solution)/shard_map/ppermute | solution.py:247
  8.3 2.2 %stage.1.refs_4_ = bf16[32,512,128]{2,1,0:T(8,128)(2,1)S(1)} custom-call(bf16[32,512,128]{2,1,0:T(8,128)(2,1)} %maps_hbm.1, bf16[64,512]{1,0:T(8,128)(2,1)S(1)} %get-tuple-element.13.after.refs_0_), custom_call_target="tpu_custom_call" | custom-call | bytes 8388608 | tf_op jit(solution)/shard_map/stage/pallas_call | solution.py:158
  10.5 0.0 collective-permute-done.refs_1_
  10.5 0.0 collective-permute-done.1.refs_2_
  10.5 0.6 %collective-permute-done.2.refs_3_ = bf16[64,512]{1,0:T(8,128)(2,1)S(1)} collective-permute-done((bf16[64,512]{1,0:T(8,128)(2,1)S(1)}, bf16[64,512]{1,0:T(8,128)(2,1)S(1)}, u32[]{:S(2)}, u32[]{:S(2)}) %collective-permute-start.2) | collective-permute-done | bytes 65568 | tf_op jit(solution)/shard_map/ppermute | solution.py:247
  11.2 0.8 %project.1 = (bf16[64,128]{1,0:T(8,128)(2,1)S(1)}, bf16[64,128]{1,0:T(8,128)(2,1)S(1)}, bf16[64,128]{1,0:T(8,128)(2,1)S(1)}, bf16[64,128]{1,0:T(8,128)(2,1)S(1)}) custom-call(bf16[64,512]{1,0:T(8,128)(2,1)S(1)} %get-tuple-element.13.after.refs_0_, bf16[64,512]{1,0:T(8,128)(2,1)S(1)} %collective-permute-done.refs_1_, ...), custom_call_target="tpu_custom_call" | custom-call | flops 33554432 | bytes 4194304 | tf_op jit(solution)/shard_map/project/pallas_call | solution.py:195
  12.0 2.0 %collective-permute-start.3 = (bf16[64,128]{1,0:T(8,128)(2,1)S(1)}, bf16[64,128]{1,0:T(8,128)(2,1)S(1)}, u32[]{:S(2)}, u32[]{:S(2)}) collective-permute-start(bf16[64,128]{1,0:T(8,128)(2,1)S(1)} %get-tuple-element.18), channel_id=1, source_target_pairs={{0,7},{1,6},{2,5},{3,4},{4,3},{5,2},{6,1},{7,0},{8,15},{9,14},{10,... | collective-permute-start | bytes 49160 | tf_op jit(solution)/shard_map/ppermute | solution.py:247
  14.0 0.0 collective-permute-start.4
  14.0 1.4 %collective-permute-start.5 = (bf16[64,128]{1,0:T(8,128)(2,1)S(1)}, bf16[64,128]{1,0:T(8,128)(2,1)S(1)}, u32[]{:S(2)}, u32[]{:S(2)}) collective-permute-start(bf16[64,128]{1,0:T(8,128)(2,1)S(1)} %get-tuple-element.20), channel_id=1, source_target_pairs={{0,6},{1,7},{2,4},{3,5},{4,2},{5,3},{6,0},{7,1},{8,14},{9,15},{10,... | collective-permute-start | bytes 49160 | tf_op jit(solution)/shard_map/ppermute | solution.py:247
  15.5 0.7 %collective-permute-done.3.refs_1_ = bf16[64,128]{1,0:T(8,128)(2,1)S(1)} collective-permute-done((bf16[64,128]{1,0:T(8,128)(2,1)S(1)}, bf16[64,128]{1,0:T(8,128)(2,1)S(1)}, u32[]{:S(2)}, u32[]{:S(2)}) %collective-permute-start.3) | collective-permute-done | bytes 16416 | tf_op jit(solution)/shard_map/ppermute | solution.py:247
  16.1 1.0 %collective-permute-done.4.refs_2_ = bf16[64,128]{1,0:T(8,128)(2,1)S(1)} collective-permute-done((bf16[64,128]{1,0:T(8,128)(2,1)S(1)}, bf16[64,128]{1,0:T(8,128)(2,1)S(1)}, u32[]{:S(2)}, u32[]{:S(2)}) %collective-permute-start.4) | collective-permute-done | bytes 16416 | tf_op jit(solution)/shard_map/ppermute | solution.py:247
  17.2 0.0 collective-permute-done.5.refs_3_
  17.2 0.7 %assemble.1 = bf16[4,32,2,128]{3,2,1,0:T(2,128)(2,1)} custom-call(bf16[64,128]{1,0:T(8,128)(2,1)S(1)} %get-tuple-element.17.refs_0_, bf16[64,128]{1,0:T(8,128)(2,1)S(1)} %collective-permute-done.3.refs_1_, bf16[64,128]{1,0:T(8,128)(2,1)S(1)} %collective-permute-done.4.refs_2_, bf16[64,128]{1,0:T(8,128)(2,1)S(1)} %collective-permute-done.5.refs_3_), custom_call_target="tpu_custom_call" | custom-call | tf_op jit(solution)/shard_map/assemble/pallas_call | solution.py:224
Async XLA Ops:
  3.1 7.4 %collective-permute-start = (bf16[64,512]{1,0:T(8,128)(2,1)S(1)}, bf16[64,512]{1,0:T(8,128)(2,1)S(1)}, u32[]{:S(2)}, u32[]{:S(2)}) collective-permute-start(bf16[64,512]{1,0:T(8,128)(2,1)S(1)} %get-tuple-element.14), channel_id=1, source_target_pairs={{0,7},{1,6},{2,5},{3,4},{4,3},{5,2},{6,1},{7,0},{8,15},{9,14},{10,... | collective-permute-start | bytes 196616 | tf_op jit(solution)/shard_map/ppermute | solution.py:247
  6.1 4.5 %collective-permute-start.1 = (bf16[64,512]{1,0:T(8,128)(2,1)S(1)}, bf16[64,512]{1,0:T(8,128)(2,1)S(1)}, u32[]{:S(2)}, u32[]{:S(2)}) collective-permute-start(bf16[64,512]{1,0:T(8,128)(2,1)S(1)} %get-tuple-element.15), channel_id=1, source_target_pairs={{0,5},{1,4},{2,7},{3,6},{4,1},{5,0},{6,3},{7,2},{8,13},{9,12},{10,... | collective-permute-start | bytes 196616 | tf_op jit(solution)/shard_map/ppermute | solution.py:247
  7.4 3.8 %collective-permute-start.2 = (bf16[64,512]{1,0:T(8,128)(2,1)S(1)}, bf16[64,512]{1,0:T(8,128)(2,1)S(1)}, u32[]{:S(2)}, u32[]{:S(2)}) collective-permute-start(bf16[64,512]{1,0:T(8,128)(2,1)S(1)} %get-tuple-element.16), channel_id=1, source_target_pairs={{0,6},{1,7},{2,4},{3,5},{4,2},{5,3},{6,0},{7,1},{8,14},{9,15},{10,... | collective-permute-start | bytes 196616 | tf_op jit(solution)/shard_map/ppermute | solution.py:247
  12.0 4.1 %collective-permute-start.3 = (bf16[64,128]{1,0:T(8,128)(2,1)S(1)}, bf16[64,128]{1,0:T(8,128)(2,1)S(1)}, u32[]{:S(2)}, u32[]{:S(2)}) collective-permute-start(bf16[64,128]{1,0:T(8,128)(2,1)S(1)} %get-tuple-element.18), channel_id=1, source_target_pairs={{0,7},{1,6},{2,5},{3,4},{4,3},{5,2},{6,1},{7,0},{8,15},{9,14},{10,... | collective-permute-start | bytes 49160 | tf_op jit(solution)/shard_map/ppermute | solution.py:247
  14.0 3.2 %collective-permute-start.4 = (bf16[64,128]{1,0:T(8,128)(2,1)S(1)}, bf16[64,128]{1,0:T(8,128)(2,1)S(1)}, u32[]{:S(2)}, u32[]{:S(2)}) collective-permute-start(bf16[64,128]{1,0:T(8,128)(2,1)S(1)} %get-tuple-element.19), channel_id=1, source_target_pairs={{0,5},{1,4},{2,7},{3,6},{4,1},{5,0},{6,3},{7,2},{8,13},{9,12},{10,... | collective-permute-start | bytes 49160 | tf_op jit(solution)/shard_map/ppermute | solution.py:247
  14.0 3.2 %collective-permute-start.5 = (bf16[64,128]{1,0:T(8,128)(2,1)S(1)}, bf16[64,128]{1,0:T(8,128)(2,1)S(1)}, u32[]{:S(2)}, u32[]{:S(2)}) collective-permute-start(bf16[64,128]{1,0:T(8,128)(2,1)S(1)} %get-tuple-element.20), channel_id=1, source_target_pairs={{0,6},{1,7},{2,4},{3,5},{4,2},{5,3},{6,0},{7,1},{8,14},{9,15},{10,... | collective-permute-start | bytes 49160 | tf_op jit(solution)/shard_map/ppermute | solution.py:247

commit v27 on v24

--- a/solution.py
+++ b/solution.py
@@ -66,21 +66,20 @@
             part = jnp.where(place < lengths[r], part, -jnp.inf)
         return part
 
-    def weigh(part, r, b):
+    def weigh(part, r, b, before):
         top = jnp.max(part, axis=1, keepdims=True)
+        if before is not None:
+            top = jnp.maximum(top, before[0])
         weight = jnp.exp2((part - top) * EXP2_SCALE)
         total = jnp.sum(weight, axis=1, keepdims=True)
         mixture = lax.dot_general(
             weight.astype(jnp.bfloat16), keys[r, :rank, b * block:(b + 1) * block],
             (((1,), (1,)), ((), ())), preferred_element_type=jnp.float32,
         )
+        if before is not None:
+            fade = jnp.exp2((before[0] - top) * EXP2_SCALE)
+            total, mixture = before[1] * fade + total, before[2] * fade + mixture
         return top, total, mixture
-
-    def merge(one, two):
-        top = jnp.maximum(one[0], two[0])
-        first = jnp.exp2((one[0] - top) * EXP2_SCALE)
-        second = jnp.exp2((two[0] - top) * EXP2_SCALE)
-        return (top,) + tuple(x * first + y * second for x, y in zip(one[1:], two[1:]))
 
     def finish(r, total, mixture):
         latent = mixture * (1.0 / total) * scale_row[:, :rank]
@@ -95,8 +94,7 @@
         state = {}
         for i, (r, b, n) in enumerate(units):
             ahead = score(scaled, *units[i + 1]) if i + 1 < len(units) else None
-            done = weigh(part, r, b)
-            state[r] = merge(state[r], done) if b else done
+            state[r] = weigh(part, r, b, state.get(r))
             if b == n - 1:
                 finish(r, *state[r][1:])
             part = ahead

time: 18.3 us -> 18.3 us (level); the launches traced: 18.4 us -> 18 us
  starting transfers between devices: 8.93 us -> 6.22 us
  Pallas kernels: 5.95 us -> 7.67 us
  waiting for transfers between devices: 3.49 us -> 4.04 us
    ppermute x6, starting transfers between devices: 8.93 us -> 6.22 us  [exchange(): lax.ppermute(part, ('grp', 'tp'), pairs(k))]
    pallas_call x1, Pallas kernels: 2.24 us -> 3.96 us  [attend(): pl.pallas_call(functools.partial(attend_kernel, owners), out_shape=[part]...]
    ppermute x6, waiting for transfers between devices: 3.49 us -> 4.04 us  [exchange(): lax.ppermute(part, ('grp', 'tp'), pairs(k))]
  transfers between devices with their start and end apart: 6 -> 6, of which waited for: 4 -> 5; matrix products, arithmetic and copies ran while one was open for 0% -> 0% of each run, Pallas kernels for 12% -> 12%
where the time goes in v27:
time: 18.3 us; the launch traced here: 18 us
  Pallas kernels  7.67 us (42%)
  starting transfers between devices  6.22 us (34%)
  waiting for transfers between devices  4.04 us (22%)
    ppermute x6, starting transfers between devices, exchange(): lax.ppermute(part, ('grp', 'tp'), pairs(k))  6.22 us
    ppermute x6, waiting for transfers between devices, exchange(): lax.ppermute(part, ('grp', 'tp'), pairs(k))  4.04 us
    pallas_call x1, Pallas kernels, attend(): pl.pallas_call(functools.partial(attend_kernel, owners), out_shape=[part]...  3.96 us
    pallas_call x1, Pallas kernels, stage(): pl.pallas_call(stage_kernel, out_shape=jax.ShapeDtypeStruct(maps.shape, m...  2.2 us
    pallas_call x1, Pallas kernels, project(): pl.pallas_call(functools.partial(project_kernel, count), out_shape=[jax.S...  0.86 us
    pallas_call x1, Pallas kernels, assemble(): pl.pallas_call(functools.partial(assemble_kernel, owners), out_shape=pltp...  0.66 us
  transfers between devices with their start and end apart: 6, of which 5 were waited for; matrix products, arithmetic and copies ran while one was open for 0% of the time, Pallas kernels for 12%

profile of v27, /device:TPU:0, one launch (start us, length us, event | category | flops | bytes accessed | tf_op | source)
XLA Modules:
  0.0 18.0 jit_solution(16329641104155946404)
XLA Ops:
  0.0 4.0 %attend.1 = (bf16[64,512]{1,0:T(8,128)(2,1)S(1)}, bf16[64,512]{1,0:T(8,128)(2,1)S(1)}, bf16[64,512]{1,0:T(8,128)(2,1)S(1)}, bf16[64,512]{1,0:T(8,128)(2,1)S(1)}) custom-call(s32[2]{0:T(128)} %lengths_hbm.1, bf16[2,576,128]{2,1,0:T(8,128)(2,1)} %bitcast.8, f32[576]{0:T(1024)} %scales_hbm.1, bf16[2,576,1536]{2,1,0:T(8,128)(2,1)} %bitcast.7), custom_call_target="tpu_custom_call" | custom-call | flops 905969664 | bytes 3538944 | tf_op jit(solution)/shard_map/attend/pallas_call | solution.py:125
  4.0 2.5 %collective-permute-start = (bf16[64,512]{1,0:T(8,128)(2,1)S(1)}, bf16[64,512]{1,0:T(8,128)(2,1)S(1)}, u32[]{:S(2)}, u32[]{:S(2)}) collective-permute-start(bf16[64,512]{1,0:T(8,128)(2,1)S(1)} %get-tuple-element.14), channel_id=1, source_target_pairs={{0,7},{1,6},{2,5},{3,4},{4,3},{5,2},{6,1},{7,0},{8,15},{9,14},{10,... | collective-permute-start | bytes 196616 | tf_op jit(solution)/shard_map/ppermute | solution.py:245
  6.5 0.8 %collective-permute-start.1 = (bf16[64,512]{1,0:T(8,128)(2,1)S(1)}, bf16[64,512]{1,0:T(8,128)(2,1)S(1)}, u32[]{:S(2)}, u32[]{:S(2)}) collective-permute-start(bf16[64,512]{1,0:T(8,128)(2,1)S(1)} %get-tuple-element.15), channel_id=1, source_target_pairs={{0,5},{1,4},{2,7},{3,6},{4,1},{5,0},{6,3},{7,2},{8,13},{9,12},{10,... | collective-permute-start | bytes 196616 | tf_op jit(solution)/shard_map/ppermute | solution.py:245
  7.3 0.0 collective-permute-start.2
  7.4 2.2 %stage.1.refs_4_ = bf16[32,512,128]{2,1,0:T(8,128)(2,1)S(1)} custom-call(bf16[32,512,128]{2,1,0:T(8,128)(2,1)} %maps_hbm.1, bf16[64,512]{1,0:T(8,128)(2,1)S(1)} %get-tuple-element.13.after.refs_0_), custom_call_target="tpu_custom_call" | custom-call | bytes 8388608 | tf_op jit(solution)/shard_map/stage/pallas_call | solution.py:156
  9.6 0.0 collective-permute-done.refs_1_
  9.6 1.3 %collective-permute-done.1.refs_2_ = bf16[64,512]{1,0:T(8,128)(2,1)S(1)} collective-permute-done((bf16[64,512]{1,0:T(8,128)(2,1)S(1)}, bf16[64,512]{1,0:T(8,128)(2,1)S(1)}, u32[]{:S(2)}, u32[]{:S(2)}) %collective-permute-start.1) | collective-permute-done | bytes 65568 | tf_op jit(solution)/shard_map/ppermute | solution.py:245
  10.9 0.1 collective-permute-done.2.refs_3_
  11.0 0.9 %project.1 = (bf16[32,2,128]{2,1,0:T(2,128)(2,1)S(1)}, bf16[32,2,128]{2,1,0:T(2,128)(2,1)S(1)}, bf16[32,2,128]{2,1,0:T(2,128)(2,1)S(1)}, bf16[32,2,128]{2,1,0:T(2,128)(2,1)S(1)}) custom-call(bf16[64,512]{1,0:T(8,128)(2,1)S(1)} %get-tuple-element.13.after.refs_0_, bf16[64,512]{1,0:T(8,128)(2,1)S(1)} %collective-permute-done.refs_1_, ...), custom_call_target="tpu_custom_call" | custom-call | flops 33554432 | bytes 4194304 | tf_op jit(solution)/shard_map/project/pallas_call | solution.py:192
  11.9 1.8 %collective-permute-start.3 = (bf16[32,2,128]{2,1,0:T(2,128)(2,1)S(1)}, bf16[32,2,128]{2,1,0:T(2,128)(2,1)S(1)}, u32[]{:S(2)}, u32[]{:S(2)}) collective-permute-start(bf16[32,2,128]{2,1,0:T(2,128)(2,1)S(1)} %get-tuple-element.18), channel_id=1, source_target_pairs={{0,7},{1,6},{2,5},{3,4},{4,3},{5,2},{6,1},{7,0},{8,15},{9,14},{10,... | collective-permute-start | bytes 49160 | tf_op jit(solution)/shard_map/ppermute | solution.py:245
  13.7 0.5 %collective-permute-start.4 = (bf16[32,2,128]{2,1,0:T(2,128)(2,1)S(1)}, bf16[32,2,128]{2,1,0:T(2,128)(2,1)S(1)}, u32[]{:S(2)}, u32[]{:S(2)}) collective-permute-start(bf16[32,2,128]{2,1,0:T(2,128)(2,1)S(1)} %get-tuple-element.19), channel_id=1, source_target_pairs={{0,5},{1,4},{2,7},{3,6},{4,1},{5,0},{6,3},{7,2},{8,13},{9,12},{10,... | collective-permute-start | bytes 49160 | tf_op jit(solution)/shard_map/ppermute | solution.py:245
  14.1 0.6 %collective-permute-start.5 = (bf16[32,2,128]{2,1,0:T(2,128)(2,1)S(1)}, bf16[32,2,128]{2,1,0:T(2,128)(2,1)S(1)}, u32[]{:S(2)}, u32[]{:S(2)}) collective-permute-start(bf16[32,2,128]{2,1,0:T(2,128)(2,1)S(1)} %get-tuple-element.20), channel_id=1, source_target_pairs={{0,6},{1,7},{2,4},{3,5},{4,2},{5,3},{6,0},{7,1},{8,14},{9,15},{10,... | collective-permute-start | bytes 49160 | tf_op jit(solution)/shard_map/ppermute | solution.py:245
  14.7 1.3 %collective-permute-done.3.refs_1_ = bf16[32,2,128]{2,1,0:T(2,128)(2,1)S(1)} collective-permute-done((bf16[32,2,128]{2,1,0:T(2,128)(2,1)S(1)}, bf16[32,2,128]{2,1,0:T(2,128)(2,1)S(1)}, u32[]{:S(2)}, u32[]{:S(2)}) %collective-permute-start.3) | collective-permute-done | bytes 16416 | tf_op jit(solution)/shard_map/ppermute | solution.py:245
  16.1 0.8 %collective-permute-done.4.refs_2_ = bf16[32,2,128]{2,1,0:T(2,128)(2,1)S(1)} collective-permute-done((bf16[32,2,128]{2,1,0:T(2,128)(2,1)S(1)}, bf16[32,2,128]{2,1,0:T(2,128)(2,1)S(1)}, u32[]{:S(2)}, u32[]{:S(2)}) %collective-permute-start.4) | collective-permute-done | bytes 16416 | tf_op jit(solution)/shard_map/ppermute | solution.py:245
  16.8 0.5 %collective-permute-done.5.refs_3_ = bf16[32,2,128]{2,1,0:T(2,128)(2,1)S(1)} collective-permute-done((bf16[32,2,128]{2,1,0:T(2,128)(2,1)S(1)}, bf16[32,2,128]{2,1,0:T(2,128)(2,1)S(1)}, u32[]{:S(2)}, u32[]{:S(2)}) %collective-permute-start.5) | collective-permute-done | bytes 16416 | tf_op jit(solution)/shard_map/ppermute | solution.py:245
  17.3 0.7 %assemble.1 = bf16[4,32,2,128]{3,2,1,0:T(2,128)(2,1)} custom-call(bf16[32,2,128]{2,1,0:T(2,128)(2,1)S(1)} %get-tuple-element.17.refs_0_, bf16[32,2,128]{2,1,0:T(2,128)(2,1)S(1)} %collective-permute-done.3.refs_1_, bf16[32,2,128]{2,1,0:T(2,128)(2,1)S(1)} %collective-permute-done.4.refs_2_, bf16[32,2,128]{2,1,0:T(2,128)(2,1)S(1)} %collective-permute-done.5.refs_3_), custom_call_target="tpu_custom_call" | custom-call | tf_op jit(solution)/shard_map/assemble/pallas_call | solution.py:222
Async XLA Ops:
  4.0 5.6 %collective-permute-start = (bf16[64,512]{1,0:T(8,128)(2,1)S(1)}, bf16[64,512]{1,0:T(8,128)(2,1)S(1)}, u32[]{:S(2)}, u32[]{:S(2)}) collective-permute-start(bf16[64,512]{1,0:T(8,128)(2,1)S(1)} %get-tuple-element.14), channel_id=1, source_target_pairs={{0,7},{1,6},{2,5},{3,4},{4,3},{5,2},{6,1},{7,0},{8,15},{9,14},{10,... | collective-permute-start | bytes 196616 | tf_op jit(solution)/shard_map/ppermute | solution.py:245
  6.5 4.4 %collective-permute-start.1 = (bf16[64,512]{1,0:T(8,128)(2,1)S(1)}, bf16[64,512]{1,0:T(8,128)(2,1)S(1)}, u32[]{:S(2)}, u32[]{:S(2)}) collective-permute-start(bf16[64,512]{1,0:T(8,128)(2,1)S(1)} %get-tuple-element.15), channel_id=1, source_target_pairs={{0,5},{1,4},{2,7},{3,6},{4,1},{5,0},{6,3},{7,2},{8,13},{9,12},{10,... | collective-permute-start | bytes 196616 | tf_op jit(solution)/shard_map/ppermute | solution.py:245
  7.3 3.7 %collective-permute-start.2 = (bf16[64,512]{1,0:T(8,128)(2,1)S(1)}, bf16[64,512]{1,0:T(8,128)(2,1)S(1)}, u32[]{:S(2)}, u32[]{:S(2)}) collective-permute-start(bf16[64,512]{1,0:T(8,128)(2,1)S(1)} %get-tuple-element.16), channel_id=1, source_target_pairs={{0,6},{1,7},{2,4},{3,5},{4,2},{5,3},{6,0},{7,1},{8,14},{9,15},{10,... | collective-permute-start | bytes 196616 | tf_op jit(solution)/shard_map/ppermute | solution.py:245
  11.9 4.2 %collective-permute-start.3 = (bf16[32,2,128]{2,1,0:T(2,128)(2,1)S(1)}, bf16[32,2,128]{2,1,0:T(2,128)(2,1)S(1)}, u32[]{:S(2)}, u32[]{:S(2)}) collective-permute-start(bf16[32,2,128]{2,1,0:T(2,128)(2,1)S(1)} %get-tuple-element.18), channel_id=1, source_target_pairs={{0,7},{1,6},{2,5},{3,4},{4,3},{5,2},{6,1},{7,0},{8,15},{9,14},{10,... | collective-permute-start | bytes 49160 | tf_op jit(solution)/shard_map/ppermute | solution.py:245
  13.7 3.2 %collective-permute-start.4 = (bf16[32,2,128]{2,1,0:T(2,128)(2,1)S(1)}, bf16[32,2,128]{2,1,0:T(2,128)(2,1)S(1)}, u32[]{:S(2)}, u32[]{:S(2)}) collective-permute-start(bf16[32,2,128]{2,1,0:T(2,128)(2,1)S(1)} %get-tuple-element.19), channel_id=1, source_target_pairs={{0,5},{1,4},{2,7},{3,6},{4,1},{5,0},{6,3},{7,2},{8,13},{9,12},{10,... | collective-permute-start | bytes 49160 | tf_op jit(solution)/shard_map/ppermute | solution.py:245
  14.1 3.2 %collective-permute-start.5 = (bf16[32,2,128]{2,1,0:T(2,128)(2,1)S(1)}, bf16[32,2,128]{2,1,0:T(2,128)(2,1)S(1)}, u32[]{:S(2)}, u32[]{:S(2)}) collective-permute-start(bf16[32,2,128]{2,1,0:T(2,128)(2,1)S(1)} %get-tuple-element.20), channel_id=1, source_target_pairs={{0,6},{1,7},{2,4},{3,5},{4,2},{5,3},{6,0},{7,1},{8,14},{9,15},{10,... | collective-permute-start | bytes 49160 | tf_op jit(solution)/shard_map/ppermute | solution.py:245
